TPU v7x, 32 devices: a whole 2x2x4 slice. The times are simulated.
32 devices in a mesh: fsdp: 16 (over z, y, core), tp: 2 (over x).
Axes of the slice: x: 2, y: 2, z: 4, core: 2. Of those that a mesh axis runs over, the one named last changes fastest.
Arguments:
- tokens: bfloat16 [4096, 2304], P(('fsdp', 'tp')), may hold values from -6 to 6
- seg_lengths: int32 [16, 13], P('fsdp'), may hold values from 1 to 64, 256 in all within a row
- parents: int32 [16, 13], P('fsdp'), may hold values from 0 to 11, as said below
- attn_gain: float32 [2304], replicated, may hold values from 0.1 to 1.9
- w_query: bfloat16 [2304, 2048], P('fsdp', 'tp'), may hold values from -0.1875 to 0.1875
- w_key: bfloat16 [2304, 1024], P('fsdp', 'tp'), may hold values from -0.1875 to 0.1875
- w_value: bfloat16 [2304, 1024], P('fsdp', 'tp'), may hold values from -0.125 to 0.125
- w_out: bfloat16 [2048, 2304], P('tp', 'fsdp'), may hold values from -0.125 to 0.125
- attn_post_gain: float32 [2304], replicated, may hold values from 0.1 to 1.9
- ffn_gain: float32 [2304], replicated, may hold values from 0.1 to 1.9
- w_gate: bfloat16 [2304, 9216], P('fsdp', 'tp'), may hold values from -0.125 to 0.125
- w_up: bfloat16 [2304, 9216], P('fsdp', 'tp'), may hold values from -0.125 to 0.125
- w_down: bfloat16 [9216, 2304], P('tp', 'fsdp'), may hold values from -0.0625 to 0.0625
- ffn_post_gain: float32 [2304], replicated, may hold values from 0.1 to 1.9
- out_grad: bfloat16 [4096, 2304], P(('fsdp', 'tp')), may hold values from -6 to 6
Outputs:
- mixed: bfloat16 [4096, 2304], P(('fsdp', 'tp'))
- grad_tokens: float32 [4096, 2304], P(('fsdp', 'tp'))
- grad_attn_gain: float32 [2304], P('fsdp')
- grad_query: float32 [2304, 2048], P('fsdp', 'tp')
- grad_key: float32 [2304, 1024], P('fsdp', 'tp')
- grad_value: float32 [2304, 1024], P('fsdp', 'tp')
- grad_out: float32 [2048, 2304], P('tp', 'fsdp')
- grad_attn_post_gain: float32 [2304], P('fsdp')
- grad_ffn_gain: float32 [2304], P('fsdp')
- grad_gate: float32 [2304, 9216], P('fsdp', 'tp')
- grad_up: float32 [2304, 9216], P('fsdp', 'tp')
- grad_down: float32 [9216, 2304], P('tp', 'fsdp')
- grad_ffn_post_gain: float32 [2304], P('fsdp')
Inputs may be any that keep to these rules, and one draw needn't show every extreme that they name: `parents`: segment 0 of each tree is its root and its own parent; every other segment's parent is a lower-numbered segment of the same tree; the last segment's parent is the one before it. `seg_lengths`: each tree's 13 lengths add up to 256.
All inputs are finite; a program needn't handle non-finite values.
Results may differ from a plain program's by a relative error of at most 0.015.
The roundings to bfloat16 on the way count: a program that leaves them out, or rounds other values in their place, can miss the bound.
Values may be sent and summed in bfloat16 or wider, within the bound.
No kernel may reach another device: no remote copies, remote signals or barrier semaphores. Data moves between devices by JAX's collectives and lax.ppermute only.
A program may use at most 512 MiB of HBM per device.

v0:
```python
import jax
import jax.numpy as jnp
from jax import lax
from jax.sharding import PartitionSpec as P

HD = 256


NORM_EPS = 1e-06
SOFT_CAP = 50.0
ROPE_BASE = 10000.0
MASK_FILL = -1e30
BLOCK_LIMIT = 512


def tree_tables(lengths_row, parents_row, row_total):
    seg_count = lengths_row.shape[0]
    seg_index = jnp.arange(seg_count, dtype=jnp.int32)
    ancestor = (seg_index[:, None] == seg_index[None, :]) | (
        parents_row[:, None] == seg_index[None, :]
    )
    for repeat in range(seg_count.bit_length()):
        ancestor = jnp.any(ancestor[:, :, None] & ancestor[None, :, :], axis=1)
    seg_ends = jnp.cumsum(lengths_row)
    seg_starts = seg_ends - lengths_row
    token_index = jnp.arange(row_total, dtype=jnp.int32)
    segment = jnp.sum((token_index[:, None] >= seg_ends[None, :]).astype(jnp.int32), axis=1)
    strict = ancestor & (seg_index[:, None] != seg_index[None, :])
    offsets = jnp.sum(jnp.where(strict, lengths_row[None, :], 0), axis=1)
    one_hot = segment[:, None] == seg_index[None, :]
    positions = (
        jnp.sum(jnp.where(one_hot, (offsets - seg_starts)[None, :], 0), axis=1) + token_index
    )
    reached = jnp.any(one_hot[:, :, None] & ancestor[None, :, :], axis=1)
    allowed = jnp.any(reached[:, None, :] & one_hot[None, :, :], axis=2) & (
        token_index[None, :] <= token_index[:, None]
    )
    return (positions, allowed)


def rope_tables(positions, width):
    half_width = width // 2
    frequency = ROPE_BASE ** (-2.0 * jnp.arange(half_width, dtype=jnp.float32) / width)
    angles = positions.astype(jnp.float32)[:, None] * frequency[None, :]
    return (jnp.cos(angles), jnp.sin(angles))


def rotate(values, cosine_table, sine_table):
    half_width = values.shape[-1] // 2
    front_half = values[..., :half_width]
    back_half = values[..., half_width:]
    cos_heads = cosine_table[:, None, :]
    sin_heads = sine_table[:, None, :]
    return jnp.concatenate(
        [
            front_half * cos_heads - back_half * sin_heads,
            back_half * cos_heads + front_half * sin_heads,
        ],
        axis=-1,
    )


def unrotate(values, cosine_table, sine_table):
    half_width = values.shape[-1] // 2
    front_half = values[..., :half_width]
    back_half = values[..., half_width:]
    cos_heads = cosine_table[:, None, :]
    sin_heads = sine_table[:, None, :]
    return jnp.concatenate(
        [
            front_half * cos_heads + back_half * sin_heads,
            back_half * cos_heads - front_half * sin_heads,
        ],
        axis=-1,
    )


def norm_back(grad_unit, unit, inverse):
    return inverse * (grad_unit - unit * jnp.mean(grad_unit * unit, axis=-1, keepdims=True))


def gating(gate_proj, upward):
    return jax.nn.gelu(gate_proj, approximate=True) * upward


def seq_gather(values):
    return lax.all_gather(values, "tp", axis=0, tiled=True)


def seq_scatter(values):
    return lax.psum_scatter(values, "tp", scatter_dimension=0, tiled=True)


def apply_rows(weight, operand):
    return jnp.dot(
        operand,
        lax.all_gather(weight, "fsdp", axis=0, tiled=True),
        preferred_element_type=jnp.float32,
    )


def apply_cols(weight, operand):
    return lax.dot_general(
        operand,
        lax.all_gather(weight, "fsdp", axis=0, tiled=True),
        (((1,), (1,)), ((), ())),
        preferred_element_type=jnp.float32,
    )


def grad_product(operand, cotangent):
    return lax.dot_general(
        operand, cotangent, (((0,), (0,)), ((), ())), preferred_element_type=jnp.float32
    )


def grad_rows(operand, cotangent):
    return lax.psum_scatter(
        grad_product(operand, cotangent), "fsdp", scatter_dimension=0, tiled=True
    )


def block_scores(query_block, key_rows, allowed_block, scaling):
    scores = jnp.einsum("qgrd,kgd->grqk", query_block, key_rows, preferred_element_type=jnp.float32)
    capped = SOFT_CAP * jnp.tanh(scores * scaling / SOFT_CAP)
    masked = jnp.where(allowed_block[None, None], capped, MASK_FILL)
    return (capped, masked)


def attend_forward(query_grid, key_rows, value_rows, allowed):
    total_rows = query_grid.shape[0]
    block_rows = min(BLOCK_LIMIT, total_rows)
    scaling = query_grid.shape[-1] ** (-0.5)
    capped, masked = block_scores(query_grid, key_rows, allowed, scaling)
    highest = jnp.max(masked, axis=-1, keepdims=True)
    weights = jnp.exp(masked - highest)
    totals = jnp.sum(weights, axis=-1, keepdims=True)
    probability = (weights / totals).astype(jnp.bfloat16)
    block_out = jnp.einsum(
        "grqk,kgd->qgrd", probability, value_rows, preferred_element_type=jnp.float32
    )
    pieces = block_out.astype(jnp.bfloat16).reshape(block_rows, -1)
    kept_sums = [highest + jnp.log(totals)]
    return (pieces, kept_sums)


def attend_backward(query_grid, key_rows, value_rows, allowed, kept_sums, grad_grid):
    total_rows = query_grid.shape[0]
    block_rows = min(BLOCK_LIMIT, total_rows)
    scaling = query_grid.shape[-1] ** (-0.5)
    key_grad = jnp.zeros(key_rows.shape, jnp.float32)
    value_grad = jnp.zeros(value_rows.shape, jnp.float32)
    query_pieces = []
    for block_number, first_row in enumerate(range(0, total_rows, block_rows)):
        capped, masked = block_scores(query_grid, key_rows, allowed, scaling)
        probability = jnp.exp(masked - kept_sums[block_number])
        prob_low = probability.astype(jnp.bfloat16)
        grad_prob = jnp.einsum(
            "qgrd,kgd->grqk", grad_grid, value_rows, preferred_element_type=jnp.float32
        )
        inner = jnp.sum(probability * grad_prob, axis=-1, keepdims=True)
        grad_cap = probability * (grad_prob - inner)
        tanh_value = capped / SOFT_CAP
        grad_score = (grad_cap * scaling * (1.0 - tanh_value * tanh_value)).astype(jnp.bfloat16)
        query_pieces.append(
            jnp.einsum("grqk,kgd->qgrd", grad_score, key_rows, preferred_element_type=jnp.float32)
        )
        key_grad = jnp.einsum(
            "grqk,qgrd->kgd", grad_score, query_grid, preferred_element_type=jnp.float32
        )
        value_grad = jnp.einsum(
            "grqk,qgrd->kgd", prob_low, grad_grid, preferred_element_type=jnp.float32
        )
    return (query_pieces[0], key_grad, value_grad)


def on_device(
    tokens,
    seg_lengths,
    parents,
    attn_gain,
    w_query,
    w_key,
    w_value,
    w_out,
    attn_post_gain,
    ffn_gain,
    w_gate,
    w_up,
    w_down,
    ffn_post_gain,
    out_grad,
):
    local_rows = tokens.shape[0]
    group_rows = local_rows * lax.axis_size("tp")
    head_size = HD
    head_cols = w_query.shape[1]
    kv_cols = w_key.shape[1]
    heads_here = head_cols // head_size
    kv_here = kv_cols // head_size
    group_size = heads_here // kv_here
    ff_here = w_gate.shape[1]
    positions, allowed = tree_tables(seg_lengths[0], parents[0], group_rows)
    cosine_table, sine_table = rope_tables(positions, head_size)
    qkv_weight = jnp.concatenate([w_query, w_key, w_value], axis=1)
    out_weight = w_out.T
    gate_up_weight = jnp.concatenate([w_gate, w_up], axis=1)
    down_weight = w_down.T
    state_in = tokens.astype(jnp.float32)
    inverse_one = lax.rsqrt(jnp.mean(state_in * state_in, axis=-1, keepdims=True) + NORM_EPS)
    unit_one = state_in * inverse_one
    normed_one_all = seq_gather((unit_one * attn_gain).astype(jnp.bfloat16))
    qkv_proj = apply_rows(qkv_weight, normed_one_all)
    queries = rotate(
        qkv_proj[:, :head_cols].reshape(group_rows, heads_here, head_size), cosine_table, sine_table
    ).astype(jnp.bfloat16)
    key_rows = rotate(
        qkv_proj[:, head_cols : head_cols + kv_cols].reshape(group_rows, kv_here, head_size),
        cosine_table,
        sine_table,
    ).astype(jnp.bfloat16)
    value_rows = (
        qkv_proj[:, head_cols + kv_cols :]
        .astype(jnp.bfloat16)
        .reshape(group_rows, kv_here, head_size)
    )
    query_grid = queries.reshape(group_rows, kv_here, group_size, head_size)
    attended, kept_sums = attend_forward(query_grid, key_rows, value_rows, allowed)
    branch = seq_scatter(apply_cols(out_weight, attended))
    inverse_two = lax.rsqrt(jnp.mean(branch * branch, axis=-1, keepdims=True) + NORM_EPS)
    unit_two = branch * inverse_two
    hidden = state_in + unit_two * attn_post_gain
    inverse_three = lax.rsqrt(jnp.mean(hidden * hidden, axis=-1, keepdims=True) + NORM_EPS)
    unit_three = hidden * inverse_three
    normed_two_all = seq_gather((unit_three * ffn_gain).astype(jnp.bfloat16))
    gate_up = apply_rows(gate_up_weight, normed_two_all)
    activated, gating_pull = jax.vjp(gating, gate_up[:, :ff_here], gate_up[:, ff_here:])
    activated_low = activated.astype(jnp.bfloat16)
    ffn_out = seq_scatter(apply_cols(down_weight, activated_low))
    inverse_four = lax.rsqrt(jnp.mean(ffn_out * ffn_out, axis=-1, keepdims=True) + NORM_EPS)
    unit_four = ffn_out * inverse_four
    mixed = (hidden + unit_four * ffn_post_gain).astype(jnp.bfloat16)
    out_cotan = out_grad.astype(jnp.float32)
    gain_four_part = jnp.sum(out_cotan * unit_four, axis=0)
    grad_ffn_all = seq_gather(
        norm_back(out_cotan * ffn_post_gain, unit_four, inverse_four).astype(jnp.bfloat16)
    )
    grad_act = apply_rows(down_weight, grad_ffn_all)
    grad_down_rows = grad_rows(grad_ffn_all, activated_low)
    grad_gate_proj, grad_upward = gating_pull(grad_act)
    grad_gate_up = jnp.concatenate([grad_gate_proj, grad_upward], axis=1).astype(jnp.bfloat16)
    normed_two_part = apply_cols(gate_up_weight, grad_gate_up)
    grad_gate_both = grad_rows(normed_two_all, grad_gate_up)
    grad_normed_two = seq_scatter(normed_two_part)
    gain_three_part = jnp.sum(grad_normed_two * unit_three, axis=0)
    grad_hidden = out_cotan + norm_back(grad_normed_two * ffn_gain, unit_three, inverse_three)
    gain_two_part = jnp.sum(grad_hidden * unit_two, axis=0)
    grad_branch_all = seq_gather(
        norm_back(grad_hidden * attn_post_gain, unit_two, inverse_two).astype(jnp.bfloat16)
    )
    grad_attended = apply_rows(out_weight, grad_branch_all).astype(jnp.bfloat16)
    grad_out_rows = grad_rows(grad_branch_all, attended)
    grad_grid = grad_attended.reshape(group_rows, kv_here, group_size, head_size)
    query_grad, key_grad, value_grad = attend_backward(
        query_grid, key_rows, value_rows, allowed, kept_sums, grad_grid
    )
    query_back = (
        unrotate(query_grad.reshape(group_rows, heads_here, head_size), cosine_table, sine_table)
        .astype(jnp.bfloat16)
        .reshape(group_rows, head_cols)
    )
    key_back = (
        unrotate(key_grad, cosine_table, sine_table)
        .astype(jnp.bfloat16)
        .reshape(group_rows, kv_cols)
    )
    value_back = value_grad.astype(jnp.bfloat16).reshape(group_rows, kv_cols)
    grad_qkv = jnp.concatenate([query_back, key_back, value_back], axis=1)
    normed_one_part = apply_cols(qkv_weight, grad_qkv)
    grad_qkv_rows = grad_rows(normed_one_all, grad_qkv)
    grad_normed_one = seq_scatter(normed_one_part)
    gain_one_part = jnp.sum(grad_normed_one * unit_one, axis=0)
    grad_tokens = grad_hidden + norm_back(grad_normed_one * attn_gain, unit_one, inverse_one)
    gain_stack = jnp.stack([gain_one_part, gain_two_part, gain_three_part, gain_four_part], axis=0)
    gain_total = lax.psum(gain_stack, ("fsdp", "tp"))
    width_here = tokens.shape[1] // lax.axis_size("fsdp")
    gain_mine = lax.dynamic_slice_in_dim(
        gain_total, lax.axis_index("fsdp") * width_here, width_here, 1
    )
    return (
        mixed,
        grad_tokens,
        gain_mine[0],
        grad_qkv_rows[:, :head_cols],
        grad_qkv_rows[:, head_cols : head_cols + kv_cols],
        grad_qkv_rows[:, head_cols + kv_cols :],
        grad_out_rows.T,
        gain_mine[1],
        gain_mine[2],
        grad_gate_both[:, :ff_here],
        grad_gate_both[:, ff_here:],
        grad_down_rows.T,
        gain_mine[3],
    )


def solution(mesh):
    return jax.shard_map(
        on_device,
        mesh=mesh,
        in_specs=(
            P(("fsdp", "tp"), None),
            P("fsdp", None),
            P("fsdp", None),
            P(),
            P("fsdp", "tp"),
            P("fsdp", "tp"),
            P("fsdp", "tp"),
            P("tp", "fsdp"),
            P(),
            P(),
            P("fsdp", "tp"),
            P("fsdp", "tp"),
            P("tp", "fsdp"),
            P(),
            P(("fsdp", "tp"), None),
        ),
        out_specs=(
            P(("fsdp", "tp"), None),
            P(("fsdp", "tp"), None),
            P("fsdp"),
            P("fsdp", "tp"),
            P("fsdp", "tp"),
            P("fsdp", "tp"),
            P("tp", "fsdp"),
            P("fsdp"),
            P("fsdp"),
            P("fsdp", "tp"),
            P("fsdp", "tp"),
            P("tp", "fsdp"),
            P("fsdp"),
        ),
        check_vma=False,
    )
```

profile of v0, /device:TPU:8, one launch (start us, length us, event | category | flops | bytes accessed | tf_op | source)
XLA Modules:
  0.0 2309.9 jit_solution(1951145417426220706)
XLA Ops:
  15.7 19.7 all-gather.9.cloned.1.call-done
  35.4 83.5 %all-gather.11.cloned.1.call-done = bf16[2304,2048]{1,0:T(8,128)(2,1)} async-done(((bf16[144,2048]{1,0:T(8,128)(2,1)}), bf16[2304,2048]{1,0:T(8,128)(2,1)}) %all-gather.11.cloned.1.call-update) | async-done | bytes 9437200 | tf_op jit(solution)/shard_map/all_gather | solution.py:97
  118.8 5.5 fusion.108
  128.1 45.4 %all-gather.13.cloned.1.call-done = bf16[2304,1024]{1,0:T(8,128)(2,1)} async-done(((bf16[144,1024]{1,0:T(8,128)(2,1)}), bf16[2304,1024]{1,0:T(8,128)(2,1)}) %all-gather.13.cloned.1.call-update) | async-done | bytes 4718608 | tf_op jit(solution)/shard_map/all_gather | solution.py:105
  173.6 5.2 fusion.109
  178.8 33.3 %reduce-scatter.9.cloned.1.call-done = f32[128,2304]{1,0:T(8,128)} async-done(((f32[256,2304]{1,0:T(8,128)}), f32[128,2304]{1,0:T(8,128)}) %reduce-scatter.9.cloned.1.call-update) | async-done | bytes 1179664 | tf_op jit(solution)/shard_map/reduce_scatter | solution.py:91
  221.0 18.4 all-gather.15.cloned.1.call-done
  239.4 212.2 %all-gather.17.cloned.1.call-done = bf16[2304,9216]{1,0:T(8,128)(2,1)} async-done(((bf16[144,9216]{1,0:T(8,128)(2,1)}), bf16[2304,9216]{1,0:T(8,128)(2,1)}) %all-gather.17.cloned.1.call-update) | async-done | bytes 42467344 | tf_op jit(solution)/shard_map/all_gather | solution.py:97
  451.6 22.8 fusion.110
  474.4 4.8 multiply_convert_fusion.1
  479.2 84.2 %all-gather.19.cloned.1.call-done = bf16[2304,4608]{1,0:T(8,128)(2,1)} async-done(((bf16[144,4608]{1,0:T(8,128)(2,1)}), bf16[2304,4608]{1,0:T(8,128)(2,1)}) %all-gather.19.cloned.1.call-update) | async-done | bytes 21233680 | tf_op jit(solution)/shard_map/all_gather | solution.py:105
  563.4 11.4 fusion.111
  574.9 34.8 %reduce-scatter.11.cloned.1.call-done = f32[128,2304]{1,0:T(8,128)} async-done(((f32[256,2304]{1,0:T(8,128)}), f32[128,2304]{1,0:T(8,128)}) %reduce-scatter.11.cloned.1.call-update) | async-done | bytes 1179664 | tf_op jit(solution)/shard_map/reduce_scatter | solution.py:91
  615.2 22.7 all-gather.21.cloned.1.call-done
  637.9 14.6 fusion.7
  654.0 19.0 fusion.9
  673.1 34.8 %reduce-scatter.13.cloned.1.call-done = f32[128,2304]{1,0:T(8,128)} async-done(((f32[256,2304]{1,0:T(8,128)}), f32[128,2304]{1,0:T(8,128)}) %reduce-scatter.13.cloned.1.call-update) | async-done | bytes 1179664 | tf_op jit(solution)/shard_map/reduce_scatter | solution.py:91
  714.1 22.6 all-gather.23.cloned.1.call-done
  736.7 4.1 convolution_convert_fusion
  743.1 3.3 convolution_bitcast_fusion.1
  746.4 3.6 fusion.38
  754.0 7.7 fusion.70
  763.0 8.3 fusion.69
  773.0 31.6 %fusion.8 = f32[2304,9216]{1,0:T(8,128)} fusion(bf16[256,2304]{1,0:T(8,128)(2,1)} %all-gather.15.cloned.1.call-done, bf16[256,4608]{1,0:T(8,128)(2,1)} %copy-done.15, bf16[256,4608]{1,0:T(8,128)(2,1)S(1)} %copy-done.14), kind=kOutput, calls=%fused_computation.15 | convolution fusion | flops 10881073152 | bytes 90832896 | tf_op jit(solution)/shard_map/dot_general | solution.py:112
  806.0 6.5 fusion.112
  814.7 21.9 fusion.113
  839.6 43.9 %psum.7 = f32[4,2304]{1,0:T(4,128)S(1)} all-reduce(f32[4,2304]{1,0:T(4,128)S(1)} %pad_maximum_fusion.13), channel_id=1, replica_groups=mesh['fsdp'=16,'tp'=2] {'fsdp','tp'}, use_global_device_ids=true, to_apply=%region_29.30 | all-reduce | flops 9216 | bytes 73728 | tf_op jit(solution)/shard_map/psum | solution.py:285
  885.5 109.9 %reduce-scatter.17.cloned.1.call-done = f32[144,2048]{1,0:T(8,128)} async-done(((f32[2304,2048]{1,0:T(8,128)}), f32[144,2048]{1,0:T(8,128)}) %reduce-scatter.17.cloned.1.call-update) | async-done | bytes 1179664 | tf_op jit(solution)/shard_map/reduce_scatter | solution.py:118
  999.3 779.2 %reduce-scatter.21.cloned.1.call-done = f32[144,9216]{1,0:T(8,128)} async-done(((f32[2304,9216]{1,0:T(8,128)}), f32[144,9216]{1,0:T(8,128)}) %reduce-scatter.21.cloned.1.call-update) | async-done | bytes 5308432 | tf_op jit(solution)/shard_map/reduce_scatter | solution.py:118
  1778.5 5.3 fusion.103
  1783.7 111.9 %reduce-scatter.19.cloned.1.call-done = f32[144,1024]{1,0:T(8,128)} async-done(((f32[2304,1024]{1,0:T(8,128)}), f32[144,1024]{1,0:T(8,128)}) %reduce-scatter.19.cloned.1.call-update) | async-done | bytes 589840 | tf_op jit(solution)/shard_map/reduce_scatter | solution.py:118
  1895.7 407.4 %reduce-scatter.23.cloned.1.call-done = f32[144,4608]{1,0:T(8,128)} async-done(((f32[2304,4608]{1,0:T(8,128)}), f32[144,4608]{1,0:T(8,128)}) %reduce-scatter.23.cloned.1.call-update) | async-done | bytes 2654224 | tf_op jit(solution)/shard_map/reduce_scatter | solution.py:118
  (219 shorter events, 55.2 us)
Async XLA Ops:
  7.2 6.1 copy-start.53
  7.2 28.1 %all-gather.9.cloned.1.call-start = ((), (), s32[]{:S(2)}) async-start(), calls=%async_computation.8 | async-start | bytes 1769472 | tf_op jit(solution)/shard_map/all_gather | solution.py:87
  11.3 107.6 %all-gather.11.cloned.1.call-start = ((), (), s32[]{:S(2)}) async-start(), calls=%async_computation.9 | async-start | bytes 10027008 | tf_op jit(solution)/shard_map/all_gather | solution.py:97
  12.3 161.3 %all-gather.13.cloned.1.call-start = ((), (), s32[]{:S(2)}) async-start(), calls=%async_computation.10 | async-start | bytes 5013504 | tf_op jit(solution)/shard_map/all_gather | solution.py:105
  13.0 199.2 %reduce-scatter.9.cloned.1.call-start = ((), (), s32[]{:S(2)}) async-start(), calls=%async_computation.11 | async-start | bytes 3538944 | tf_op jit(solution)/shard_map/reduce_scatter | solution.py:91
  14.9 112.0 %copy-start.25 = (pred[256,256]{0,1:T(8,128)(4,1)}, pred[256,256]{0,1:T(8,128)(4,1)S(1)}, u32[]{:S(2)}) copy-start(pred[256,256]{0,1:T(8,128)(4,1)S(1)} %copy.66) | copy-start | bytes 196612
  15.7 110.4 %copy-start.9 = (f32[256,128]{1,0:T(8,128)}, f32[256,128]{1,0:T(8,128)S(1)}, u32[]{:S(2)}) copy-start(f32[256,128]{1,0:T(8,128)S(1)} %get-tuple-element.48) | copy-start | bytes 393220
  15.7 110.4 %copy-start.11 = (f32[256,128]{1,0:T(8,128)}, f32[256,128]{1,0:T(8,128)S(1)}, u32[]{:S(2)}) copy-start(f32[256,128]{1,0:T(8,128)S(1)} %get-tuple-element.49) | copy-start | bytes 393220
  128.1 50.6 %copy-start.22 = (bf16[2,256,2,256]{3,1,2,0:T(8,128)(2,1)}, bf16[2,256,2,256]{3,1,2,0:T(8,128)(2,1)S(1)}, u32[]{:S(2)}) copy-start(bf16[2,256,2,256]{3,1,2,0:T(8,128)(2,1)S(1)} %convolution_convert_fusion.1) | copy-start | bytes 1572868
  178.8 34.9 %copy-start.1 = (bf16[128,2304]{1,0:T(8,128)(2,1)S(1)}, bf16[128,2304]{1,0:T(8,128)(2,1)}, u32[]{:S(2)}) copy-start(bf16[128,2304]{1,0:T(8,128)(2,1)} %param.15) | copy-start | bytes 1769476
  178.8 34.9 %copy-start.37 = (f32[2304]{0:T(1024)S(1)}, f32[2304]{0:T(1024)}, u32[]{:S(2)}) copy-start(f32[2304]{0:T(1024)} %param.23) | copy-start | bytes 27652
  178.8 36.6 %copy-start.36 = (f32[2304]{0:T(1024)S(1)}, f32[2304]{0:T(1024)}, u32[]{:S(2)}) copy-start(f32[2304]{0:T(1024)} %param.24) | copy-start | bytes 27652
  178.8 60.6 %all-gather.15.cloned.1.call-start = ((), (), s32[]{:S(2)}) async-start(), calls=%async_computation.12 | async-start | bytes 1769472 | tf_op jit(solution)/shard_map/all_gather | solution.py:87
  216.4 235.1 %all-gather.17.cloned.1.call-start = ((), (), s32[]{:S(2)}) async-start(), calls=%async_computation.13 | async-start | bytes 45121536 | tf_op jit(solution)/shard_map/all_gather | solution.py:97
  219.7 343.7 %all-gather.19.cloned.1.call-start = ((), (), s32[]{:S(2)}) async-start(), calls=%async_computation.14 | async-start | bytes 22560768 | tf_op jit(solution)/shard_map/all_gather | solution.py:105
  220.4 389.3 %reduce-scatter.11.cloned.1.call-start = ((), (), s32[]{:S(2)}) async-start(), calls=%async_computation.15 | async-start | bytes 3538944 | tf_op jit(solution)/shard_map/reduce_scatter | solution.py:91
  479.1 95.7 %copy-start.4 = (bf16[256,4608]{1,0:T(8,128)(2,1)}, bf16[256,4608]{1,0:T(8,128)(2,1)S(1)}, u32[]{:S(2)}) copy-start(bf16[256,4608]{1,0:T(8,128)(2,1)S(1)} %multiply_convert_fusion.1) | copy-start | bytes 7077892
  574.8 36.4 %copy-start.6 = (bf16[128,2304]{1,0:T(8,128)(2,1)S(1)}, bf16[128,2304]{1,0:T(8,128)(2,1)}, u32[]{:S(2)}) copy-start(bf16[128,2304]{1,0:T(8,128)(2,1)} %param.29) | copy-start | bytes 1769476
  574.8 36.4 %copy-start.42 = (f32[2304]{0:T(1024)S(1)}, f32[2304]{0:T(1024)}, u32[]{:S(2)}) copy-start(f32[2304]{0:T(1024)} %param.28) | copy-start | bytes 27652
  574.8 63.1 %all-gather.21.cloned.1.call-start = ((), (), s32[]{:S(2)}) async-start(), calls=%async_computation.16 | async-start | bytes 1769472 | tf_op jit(solution)/shard_map/all_gather | solution.py:87
  615.0 92.9 %reduce-scatter.13.cloned.1.call-start = ((), (), s32[]{:S(2)}) async-start(), calls=%async_computation.17 | async-start | bytes 3538944 | tf_op jit(solution)/shard_map/reduce_scatter | solution.py:91
  652.5 20.5 copy-start.15
  673.0 34.9 %copy-start.47 = (f32[128]{0:T(128)S(1)}, f32[128]{0:T(128)}, u32[]{:S(2)}) copy-start(f32[128]{0:T(128)} %copy-done.46) | copy-start | bytes 1540
  673.0 37.2 %copy-start = (f32[128,2304]{1,0:T(8,128)S(1)}, f32[128,2304]{1,0:T(8,128)}, u32[]{:S(2)}) copy-start(f32[128,2304]{1,0:T(8,128)} %reduce-scatter.9.cloned.1.call-done) | copy-start | bytes 3538948
  673.0 63.7 %all-gather.23.cloned.1.call-start = ((), (), s32[]{:S(2)}) async-start(), calls=%async_computation.18 | async-start | bytes 1769472 | tf_op jit(solution)/shard_map/all_gather | solution.py:87
  713.8 123.6 %reduce-scatter.15.cloned.1.call-start = ((), (), s32[]{:S(2)}) async-start(), calls=%async_computation.19 | async-start | bytes 3538944 | tf_op jit(solution)/shard_map/reduce_scatter | solution.py:91
  714.1 27.0 %copy-start.20 = (bf16[256,2,256]{2,1,0:T(2,128)(2,1)S(1)}, bf16[256,2,256]{2,1,0:T(2,128)(2,1)}, u32[]{:S(2)}) copy-start(bf16[256,2,256]{2,1,0:T(2,128)(2,1)} %copy-done.19) | copy-start | bytes 786436
  761.8 233.7 %reduce-scatter.17.cloned.1.call-start = ((), (), s32[]{:S(2)}) async-start(), calls=%async_computation.20 | async-start | bytes 20054016 | tf_op jit(solution)/shard_map/reduce_scatter | solution.py:118
  771.3 1007.1 %reduce-scatter.21.cloned.1.call-start = ((), (), s32[]{:S(2)}) async-start(), calls=%async_computation.22 | async-start | bytes 90243072 | tf_op jit(solution)/shard_map/reduce_scatter | solution.py:118
  804.6 1091.1 %reduce-scatter.19.cloned.1.call-start = ((), (), s32[]{:S(2)}) async-start(), calls=%async_computation.21 | async-start | bytes 10027008 | tf_op jit(solution)/shard_map/reduce_scatter | solution.py:118
  812.6 1490.5 %reduce-scatter.23.cloned.1.call-start = ((), (), s32[]{:S(2)}) async-start(), calls=%async_computation.23 | async-start | bytes 45121536 | tf_op jit(solution)/shard_map/reduce_scatter | solution.py:118
  837.7 46.4 %copy-start.7 = (f32[128,2304]{1,0:T(8,128)S(1)}, f32[128,2304]{1,0:T(8,128)}, u32[]{:S(2)}) copy-start(f32[128,2304]{1,0:T(8,128)} %reduce-scatter.15.cloned.1.call-done) | copy-start | bytes 3538948
  (38 other events, 81.8 us)
Sparse Core Ops, SparseCore 0:
  11.4 23.9 all-gather.8
  38.2 80.5 all-gather.10
  121.1 52.4 all-gather.12
  178.9 33.2 reduce-scatter.8
  216.6 22.7 all-gather.14
  241.5 210.0 all-gather.16
  453.3 110.0 all-gather.18
  575.0 34.6 reduce-scatter.10
  615.1 22.7 all-gather.20
  673.1 34.7 reduce-scatter.12
  713.9 22.7 all-gather.22
  761.9 34.6 reduce-scatter.14
  800.7 194.6 reduce-scatter.16
  999.5 778.8 reduce-scatter.20
  1783.5 112.0 reduce-scatter.18
  1900.3 402.7 reduce-scatter.22
where the time goes:
time: 2320 us; the launch traced here: 2310 us
  waiting for transfers between devices  2020 us (87%)
  matrix products  168 us (7%)
  blocking collectives  43.9 us (2%)
  other arithmetic  35.4 us (2%)
  local copies, waits for them, and re-layouts  23.4 us (1%)
    reduce_scatter x4, waiting for transfers between devices, grad_rows(): lax.psum_scatter(grad_product(operand, cotangent), 'fsdp', scatter_dimens...  1410 us
    all_gather x2, waiting for transfers between devices, apply_rows(): lax.all_gather(weight, 'fsdp', axis=0, tiled=True)  296 us
    all_gather x2, waiting for transfers between devices, apply_cols(): lax.all_gather(weight, 'fsdp', axis=0, tiled=True)  130 us
    reduce_scatter x4, waiting for transfers between devices, seq_scatter(): return lax.psum_scatter(values, 'tp', scatter_dimension=0, tiled=True)  103 us
    all_gather x4, waiting for transfers between devices, seq_gather(): return lax.all_gather(values, 'tp', axis=0, tiled=True)  83.5 us
    dot_general x4, matrix products, grad_product(): lax.dot_general(operand, cotangent, (((0,), (0,)), ((), ())), preferred_e...  68.4 us
    dot_general x4, matrix products, apply_rows(): jnp.dot(operand, lax.all_gather(weight, 'fsdp', axis=0, tiled=True), pref...  47 us
  transfers between devices with their start and end apart: 16, of which 15 were waited for; matrix products, arithmetic and copies ran while one was open for 5% of the time, Pallas kernels for 0%

commit v1 on v0

v1 whole, which is shorter than its diff:
```python
import jax
import jax.numpy as jnp
from jax import lax
from jax.sharding import Mesh
from jax.sharding import PartitionSpec as P

HD = 256
NORM_EPS = 1e-06
SOFT_CAP = 50.0
ROPE_BASE = 10000.0
MASK_FILL = -1e30
BF = jnp.bfloat16
F32 = jnp.float32


def tree_tables(lengths_row, parents_row, row_total):
    seg_count = lengths_row.shape[0]
    seg_index = jnp.arange(seg_count, dtype=jnp.int32)
    ancestor = (seg_index[:, None] == seg_index[None, :]) | (
        parents_row[:, None] == seg_index[None, :]
    )
    for repeat in range(seg_count.bit_length()):
        ancestor = jnp.any(ancestor[:, :, None] & ancestor[None, :, :], axis=1)
    seg_ends = jnp.cumsum(lengths_row)
    seg_starts = seg_ends - lengths_row
    token_index = jnp.arange(row_total, dtype=jnp.int32)
    segment = jnp.sum((token_index[:, None] >= seg_ends[None, :]).astype(jnp.int32), axis=1)
    strict = ancestor & (seg_index[:, None] != seg_index[None, :])
    offsets = jnp.sum(jnp.where(strict, lengths_row[None, :], 0), axis=1)
    one_hot = segment[:, None] == seg_index[None, :]
    positions = (
        jnp.sum(jnp.where(one_hot, (offsets - seg_starts)[None, :], 0), axis=1) + token_index
    )
    reached = jnp.any(one_hot[:, :, None] & ancestor[None, :, :], axis=1)
    allowed = jnp.any(reached[:, None, :] & one_hot[None, :, :], axis=2) & (
        token_index[None, :] <= token_index[:, None]
    )
    return (positions, allowed)


def rope_tables(positions, width):
    half_width = width // 2
    frequency = ROPE_BASE ** (-2.0 * jnp.arange(half_width, dtype=F32) / width)
    angles = positions.astype(F32)[:, None] * frequency[None, :]
    return (jnp.cos(angles), jnp.sin(angles))


def rotate(values, cosine_table, sine_table):
    half_width = values.shape[-1] // 2
    front_half = values[..., :half_width]
    back_half = values[..., half_width:]
    cos_heads = cosine_table[:, None, :]
    sin_heads = sine_table[:, None, :]
    return jnp.concatenate(
        [
            front_half * cos_heads - back_half * sin_heads,
            back_half * cos_heads + front_half * sin_heads,
        ],
        axis=-1,
    )


def norm_back(grad_unit, unit, inverse):
    return inverse * (grad_unit - unit * jnp.mean(grad_unit * unit, axis=-1, keepdims=True))


def gating(gate_proj, upward):
    return jax.nn.gelu(gate_proj, approximate=True) * upward


def swap(values, axis, mask):
    size = lax.axis_size(axis)
    return lax.ppermute(values, axis, [(i, i ^ mask) for i in range(size)])


def rows_dot(left, right):
    return lax.dot_general(left, right, (((1,), (0,)), ((), ())), preferred_element_type=F32)


def cols_dot(left, right):
    return lax.dot_general(left, right, (((1,), (1,)), ((), ())), preferred_element_type=F32)


def outer_dot(left, right):
    return lax.dot_general(left, right, (((0,), (0,)), ((), ())), preferred_element_type=F32)


def pair_gather(values, axis):
    mine = lax.axis_index(axis)
    other = swap(values, axis, 1)
    first = jnp.where(mine == 0, values, other)
    second = jnp.where(mine == 0, other, values)
    return jnp.concatenate([first, second], axis=0)


def pair_sum(partial, axis):
    rows = partial.shape[0] // 2
    mine = lax.axis_index(axis)
    sent = lax.dynamic_slice_in_dim(partial, (1 - mine) * rows, rows, 0).astype(BF)
    kept = lax.dynamic_slice_in_dim(partial, mine * rows, rows, 0)
    return kept + swap(sent, axis, 1).astype(F32)


def line_gather(values):
    return jnp.concatenate([values] + [swap(values, "z", k) for k in (1, 2, 3)], axis=0)


def line_sum(partial):
    rows = partial.shape[0] // 4
    total = partial[:rows]
    for k in (1, 2, 3):
        total = total + swap(partial[k * rows : (k + 1) * rows].astype(BF), "z", k).astype(F32)
    return total


def line_exchange(weight):
    rows, parts, count, cols = weight.shape
    here = lax.axis_index("z")
    held = jnp.zeros((count, rows, parts * cols), weight.dtype)
    for k in range(count):
        piece = lax.dynamic_index_in_dim(weight, here ^ k, 2, keepdims=False).reshape(
            rows, parts * cols
        )
        piece = piece if k == 0 else swap(piece, "z", k)
        held = lax.dynamic_update_index_in_dim(held, piece, here ^ k, 0)
    return held.reshape(count * rows, parts * cols)


def attend_forward(query_grid, key_rows, value_rows, allowed):
    total_rows = query_grid.shape[0]
    scaling = query_grid.shape[-1] ** (-0.5)
    scores = jnp.einsum("qgrd,kgd->grqk", query_grid, key_rows, preferred_element_type=F32)
    capped = SOFT_CAP * jnp.tanh(scores * scaling / SOFT_CAP)
    masked = jnp.where(allowed[None, None], capped, MASK_FILL)
    highest = jnp.max(masked, axis=-1, keepdims=True)
    weights = jnp.exp(masked - highest)
    totals = jnp.sum(weights, axis=-1, keepdims=True)
    probability = weights / totals
    prob_low = probability.astype(BF)
    out = jnp.einsum("grqk,kgd->qgrd", prob_low, value_rows, preferred_element_type=F32)
    return (out.astype(BF).reshape(total_rows, -1), capped, probability)


def attend_backward(query_grid, key_rows, value_rows, capped, probability, grad_grid):
    scaling = query_grid.shape[-1] ** (-0.5)
    prob_low = probability.astype(BF)
    grad_prob = jnp.einsum("qgrd,kgd->grqk", grad_grid, value_rows, preferred_element_type=F32)
    inner = jnp.sum(probability * grad_prob, axis=-1, keepdims=True)
    grad_cap = probability * (grad_prob - inner)
    tanh_value = capped / SOFT_CAP
    grad_score = (grad_cap * scaling * (1.0 - tanh_value * tanh_value)).astype(BF)
    query_grad = jnp.einsum("grqk,kgd->qgrd", grad_score, key_rows, preferred_element_type=F32)
    key_grad = jnp.einsum("grqk,qgrd->kgd", grad_score, query_grid, preferred_element_type=F32)
    value_grad = jnp.einsum("grqk,qgrd->kgd", prob_low, grad_grid, preferred_element_type=F32)
    return (query_grad, key_grad, value_grad)


def row_sum(parts, axes):
    return lax.psum_scatter(parts, axes, scatter_dimension=0, tiled=True)


def gain_sum(parts):
    parts = lax.psum(parts, ("z", "y", "c", "x"))
    width = parts.shape[1] // (lax.axis_size("z") * lax.axis_size("y") * lax.axis_size("c"))
    at = (lax.axis_index("c") * lax.axis_size("y") + lax.axis_index("y")) * lax.axis_size(
        "z"
    ) + lax.axis_index("z")
    return lax.dynamic_slice_in_dim(parts, at * width, width, 1)


def on_device(
    tokens,
    seg_lengths,
    parents,
    attn_gain,
    w_query,
    w_key,
    w_value,
    w_out,
    attn_post_gain,
    ffn_gain,
    w_gate,
    w_up,
    w_down,
    ffn_post_gain,
    out_grad,
):
    local_rows, width = tokens.shape
    z_size, y_size, c_size = lax.axis_size("z"), lax.axis_size("y"), lax.axis_size("c")
    shard = width // (z_size * y_size * c_size)
    group_rows = local_rows * lax.axis_size("x")
    head_cols = w_query.shape[1]
    kv_cols = w_key.shape[1]
    heads_here = head_cols // HD
    kv_here = kv_cols // HD
    group_size = heads_here // kv_here
    ff_here = w_gate.shape[1]
    ff_cut = ff_here // z_size

    def inward(values):
        lead = values.shape[:-1]
        cut = values.reshape(lead + (z_size, y_size, c_size, shard))
        count = len(lead)
        order = tuple(range(count)) + (count + 2, count + 1, count, count + 3)
        return cut.transpose(order).reshape(lead + (width,))

    def outward(values):
        lead = values.shape[:-1]
        cut = values.reshape(lead + (c_size, y_size, z_size, shard))
        count = len(lead)
        order = tuple(range(count)) + (count + 2, count + 1, count, count + 3)
        return cut.transpose(order).reshape(lead + (width,))

    row_axes = ("c", "y", "z")
    positions, allowed = tree_tables(seg_lengths[0], parents[0], group_rows)
    cosine_table, sine_table = rope_tables(positions, HD)
    attn_gain, attn_post_gain = inward(attn_gain), inward(attn_post_gain)
    ffn_gain, ffn_post_gain = inward(ffn_gain), inward(ffn_post_gain)
    state_in = inward(tokens).astype(F32)
    out_cotan = inward(out_grad).astype(F32)

    qkv_here = jnp.concatenate([w_query, w_key, w_value], axis=1)
    qkv_weight = lax.all_gather(qkv_here, row_axes, axis=0, tiled=True)
    out_weight = lax.all_gather(w_out.T, row_axes, axis=0, tiled=True)
    up_here = jnp.stack([w_gate, w_up], axis=1).reshape(shard, 2, z_size, ff_cut)
    up_line = line_exchange(up_here)
    down_line = line_exchange(w_down.T.reshape(shard, 1, z_size, ff_cut))
    up_weight = lax.all_gather(up_line, ("x", "c", "y"), axis=0, tiled=True).reshape(
        2, width, 2 * ff_cut
    )
    down_weight = lax.all_gather(down_line, ("x", "c", "y"), axis=0, tiled=True).reshape(
        2, width, ff_cut
    )

    inverse_one = lax.rsqrt(jnp.mean(state_in * state_in, axis=-1, keepdims=True) + NORM_EPS)
    unit_one = state_in * inverse_one
    normed_one = pair_gather((unit_one * attn_gain).astype(BF), "x")
    qkv_proj = rows_dot(normed_one, qkv_weight)
    queries = rotate(
        qkv_proj[:, :head_cols].reshape(group_rows, heads_here, HD), cosine_table, sine_table
    ).astype(BF)
    key_rows = rotate(
        qkv_proj[:, head_cols : head_cols + kv_cols].reshape(group_rows, kv_here, HD),
        cosine_table,
        sine_table,
    ).astype(BF)
    value_rows = qkv_proj[:, head_cols + kv_cols :].astype(BF).reshape(group_rows, kv_here, HD)
    query_grid = queries.reshape(group_rows, kv_here, group_size, HD)
    attended, capped, probability = attend_forward(query_grid, key_rows, value_rows, allowed)
    branch = pair_sum(cols_dot(attended, out_weight), "x")
    inverse_two = lax.rsqrt(jnp.mean(branch * branch, axis=-1, keepdims=True) + NORM_EPS)
    unit_two = branch * inverse_two
    hidden = state_in + unit_two * attn_post_gain
    inverse_three = lax.rsqrt(jnp.mean(hidden * hidden, axis=-1, keepdims=True) + NORM_EPS)
    unit_three = hidden * inverse_three

    normed_two = line_gather((unit_three * ffn_gain).astype(BF))
    acts, pulls, ffn_part = [], [], 0.0
    for half in range(2):
        gate_up = rows_dot(normed_two, up_weight[half])
        act, pull = jax.vjp(gating, gate_up[:, :ff_cut], gate_up[:, ff_cut:])
        acts.append(act.astype(BF))
        pulls.append(pull)
        ffn_part = ffn_part + cols_dot(acts[half], down_weight[half])
    ffn_out = line_sum(ffn_part)
    inverse_four = lax.rsqrt(jnp.mean(ffn_out * ffn_out, axis=-1, keepdims=True) + NORM_EPS)
    unit_four = ffn_out * inverse_four
    mixed = (hidden + unit_four * ffn_post_gain).astype(BF)
    gain_four = jnp.sum(out_cotan * unit_four, axis=0)
    d_ffn = line_gather(
        norm_back(out_cotan * ffn_post_gain, unit_four, inverse_four).astype(BF)
    )
    d_ups, normed_part = [], 0.0
    for half in range(2):
        d_act = rows_dot(d_ffn, down_weight[half])
        d_ups.append(jnp.concatenate(pulls[half](d_act), axis=1).astype(BF))
        normed_part = normed_part + cols_dot(d_ups[half], up_weight[half])
    d_normed_two = line_sum(normed_part)
    grad_ffn = []
    for half in range(2):
        part = jnp.concatenate(
            [outer_dot(normed_two, d_ups[half]), outer_dot(d_ffn, acts[half])], axis=1
        ).astype(BF)
        grad_ffn.append(row_sum(part, ("c", "y")))
    x_here = lax.axis_index("x")
    grad_ffn = jnp.where(x_here == 0, grad_ffn[0], grad_ffn[1]).astype(F32) + swap(
        jnp.where(x_here == 0, grad_ffn[1], grad_ffn[0]), "x", 1
    ).astype(F32)
    grad_ffn = grad_ffn.astype(BF).reshape(z_size, shard, 3 * ff_cut)
    grad_cut = jnp.zeros((z_size, shard, 3 * ff_cut), F32)
    z_here = lax.axis_index("z")
    for k in range(z_size):
        piece = lax.dynamic_index_in_dim(grad_ffn, z_here ^ k, 0, keepdims=False)
        piece = piece if k == 0 else swap(piece, "z", k)
        grad_cut = lax.dynamic_update_index_in_dim(grad_cut, piece.astype(F32), z_here ^ k, 0)
    grad_cut = grad_cut.reshape(z_size, shard, 3, ff_cut).transpose(2, 1, 0, 3)
    grad_cut = grad_cut.reshape(3, shard, ff_here)

    gain_three = jnp.sum(d_normed_two * unit_three, axis=0)
    d_hidden = out_cotan + norm_back(d_normed_two * ffn_gain, unit_three, inverse_three)
    gain_two = jnp.sum(d_hidden * unit_two, axis=0)
    d_branch = pair_gather(
        norm_back(d_hidden * attn_post_gain, unit_two, inverse_two).astype(BF), "x"
    )
    d_attended = rows_dot(d_branch, out_weight).astype(BF)
    grad_grid = d_attended.reshape(group_rows, kv_here, group_size, HD)
    query_grad, key_grad, value_grad = attend_backward(
        query_grid, key_rows, value_rows, capped, probability, grad_grid
    )
    query_back = rotate(
        query_grad.reshape(group_rows, heads_here, HD), cosine_table, -sine_table
    ).astype(BF)
    key_back = rotate(key_grad, cosine_table, -sine_table).astype(BF)
    d_qkv = jnp.concatenate(
        [
            query_back.reshape(group_rows, head_cols),
            key_back.reshape(group_rows, kv_cols),
            value_grad.astype(BF).reshape(group_rows, kv_cols),
        ],
        axis=1,
    )
    d_normed_one = pair_sum(cols_dot(d_qkv, qkv_weight), "x")
    gain_one = jnp.sum(d_normed_one * unit_one, axis=0)
    grad_tokens = d_hidden + norm_back(d_normed_one * attn_gain, unit_one, inverse_one)
    grad_attn = jnp.concatenate(
        [outer_dot(normed_one, d_qkv), outer_dot(d_branch, attended)], axis=1
    ).astype(BF)
    grad_attn = row_sum(grad_attn, row_axes).astype(F32)
    gains = gain_sum(jnp.stack([gain_one, gain_two, gain_three, gain_four], axis=0))
    key_from, value_from = head_cols, head_cols + kv_cols
    out_from = head_cols + 2 * kv_cols
    return (
        outward(mixed),
        outward(grad_tokens),
        gains[0],
        grad_attn[:, :key_from],
        grad_attn[:, key_from:value_from],
        grad_attn[:, value_from:out_from],
        grad_attn[:, out_from:].T,
        gains[1],
        gains[2],
        grad_cut[0],
        grad_cut[1],
        grad_cut[2].T,
        gains[3],
    )


def solution(mesh):
    count, pair = mesh.devices.shape
    grid = Mesh(mesh.devices.reshape(4, count // 8, 2, pair), ("z", "y", "c", "x"))
    rows = ("z", "y", "c")
    return jax.shard_map(
        on_device,
        mesh=grid,
        in_specs=(
            P(rows + ("x",), None),
            P(rows, None),
            P(rows, None),
            P(),
            P(rows, "x"),
            P(rows, "x"),
            P(rows, "x"),
            P("x", rows),
            P(),
            P(),
            P(rows, "x"),
            P(rows, "x"),
            P("x", rows),
            P(),
            P(rows + ("x",), None),
        ),
        out_specs=(
            P(rows + ("x",), None),
            P(rows + ("x",), None),
            P(rows),
            P(rows, "x"),
            P(rows, "x"),
            P(rows, "x"),
            P("x", rows),
            P(rows),
            P(rows),
            P(rows, "x"),
            P(rows, "x"),
            P("x", rows),
            P(rows),
        ),
        check_vma=False,
    )
```

time: 2320 us -> 1130 us (0.49)
  waiting for transfers between devices: 2020 us -> 595 us
  local copies, waits for them, and re-layouts: 23.4 us -> 176 us
  other arithmetic: 35.4 us -> 100 us
  starting transfers between devices: 1.82 us -> 36.1 us
    reduce_scatter x8 -> x2, waiting for transfers between devices: 1510 us -> 27.8 us  [row_sum(): return lax.psum_scatter(parts, axes, scatter_dimension=0, tiled=True)]
    ppermute x0 -> x26, waiting for transfers between devices: none -> 493 us  [swap(): return lax.ppermute(values, axis, [(i, i ^ mask) for i in range(size)])]
    all_gather x8 -> x4, waiting for transfers between devices: 509 us -> 73.7 us  [the longest x1 39.5 us: on_device(): lax.all_gather(up_line, ('x', 'c', 'y'), axis=0, tiled=True)]
    unnamed x111 -> x226, local copies, waits for them, and re-layouts: 10.3 us -> 91.4 us
    concatenate x4 -> x6, other arithmetic: 4.3 us -> 49.8 us  [the longest x2 31.8 us: on_device(): jnp.concatenate([outer_dot(normed_two, d_ups[half]), outer_dot(d_ffn, act...]
    ppermute x0 -> x26, starting transfers between devices: none -> 35.5 us  [swap(): return lax.ppermute(values, axis, [(i, i ^ mask) for i in range(size)])]
    dot_general x14 -> x20, matrix products: 160 us -> 139 us  [the longest x6 55.3 us: rows_dot(): lax.dot_general(left, right, (((1,), (0,)), ((), ())), preferred_element_...]
  transfers between devices with their start and end apart: 16 -> 33, of which waited for: 15 -> 24; matrix products, arithmetic and copies ran while one was open for 5% -> 26% of each run, Pallas kernels for 0% -> 0%
where the time goes in v1:
time: 1130 us; the launch traced here: 1120 us
  waiting for transfers between devices  595 us (53%)
  local copies, waits for them, and re-layouts  176 us (16%)
  matrix products  153 us (14%)
  other arithmetic  100 us (9%)
  blocking collectives  43 us (4%)
  starting transfers between devices  36.1 us (3%)
  between operations  16.1 us (1%)
    ppermute x26, waiting for transfers between devices, swap(): return lax.ppermute(values, axis, [(i, i ^ mask) for i in range(size)])  493 us
    unnamed x226, local copies, waits for them, and re-layouts  91.4 us
    dot_general x6, matrix products, rows_dot(): lax.dot_general(left, right, (((1,), (0,)), ((), ())), preferred_element_...  55.3 us
    dot_general x6, matrix products, cols_dot(): lax.dot_general(left, right, (((1,), (1,)), ((), ())), preferred_element_...  46.4 us
    psum x1, blocking collectives, gain_sum(): parts = lax.psum(parts, ('z', 'y', 'c', 'x'))  43 us
    all_gather x1, waiting for transfers between devices, on_device(): lax.all_gather(up_line, ('x', 'c', 'y'), axis=0, tiled=True)  39.5 us
    ppermute x26, starting transfers between devices, swap(): return lax.ppermute(values, axis, [(i, i ^ mask) for i in range(size)])  35.5 us
    all_gather x1, waiting for transfers between devices, on_device(): lax.all_gather(down_line, ('x', 'c', 'y'), axis=0, tiled=True)  34.2 us
  transfers between devices with their start and end apart: 33, of which 24 were waited for; matrix products, arithmetic and copies ran while one was open for 26% of the time, Pallas kernels for 0%

profile of v1, /device:TPU:8, one launch (start us, length us, event | category | flops | bytes accessed | tf_op | source)
XLA Modules:
  0.0 1119.5 jit_solution(8469296473390791582)
XLA Ops:
  40.7 30.7 %collective-permute-done.5 = bf16[144,2304]{1,0:T(8,128)(2,1)} collective-permute-done((bf16[144,2304]{1,0:T(8,128)(2,1)}, bf16[144,2304]{1,0:T(8,128)(2,1)}, u32[]{:S(2)}, u32[]{:S(2)}) %collective-permute-start.5) | collective-permute-done | bytes 663584 | tf_op jit(solution)/shard_map/ppermute | solution.py:73
  77.1 55.6 %collective-permute-done.7 = bf16[144,2304]{1,0:T(8,128)(2,1)} collective-permute-done((bf16[144,2304]{1,0:T(8,128)(2,1)}, bf16[144,2304]{1,0:T(8,128)(2,1)}, u32[]{:S(2)}, u32[]{:S(2)}) %collective-permute-start.7) | collective-permute-done | bytes 663584 | tf_op jit(solution)/shard_map/ppermute | solution.py:73
  145.1 10.9 collective-permute-done.8
  156.1 17.3 %collective-permute-done.9 = bf16[144,1152]{1,0:T(8,128)(2,1)S(1)} collective-permute-done((bf16[144,1152]{1,0:T(8,128)(2,1)S(1)}, bf16[144,1152]{1,0:T(8,128)(2,1)S(1)}, u32[]{:S(2)}, u32[]{:S(2)}) %collective-permute-start.9) | collective-permute-done | bytes 331808 | tf_op jit(solution)/shard_map/ppermute | solution.py:73
  227.0 18.9 %collective-permute-done.1 = bf16[128,2304]{1,0:T(8,128)(2,1)} collective-permute-done((bf16[128,2304]{1,0:T(8,128)(2,1)}, bf16[128,2304]{1,0:T(8,128)(2,1)}, u32[]{:S(2)}, u32[]{:S(2)}) %collective-permute-start.1) | collective-permute-done | bytes 589856 | tf_op jit(solution)/shard_map/ppermute | solution.py:73
  251.7 26.3 %collective-permute-done.4 = bf16[128,2304]{1,0:T(8,128)(2,1)S(1)} collective-permute-done((bf16[128,2304]{1,0:T(8,128)(2,1)S(1)}, bf16[128,2304]{1,0:T(8,128)(2,1)S(1)}, u32[]{:S(2)}, u32[]{:S(2)}) %collective-permute-start.4) | collective-permute-done | bytes 589856 | tf_op jit(solution)/shard_map/ppermute | solution.py:73
  278.0 9.4 collective-permute-done.3
  287.4 39.5 %all-gather.9.cloned.1.call-done = bf16[4608,2304]{1,0:T(8,128)(2,1)} async-done(((bf16[576,2304]{1,0:T(8,128)(2,1)}), bf16[4608,2304]{1,0:T(8,128)(2,1)}) %all-gather.9.cloned.1.call-update) | async-done | bytes 21233680 | tf_op jit(solution)/shard_map/all_gather | solution.py:228
  338.2 17.7 %fusion.4 = f32[512,2304]{1,0:T(8,128)S(1)} fusion(bf16[4608,2304]{1,0:T(8,128)(2,1)} %all-gather.9.cloned.1.call-done, bf16[128,2304]{1,0:T(8,128)(2,1)S(1)} %collective-permute-done.4, bf16[128,2304]{1,0:T(8,128)(2,1)S(1)} %copy-done.79, bf16[128,2304]{1,0:T(8,128)(2,1)S(1)} %copy-done.83, bf16[128,2304]{1,0:T(8,128)(2,1)S(1)} %multiply_convert_fusion.6), kind=kOutput, calls=%fused_computation.12 | convolution fusion | flops 5445255168 | bytes 17694720 | tf_op jit(solution)/shard_map/dot_general | solution.py:77
  358.8 34.2 %all-gather.11.cloned.1.call-done = bf16[4608,1152]{1,0:T(8,128)(2,1)} async-done(((bf16[576,1152]{1,0:T(8,128)(2,1)}), bf16[4608,1152]{1,0:T(8,128)(2,1)}) %all-gather.11.cloned.1.call-update) | async-done | bytes 10616848 | tf_op jit(solution)/shard_map/all_gather | solution.py:231
  410.3 36.6 %collective-permute-done.13 = bf16[128,2304]{1,0:T(8,128)(2,1)} collective-permute-done((bf16[128,2304]{1,0:T(8,128)(2,1)}, bf16[128,2304]{1,0:T(8,128)(2,1)}, u32[]{:S(2)}, u32[]{:S(2)}) %collective-permute-start.13) | collective-permute-done | bytes 589856 | tf_op jit(solution)/shard_map/ppermute | solution.py:73
  446.9 11.0 collective-permute-done.12
  467.1 36.7 %collective-permute-done.16 = bf16[128,2304]{1,0:T(8,128)(2,1)S(1)} collective-permute-done((bf16[128,2304]{1,0:T(8,128)(2,1)S(1)}, bf16[128,2304]{1,0:T(8,128)(2,1)S(1)}, u32[]{:S(2)}, u32[]{:S(2)}) %collective-permute-start.16) | collective-permute-done | bytes 589856 | tf_op jit(solution)/shard_map/ppermute | solution.py:73
  512.9 9.9 fusion.33
  535.7 15.9 %pad_maximum_fusion.1 = bf16[2304,3456]{0,1:T(8,128)(2,1)} fusion(bf16[2304,1152]{0,1:T(8,128)(2,1)} %convolution_convert_fusion.2, bf16[2304,2304]{0,1:T(8,128)(2,1)S(1)} %convolution_convert_fusion), kind=kLoop, calls=%fused_computation.5 | loop fusion | flops 31850496 | bytes 31850496 | tf_op jit(solution)/shard_map/concatenate | solution.py:281
  551.6 20.2 %copy.275 = bf16[2304,3456]{1,0:T(8,128)(2,1)} copy(bf16[2304,3456]{0,1:T(8,128)(2,1)} %pad_maximum_fusion.1) | data formatting | bytes 31850496
  580.4 11.8 %fusion.26 = (bf16[512,1152]{1,0:T(8,128)(2,1)S(1)}, bf16[512,1152]{1,0:T(8,128)(2,1)}) fusion(f32[512,2304]{1,0:T(8,128)} %copy-done.7, bf16[4608,1152]{1,0:T(8,128)(2,1)} %all-gather.11.cloned.1.call-done, bf16[128,2304]{1,0:T(8,128)(2,1)S(1)} %copy-done.87, bf16[128,2304]{1,0:T(8,128)(2,1)S(1)} %copy-done.89, bf16[128,2304]{1,0:T(8,128)(2,1)S(1)} %copy-done.91, ...), kind=kOutput, calls=%fused_computation.41 | convolution fusion | flops 2741501952 | bytes 14745600 | tf_op jit(solution)/shard_map/dot_general | solution.py:77
  600.5 15.9 %pad_maximum_fusion = bf16[2304,3456]{0,1:T(8,128)(2,1)} fusion(bf16[2304,1152]{0,1:T(8,128)(2,1)} %convolution_convert_fusion.3, bf16[2304,2304]{0,1:T(8,128)(2,1)S(1)} %convolution_convert_fusion.1), kind=kLoop, calls=%fused_computation.4 | loop fusion | flops 31850496 | bytes 31850496 | tf_op jit(solution)/shard_map/concatenate | solution.py:281
  616.4 20.1 %copy.273 = bf16[2304,3456]{1,0:T(8,128)(2,1)} copy(bf16[2304,3456]{0,1:T(8,128)(2,1)} %pad_maximum_fusion) | data formatting | bytes 31850496
  637.8 12.0 %fusion.2 = f32[512,2304]{1,0:T(8,128)} fusion(bf16[4608,2304]{1,0:T(8,128)(2,1)} %all-gather.9.cloned.1.call-done, bf16[512,1152]{1,0:T(8,128)(2,1)} %get-tuple-element.100, bf16[512,1152]{1,0:T(8,128)(2,1)S(1)} %copy-done.93), kind=kOutput, calls=%fused_computation.10 | convolution fusion | flops 5440536576 | bytes 17694720 | tf_op jit(solution)/shard_map/dot_general | solution.py:81
  649.7 12.8 %fusion.107 = (bf16[512,2304]{1,0:T(8,128)(2,1)S(1)}, f32[512,2304]{1,0:T(8,128)}) fusion(f32[512,2304]{1,0:T(8,128)} %fusion.2, bf16[4608,2304]{1,0:T(8,128)(2,1)} %all-gather.9.cloned.1.call-done, bf16[512,1152]{1,0:T(8,128)(2,1)S(1)} %copy-done.96, bf16[512,1152]{1,0:T(8,128)(2,1)S(1)} %copy-done.95), kind=kOutput, calls=%fused_computation.238 | convolution fusion | flops 5442895872 | bytes 24772608 | tf_op jit(solution)/shard_map/dot_general | solution.py:81
  668.9 35.4 %collective-permute-done.19 = bf16[128,2304]{1,0:T(8,128)(2,1)S(1)} collective-permute-done((bf16[128,2304]{1,0:T(8,128)(2,1)S(1)}, bf16[128,2304]{1,0:T(8,128)(2,1)S(1)}, u32[]{:S(2)}, u32[]{:S(2)}) %collective-permute-start.19) | collective-permute-done | bytes 589856 | tf_op jit(solution)/shard_map/ppermute | solution.py:73
  755.3 15.6 %pad_maximum_fusion.2 = bf16[2304,3072]{0,1:T(8,128)(2,1)} fusion(bf16[2304,1024]{0,1:T(8,128)(2,1)S(1)} %convolution_convert_fusion.5, bf16[2304,2048]{0,1:T(8,128)(2,1)S(1)} %convolution_convert_fusion.4), kind=kLoop, calls=%fused_computation.6 | loop fusion | flops 28311552 | bytes 28311552 | tf_op jit(solution)/shard_map/concatenate | solution.py:325
  770.9 18.9 %copy.271 = bf16[2304,3072]{1,0:T(8,128)(2,1)} copy(bf16[2304,3072]{0,1:T(8,128)(2,1)} %pad_maximum_fusion.2) | data formatting | bytes 28311552
  789.9 27.8 %reduce-scatter.12.cloned.1.call-done = bf16[576,3456]{1,0:T(8,128)(2,1)} async-done(((bf16[2304,3456]{1,0:T(8,128)(2,1)}), bf16[576,3456]{1,0:T(8,128)(2,1)}) %reduce-scatter.12.cloned.1.call-update) | async-done | bytes 3981328 | tf_op jit(solution)/shard_map/reduce_scatter | solution.py:159
  838.3 84.5 %collective-permute-done.21 = bf16[128,2304]{1,0:T(8,128)(2,1)} collective-permute-done((bf16[128,2304]{1,0:T(8,128)(2,1)}, bf16[128,2304]{1,0:T(8,128)(2,1)}, u32[]{:S(2)}, u32[]{:S(2)}) %collective-permute-start.21) | collective-permute-done | bytes 589856 | tf_op jit(solution)/shard_map/ppermute | solution.py:73
  928.8 43.0 %psum.7 = f32[4,2304]{1,0:T(4,128)S(1)} all-reduce(f32[4,2304]{1,0:T(4,128)S(1)} %pad_maximum_fusion.30), channel_id=1, replica_groups=mesh['z'=4,'y'=2,'c'=2,'x'=2] {'z','y','c','x'}, use_global_device_ids=true, to_apply=%region_25.26 | all-reduce | flops 9216 | bytes 73728 | tf_op jit(solution)/shard_map/psum | solution.py:163
  999.0 24.6 %collective-permute-done.23 = bf16[144,3456]{1,0:T(8,128)(2,1)} collective-permute-done((bf16[144,3456]{1,0:T(8,128)(2,1)}, bf16[144,3456]{1,0:T(8,128)(2,1)}, u32[]{:S(2)}, u32[]{:S(2)}) %collective-permute-start.23) | collective-permute-done | bytes 995360 | tf_op jit(solution)/shard_map/ppermute | solution.py:73
  1026.3 31.4 %collective-permute-done.24 = bf16[144,3456]{1,0:T(8,128)(2,1)S(1)} collective-permute-done((bf16[144,3456]{1,0:T(8,128)(2,1)S(1)}, bf16[144,3456]{1,0:T(8,128)(2,1)S(1)}, u32[]{:S(2)}, u32[]{:S(2)}) %collective-permute-start.24) | collective-permute-done | bytes 995360 | tf_op jit(solution)/shard_map/ppermute | solution.py:73
  1059.1 18.2 %collective-permute-done.25 = bf16[144,3456]{1,0:T(8,128)(2,1)S(1)} collective-permute-done((bf16[144,3456]{1,0:T(8,128)(2,1)S(1)}, bf16[144,3456]{1,0:T(8,128)(2,1)S(1)}, u32[]{:S(2)}, u32[]{:S(2)}) %collective-permute-start.25) | collective-permute-done | bytes 995360 | tf_op jit(solution)/shard_map/ppermute | solution.py:73
  1078.7 12.0 %reshape.467 = f32[4,144,3,1152]{3,2,1,0:T(4,128)} reshape(f32[4,144,3456]{2,1,0:T(8,128)} %convert_dynamic-update-slice_fusion) | data formatting | bytes 15925248 | tf_op jit(solution)/shard_map/reshape | solution.py:296
  1090.7 13.4 %fusion.98 = (f32[1,144,4,1152]{3,0,1,2:T(1,128)S(1)}, f32[1,144,4,1152]{3,0,1,2:T(1,128)S(1)}, f32[1,144,4,1152]{3,0,1,2:T(1,128)S(1)}) fusion(f32[3,144,4,1152]{3,0,1,2:T(4,128)} %bitcast.197), kind=kLoop, calls=%fused_computation.229 | loop fusion | bytes 15925248 | tf_op jit(solution)/shard_map/slice | solution.py:344
  (430 shorter events, 315.5 us)
Async XLA Ops:
  7.2 190.8 %all-gather.5.cloned.1.call-start = ((), (), s32[]{:S(2)}) async-start(), calls=%async_computation.3 | async-start | bytes 10027008 | tf_op jit(solution)/shard_map/all_gather | solution.py:223
  9.3 204.4 %all-gather.7.cloned.1.call-start = ((), (), s32[]{:S(2)}) async-start(), calls=%async_computation.4 | async-start | bytes 5013504 | tf_op jit(solution)/shard_map/all_gather | solution.py:224
  10.1 316.8 %all-gather.9.cloned.1.call-start = ((), (), s32[]{:S(2)}) async-start(), calls=%async_computation.5 | async-start | bytes 23887872 | tf_op jit(solution)/shard_map/all_gather | solution.py:228
  30.3 41.1 %collective-permute-start.5 = (bf16[144,2304]{1,0:T(8,128)(2,1)}, bf16[144,2304]{1,0:T(8,128)(2,1)}, u32[]{:S(2)}, u32[]{:S(2)}) collective-permute-start(bf16[144,2304]{1,0:T(8,128)(2,1)} %bitcast.94), channel_id=1, source_target_pairs={{0,8},{8,0},{16,24},{24,16},{1,9},{9,1},{17,25},{25,17},{2,10},{10... | collective-permute-start | bytes 1990664 | tf_op jit(solution)/shard_map/ppermute | solution.py:73
  33.9 42.1 %collective-permute-start.6 = (bf16[144,2304]{1,0:T(8,128)(2,1)}, bf16[144,2304]{1,0:T(8,128)(2,1)}, u32[]{:S(2)}, u32[]{:S(2)}) collective-permute-start(bf16[144,2304]{1,0:T(8,128)(2,1)} %bitcast.98), channel_id=1, source_target_pairs={{0,16},{8,24},{16,0},{24,8},{1,17},{9,25},{17,1},{25,9},{2,18},{10... | collective-permute-start | bytes 1990664 | tf_op jit(solution)/shard_map/ppermute | solution.py:73
  37.8 94.9 %collective-permute-start.7 = (bf16[144,2304]{1,0:T(8,128)(2,1)}, bf16[144,2304]{1,0:T(8,128)(2,1)}, u32[]{:S(2)}, u32[]{:S(2)}) collective-permute-start(bf16[144,2304]{1,0:T(8,128)(2,1)} %bitcast.102), channel_id=1, source_target_pairs={{0,24},{8,16},{16,8},{24,0},{1,25},{9,17},{17,9},{25,1},{2,26},{10... | collective-permute-start | bytes 1990664 | tf_op jit(solution)/shard_map/ppermute | solution.py:73
  135.4 257.6 %all-gather.11.cloned.1.call-start = ((), (), s32[]{:S(2)}) async-start(), calls=%async_computation.6 | async-start | bytes 11943936 | tf_op jit(solution)/shard_map/all_gather | solution.py:231
  141.2 14.9 %collective-permute-start.8 = (bf16[144,1152]{1,0:T(8,128)(2,1)S(1)}, bf16[144,1152]{1,0:T(8,128)(2,1)S(1)}, u32[]{:S(2)}, u32[]{:S(2)}) collective-permute-start(bf16[144,1152]{1,0:T(8,128)(2,1)S(1)} %bitcast.233), channel_id=1, source_target_pairs={{0,8},{8,0},{16,24},{24,16},{1,9},{9,1},{17,25},{25,17},{2,10},{10... | collective-permute-start | bytes 995336 | tf_op jit(solution)/shard_map/ppermute | solution.py:73
  141.3 32.2 %collective-permute-start.9 = (bf16[144,1152]{1,0:T(8,128)(2,1)S(1)}, bf16[144,1152]{1,0:T(8,128)(2,1)S(1)}, u32[]{:S(2)}, u32[]{:S(2)}) collective-permute-start(bf16[144,1152]{1,0:T(8,128)(2,1)S(1)} %bitcast.232), channel_id=1, source_target_pairs={{0,16},{8,24},{16,0},{24,8},{1,17},{9,25},{17,1},{25,9},{2,18},{10... | collective-permute-start | bytes 995336 | tf_op jit(solution)/shard_map/ppermute | solution.py:73
  144.1 36.6 %collective-permute-start.10 = (bf16[144,1152]{1,0:T(8,128)(2,1)S(1)}, bf16[144,1152]{1,0:T(8,128)(2,1)S(1)}, u32[]{:S(2)}, u32[]{:S(2)}) collective-permute-start(bf16[144,1152]{1,0:T(8,128)(2,1)S(1)} %bitcast.231), channel_id=1, source_target_pairs={{0,24},{8,16},{16,8},{24,0},{1,25},{9,17},{17,9},{25,1},{2,26},{10... | collective-permute-start | bytes 995336 | tf_op jit(solution)/shard_map/ppermute | solution.py:73
  181.9 608.0 %reduce-scatter.14.cloned.1.call-start = ((), (), s32[]{:S(2)}) async-start(), calls=%async_computation.9 | async-start | bytes 19906560 | tf_op jit(solution)/shard_map/reduce_scatter | solution.py:159
  183.8 13.8 %collective-permute-start = (bf16[128,2304]{1,0:T(8,128)(2,1)S(1)}, bf16[128,2304]{1,0:T(8,128)(2,1)S(1)}, u32[]{:S(2)}, u32[]{:S(2)}) collective-permute-start(bf16[128,2304]{1,0:T(8,128)(2,1)S(1)} %multiply_convert_fusion.7), channel_id=1, source_target_pairs={{0,1},{1,0},{2,3},{3,2},{4,5},{5,4},{6,7},{7,6},{8,9},{9,8},{10,11... | collective-permute-start | bytes 1769480 | tf_op jit(solution)/shard_map/ppermute | solution.py:73
  219.1 26.7 %collective-permute-start.1 = (bf16[128,2304]{1,0:T(8,128)(2,1)}, bf16[128,2304]{1,0:T(8,128)(2,1)}, u32[]{:S(2)}, u32[]{:S(2)}) collective-permute-start(bf16[128,2304]{1,0:T(8,128)(2,1)} %dynamic-slice_convert_fusion.1), channel_id=1, source_target_pairs={{0,1},{1,0},{2,3},{3,2},{4,5},{5,4},{6,7},{7,6},{8,9},{9,8},{10,11... | collective-permute-start | bytes 1769480 | tf_op jit(solution)/shard_map/ppermute | solution.py:73
  248.2 29.8 %collective-permute-start.4 = (bf16[128,2304]{1,0:T(8,128)(2,1)S(1)}, bf16[128,2304]{1,0:T(8,128)(2,1)S(1)}, u32[]{:S(2)}, u32[]{:S(2)}) collective-permute-start(bf16[128,2304]{1,0:T(8,128)(2,1)S(1)} %multiply_convert_fusion.6), channel_id=1, source_target_pairs={{0,24},{8,16},{16,8},{24,0},{1,25},{9,17},{17,9},{25,1},{2,26},{10... | collective-permute-start | bytes 1769480 | tf_op jit(solution)/shard_map/ppermute | solution.py:73
  248.2 39.2 %collective-permute-start.3 = (bf16[128,2304]{1,0:T(8,128)(2,1)S(1)}, bf16[128,2304]{1,0:T(8,128)(2,1)S(1)}, u32[]{:S(2)}, u32[]{:S(2)}) collective-permute-start(bf16[128,2304]{1,0:T(8,128)(2,1)S(1)} %multiply_convert_fusion.6), channel_id=1, source_target_pairs={{0,16},{8,24},{16,0},{24,8},{1,17},{9,25},{17,1},{25,9},{2,18},{10... | collective-permute-start | bytes 1769480 | tf_op jit(solution)/shard_map/ppermute | solution.py:73
  248.3 39.1 %collective-permute-start.2 = (bf16[128,2304]{1,0:T(8,128)(2,1)S(1)}, bf16[128,2304]{1,0:T(8,128)(2,1)S(1)}, u32[]{:S(2)}, u32[]{:S(2)}) collective-permute-start(bf16[128,2304]{1,0:T(8,128)(2,1)S(1)} %multiply_convert_fusion.6), channel_id=1, source_target_pairs={{0,8},{8,0},{16,24},{24,16},{1,9},{9,1},{17,25},{25,17},{2,10},{10... | collective-permute-start | bytes 1769480 | tf_op jit(solution)/shard_map/ppermute | solution.py:73
  405.1 41.8 %collective-permute-start.13 = (bf16[128,2304]{1,0:T(8,128)(2,1)}, bf16[128,2304]{1,0:T(8,128)(2,1)}, u32[]{:S(2)}, u32[]{:S(2)}) collective-permute-start(bf16[128,2304]{1,0:T(8,128)(2,1)} %get-tuple-element.111), channel_id=1, source_target_pairs={{0,24},{8,16},{16,8},{24,0},{1,25},{9,17},{17,9},{25,1},{2,26},{10... | collective-permute-start | bytes 1769480 | tf_op jit(solution)/shard_map/ppermute | solution.py:73
  406.6 51.2 %collective-permute-start.12 = (bf16[128,2304]{1,0:T(8,128)(2,1)}, bf16[128,2304]{1,0:T(8,128)(2,1)}, u32[]{:S(2)}, u32[]{:S(2)}) collective-permute-start(bf16[128,2304]{1,0:T(8,128)(2,1)} %get-tuple-element.112), channel_id=1, source_target_pairs={{0,16},{8,24},{16,0},{24,8},{1,17},{9,25},{17,1},{25,9},{2,18},{10... | collective-permute-start | bytes 1769480 | tf_op jit(solution)/shard_map/ppermute | solution.py:73
  408.0 49.8 %collective-permute-start.11 = (bf16[128,2304]{1,0:T(8,128)(2,1)}, bf16[128,2304]{1,0:T(8,128)(2,1)}, u32[]{:S(2)}, u32[]{:S(2)}) collective-permute-start(bf16[128,2304]{1,0:T(8,128)(2,1)} %get-tuple-element.110), channel_id=1, source_target_pairs={{0,8},{8,0},{16,24},{24,16},{1,9},{9,1},{17,25},{25,17},{2,10},{10... | collective-permute-start | bytes 1769480 | tf_op jit(solution)/shard_map/ppermute | solution.py:73
  462.2 41.5 %collective-permute-start.16 = (bf16[128,2304]{1,0:T(8,128)(2,1)S(1)}, bf16[128,2304]{1,0:T(8,128)(2,1)S(1)}, u32[]{:S(2)}, u32[]{:S(2)}) collective-permute-start(bf16[128,2304]{1,0:T(8,128)(2,1)S(1)} %get-tuple-element.123), channel_id=1, source_target_pairs={{0,24},{8,16},{16,8},{24,0},{1,25},{9,17},{17,9},{25,1},{2,26},{10... | collective-permute-start | bytes 1769480 | tf_op jit(solution)/shard_map/ppermute | solution.py:73
  462.8 50.1 %collective-permute-start.15 = (bf16[128,2304]{1,0:T(8,128)(2,1)S(1)}, bf16[128,2304]{1,0:T(8,128)(2,1)S(1)}, u32[]{:S(2)}, u32[]{:S(2)}) collective-permute-start(bf16[128,2304]{1,0:T(8,128)(2,1)S(1)} %get-tuple-element.123), channel_id=1, source_target_pairs={{0,16},{8,24},{16,0},{24,8},{1,17},{9,25},{17,1},{25,9},{2,18},{10... | collective-permute-start | bytes 1769480 | tf_op jit(solution)/shard_map/ppermute | solution.py:73
  467.1 45.8 %collective-permute-start.14 = (bf16[128,2304]{1,0:T(8,128)(2,1)S(1)}, bf16[128,2304]{1,0:T(8,128)(2,1)S(1)}, u32[]{:S(2)}, u32[]{:S(2)}) collective-permute-start(bf16[128,2304]{1,0:T(8,128)(2,1)S(1)} %get-tuple-element.123), channel_id=1, source_target_pairs={{0,8},{8,0},{16,24},{24,16},{1,9},{9,1},{17,25},{25,17},{2,10},{10... | collective-permute-start | bytes 1769480 | tf_op jit(solution)/shard_map/ppermute | solution.py:73
  571.8 245.8 %reduce-scatter.12.cloned.1.call-start = ((), (), s32[]{:S(2)}) async-start(), calls=%async_computation.8 | async-start | bytes 19906560 | tf_op jit(solution)/shard_map/reduce_scatter | solution.py:159
  636.5 336.0 %reduce-scatter.10.cloned.1.call-start = ((), (), s32[]{:S(2)}) async-start(), calls=%async_computation.7 | async-start | bytes 15040512
  662.7 41.6 %collective-permute-start.19 = (bf16[128,2304]{1,0:T(8,128)(2,1)S(1)}, bf16[128,2304]{1,0:T(8,128)(2,1)S(1)}, u32[]{:S(2)}, u32[]{:S(2)}) collective-permute-start(bf16[128,2304]{1,0:T(8,128)(2,1)S(1)} %get-tuple-element.108), channel_id=1, source_target_pairs={{0,24},{8,16},{16,8},{24,0},{1,25},{9,17},{17,9},{25,1},{2,26},{10... | collective-permute-start | bytes 1769480 | tf_op jit(solution)/shard_map/ppermute | solution.py:73
  664.2 48.2 %collective-permute-start.18 = (bf16[128,2304]{1,0:T(8,128)(2,1)S(1)}, bf16[128,2304]{1,0:T(8,128)(2,1)S(1)}, u32[]{:S(2)}, u32[]{:S(2)}) collective-permute-start(bf16[128,2304]{1,0:T(8,128)(2,1)S(1)} %get-tuple-element.109), channel_id=1, source_target_pairs={{0,16},{8,24},{16,0},{24,8},{1,17},{9,25},{17,1},{25,9},{2,18},{10... | collective-permute-start | bytes 1769480 | tf_op jit(solution)/shard_map/ppermute | solution.py:73
  668.9 43.5 %collective-permute-start.17 = (bf16[128,2304]{1,0:T(8,128)(2,1)S(1)}, bf16[128,2304]{1,0:T(8,128)(2,1)S(1)}, u32[]{:S(2)}, u32[]{:S(2)}) collective-permute-start(bf16[128,2304]{1,0:T(8,128)(2,1)S(1)} %get-tuple-element.107), channel_id=1, source_target_pairs={{0,8},{8,0},{16,24},{24,16},{1,9},{9,1},{17,25},{25,17},{2,10},{10... | collective-permute-start | bytes 1769480 | tf_op jit(solution)/shard_map/ppermute | solution.py:73
  822.1 155.1 %collective-permute-start.22 = (bf16[576,3456]{1,0:T(8,128)(2,1)}, bf16[576,3456]{1,0:T(8,128)(2,1)}, u32[]{:S(2)}, u32[]{:S(2)}) collective-permute-start(bf16[576,3456]{1,0:T(8,128)(2,1)} %broadcast_select_fusion), channel_id=1, source_target_pairs={{0,1},{1,0},{2,3},{3,2},{4,5},{5,4},{6,7},{7,6},{8,9},{9,8},{10,11... | collective-permute-start | bytes 11943944 | tf_op jit(solution)/shard_map/ppermute | solution.py:73
  832.2 90.6 %collective-permute-start.21 = (bf16[128,2304]{1,0:T(8,128)(2,1)}, bf16[128,2304]{1,0:T(8,128)(2,1)}, u32[]{:S(2)}, u32[]{:S(2)}) collective-permute-start(bf16[128,2304]{1,0:T(8,128)(2,1)} %dynamic-slice_convert_fusion), channel_id=1, source_target_pairs={{0,1},{1,0},{2,3},{3,2},{4,5},{5,4},{6,7},{7,6},{8,9},{9,8},{10,11... | collective-permute-start | bytes 1769480 | tf_op jit(solution)/shard_map/ppermute | solution.py:73
  984.9 38.7 %collective-permute-start.23 = (bf16[144,3456]{1,0:T(8,128)(2,1)}, bf16[144,3456]{1,0:T(8,128)(2,1)}, u32[]{:S(2)}, u32[]{:S(2)}) collective-permute-start(bf16[144,3456]{1,0:T(8,128)(2,1)} %get-tuple-element.106), channel_id=1, source_target_pairs={{0,8},{8,0},{16,24},{24,16},{1,9},{9,1},{17,25},{25,17},{2,10},{10... | collective-permute-start | bytes 2985992 | tf_op jit(solution)/shard_map/ppermute | solution.py:73
  989.5 68.2 %collective-permute-start.24 = (bf16[144,3456]{1,0:T(8,128)(2,1)S(1)}, bf16[144,3456]{1,0:T(8,128)(2,1)S(1)}, u32[]{:S(2)}, u32[]{:S(2)}) collective-permute-start(bf16[144,3456]{1,0:T(8,128)(2,1)S(1)} %copy-done.35), channel_id=1, source_target_pairs={{0,16},{8,24},{16,0},{24,8},{1,17},{9,25},{17,1},{25,9},{2,18},{10... | collective-permute-start | bytes 2985992 | tf_op jit(solution)/shard_map/ppermute | solution.py:73
  998.9 78.4 %collective-permute-start.25 = (bf16[144,3456]{1,0:T(8,128)(2,1)S(1)}, bf16[144,3456]{1,0:T(8,128)(2,1)S(1)}, u32[]{:S(2)}, u32[]{:S(2)}) collective-permute-start(bf16[144,3456]{1,0:T(8,128)(2,1)S(1)} %copy-done.34), channel_id=1, source_target_pairs={{0,24},{8,16},{16,8},{24,0},{1,25},{9,17},{17,9},{25,1},{2,26},{10... | collective-permute-start | bytes 2985992 | tf_op jit(solution)/shard_map/ppermute | solution.py:73
  (103 other events, 1556.8 us)
Sparse Core Ops, SparseCore 0:
  10.9 125.5 all-gather.4
  138.8 68.6 all-gather.6
  210.0 116.8 all-gather.8
  329.1 63.8 all-gather.10
  572.0 121.9 reduce-scatter.13
  696.6 120.9 reduce-scatter.11
  821.8 145.6 reduce-scatter.9

commit v2 on v1

--- a/solution.py
+++ b/solution.py
@@ -85,20 +85,41 @@
     return lax.dot_general(left, right, (((0,), (0,)), ((), ())), preferred_element_type=F32)
 
 
-def pair_gather(values, axis):
-    mine = lax.axis_index(axis)
-    other = swap(values, axis, 1)
+def pair_gather(values):
+    mine = lax.axis_index("x")
+    other = swap(values, "x", 1)
     first = jnp.where(mine == 0, values, other)
     second = jnp.where(mine == 0, other, values)
     return jnp.concatenate([first, second], axis=0)
 
 
-def pair_sum(partial, axis):
+def pair_sum(partial):
     rows = partial.shape[0] // 2
-    mine = lax.axis_index(axis)
+    mine = lax.axis_index("x")
     sent = lax.dynamic_slice_in_dim(partial, (1 - mine) * rows, rows, 0).astype(BF)
     kept = lax.dynamic_slice_in_dim(partial, mine * rows, rows, 0)
-    return kept + swap(sent, axis, 1).astype(F32)
+    return kept + swap(sent, "x", 1).astype(F32)
+
+
+def masks(axis):
+    return [1 << i for i in range(lax.axis_size(axis).bit_length() - 1)]
+
+
+def fold(values, axis):
+    for mask in reversed(masks(axis)):
+        rows = values.shape[0] // 2
+        values = add_low(values[:rows], swap(values[rows:], axis, mask))
+    return values
+
+
+def spread(values, axis):
+    for mask in masks(axis):
+        values = jnp.concatenate([values, swap(values, axis, mask)], axis=0)
+    return values
+
+
+def add_low(left, right):
+    return (left.astype(F32) + right.astype(F32)).astype(BF)
 
 
 def line_gather(values):
@@ -113,17 +134,90 @@
     return total
 
 
+def line_place(pieces):
+    here = lax.axis_index("z")
+    held = jnp.zeros((len(pieces),) + pieces[0].shape, pieces[0].dtype)
+    for k, piece in enumerate(pieces):
+        held = lax.dynamic_update_index_in_dim(held, piece, here ^ k, 0)
+    return held
+
+
 def line_exchange(weight):
-    rows, parts, count, cols = weight.shape
+    rows, cols = weight.shape
+    here, cut = lax.axis_index("z"), cols // 4
+    pieces = []
+    for k in range(4):
+        piece = lax.dynamic_slice_in_dim(weight, (here ^ k) * cut, cut, 1)
+        pieces.append(piece if k == 0 else swap(piece, "z", k))
+    return line_place(pieces).reshape(4 * rows, cut)
+
+
+def line_return(grad):
+    rows, cols = grad.shape[0] // 4, grad.shape[1]
     here = lax.axis_index("z")
-    held = jnp.zeros((count, rows, parts * cols), weight.dtype)
-    for k in range(count):
-        piece = lax.dynamic_index_in_dim(weight, here ^ k, 2, keepdims=False).reshape(
-            rows, parts * cols
+    held = jnp.zeros((rows, 4 * cols), F32)
+    for k in range(4):
+        piece = lax.dynamic_slice_in_dim(grad, (here ^ k) * rows, rows, 0)
+        piece = piece if k == 0 else swap(piece, "z", k)
+        held = lax.dynamic_update_slice_in_dim(held, piece.astype(F32), (here ^ k) * cols, 1)
+    return held
+
+
+def line_fold(grad):
+    rows = grad.shape[0] // 4
+    here = lax.axis_index("z")
+    total = lax.dynamic_slice_in_dim(grad, here * rows, rows, 0).astype(F32)
+    for k in (1, 2, 3):
+        piece = lax.dynamic_slice_in_dim(grad, (here ^ k) * rows, rows, 0)
+        total = total + swap(piece, "z", k).astype(F32)
+    return total
+
+
+def gather_rows(weight):
+    line = line_place([weight] + [swap(weight, "z", k) for k in (1, 2, 3)])
+    return spread(spread(line.reshape(-1, weight.shape[1]), "y"), "c")
+
+
+def gather_cut(weight, x_first):
+    if x_first:
+        halves = [weight, swap(weight, "x", 1)]
+        halves = [spread(half, "y") for half in halves]
+    else:
+        mine = spread(weight, "y")
+        halves = [mine, swap(mine, "x", 1)]
+    return [spread(half, "c") for half in halves]
+
+
+def fold_cut(mine, other, x_first):
+    if x_first:
+        return fold(add_low(mine, swap(other, "x", 1)), "y")
+    mine, other = fold(mine, "y"), fold(other, "y")
+    return add_low(mine, swap(other, "x", 1))
+
+
+def outer_low(left, right):
+    cut = left.shape[1] // 2
+    sent = outer_dot(left[:, cut:], right).astype(BF)
+    return (outer_dot(left[:, :cut], right) + swap(sent, "c", 1).astype(F32)).astype(BF)
+
+
+def gain_sum(parts):
+    count, width = parts.shape
+    z_size = lax.axis_size("z")
+    blocks = lax.axis_size("c") * lax.axis_size("y") * z_size
+    parts = parts.reshape(count, blocks, width // blocks).transpose(1, 0, 2)
+    parts = parts + swap(parts, "x", 1)
+    for axis in ("c", "y"):
+        for mask in reversed(masks(axis)):
+            rows = parts.shape[0] // 2
+            parts = parts[:rows] + swap(parts[rows:], axis, mask)
+    here = lax.axis_index("z")
+    total = lax.dynamic_index_in_dim(parts, here, 0, keepdims=False)
+    for k in (1, 2, 3):
+        total = total + swap(
+            lax.dynamic_index_in_dim(parts, here ^ k, 0, keepdims=False), "z", k
         )
-        piece = piece if k == 0 else swap(piece, "z", k)
-        held = lax.dynamic_update_index_in_dim(held, piece, here ^ k, 0)
-    return held.reshape(count * rows, parts * cols)
+    return total
 
 
 def attend_forward(query_grid, key_rows, value_rows, allowed):
@@ -153,19 +247,6 @@
     key_grad = jnp.einsum("grqk,qgrd->kgd", grad_score, query_grid, preferred_element_type=F32)
     value_grad = jnp.einsum("grqk,qgrd->kgd", prob_low, grad_grid, preferred_element_type=F32)
     return (query_grad, key_grad, value_grad)
-
-
-def row_sum(parts, axes):
-    return lax.psum_scatter(parts, axes, scatter_dimension=0, tiled=True)
-
-
-def gain_sum(parts):
-    parts = lax.psum(parts, ("z", "y", "c", "x"))
-    width = parts.shape[1] // (lax.axis_size("z") * lax.axis_size("y") * lax.axis_size("c"))
-    at = (lax.axis_index("c") * lax.axis_size("y") + lax.axis_index("y")) * lax.axis_size(
-        "z"
-    ) + lax.axis_index("z")
-    return lax.dynamic_slice_in_dim(parts, at * width, width, 1)
 
 
 def on_device(
@@ -194,24 +275,32 @@
     heads_here = head_cols // HD
     kv_here = kv_cols // HD
     group_size = heads_here // kv_here
-    ff_here = w_gate.shape[1]
-    ff_cut = ff_here // z_size
+
+    def crossed(values, axis, at):
+        here = lax.axis_index(axis)
+        for mask in masks(axis):
+            shape = values.shape
+            halves = values.reshape(shape[:at] + (-1, 2, mask) + shape[at + 1 :])
+            values = jnp.where((here & mask) != 0, jnp.flip(halves, at + 1), halves)
+            values = values.reshape(shape)
+        return values
 
     def inward(values):
         lead = values.shape[:-1]
         cut = values.reshape(lead + (z_size, y_size, c_size, shard))
         count = len(lead)
         order = tuple(range(count)) + (count + 2, count + 1, count, count + 3)
-        return cut.transpose(order).reshape(lead + (width,))
+        cut = crossed(crossed(cut.transpose(order), "c", count), "y", count + 1)
+        return cut.reshape(lead + (width,))
 
     def outward(values):
         lead = values.shape[:-1]
         cut = values.reshape(lead + (c_size, y_size, z_size, shard))
         count = len(lead)
         order = tuple(range(count)) + (count + 2, count + 1, count, count + 3)
+        cut = crossed(crossed(cut, "c", count), "y", count + 1)
         return cut.transpose(order).reshape(lead + (width,))
 
-    row_axes = ("c", "y", "z")
     positions, allowed = tree_tables(seg_lengths[0], parents[0], group_rows)
     cosine_table, sine_table = rope_tables(positions, HD)
     attn_gain, attn_post_gain = inward(attn_gain), inward(attn_post_gain)
@@ -220,21 +309,15 @@
     out_cotan = inward(out_grad).astype(F32)
 
     qkv_here = jnp.concatenate([w_query, w_key, w_value], axis=1)
-    qkv_weight = lax.all_gather(qkv_here, row_axes, axis=0, tiled=True)
-    out_weight = lax.all_gather(w_out.T, row_axes, axis=0, tiled=True)
-    up_here = jnp.stack([w_gate, w_up], axis=1).reshape(shard, 2, z_size, ff_cut)
-    up_line = line_exchange(up_here)
-    down_line = line_exchange(w_down.T.reshape(shard, 1, z_size, ff_cut))
-    up_weight = lax.all_gather(up_line, ("x", "c", "y"), axis=0, tiled=True).reshape(
-        2, width, 2 * ff_cut
-    )
-    down_weight = lax.all_gather(down_line, ("x", "c", "y"), axis=0, tiled=True).reshape(
-        2, width, ff_cut
-    )
+    qkv_weight = gather_rows(qkv_here)
+    out_weight = gather_rows(w_out.T)
+    gate_weight = gather_cut(line_exchange(w_gate), True)
+    up_weight = gather_cut(line_exchange(w_up), False)
+    down_weight = gather_cut(line_exchange(w_down.T), False)
 
     inverse_one = lax.rsqrt(jnp.mean(state_in * state_in, axis=-1, keepdims=True) + NORM_EPS)
     unit_one = state_in * inverse_one
-    normed_one = pair_gather((unit_one * attn_gain).astype(BF), "x")
+    normed_one = pair_gather((unit_one * attn_gain).astype(BF))
     qkv_proj = rows_dot(normed_one, qkv_weight)
     queries = rotate(
         qkv_proj[:, :head_cols].reshape(group_rows, heads_here, HD), cosine_table, sine_table
@@ -247,7 +330,7 @@
     value_rows = qkv_proj[:, head_cols + kv_cols :].astype(BF).reshape(group_rows, kv_here, HD)
     query_grid = queries.reshape(group_rows, kv_here, group_size, HD)
     attended, capped, probability = attend_forward(query_grid, key_rows, value_rows, allowed)
-    branch = pair_sum(cols_dot(attended, out_weight), "x")
+    branch = pair_sum(cols_dot(attended, out_weight))
     inverse_two = lax.rsqrt(jnp.mean(branch * branch, axis=-1, keepdims=True) + NORM_EPS)
     unit_two = branch * inverse_two
     hidden = state_in + unit_two * attn_post_gain
@@ -257,8 +340,9 @@
     normed_two = line_gather((unit_three * ffn_gain).astype(BF))
     acts, pulls, ffn_part = [], [], 0.0
     for half in range(2):
-        gate_up = rows_dot(normed_two, up_weight[half])
-        act, pull = jax.vjp(gating, gate_up[:, :ff_cut], gate_up[:, ff_cut:])
+        gate = rows_dot(normed_two, gate_weight[half])
+        up = rows_dot(normed_two, up_weight[half])
+        act, pull = jax.vjp(gating, gate, up)
         acts.append(act.astype(BF))
         pulls.append(pull)
         ffn_part = ffn_part + cols_dot(acts[half], down_weight[half])
@@ -270,37 +354,23 @@
     d_ffn = line_gather(
         norm_back(out_cotan * ffn_post_gain, unit_four, inverse_four).astype(BF)
     )
-    d_ups, normed_part = [], 0.0
+    d_gates, d_ups, normed_part = [], [], 0.0
     for half in range(2):
-        d_act = rows_dot(d_ffn, down_weight[half])
-        d_ups.append(jnp.concatenate(pulls[half](d_act), axis=1).astype(BF))
+        d_gate, d_up = pulls[half](rows_dot(d_ffn, down_weight[half]))
+        d_gates.append(d_gate.astype(BF))
+        d_ups.append(d_up.astype(BF))
+        normed_part = normed_part + cols_dot(d_gates[half], gate_weight[half])
         normed_part = normed_part + cols_dot(d_ups[half], up_weight[half])
     d_normed_two = line_sum(normed_part)
-    grad_ffn = []
-    for half in range(2):
-        part = jnp.concatenate(
-            [outer_dot(normed_two, d_ups[half]), outer_dot(d_ffn, acts[half])], axis=1
-        ).astype(BF)
-        grad_ffn.append(row_sum(part, ("c", "y")))
-    x_here = lax.axis_index("x")
-    grad_ffn = jnp.where(x_here == 0, grad_ffn[0], grad_ffn[1]).astype(F32) + swap(
-        jnp.where(x_here == 0, grad_ffn[1], grad_ffn[0]), "x", 1
-    ).astype(F32)
-    grad_ffn = grad_ffn.astype(BF).reshape(z_size, shard, 3 * ff_cut)
-    grad_cut = jnp.zeros((z_size, shard, 3 * ff_cut), F32)
-    z_here = lax.axis_index("z")
-    for k in range(z_size):
-        piece = lax.dynamic_index_in_dim(grad_ffn, z_here ^ k, 0, keepdims=False)
-        piece = piece if k == 0 else swap(piece, "z", k)
-        grad_cut = lax.dynamic_update_index_in_dim(grad_cut, piece.astype(F32), z_here ^ k, 0)
-    grad_cut = grad_cut.reshape(z_size, shard, 3, ff_cut).transpose(2, 1, 0, 3)
-    grad_cut = grad_cut.reshape(3, shard, ff_here)
+    grad_down = line_return(fold_cut(*[outer_low(d_ffn, act) for act in acts], False))
+    grad_up = line_return(fold_cut(*[outer_low(normed_two, d_up) for d_up in d_ups], True))
+    grad_gate = line_return(fold_cut(*[outer_low(normed_two, d_gate) for d_gate in d_gates], True))
 
     gain_three = jnp.sum(d_normed_two * unit_three, axis=0)
     d_hidden = out_cotan + norm_back(d_normed_two * ffn_gain, unit_three, inverse_three)
     gain_two = jnp.sum(d_hidden * unit_two, axis=0)
     d_branch = pair_gather(
-        norm_back(d_hidden * attn_post_gain, unit_two, inverse_two).astype(BF), "x"
+        norm_back(d_hidden * attn_post_gain, unit_two, inverse_two).astype(BF)
     )
     d_attended = rows_dot(d_branch, out_weight).astype(BF)
     grad_grid = d_attended.reshape(group_rows, kv_here, group_size, HD)
@@ -319,29 +389,26 @@
         ],
         axis=1,
     )
-    d_normed_one = pair_sum(cols_dot(d_qkv, qkv_weight), "x")
+    d_normed_one = pair_sum(cols_dot(d_qkv, qkv_weight))
     gain_one = jnp.sum(d_normed_one * unit_one, axis=0)
     grad_tokens = d_hidden + norm_back(d_normed_one * attn_gain, unit_one, inverse_one)
-    grad_attn = jnp.concatenate(
-        [outer_dot(normed_one, d_qkv), outer_dot(d_branch, attended)], axis=1
-    ).astype(BF)
-    grad_attn = row_sum(grad_attn, row_axes).astype(F32)
+    grad_qkv = line_fold(fold(outer_low(normed_one, d_qkv), "y"))
+    grad_out = line_fold(fold(outer_low(d_branch, attended), "y"))
     gains = gain_sum(jnp.stack([gain_one, gain_two, gain_three, gain_four], axis=0))
     key_from, value_from = head_cols, head_cols + kv_cols
-    out_from = head_cols + 2 * kv_cols
     return (
         outward(mixed),
         outward(grad_tokens),
         gains[0],
-        grad_attn[:, :key_from],
-        grad_attn[:, key_from:value_from],
-        grad_attn[:, value_from:out_from],
-        grad_attn[:, out_from:].T,
+        grad_qkv[:, :key_from],
+        grad_qkv[:, key_from:value_from],
+        grad_qkv[:, value_from:],
+        grad_out.T,
         gains[1],
         gains[2],
-        grad_cut[0],
-        grad_cut[1],
-        grad_cut[2].T,
+        grad_gate,
+        grad_up,
+        grad_down.T,
         gains[3],
     )
 

time: 1130 us -> 1140 us (level)
  waiting for transfers between devices: 595 us -> 696 us
  local copies, waits for them, and re-layouts: 176 us -> 98.1 us
  starting transfers between devices: 36.1 us -> 109 us
  other arithmetic: 100 us -> 53.1 us
  blocking collectives: 43 us -> 0 us
  matrix products: 153 us -> 171 us
  between operations: 16.1 us -> 3.33 us
    ppermute x26 -> x86, waiting for transfers between devices: 493 us -> 696 us  [swap(): return lax.ppermute(values, axis, [(i, i ^ mask) for i in range(size)])]
    all_gather x4 -> x0, waiting for transfers between devices: 73.7 us -> none  [the longest x1 39.5 us: on_device(): lax.all_gather(up_line, ('x', 'c', 'y'), axis=0, tiled=True)]
    ppermute x26 -> x86, starting transfers between devices: 35.5 us -> 109 us  [swap(): return lax.ppermute(values, axis, [(i, i ^ mask) for i in range(size)])]
    unnamed x226 -> x318, local copies, waits for them, and re-layouts: 91.4 us -> 23.4 us
    psum x1 -> x0, blocking collectives: 43 us -> none  [gain_sum(): parts = lax.psum(parts, ('z', 'y', 'c', 'x'))]
    concatenate x4 -> x8, other arithmetic: 49.5 us -> 15.4 us  [the longest x6 12.1 us: spread(): values = jnp.concatenate([values, swap(values, axis, mask)], axis=0)]
    reduce_scatter x2 -> x0, waiting for transfers between devices: 27.8 us -> none  [row_sum(): return lax.psum_scatter(parts, axes, scatter_dimension=0, tiled=True)]
    dot_general x6 -> x16, matrix products: 33 us -> 56.1 us  [outer_dot(): lax.dot_general(left, right, (((0,), (0,)), ((), ())), preferred_element_...]
  transfers between devices with their start and end apart: 33 -> 86, of which waited for: 24 -> 50; matrix products, arithmetic and copies ran while one was open for 26% -> 18% of each run, Pallas kernels for 0% -> 0%
where the time goes in v2:
time: 1140 us; the launch traced here: 1130 us
  waiting for transfers between devices  696 us (61%)
  matrix products  171 us (15%)
  starting transfers between devices  109 us (10%)
  local copies, waits for them, and re-layouts  98.1 us (9%)
  other arithmetic  53.1 us (5%)
    ppermute x86, waiting for transfers between devices, swap(): return lax.ppermute(values, axis, [(i, i ^ mask) for i in range(size)])  696 us
    ppermute x86, starting transfers between devices, swap(): return lax.ppermute(values, axis, [(i, i ^ mask) for i in range(size)])  109 us
    dot_general x16, matrix products, outer_dot(): lax.dot_general(left, right, (((0,), (0,)), ((), ())), preferred_element_...  56.1 us
    dot_general x8, matrix products, cols_dot(): lax.dot_general(left, right, (((1,), (1,)), ((), ())), preferred_element_...  54.9 us
    dot_general x8, matrix products, rows_dot(): lax.dot_general(left, right, (((1,), (0,)), ((), ())), preferred_element_...  44 us
    unnamed x318, local copies, waits for them, and re-layouts  23.4 us
  transfers between devices with their start and end apart: 86, of which 50 were waited for; matrix products, arithmetic and copies ran while one was open for 18% of the time, Pallas kernels for 0%

profile of v2, /device:TPU:8, one launch (start us, length us, event | category | flops | bytes accessed | tf_op | source)
XLA Modules:
  0.0 1130.5 jit_solution(8245849175677049303)
XLA Ops:
  57.0 22.6 %collective-permute-done.7 = bf16[144,1024]{1,0:T(8,128)(2,1)} collective-permute-done((bf16[144,1024]{1,0:T(8,128)(2,1)}, bf16[144,1024]{1,0:T(8,128)(2,1)}, u32[]{:S(2)}, u32[]{:S(2)}) %collective-permute-start.7) | collective-permute-done | bytes 294944 | tf_op jit(solution)/shard_map/ppermute | solution.py:73
  91.4 16.6 %collective-permute-done.16 = bf16[144,1152]{1,0:T(8,128)(2,1)S(1)} collective-permute-done((bf16[144,1152]{1,0:T(8,128)(2,1)}, bf16[144,1152]{1,0:T(8,128)(2,1)S(1)}, u32[]{:S(2)}, u32[]{:S(2)}) %collective-permute-start.16) | collective-permute-done | bytes 331808 | tf_op jit(solution)/shard_map/ppermute | solution.py:73
  119.7 8.9 collective-permute-done.21
  131.4 13.3 %collective-permute-done.22 = bf16[144,1152]{1,0:T(8,128)(2,1)S(1)} collective-permute-done((bf16[144,1152]{1,0:T(8,128)(2,1)S(1)}, bf16[144,1152]{1,0:T(8,128)(2,1)S(1)}, u32[]{:S(2)}, u32[]{:S(2)}) %collective-permute-start.22) | collective-permute-done | bytes 331808 | tf_op jit(solution)/shard_map/ppermute | solution.py:73
  159.3 11.7 %collective-permute-done.26 = bf16[144,1152]{1,0:T(8,128)(2,1)S(1)} collective-permute-done((bf16[144,1152]{1,0:T(8,128)(2,1)S(1)}, bf16[144,1152]{1,0:T(8,128)(2,1)S(1)}, u32[]{:S(2)}, u32[]{:S(2)}) %collective-permute-start.26) | collective-permute-done | bytes 331808 | tf_op jit(solution)/shard_map/ppermute | solution.py:73
  180.9 30.3 %collective-permute-done.4 = bf16[576,2048]{1,0:T(8,128)(2,1)S(1)} collective-permute-done((bf16[576,2048]{1,0:T(8,128)(2,1)S(1)}, bf16[576,2048]{1,0:T(8,128)(2,1)S(1)}, u32[]{:S(2)}, u32[]{:S(2)}) %collective-permute-start.4) | collective-permute-done | bytes 2359328 | tf_op jit(solution)/shard_map/ppermute | solution.py:73
  213.4 51.5 %collective-permute-done.23 = bf16[576,1152]{1,0:T(8,128)(2,1)S(1)} collective-permute-done((bf16[576,1152]{1,0:T(8,128)(2,1)S(1)}, bf16[576,1152]{1,0:T(8,128)(2,1)S(1)}, u32[]{:S(2)}, u32[]{:S(2)}) %collective-permute-start.23) | collective-permute-done | bytes 1327136 | tf_op jit(solution)/shard_map/ppermute | solution.py:73
  266.9 26.5 %collective-permute-done.28 = bf16[576,1152]{1,0:T(8,128)(2,1)S(1)} collective-permute-done((bf16[576,1152]{1,0:T(8,128)(2,1)}, bf16[576,1152]{1,0:T(8,128)(2,1)S(1)}, u32[]{:S(2)}, u32[]{:S(2)}) %collective-permute-start.28) | collective-permute-done | bytes 1327136 | tf_op jit(solution)/shard_map/ppermute | solution.py:73
  303.0 18.8 %collective-permute-done.18 = bf16[576,1152]{1,0:T(8,128)(2,1)S(1)} collective-permute-done((bf16[576,1152]{1,0:T(8,128)(2,1)S(1)}, bf16[576,1152]{1,0:T(8,128)(2,1)S(1)}, u32[]{:S(2)}, u32[]{:S(2)}) %collective-permute-start.18) | collective-permute-done | bytes 1327136 | tf_op jit(solution)/shard_map/ppermute | solution.py:73
  323.8 18.3 %collective-permute-done.31 = bf16[576,1152]{1,0:T(8,128)(2,1)S(1)} collective-permute-done((bf16[576,1152]{1,0:T(8,128)(2,1)S(1)}, bf16[576,1152]{1,0:T(8,128)(2,1)S(1)}, u32[]{:S(2)}, u32[]{:S(2)}) %collective-permute-start.31) | collective-permute-done | bytes 1327136 | tf_op jit(solution)/shard_map/ppermute | solution.py:73
  345.4 8.8 collective-permute-done.33
  357.7 36.0 %collective-permute-done.35 = bf16[1152,1152]{1,0:T(8,128)(2,1)S(1)} collective-permute-done((bf16[1152,1152]{1,0:T(8,128)(2,1)}, bf16[1152,1152]{1,0:T(8,128)(2,1)S(1)}, u32[]{:S(2)}, u32[]{:S(2)}) %collective-permute-start.35) | collective-permute-done | bytes 2654240 | tf_op jit(solution)/shard_map/ppermute | solution.py:73
  417.9 11.2 collective-permute-done.11
  438.6 33.2 %collective-permute-done.14 = bf16[128,2304]{1,0:T(8,128)(2,1)S(1)} collective-permute-done((bf16[128,2304]{1,0:T(8,128)(2,1)S(1)}, bf16[128,2304]{1,0:T(8,128)(2,1)S(1)}, u32[]{:S(2)}, u32[]{:S(2)}) %collective-permute-start.14) | collective-permute-done | bytes 589856 | tf_op jit(solution)/shard_map/ppermute | solution.py:73
  472.2 9.6 collective-permute-done.13
  481.9 13.8 %collective-permute-done.12 = bf16[128,2304]{1,0:T(8,128)(2,1)S(1)} collective-permute-done((bf16[128,2304]{1,0:T(8,128)(2,1)S(1)}, bf16[128,2304]{1,0:T(8,128)(2,1)S(1)}, u32[]{:S(2)}, u32[]{:S(2)}) %collective-permute-start.12) | collective-permute-done | bytes 589856 | tf_op jit(solution)/shard_map/ppermute | solution.py:73
  543.5 28.8 %collective-permute-done.39 = bf16[128,2304]{1,0:T(8,128)(2,1)} collective-permute-done((bf16[128,2304]{1,0:T(8,128)(2,1)}, bf16[128,2304]{1,0:T(8,128)(2,1)}, u32[]{:S(2)}, u32[]{:S(2)}) %collective-permute-start.39) | collective-permute-done | bytes 589856 | tf_op jit(solution)/shard_map/ppermute | solution.py:73
  572.3 9.5 collective-permute-done.38
  602.1 26.2 %collective-permute-done.42 = bf16[128,2304]{1,0:T(8,128)(2,1)} collective-permute-done((bf16[128,2304]{1,0:T(8,128)(2,1)}, bf16[128,2304]{1,0:T(8,128)(2,1)}, u32[]{:S(2)}, u32[]{:S(2)}) %collective-permute-start.42) | collective-permute-done | bytes 589856 | tf_op jit(solution)/shard_map/ppermute | solution.py:73
  628.3 10.0 collective-permute-done.41
  638.3 9.1 multiply_convert_fusion
  678.1 10.1 fusion.15
  704.1 31.5 %collective-permute-done.45 = bf16[128,2304]{1,0:T(8,128)(2,1)S(1)} collective-permute-done((bf16[128,2304]{1,0:T(8,128)(2,1)S(1)}, bf16[128,2304]{1,0:T(8,128)(2,1)S(1)}, u32[]{:S(2)}, u32[]{:S(2)}) %collective-permute-start.45) | collective-permute-done | bytes 589856 | tf_op jit(solution)/shard_map/ppermute | solution.py:73
  845.3 16.3 %collective-permute-done.60 = bf16[576,1024]{1,0:T(8,128)(2,1)} collective-permute-done((bf16[576,1024]{1,0:T(8,128)(2,1)}, bf16[576,1024]{1,0:T(8,128)(2,1)}, u32[]{:S(2)}, u32[]{:S(2)}) %collective-permute-start.60) | collective-permute-done | bytes 1179680 | tf_op jit(solution)/shard_map/ppermute | solution.py:73
  911.4 21.6 %collective-permute-done.79 = bf16[576,1152]{1,0:T(8,128)(2,1)S(1)} collective-permute-done((bf16[576,1152]{1,0:T(8,128)(2,1)S(1)}, bf16[576,1152]{1,0:T(8,128)(2,1)S(1)}, u32[]{:S(2)}, u32[]{:S(2)}) %collective-permute-start.79) | collective-permute-done | bytes 1327136 | tf_op jit(solution)/shard_map/ppermute | solution.py:73
  934.5 42.4 %collective-permute-done.82 = bf16[576,1152]{1,0:T(8,128)(2,1)S(1)} collective-permute-done((bf16[576,1152]{1,0:T(8,128)(2,1)S(1)}, bf16[576,1152]{1,0:T(8,128)(2,1)S(1)}, u32[]{:S(2)}, u32[]{:S(2)}) %collective-permute-start.82) | collective-permute-done | bytes 1327136 | tf_op jit(solution)/shard_map/ppermute | solution.py:73
  990.9 18.6 %collective-permute-done.84 = bf16[144,1152]{1,0:T(8,128)(2,1)S(1)} collective-permute-done((bf16[144,1152]{1,0:T(8,128)(2,1)S(1)}, bf16[144,1152]{1,0:T(8,128)(2,1)S(1)}, u32[]{:S(2)}, u32[]{:S(2)}) %collective-permute-start.84) | collective-permute-done | bytes 331808 | tf_op jit(solution)/shard_map/ppermute | solution.py:73
  1025.1 9.0 collective-permute-done.68
  1045.4 21.9 %collective-permute-done.70 = bf16[144,1152]{1,0:T(8,128)(2,1)S(1)} collective-permute-done((bf16[144,1152]{1,0:T(8,128)(2,1)S(1)}, bf16[144,1152]{1,0:T(8,128)(2,1)S(1)}, u32[]{:S(2)}, u32[]{:S(2)}) %collective-permute-start.70) | collective-permute-done | bytes 331808 | tf_op jit(solution)/shard_map/ppermute | solution.py:73
  1075.0 23.6 %collective-permute-done.76 = bf16[144,1152]{1,0:T(8,128)(2,1)S(1)} collective-permute-done((bf16[144,1152]{1,0:T(8,128)(2,1)S(1)}, bf16[144,1152]{1,0:T(8,128)(2,1)S(1)}, u32[]{:S(2)}, u32[]{:S(2)}) %collective-permute-start.76) | collective-permute-done | bytes 331808 | tf_op jit(solution)/shard_map/ppermute | solution.py:73
  1106.9 12.6 %collective-permute-done.58 = bf16[144,2048]{1,0:T(8,128)(2,1)S(1)} collective-permute-done((bf16[144,2048]{1,0:T(8,128)(2,1)S(1)}, bf16[144,2048]{1,0:T(8,128)(2,1)S(1)}, u32[]{:S(2)}, u32[]{:S(2)}) %collective-permute-start.58) | collective-permute-done | bytes 589856 | tf_op jit(solution)/shard_map/ppermute | solution.py:73
  1119.4 8.7 collective-permute-done.57
  (696 shorter events, 496.2 us)
Async XLA Ops:
  5.5 140.7 %collective-permute-start.1 = (bf16[144,2048]{1,0:T(8,128)(2,1)}, bf16[144,2048]{1,0:T(8,128)(2,1)}, u32[]{:S(2)}, u32[]{:S(2)}) collective-permute-start(bf16[144,2048]{1,0:T(8,128)(2,1)} %constant_dynamic-update-slice_fusion), channel_id=1, source_target_pairs={{0,8},{8,0},{16,24},{24,16},{1,9},{9,1},{17,25},{25,17},{2,10},{10... | collective-permute-start | bytes 1769480 | tf_op jit(solution)/shard_map/ppermute | solution.py:73
  5.5 142.3 %collective-permute-start.2 = (bf16[144,2048]{1,0:T(8,128)(2,1)}, bf16[144,2048]{1,0:T(8,128)(2,1)}, u32[]{:S(2)}, u32[]{:S(2)}) collective-permute-start(bf16[144,2048]{1,0:T(8,128)(2,1)} %constant_dynamic-update-slice_fusion), channel_id=1, source_target_pairs={{0,16},{8,24},{16,0},{24,8},{1,17},{9,25},{17,1},{25,9},{2,18},{10... | collective-permute-start | bytes 1769480 | tf_op jit(solution)/shard_map/ppermute | solution.py:73
  8.5 142.0 %collective-permute-start.3 = (bf16[144,2048]{1,0:T(8,128)(2,1)}, bf16[144,2048]{1,0:T(8,128)(2,1)}, u32[]{:S(2)}, u32[]{:S(2)}) collective-permute-start(bf16[144,2048]{1,0:T(8,128)(2,1)} %constant_dynamic-update-slice_fusion), channel_id=1, source_target_pairs={{0,24},{8,16},{16,8},{24,0},{1,25},{9,17},{17,9},{25,1},{2,26},{10... | collective-permute-start | bytes 1769480 | tf_op jit(solution)/shard_map/ppermute | solution.py:73
  10.1 69.4 %collective-permute-start.7 = (bf16[144,1024]{1,0:T(8,128)(2,1)}, bf16[144,1024]{1,0:T(8,128)(2,1)}, u32[]{:S(2)}, u32[]{:S(2)}) collective-permute-start(bf16[144,1024]{1,0:T(8,128)(2,1)} %bitcast.272), channel_id=1, source_target_pairs={{0,16},{8,24},{16,0},{24,8},{1,17},{9,25},{17,1},{25,9},{2,18},{10... | collective-permute-start | bytes 884744 | tf_op jit(solution)/shard_map/ppermute | solution.py:73
  88.7 90.6 %collective-permute-start.17 = (bf16[144,1152]{1,0:T(8,128)(2,1)}, bf16[144,1152]{1,0:T(8,128)(2,1)S(1)}, u32[]{:S(2)}, u32[]{:S(2)}) collective-permute-start(bf16[144,1152]{1,0:T(8,128)(2,1)} %get-tuple-element.93), channel_id=1, source_target_pairs={{0,24},{8,16},{16,8},{24,0},{1,25},{9,17},{17,9},{25,1},{2,26},{10... | collective-permute-start | bytes 995336 | tf_op jit(solution)/shard_map/ppermute | solution.py:73
  157.0 54.2 %collective-permute-start.4 = (bf16[576,2048]{1,0:T(8,128)(2,1)S(1)}, bf16[576,2048]{1,0:T(8,128)(2,1)S(1)}, u32[]{:S(2)}, u32[]{:S(2)}) collective-permute-start(bf16[576,2048]{1,0:T(8,128)(2,1)S(1)} %bitcast.228), channel_id=1, source_target_pairs={{0,4},{4,0},{1,5},{5,1},{2,6},{6,2},{3,7},{7,3},{8,12},{12,8},{9,1... | collective-permute-start | bytes 7077896 | tf_op jit(solution)/shard_map/ppermute | solution.py:73
  171.0 127.5 %collective-permute-start.9 = (bf16[576,1024]{1,0:T(8,128)(2,1)}, bf16[576,1024]{1,0:T(8,128)(2,1)S(1)}, u32[]{:S(2)}, u32[]{:S(2)}) collective-permute-start(bf16[576,1024]{1,0:T(8,128)(2,1)} %bitcast.29), channel_id=1, source_target_pairs={{0,4},{4,0},{1,5},{5,1},{2,6},{6,2},{3,7},{7,3},{8,12},{12,8},{9,1... | collective-permute-start | bytes 3538952 | tf_op jit(solution)/shard_map/ppermute | solution.py:73
  177.1 87.9 %collective-permute-start.23 = (bf16[576,1152]{1,0:T(8,128)(2,1)S(1)}, bf16[576,1152]{1,0:T(8,128)(2,1)S(1)}, u32[]{:S(2)}, u32[]{:S(2)}) collective-permute-start(bf16[576,1152]{1,0:T(8,128)(2,1)S(1)} %bitcast.237), channel_id=1, source_target_pairs={{0,4},{4,0},{1,5},{5,1},{2,6},{6,2},{3,7},{7,3},{8,12},{12,8},{9,1... | collective-permute-start | bytes 3981320 | tf_op jit(solution)/shard_map/ppermute | solution.py:73
  179.4 114.0 %collective-permute-start.28 = (bf16[576,1152]{1,0:T(8,128)(2,1)}, bf16[576,1152]{1,0:T(8,128)(2,1)S(1)}, u32[]{:S(2)}, u32[]{:S(2)}) collective-permute-start(bf16[576,1152]{1,0:T(8,128)(2,1)} %bitcast.50), channel_id=1, source_target_pairs={{0,4},{4,0},{1,5},{5,1},{2,6},{6,2},{3,7},{7,3},{8,12},{12,8},{9,1... | collective-permute-start | bytes 3981320 | tf_op jit(solution)/shard_map/ppermute | solution.py:73
  179.9 114.0 %collective-permute-start.30 = (bf16[576,1152]{1,0:T(8,128)(2,1)S(1)}, bf16[576,1152]{1,0:T(8,128)(2,1)S(1)}, u32[]{:S(2)}, u32[]{:S(2)}) collective-permute-start(bf16[576,1152]{1,0:T(8,128)(2,1)S(1)} %bitcast.232), channel_id=1, source_target_pairs={{0,1},{1,0},{2,3},{3,2},{4,5},{5,4},{6,7},{7,6},{8,9},{9,8},{10,11... | collective-permute-start | bytes 3981320 | tf_op jit(solution)/shard_map/ppermute | solution.py:73
  211.2 110.6 %collective-permute-start.18 = (bf16[576,1152]{1,0:T(8,128)(2,1)S(1)}, bf16[576,1152]{1,0:T(8,128)(2,1)S(1)}, u32[]{:S(2)}, u32[]{:S(2)}) collective-permute-start(bf16[576,1152]{1,0:T(8,128)(2,1)S(1)} %bitcast.233), channel_id=1, source_target_pairs={{0,4},{4,0},{1,5},{5,1},{2,6},{6,2},{3,7},{7,3},{8,12},{12,8},{9,1... | collective-permute-start | bytes 3981320 | tf_op jit(solution)/shard_map/ppermute | solution.py:73
  265.0 131.2 %collective-permute-start.5 = (bf16[1152,2048]{1,0:T(8,128)(2,1)S(1)}, bf16[1152,2048]{1,0:T(8,128)(2,1)S(1)}, u32[]{:S(2)}, u32[]{:S(2)}) collective-permute-start(bf16[1152,2048]{1,0:T(8,128)(2,1)S(1)} %pad_maximum_fusion.4), channel_id=1, source_target_pairs={{0,2},{2,0},{1,3},{3,1},{4,6},{6,4},{5,7},{7,5},{8,10},{10,8},{9,1... | collective-permute-start | bytes 14155784 | tf_op jit(solution)/shard_map/ppermute | solution.py:73
  293.4 60.8 %collective-permute-start.33 = (bf16[1152,1152]{1,0:T(8,128)(2,1)}, bf16[1152,1152]{1,0:T(8,128)(2,1)}, u32[]{:S(2)}, u32[]{:S(2)}) collective-permute-start(bf16[1152,1152]{1,0:T(8,128)(2,1)} %pad_maximum_fusion.9), channel_id=1, source_target_pairs={{0,1},{1,0},{2,3},{3,2},{4,5},{5,4},{6,7},{7,6},{8,9},{9,8},{10,11... | collective-permute-start | bytes 7962632 | tf_op jit(solution)/shard_map/ppermute | solution.py:73
  298.5 95.3 %collective-permute-start.35 = (bf16[1152,1152]{1,0:T(8,128)(2,1)}, bf16[1152,1152]{1,0:T(8,128)(2,1)S(1)}, u32[]{:S(2)}, u32[]{:S(2)}) collective-permute-start(bf16[1152,1152]{1,0:T(8,128)(2,1)} %pad_maximum_fusion.10), channel_id=1, source_target_pairs={{0,1},{1,0},{2,3},{3,2},{4,5},{5,4},{6,7},{7,6},{8,9},{9,8},{10,11... | collective-permute-start | bytes 7962632 | tf_op jit(solution)/shard_map/ppermute | solution.py:73
  321.8 86.2 %collective-permute-start.10 = (bf16[1152,1024]{1,0:T(8,128)(2,1)}, bf16[1152,1024]{1,0:T(8,128)(2,1)}, u32[]{:S(2)}, u32[]{:S(2)}) collective-permute-start(bf16[1152,1024]{1,0:T(8,128)(2,1)} %pad_maximum_fusion.12), channel_id=1, source_target_pairs={{0,2},{2,0},{1,3},{3,1},{4,6},{6,4},{5,7},{7,5},{8,10},{10,8},{9,1... | collective-permute-start | bytes 7077896 | tf_op jit(solution)/shard_map/ppermute | solution.py:73
  342.1 162.9 %collective-permute-start.24 = (bf16[1152,1152]{1,0:T(8,128)(2,1)}, bf16[1152,1152]{1,0:T(8,128)(2,1)}, u32[]{:S(2)}, u32[]{:S(2)}) collective-permute-start(bf16[1152,1152]{1,0:T(8,128)(2,1)} %pad_maximum_fusion.9), channel_id=1, source_target_pairs={{0,2},{2,0},{1,3},{3,1},{4,6},{6,4},{5,7},{7,5},{8,10},{10,8},{9,1... | collective-permute-start | bytes 7962632 | tf_op jit(solution)/shard_map/ppermute | solution.py:73
  354.2 158.2 %collective-permute-start.29 = (bf16[1152,1152]{1,0:T(8,128)(2,1)}, bf16[1152,1152]{1,0:T(8,128)(2,1)}, u32[]{:S(2)}, u32[]{:S(2)}) collective-permute-start(bf16[1152,1152]{1,0:T(8,128)(2,1)} %pad_maximum_fusion.10), channel_id=1, source_target_pairs={{0,2},{2,0},{1,3},{3,1},{4,6},{6,4},{5,7},{7,5},{8,10},{10,8},{9,1... | collective-permute-start | bytes 7962632 | tf_op jit(solution)/shard_map/ppermute | solution.py:73
  429.1 71.2 %collective-permute-start.19 = (bf16[1152,1152]{1,0:T(8,128)(2,1)S(1)}, bf16[1152,1152]{1,0:T(8,128)(2,1)S(1)}, u32[]{:S(2)}, u32[]{:S(2)}) collective-permute-start(bf16[1152,1152]{1,0:T(8,128)(2,1)S(1)} %copy-done.20), channel_id=1, source_target_pairs={{0,2},{2,0},{1,3},{3,1},{4,6},{6,4},{5,7},{7,5},{8,10},{10,8},{9,1... | collective-permute-start | bytes 7962632 | tf_op jit(solution)/shard_map/ppermute | solution.py:73
  530.8 51.0 %collective-permute-start.38 = (bf16[128,2304]{1,0:T(8,128)(2,1)}, bf16[128,2304]{1,0:T(8,128)(2,1)}, u32[]{:S(2)}, u32[]{:S(2)}) collective-permute-start(bf16[128,2304]{1,0:T(8,128)(2,1)} %get-tuple-element.80), channel_id=1, source_target_pairs={{0,16},{8,24},{16,0},{24,8},{1,17},{9,25},{17,1},{25,9},{2,18},{10... | collective-permute-start | bytes 1769480 | tf_op jit(solution)/shard_map/ppermute | solution.py:73
  819.5 53.2 %collective-permute-start.72 = (bf16[1152,1152]{1,0:T(8,128)(2,1)}, bf16[1152,1152]{1,0:T(8,128)(2,1)}, u32[]{:S(2)}, u32[]{:S(2)}) collective-permute-start(bf16[1152,1152]{1,0:T(8,128)(2,1)} %convolution_convert_fusion.2), channel_id=1, source_target_pairs={{0,2},{2,0},{1,3},{3,1},{4,6},{6,4},{5,7},{7,5},{8,10},{10,8},{9,1... | collective-permute-start | bytes 7962632 | tf_op jit(solution)/shard_map/ppermute | solution.py:73
  819.6 60.2 %collective-permute-start.64 = (bf16[1152,1152]{1,0:T(8,128)(2,1)}, bf16[1152,1152]{1,0:T(8,128)(2,1)}, u32[]{:S(2)}, u32[]{:S(2)}) collective-permute-start(bf16[1152,1152]{1,0:T(8,128)(2,1)} %convolution_convert_fusion.5), channel_id=1, source_target_pairs={{0,2},{2,0},{1,3},{3,1},{4,6},{6,4},{5,7},{7,5},{8,10},{10,8},{9,1... | collective-permute-start | bytes 7962632 | tf_op jit(solution)/shard_map/ppermute | solution.py:73
  831.0 73.7 %collective-permute-start.66 = (bf16[1152,1152]{1,0:T(8,128)(2,1)}, bf16[1152,1152]{1,0:T(8,128)(2,1)}, u32[]{:S(2)}, u32[]{:S(2)}) collective-permute-start(bf16[1152,1152]{1,0:T(8,128)(2,1)} %fusion.7), channel_id=1, source_target_pairs={{0,1},{1,0},{2,3},{3,2},{4,5},{5,4},{6,7},{7,6},{8,9},{9,8},{10,11... | collective-permute-start | bytes 7962632 | tf_op jit(solution)/shard_map/ppermute | solution.py:73
  879.9 100.7 %collective-permute-start.71 = (bf16[1152,1152]{1,0:T(8,128)(2,1)S(1)}, bf16[1152,1152]{1,0:T(8,128)(2,1)S(1)}, u32[]{:S(2)}, u32[]{:S(2)}) collective-permute-start(bf16[1152,1152]{1,0:T(8,128)(2,1)S(1)} %copy-done.121), channel_id=1, source_target_pairs={{0,2},{2,0},{1,3},{3,1},{4,6},{6,4},{5,7},{7,5},{8,10},{10,8},{9,1... | collective-permute-start | bytes 7962632 | tf_op jit(solution)/shard_map/ppermute | solution.py:73
  888.5 127.9 %collective-permute-start.54 = (bf16[1152,2048]{1,0:T(8,128)(2,1)S(1)}, bf16[1152,2048]{1,0:T(8,128)(2,1)S(1)}, u32[]{:S(2)}, u32[]{:S(2)}) collective-permute-start(bf16[1152,2048]{1,0:T(8,128)(2,1)S(1)} %bitcast.301), channel_id=1, source_target_pairs={{0,2},{2,0},{1,3},{3,1},{4,6},{6,4},{5,7},{7,5},{8,10},{10,8},{9,1... | collective-permute-start | bytes 14155784 | tf_op jit(solution)/shard_map/ppermute | solution.py:73
  889.8 90.8 %collective-permute-start.73 = (bf16[1152,1152]{1,0:T(8,128)(2,1)S(1)}, bf16[1152,1152]{1,0:T(8,128)(2,1)}, u32[]{:S(2)}, u32[]{:S(2)}) collective-permute-start(bf16[1152,1152]{1,0:T(8,128)(2,1)S(1)} %fusion.12), channel_id=1, source_target_pairs={{0,1},{1,0},{2,3},{3,2},{4,5},{5,4},{6,7},{7,6},{8,9},{9,8},{10,11... | collective-permute-start | bytes 7962632 | tf_op jit(solution)/shard_map/ppermute | solution.py:73
  904.7 72.2 %collective-permute-start.82 = (bf16[576,1152]{1,0:T(8,128)(2,1)S(1)}, bf16[576,1152]{1,0:T(8,128)(2,1)S(1)}, u32[]{:S(2)}, u32[]{:S(2)}) collective-permute-start(bf16[576,1152]{1,0:T(8,128)(2,1)S(1)} %add_convert_fusion.2), channel_id=1, source_target_pairs={{0,1},{1,0},{2,3},{3,2},{4,5},{5,4},{6,7},{7,6},{8,9},{9,8},{10,11... | collective-permute-start | bytes 3981320 | tf_op jit(solution)/shard_map/ppermute | solution.py:73
  933.0 85.9 %collective-permute-start.67 = (bf16[576,1152]{1,0:T(8,128)(2,1)S(1)}, bf16[576,1152]{1,0:T(8,128)(2,1)S(1)}, u32[]{:S(2)}, u32[]{:S(2)}) collective-permute-start(bf16[576,1152]{1,0:T(8,128)(2,1)S(1)} %slice.259), channel_id=1, source_target_pairs={{0,4},{4,0},{1,5},{5,1},{2,6},{6,2},{3,7},{7,3},{8,12},{12,8},{9,1... | collective-permute-start | bytes 3981320 | tf_op jit(solution)/shard_map/ppermute | solution.py:73
  1018.3 52.0 %collective-permute-start.55 = (bf16[576,2048]{1,0:T(8,128)(2,1)S(1)}, bf16[576,2048]{1,0:T(8,128)(2,1)S(1)}, u32[]{:S(2)}, u32[]{:S(2)}) collective-permute-start(bf16[576,2048]{1,0:T(8,128)(2,1)S(1)} %slice.244), channel_id=1, source_target_pairs={{0,4},{4,0},{1,5},{5,1},{2,6},{6,2},{3,7},{7,3},{8,12},{12,8},{9,1... | collective-permute-start | bytes 7077896 | tf_op jit(solution)/shard_map/ppermute | solution.py:73
  1034.1 64.6 %collective-permute-start.76 = (bf16[144,1152]{1,0:T(8,128)(2,1)S(1)}, bf16[144,1152]{1,0:T(8,128)(2,1)S(1)}, u32[]{:S(2)}, u32[]{:S(2)}) collective-permute-start(bf16[144,1152]{1,0:T(8,128)(2,1)S(1)} %get-tuple-element.85), channel_id=1, source_target_pairs={{0,16},{8,24},{16,0},{24,8},{1,17},{9,25},{17,1},{25,9},{2,18},{10... | collective-permute-start | bytes 995336 | tf_op jit(solution)/shard_map/ppermute | solution.py:73
  1044.9 61.9 %collective-permute-start.77 = (bf16[144,1152]{1,0:T(8,128)(2,1)S(1)}, bf16[144,1152]{1,0:T(8,128)(2,1)S(1)}, u32[]{:S(2)}, u32[]{:S(2)}) collective-permute-start(bf16[144,1152]{1,0:T(8,128)(2,1)S(1)} %get-tuple-element.84), channel_id=1, source_target_pairs={{0,24},{8,16},{16,8},{24,0},{1,25},{9,17},{17,9},{25,1},{2,26},{10... | collective-permute-start | bytes 995336 | tf_op jit(solution)/shard_map/ppermute | solution.py:73
  1073.1 55.0 %collective-permute-start.57 = (bf16[144,2048]{1,0:T(8,128)(2,1)S(1)}, bf16[144,2048]{1,0:T(8,128)(2,1)S(1)}, u32[]{:S(2)}, u32[]{:S(2)}) collective-permute-start(bf16[144,2048]{1,0:T(8,128)(2,1)S(1)} %get-tuple-element.74), channel_id=1, source_target_pairs={{0,16},{8,24},{16,0},{24,8},{1,17},{9,25},{17,1},{25,9},{2,18},{10... | collective-permute-start | bytes 1769480 | tf_op jit(solution)/shard_map/ppermute | solution.py:73
  1073.1 55.0 %collective-permute-start.56 = (bf16[144,2048]{1,0:T(8,128)(2,1)S(1)}, bf16[144,2048]{1,0:T(8,128)(2,1)S(1)}, u32[]{:S(2)}, u32[]{:S(2)}) collective-permute-start(bf16[144,2048]{1,0:T(8,128)(2,1)S(1)} %get-tuple-element.72), channel_id=1, source_target_pairs={{0,8},{8,0},{16,24},{24,16},{1,9},{9,1},{17,25},{25,17},{2,10},{10... | collective-permute-start | bytes 1769480 | tf_op jit(solution)/shard_map/ppermute | solution.py:73
  (206 other events, 5580.8 us)

commit v3 on v2

--- a/solution.py
+++ b/solution.py
@@ -85,37 +85,43 @@
     return lax.dot_general(left, right, (((0,), (0,)), ((), ())), preferred_element_type=F32)
 
 
-def pair_gather(values):
+def meet(*values):
+    return lax.optimization_barrier(values)
+
+
+def pair_gather(values, other):
     mine = lax.axis_index("x")
-    other = swap(values, "x", 1)
     first = jnp.where(mine == 0, values, other)
     second = jnp.where(mine == 0, other, values)
     return jnp.concatenate([first, second], axis=0)
 
 
-def pair_sum(partial):
+def pair_parts(partial):
     rows = partial.shape[0] // 2
     mine = lax.axis_index("x")
     sent = lax.dynamic_slice_in_dim(partial, (1 - mine) * rows, rows, 0).astype(BF)
-    kept = lax.dynamic_slice_in_dim(partial, mine * rows, rows, 0)
+    return sent, lax.dynamic_slice_in_dim(partial, mine * rows, rows, 0)
+
+
+def pair_sum(partial):
+    sent, kept = pair_parts(partial)
     return kept + swap(sent, "x", 1).astype(F32)
 
 
-def masks(axis):
-    return [1 << i for i in range(lax.axis_size(axis).bit_length() - 1)]
-
-
-def fold(values, axis):
-    for mask in reversed(masks(axis)):
-        rows = values.shape[0] // 2
-        values = add_low(values[:rows], swap(values[rows:], axis, mask))
-    return values
-
-
-def spread(values, axis):
-    for mask in masks(axis):
-        values = jnp.concatenate([values, swap(values, axis, mask)], axis=0)
-    return values
+def rows_sum(values, axis):
+    size = lax.axis_size(axis)
+    if size != 2:
+        return lax.psum_scatter(values, axis, scatter_dimension=0, tiled=True)
+    rows, mine = values.shape[0] // 2, lax.axis_index(axis)
+    sent = lax.dynamic_slice_in_dim(values, (1 - mine) * rows, rows, 0)
+    return add_low(lax.dynamic_slice_in_dim(values, mine * rows, rows, 0), swap(sent, axis, 1))
+
+
+def placed(rows, *pieces):
+    held = jnp.zeros((rows,) + pieces[0][1].shape[1:], pieces[0][1].dtype)
+    for offset, piece in pieces:
+        held = lax.dynamic_update_slice_in_dim(held, piece, offset, 0)
+    return held
 
 
 def add_low(left, right):
@@ -135,21 +141,17 @@
 
 
 def line_place(pieces):
-    here = lax.axis_index("z")
-    held = jnp.zeros((len(pieces),) + pieces[0].shape, pieces[0].dtype)
-    for k, piece in enumerate(pieces):
-        held = lax.dynamic_update_index_in_dim(held, piece, here ^ k, 0)
-    return held
-
-
-def line_exchange(weight):
-    rows, cols = weight.shape
-    here, cut = lax.axis_index("z"), cols // 4
-    pieces = []
-    for k in range(4):
-        piece = lax.dynamic_slice_in_dim(weight, (here ^ k) * cut, cut, 1)
-        pieces.append(piece if k == 0 else swap(piece, "z", k))
-    return line_place(pieces).reshape(4 * rows, cut)
+    here, rows = lax.axis_index("z"), pieces[0].shape[0]
+    return placed(len(pieces) * rows, *[((here ^ k) * rows, p) for k, p in enumerate(pieces)])
+
+
+def line_cuts(weight):
+    here, cut = lax.axis_index("z"), weight.shape[1] // 4
+    return [lax.dynamic_slice_in_dim(weight, (here ^ k) * cut, cut, 1) for k in range(4)]
+
+
+def line_swaps(cuts):
+    return [cuts[0]] + [swap(cuts[k], "z", k) for k in (1, 2, 3)]
 
 
 def line_return(grad):
@@ -173,44 +175,137 @@
     return total
 
 
-def gather_rows(weight):
-    line = line_place([weight] + [swap(weight, "z", k) for k in (1, 2, 3)])
-    return spread(spread(line.reshape(-1, weight.shape[1]), "y"), "c")
-
-
-def gather_cut(weight, x_first):
-    if x_first:
-        halves = [weight, swap(weight, "x", 1)]
-        halves = [spread(half, "y") for half in halves]
-    else:
-        mine = spread(weight, "y")
-        halves = [mine, swap(mine, "x", 1)]
-    return [spread(half, "c") for half in halves]
-
-
-def fold_cut(mine, other, x_first):
-    if x_first:
-        return fold(add_low(mine, swap(other, "x", 1)), "y")
-    mine, other = fold(mine, "y"), fold(other, "y")
-    return add_low(mine, swap(other, "x", 1))
+def both_cores(rows):
+    return pair_rows(rows, swap(rows, "c", 1), "c")
+
+
+def pair_rows(mine, other, axis):
+    rows, here = mine.shape[0], lax.axis_index(axis)
+    return placed(2 * rows, (here * rows, mine), ((1 - here) * rows, other))
+
+
+class Cut:
+    def __init__(self, own):
+        self.own, self.pairs = own, lax.axis_size("y") == 2
+
+    def first(self):
+        self.via_x = swap(self.own, "x", 1)
+        if self.pairs:
+            self.via_y = swap(self.own, "y", 1)
+            return [self.via_x, self.via_y]
+        return [self.via_x]
+
+    def take(self, values):
+        self.via_x = values[0]
+        if self.pairs:
+            self.via_y = values[1]
+
+    def second(self, over_x):
+        if not self.pairs:
+            return []
+        self.across = []
+        if over_x:
+            self.across.append(swap(self.via_y[:over_x], "x", 1))
+        if over_x < self.own.shape[0]:
+            self.across.append(swap(self.via_x[over_x:], "y", 1))
+        return list(self.across)
+
+    def take_second(self, values):
+        self.across = list(values)
+
+    def whole(self):
+        if not self.pairs:
+            halves = [lax.all_gather(v, "y", axis=0, tiled=True) for v in (self.own, self.via_x)]
+            return [both_cores(half) for half in halves]
+        rows, here = self.own.shape[0], lax.axis_index("y")
+        mine = pair_rows(self.own, self.via_y, "y")
+        pieces, at = [(here * rows, self.via_x)], (1 - here) * rows
+        for piece in self.across:
+            pieces.append((at, piece))
+            at = at + piece.shape[0]
+        return [both_cores(mine), both_cores(placed(2 * rows, *pieces))]
+
+
+class Fold:
+    def __init__(self, mine, other, over_x):
+        self.mine, self.other, self.over_x = mine, other, over_x
+        self.pairs = lax.axis_size("y") == 2
+
+    def halves(self, values):
+        rows, here = values.shape[0] // 2, lax.axis_index("y")
+        return (
+            lax.dynamic_slice_in_dim(values, here * rows, rows, 0),
+            lax.dynamic_slice_in_dim(values, (1 - here) * rows, rows, 0),
+        )
+
+    def first(self):
+        if not self.pairs:
+            self.mine = rows_sum(self.mine, "y")
+            self.other = rows_sum(self.other, "y")
+            return []
+        self.mine, self.mine_far = self.halves(self.mine)
+        self.other, self.other_far = self.halves(self.other)
+        self.got = []
+        if self.over_x:
+            self.got.append(swap(self.other_far[: self.over_x], "x", 1))
+        if self.over_x < self.mine.shape[0]:
+            self.got.append(swap(self.other_far[self.over_x :], "y", 1))
+        return list(self.got)
+
+    def take(self, values):
+        self.got = list(values)
+
+    def second(self):
+        if self.pairs:
+            got, at = list(self.got), self.over_x
+            if at:
+                piece = add_low(self.mine_far[:at], got.pop(0))
+                self.mine_far = (
+                    jnp.concatenate([piece, self.mine_far[at:]], axis=0) if got else piece
+                )
+            if got:
+                piece = add_low(self.other[at:], got[0])
+                self.other = jnp.concatenate([self.other[:at], piece], axis=0) if at else piece
+            self.last = [swap(self.other, "x", 1), swap(self.mine_far, "y", 1)]
+        else:
+            self.last = [swap(self.other, "x", 1)]
+        return list(self.last)
+
+    def take_second(self, values):
+        self.last = list(values)
+
+    def whole(self):
+        total = self.mine.astype(F32)
+        for piece in self.last:
+            total = total + piece.astype(F32)
+        return total.astype(BF)
 
 
 def outer_low(left, right):
     cut = left.shape[1] // 2
-    sent = outer_dot(left[:, cut:], right).astype(BF)
-    return (outer_dot(left[:, :cut], right) + swap(sent, "c", 1).astype(F32)).astype(BF)
+    here = lax.axis_index("c")
+    theirs = lax.dynamic_slice_in_dim(left, (1 - here) * cut, cut, 1)
+    mine = lax.dynamic_slice_in_dim(left, here * cut, cut, 1)
+    sent = outer_dot(theirs, right).astype(BF)
+    return (outer_dot(mine, right) + swap(sent, "c", 1).astype(F32)).astype(BF)
 
 
 def gain_sum(parts):
     count, width = parts.shape
-    z_size = lax.axis_size("z")
-    blocks = lax.axis_size("c") * lax.axis_size("y") * z_size
+    blocks = lax.axis_size("c") * lax.axis_size("y") * lax.axis_size("z")
     parts = parts.reshape(count, blocks, width // blocks).transpose(1, 0, 2)
     parts = parts + swap(parts, "x", 1)
-    for axis in ("c", "y"):
-        for mask in reversed(masks(axis)):
-            rows = parts.shape[0] // 2
-            parts = parts[:rows] + swap(parts[rows:], axis, mask)
+    here, rows = lax.axis_index("c"), blocks // 2
+    parts = lax.dynamic_slice_in_dim(parts, here * rows, rows, 0) + swap(
+        lax.dynamic_slice_in_dim(parts, (1 - here) * rows, rows, 0), "c", 1
+    )
+    if lax.axis_size("y") == 2:
+        here, rows = lax.axis_index("y"), blocks // 4
+        parts = lax.dynamic_slice_in_dim(parts, here * rows, rows, 0) + swap(
+            lax.dynamic_slice_in_dim(parts, (1 - here) * rows, rows, 0), "y", 1
+        )
+    else:
+        parts = lax.psum_scatter(parts, "y", scatter_dimension=0, tiled=True)
     here = lax.axis_index("z")
     total = lax.dynamic_index_in_dim(parts, here, 0, keepdims=False)
     for k in (1, 2, 3):
@@ -218,6 +313,37 @@
             lax.dynamic_index_in_dim(parts, here ^ k, 0, keepdims=False), "z", k
         )
     return total
+
+
+def attend_weights(query_grid, key_rows, allowed):
+    scaling = query_grid.shape[-1] ** (-0.5)
+    scores = jnp.einsum("qgrd,kgd->grqk", query_grid, key_rows, preferred_element_type=F32)
+    capped = SOFT_CAP * jnp.tanh(scores * scaling / SOFT_CAP)
+    masked = jnp.where(allowed[None, None], capped, MASK_FILL)
+    highest = jnp.max(masked, axis=-1, keepdims=True)
+    weights = jnp.exp(masked - highest)
+    return (capped, weights / jnp.sum(weights, axis=-1, keepdims=True))
+
+
+def attend_values(probability, value_rows):
+    out = jnp.einsum(
+        "grqk,kgd->qgrd", probability.astype(BF), value_rows, preferred_element_type=F32
+    )
+    return out.astype(BF).reshape(out.shape[0], -1)
+
+
+def attend_backward(query_grid, key_rows, value_rows, capped, probability, grad_grid):
+    scaling = query_grid.shape[-1] ** (-0.5)
+    prob_low = probability.astype(BF)
+    grad_prob = jnp.einsum("qgrd,kgd->grqk", grad_grid, value_rows, preferred_element_type=F32)
+    inner = jnp.sum(probability * grad_prob, axis=-1, keepdims=True)
+    grad_cap = probability * (grad_prob - inner)
+    tanh_value = capped / SOFT_CAP
+    grad_score = (grad_cap * scaling * (1.0 - tanh_value * tanh_value)).astype(BF)
+    query_grad = jnp.einsum("grqk,kgd->qgrd", grad_score, key_rows, preferred_element_type=F32)
+    key_grad = jnp.einsum("grqk,qgrd->kgd", grad_score, query_grid, preferred_element_type=F32)
+    value_grad = jnp.einsum("grqk,qgrd->kgd", prob_low, grad_grid, preferred_element_type=F32)
+    return (query_grad, key_grad, value_grad)
 
 
 def attend_forward(query_grid, key_rows, value_rows, allowed):
@@ -276,31 +402,21 @@
     kv_here = kv_cols // HD
     group_size = heads_here // kv_here
 
-    def crossed(values, axis, at):
-        here = lax.axis_index(axis)
-        for mask in masks(axis):
-            shape = values.shape
-            halves = values.reshape(shape[:at] + (-1, 2, mask) + shape[at + 1 :])
-            values = jnp.where((here & mask) != 0, jnp.flip(halves, at + 1), halves)
-            values = values.reshape(shape)
-        return values
-
     def inward(values):
         lead = values.shape[:-1]
         cut = values.reshape(lead + (z_size, y_size, c_size, shard))
         count = len(lead)
         order = tuple(range(count)) + (count + 2, count + 1, count, count + 3)
-        cut = crossed(crossed(cut.transpose(order), "c", count), "y", count + 1)
-        return cut.reshape(lead + (width,))
+        return cut.transpose(order).reshape(lead + (width,))
 
     def outward(values):
         lead = values.shape[:-1]
         cut = values.reshape(lead + (c_size, y_size, z_size, shard))
         count = len(lead)
         order = tuple(range(count)) + (count + 2, count + 1, count, count + 3)
-        cut = crossed(crossed(cut, "c", count), "y", count + 1)
         return cut.transpose(order).reshape(lead + (width,))
 
+    row_axes = ("c", "y", "z")
     positions, allowed = tree_tables(seg_lengths[0], parents[0], group_rows)
     cosine_table, sine_table = rope_tables(positions, HD)
     attn_gain, attn_post_gain = inward(attn_gain), inward(attn_post_gain)
@@ -309,15 +425,34 @@
     out_cotan = inward(out_grad).astype(F32)
 
     qkv_here = jnp.concatenate([w_query, w_key, w_value], axis=1)
-    qkv_weight = gather_rows(qkv_here)
-    out_weight = gather_rows(w_out.T)
-    gate_weight = gather_cut(line_exchange(w_gate), True)
-    up_weight = gather_cut(line_exchange(w_up), False)
-    down_weight = gather_cut(line_exchange(w_down.T), False)
-
     inverse_one = lax.rsqrt(jnp.mean(state_in * state_in, axis=-1, keepdims=True) + NORM_EPS)
     unit_one = state_in * inverse_one
-    normed_one = pair_gather((unit_one * attn_gain).astype(BF))
+    normed_here = (unit_one * attn_gain).astype(BF)
+
+    qkv_weight = lax.all_gather(qkv_here, row_axes, axis=0, tiled=True)
+    out_weight = lax.all_gather(w_out.T, row_axes, axis=0, tiled=True)
+
+    gate_z, normed_other = line_swaps(line_cuts(w_gate)), swap(normed_here, "x", 1)
+    met = meet(normed_other, *gate_z, *line_cuts(w_up), *line_cuts(w_down.T))
+    normed_other, gate_z, up_cuts, down_cuts = met[0], met[1:5], met[5:9], met[9:]
+
+    normed_one = pair_gather(normed_here, normed_other)
+    gate = Cut(line_place(gate_z))
+    gate_got = gate.first()
+    up_z = line_swaps(up_cuts)
+    met = meet(normed_one, *up_z, *down_cuts, *gate_got)
+    normed_one, up_z, down_cuts = met[0], met[1:5], met[5:9]
+    gate.take(met[9:])
+
+    up = Cut(line_place(up_z))
+    up_got = up.first()
+    down_z = line_swaps(down_cuts)
+    met = meet(normed_one, qkv_weight, *down_z, *up_got)
+    normed_one, qkv_weight, down_z = met[0], met[1], met[2:6]
+    up.take(met[6:])
+
+    down = Cut(line_place(down_z))
+    gate_got, up_got = gate.second(2 * shard), up.second(2 * shard)
     qkv_proj = rows_dot(normed_one, qkv_weight)
     queries = rotate(
         qkv_proj[:, :head_cols].reshape(group_rows, heads_here, HD), cosine_table, sine_table
@@ -329,15 +464,29 @@
     ).astype(BF)
     value_rows = qkv_proj[:, head_cols + kv_cols :].astype(BF).reshape(group_rows, kv_here, HD)
     query_grid = queries.reshape(group_rows, kv_here, group_size, HD)
-    attended, capped, probability = attend_forward(query_grid, key_rows, value_rows, allowed)
-    branch = pair_sum(cols_dot(attended, out_weight))
+    capped, probability = attend_weights(query_grid, key_rows, allowed)
+    attended = attend_values(probability, value_rows)
+    met = meet(attended, down.own, *gate_got, *up_got)
+    attended, down.own, met = met[0], met[1], met[2:]
+    gate.take_second(met[: len(gate_got)])
+    up.take_second(met[len(gate_got) :])
+
+    down_got = down.first()
+    branch_sent, branch_kept = pair_parts(cols_dot(attended, out_weight))
+    met = meet(branch_kept, swap(branch_sent, "x", 1), *down_got)
+    branch = met[0] + met[1].astype(F32)
+    down.take(met[2:])
     inverse_two = lax.rsqrt(jnp.mean(branch * branch, axis=-1, keepdims=True) + NORM_EPS)
     unit_two = branch * inverse_two
     hidden = state_in + unit_two * attn_post_gain
     inverse_three = lax.rsqrt(jnp.mean(hidden * hidden, axis=-1, keepdims=True) + NORM_EPS)
     unit_three = hidden * inverse_three
 
-    normed_two = line_gather((unit_three * ffn_gain).astype(BF))
+    normed_two = (unit_three * ffn_gain).astype(BF)
+
+    normed_two = line_gather(normed_two)
+    down.second(2 * shard)
+    gate_weight, up_weight, down_weight = gate.whole(), up.whole(), down.whole()
     acts, pulls, ffn_part = [], [], 0.0
     for half in range(2):
         gate = rows_dot(normed_two, gate_weight[half])
@@ -362,16 +511,27 @@
         normed_part = normed_part + cols_dot(d_gates[half], gate_weight[half])
         normed_part = normed_part + cols_dot(d_ups[half], up_weight[half])
     d_normed_two = line_sum(normed_part)
-    grad_down = line_return(fold_cut(*[outer_low(d_ffn, act) for act in acts], False))
-    grad_up = line_return(fold_cut(*[outer_low(normed_two, d_up) for d_up in d_ups], True))
-    grad_gate = line_return(fold_cut(*[outer_low(normed_two, d_gate) for d_gate in d_gates], True))
+    tails = [
+        Fold(outer_low(d_ffn, acts[0]), outer_low(d_ffn, acts[1]), 2 * shard),
+        Fold(outer_low(normed_two, d_ups[0]), outer_low(normed_two, d_ups[1]), 2 * shard),
+        Fold(outer_low(normed_two, d_gates[0]), outer_low(normed_two, d_gates[1]), 4 * shard),
+    ]
+    grads, earlier = [], []
+    for tail in tails:
+        if earlier:
+            tail.mine, tail.other, *_ = meet(tail.mine, tail.other, *earlier)
+        met = tail.first()
+        tail.take(meet(*met) if met else [])
+        earlier = tail.second()
+        tail.take_second(earlier)
+        grads.append(line_return(tail.whole()))
+    grad_down, grad_up, grad_gate = grads
 
     gain_three = jnp.sum(d_normed_two * unit_three, axis=0)
     d_hidden = out_cotan + norm_back(d_normed_two * ffn_gain, unit_three, inverse_three)
     gain_two = jnp.sum(d_hidden * unit_two, axis=0)
-    d_branch = pair_gather(
-        norm_back(d_hidden * attn_post_gain, unit_two, inverse_two).astype(BF)
-    )
+    d_branch = norm_back(d_hidden * attn_post_gain, unit_two, inverse_two).astype(BF)
+    d_branch = pair_gather(d_branch, swap(d_branch, "x", 1))
     d_attended = rows_dot(d_branch, out_weight).astype(BF)
     grad_grid = d_attended.reshape(group_rows, kv_here, group_size, HD)
     query_grad, key_grad, value_grad = attend_backward(
@@ -392,8 +552,8 @@
     d_normed_one = pair_sum(cols_dot(d_qkv, qkv_weight))
     gain_one = jnp.sum(d_normed_one * unit_one, axis=0)
     grad_tokens = d_hidden + norm_back(d_normed_one * attn_gain, unit_one, inverse_one)
-    grad_qkv = line_fold(fold(outer_low(normed_one, d_qkv), "y"))
-    grad_out = line_fold(fold(outer_low(d_branch, attended), "y"))
+    grad_qkv = line_fold(rows_sum(outer_low(normed_one, d_qkv), "y"))
+    grad_out = line_fold(rows_sum(outer_low(d_branch, attended), "y"))
     gains = gain_sum(jnp.stack([gain_one, gain_two, gain_three, gain_four], axis=0))
     key_from, value_from = head_cols, head_cols + kv_cols
     return (

time: 1140 us -> 942 us (0.83)
  waiting for transfers between devices: 696 us -> 491 us
  local copies, waits for them, and re-layouts: 98.1 us -> 127 us
  other arithmetic: 53.1 us -> 33.8 us
  between operations: 3.33 us -> 17 us
  starting transfers between devices: 109 us -> 95.9 us
    ppermute x86 -> x85, waiting for transfers between devices: 696 us -> 491 us  [swap(): return lax.ppermute(values, axis, [(i, i ^ mask) for i in range(size)])]
    dynamic_update_slice x20 -> x39, local copies, waits for them, and re-layouts: 16.8 us -> 53.3 us  [placed(): held = lax.dynamic_update_slice_in_dim(held, piece, offset, 0)]
    dot_general x8, matrix products: 44 us -> 59.7 us  [rows_dot(): lax.dot_general(left, right, (((1,), (0,)), ((), ())), preferred_element_...]
    ppermute x86 -> x85, starting transfers between devices: 109 us -> 95.8 us  [swap(): return lax.ppermute(values, axis, [(i, i ^ mask) for i in range(size)])]
    another operation x12 -> x20, local copies, waits for them, and re-layouts: 5.29 us -> 17.9 us
    dot_general x8, matrix products: 54.9 us -> 43.1 us  [cols_dot(): lax.dot_general(left, right, (((1,), (1,)), ((), ())), preferred_element_...]
    unnamed x318 -> x290, local copies, waits for them, and re-layouts: 23.4 us -> 15.2 us
  transfers between devices with their start and end apart: 86 -> 87, of which waited for: 50 -> 44; matrix products, arithmetic and copies ran while one was open for 18% -> 25% of each run, Pallas kernels for 0% -> 0%
where the time goes in v3:
time: 942 us; the launch traced here: 934 us
  waiting for transfers between devices  491 us (52%)
  matrix products  170 us (18%)
  local copies, waits for them, and re-layouts  127 us (13%)
  starting transfers between devices  95.9 us (10%)
  other arithmetic  33.8 us (4%)
  between operations  17 us (2%)
    ppermute x85, waiting for transfers between devices, swap(): return lax.ppermute(values, axis, [(i, i ^ mask) for i in range(size)])  491 us
    ppermute x85, starting transfers between devices, swap(): return lax.ppermute(values, axis, [(i, i ^ mask) for i in range(size)])  95.8 us
    dot_general x8, matrix products, rows_dot(): lax.dot_general(left, right, (((1,), (0,)), ((), ())), preferred_element_...  59.7 us
    dynamic_update_slice x39, local copies, waits for them, and re-layouts, placed(): held = lax.dynamic_update_slice_in_dim(held, piece, offset, 0)  53.3 us
    dot_general x16, matrix products, outer_dot(): lax.dot_general(left, right, (((0,), (0,)), ((), ())), preferred_element_...  49.5 us
    dot_general x8, matrix products, cols_dot(): lax.dot_general(left, right, (((1,), (1,)), ((), ())), preferred_element_...  43.1 us
  transfers between devices with their start and end apart: 87, of which 44 were waited for; matrix products, arithmetic and copies ran while one was open for 25% of the time, Pallas kernels for 0%

profile of v3, /device:TPU:8, one launch (start us, length us, event | category | flops | bytes accessed | tf_op | source)
XLA Modules:
  0.0 933.7 jit_solution(14244778600321620416)
XLA Ops:
  28.3 13.7 %collective-permute-done.2 = bf16[144,1152]{1,0:T(8,128)(2,1)} collective-permute-done((bf16[144,1152]{1,0:T(8,128)(2,1)}, bf16[144,1152]{1,0:T(8,128)(2,1)}, u32[]{:S(2)}, u32[]{:S(2)}) %collective-permute-start.2) | collective-permute-done | bytes 331808 | tf_op jit(solution)/shard_map/ppermute | solution.py:73
  42.1 18.8 %collective-permute-done.3 = bf16[144,1152]{1,0:T(8,128)(2,1)} collective-permute-done((bf16[144,1152]{1,0:T(8,128)(2,1)}, bf16[144,1152]{1,0:T(8,128)(2,1)}, u32[]{:S(2)}, u32[]{:S(2)}) %collective-permute-start.3) | collective-permute-done | bytes 331808 | tf_op jit(solution)/shard_map/ppermute | solution.py:73
  76.5 8.9 collective-permute-done.4
  85.4 22.7 %collective-permute-done.5 = bf16[144,1152]{1,0:T(8,128)(2,1)S(1)} collective-permute-done((bf16[144,1152]{1,0:T(8,128)(2,1)S(1)}, bf16[144,1152]{1,0:T(8,128)(2,1)S(1)}, u32[]{:S(2)}, u32[]{:S(2)}) %collective-permute-start.5) | collective-permute-done | bytes 331808 | tf_op jit(solution)/shard_map/ppermute | solution.py:73
  108.1 19.8 %collective-permute-done.6 = bf16[144,1152]{1,0:T(8,128)(2,1)S(1)} collective-permute-done((bf16[144,1152]{1,0:T(8,128)(2,1)S(1)}, bf16[144,1152]{1,0:T(8,128)(2,1)S(1)}, u32[]{:S(2)}, u32[]{:S(2)}) %collective-permute-start.6) | collective-permute-done | bytes 331808 | tf_op jit(solution)/shard_map/ppermute | solution.py:73
  156.5 8.2 collective-permute-done.10
  167.1 9.3 %collective-permute-done.11 = bf16[144,1152]{1,0:T(8,128)(2,1)S(1)} collective-permute-done((bf16[144,1152]{1,0:T(8,128)(2,1)S(1)}, bf16[144,1152]{1,0:T(8,128)(2,1)S(1)}, u32[]{:S(2)}, u32[]{:S(2)}) %collective-permute-start.11) | collective-permute-done | bytes 331808 | tf_op jit(solution)/shard_map/ppermute | solution.py:73
  242.8 20.5 %collective-permute-done.18 = bf16[128,2304]{1,0:T(8,128)(2,1)S(1)} collective-permute-done((bf16[128,2304]{1,0:T(8,128)(2,1)S(1)}, bf16[128,2304]{1,0:T(8,128)(2,1)S(1)}, u32[]{:S(2)}, u32[]{:S(2)}) %collective-permute-start.18) | collective-permute-done | bytes 589856 | tf_op jit(solution)/shard_map/ppermute | solution.py:73
  274.5 13.9 %collective-permute-done.21 = bf16[128,2304]{1,0:T(8,128)(2,1)S(1)} collective-permute-done((bf16[128,2304]{1,0:T(8,128)(2,1)S(1)}, bf16[128,2304]{1,0:T(8,128)(2,1)S(1)}, u32[]{:S(2)}, u32[]{:S(2)}) %collective-permute-start.21) | collective-permute-done | bytes 589856 | tf_op jit(solution)/shard_map/ppermute | solution.py:73
  288.3 16.2 %collective-permute-done.22 = bf16[128,2304]{1,0:T(8,128)(2,1)S(1)} collective-permute-done((bf16[128,2304]{1,0:T(8,128)(2,1)S(1)}, bf16[128,2304]{1,0:T(8,128)(2,1)S(1)}, u32[]{:S(2)}, u32[]{:S(2)}) %collective-permute-start.22) | collective-permute-done | bytes 589856 | tf_op jit(solution)/shard_map/ppermute | solution.py:73
  306.0 11.1 %collective-permute-done.23 = bf16[128,2304]{1,0:T(8,128)(2,1)S(1)} collective-permute-done((bf16[128,2304]{1,0:T(8,128)(2,1)S(1)}, bf16[128,2304]{1,0:T(8,128)(2,1)S(1)}, u32[]{:S(2)}, u32[]{:S(2)}) %collective-permute-start.23) | collective-permute-done | bytes 589856 | tf_op jit(solution)/shard_map/ppermute | solution.py:73
  319.8 17.9 %fusion.124 = f32[512,1152]{1,0:T(8,128)} fusion(bf16[2304,1152]{1,0:T(8,128)(2,1)} %constant_dynamic-update-slice_fusion.23, bf16[128,2304]{1,0:T(8,128)(2,1)S(1)} %collective-permute-done.23, bf16[128,2304]{1,0:T(8,128)(2,1)S(1)} %collective-permute-done.22, bf16[128,2304]{1,0:T(8,128)(2,1)S(1)} %collective-permute-done.21, ...), kind=kOutput, calls=%fused_computation.356 | convolution fusion | flops 2727346176 | bytes 10027008 | tf_op jit(solution)/shard_map/dot_general | solution.py:77
  342.9 8.9 multiply_convert_fusion.3
  391.0 13.0 %collective-permute-done.32 = bf16[128,2304]{1,0:T(8,128)(2,1)} collective-permute-done((bf16[128,2304]{1,0:T(8,128)(2,1)}, bf16[128,2304]{1,0:T(8,128)(2,1)}, u32[]{:S(2)}, u32[]{:S(2)}) %collective-permute-start.32) | collective-permute-done | bytes 589856 | tf_op jit(solution)/shard_map/ppermute | solution.py:73
  404.0 16.4 %collective-permute-done.33 = bf16[128,2304]{1,0:T(8,128)(2,1)} collective-permute-done((bf16[128,2304]{1,0:T(8,128)(2,1)}, bf16[128,2304]{1,0:T(8,128)(2,1)}, u32[]{:S(2)}, u32[]{:S(2)}) %collective-permute-start.33) | collective-permute-done | bytes 589856 | tf_op jit(solution)/shard_map/ppermute | solution.py:73
  420.4 14.4 %collective-permute-done.34 = bf16[128,2304]{1,0:T(8,128)(2,1)} collective-permute-done((bf16[128,2304]{1,0:T(8,128)(2,1)}, bf16[128,2304]{1,0:T(8,128)(2,1)}, u32[]{:S(2)}, u32[]{:S(2)}) %collective-permute-start.34) | collective-permute-done | bytes 589856 | tf_op jit(solution)/shard_map/ppermute | solution.py:73
  461.9 17.9 %collective-permute-done.36 = bf16[128,2304]{1,0:T(8,128)(2,1)} collective-permute-done((bf16[128,2304]{1,0:T(8,128)(2,1)}, bf16[128,2304]{1,0:T(8,128)(2,1)}, u32[]{:S(2)}, u32[]{:S(2)}) %collective-permute-start.36) | collective-permute-done | bytes 589856 | tf_op jit(solution)/shard_map/ppermute | solution.py:73
  479.8 13.1 %collective-permute-done.37 = bf16[128,2304]{1,0:T(8,128)(2,1)} collective-permute-done((bf16[128,2304]{1,0:T(8,128)(2,1)}, bf16[128,2304]{1,0:T(8,128)(2,1)}, u32[]{:S(2)}, u32[]{:S(2)}) %collective-permute-start.37) | collective-permute-done | bytes 589856 | tf_op jit(solution)/shard_map/ppermute | solution.py:73
  492.9 9.1 fusion.18
  543.3 12.1 %collective-permute-done.38 = bf16[128,2304]{1,0:T(8,128)(2,1)S(1)} collective-permute-done((bf16[128,2304]{1,0:T(8,128)(2,1)S(1)}, bf16[128,2304]{1,0:T(8,128)(2,1)S(1)}, u32[]{:S(2)}, u32[]{:S(2)}) %collective-permute-start.38) | collective-permute-done | bytes 589856 | tf_op jit(solution)/shard_map/ppermute | solution.py:73
  555.4 19.5 %collective-permute-done.39 = bf16[128,2304]{1,0:T(8,128)(2,1)S(1)} collective-permute-done((bf16[128,2304]{1,0:T(8,128)(2,1)S(1)}, bf16[128,2304]{1,0:T(8,128)(2,1)S(1)}, u32[]{:S(2)}, u32[]{:S(2)}) %collective-permute-start.39) | collective-permute-done | bytes 589856 | tf_op jit(solution)/shard_map/ppermute | solution.py:73
  574.9 12.0 %collective-permute-done.40 = bf16[128,2304]{1,0:T(8,128)(2,1)S(1)} collective-permute-done((bf16[128,2304]{1,0:T(8,128)(2,1)S(1)}, bf16[128,2304]{1,0:T(8,128)(2,1)S(1)}, u32[]{:S(2)}, u32[]{:S(2)}) %collective-permute-start.40) | collective-permute-done | bytes 589856 | tf_op jit(solution)/shard_map/ppermute | solution.py:73
  702.1 22.5 %collective-permute-done.68 = bf16[576,1152]{1,0:T(8,128)(2,1)S(1)} collective-permute-done((bf16[576,1152]{1,0:T(8,128)(2,1)S(1)}, bf16[576,1152]{1,0:T(8,128)(2,1)S(1)}, u32[]{:S(2)}, u32[]{:S(2)}) %collective-permute-start.68) | collective-permute-done | bytes 1327136 | tf_op jit(solution)/shard_map/ppermute | solution.py:73
  730.1 18.0 %collective-permute-done.55 = bf16[576,1024]{1,0:T(8,128)(2,1)S(1)} collective-permute-done((bf16[576,1024]{1,0:T(8,128)(2,1)S(1)}, bf16[576,1024]{1,0:T(8,128)(2,1)S(1)}, u32[]{:S(2)}, u32[]{:S(2)}) %collective-permute-start.55) | collective-permute-done | bytes 1179680 | tf_op jit(solution)/shard_map/ppermute | solution.py:73
  754.8 8.3 collective-permute-done.70
  773.0 19.7 %collective-permute-done.72 = bf16[576,1152]{1,0:T(8,128)(2,1)S(1)} collective-permute-done((bf16[576,1152]{1,0:T(8,128)(2,1)S(1)}, bf16[576,1152]{1,0:T(8,128)(2,1)S(1)}, u32[]{:S(2)}, u32[]{:S(2)}) %collective-permute-start.72) | collective-permute-done | bytes 1327136 | tf_op jit(solution)/shard_map/ppermute | solution.py:73
  811.9 15.0 %collective-permute-done.74 = bf16[576,1152]{1,0:T(8,128)(2,1)S(1)} collective-permute-done((bf16[576,1152]{1,0:T(8,128)(2,1)S(1)}, bf16[576,1152]{1,0:T(8,128)(2,1)S(1)}, u32[]{:S(2)}, u32[]{:S(2)}) %collective-permute-start.74) | collective-permute-done | bytes 1327136 | tf_op jit(solution)/shard_map/ppermute | solution.py:73
  827.7 19.3 %collective-permute-done.50 = bf16[576,2048]{1,0:T(8,128)(2,1)S(1)} collective-permute-done((bf16[576,2048]{1,0:T(8,128)(2,1)S(1)}, bf16[576,2048]{1,0:T(8,128)(2,1)S(1)}, u32[]{:S(2)}, u32[]{:S(2)}) %collective-permute-start.50) | collective-permute-done | bytes 2359328 | tf_op jit(solution)/shard_map/ppermute | solution.py:73
  853.6 17.2 %collective-permute-done.51 = bf16[144,2048]{1,0:T(8,128)(2,1)S(1)} collective-permute-done((bf16[144,2048]{1,0:T(8,128)(2,1)S(1)}, bf16[144,2048]{1,0:T(8,128)(2,1)S(1)}, u32[]{:S(2)}, u32[]{:S(2)}) %collective-permute-start.51) | collective-permute-done | bytes 589856 | tf_op jit(solution)/shard_map/ppermute | solution.py:73
  870.8 16.5 %collective-permute-done.52 = bf16[144,2048]{1,0:T(8,128)(2,1)S(1)} collective-permute-done((bf16[144,2048]{1,0:T(8,128)(2,1)S(1)}, bf16[144,2048]{1,0:T(8,128)(2,1)S(1)}, u32[]{:S(2)}, u32[]{:S(2)}) %collective-permute-start.52) | collective-permute-done | bytes 589856 | tf_op jit(solution)/shard_map/ppermute | solution.py:73
  887.3 8.3 collective-permute-done.53
  908.4 10.4 %collective-permute-done.77 = bf16[144,1152]{1,0:T(8,128)(2,1)S(1)} collective-permute-done((bf16[144,1152]{1,0:T(8,128)(2,1)S(1)}, bf16[144,1152]{1,0:T(8,128)(2,1)S(1)}, u32[]{:S(2)}, u32[]{:S(2)}) %collective-permute-start.77) | collective-permute-done | bytes 331808 | tf_op jit(solution)/shard_map/ppermute | solution.py:73
  (689 shorter events, 444.1 us)
Async XLA Ops:
  7.2 172.7 %all-gather.3.cloned.1.call-start = ((), (), s32[]{:S(2)}) async-start(), calls=%async_computation | async-start | bytes 10027008 | tf_op jit(solution)/shard_map/all_gather | solution.py:432
  9.4 214.4 %all-gather.5.cloned.1.call-start = ((), (), s32[]{:S(2)}) async-start(), calls=%async_computation.1 | async-start | bytes 5013504 | tf_op jit(solution)/shard_map/all_gather | solution.py:433
  13.5 47.4 %collective-permute-start.3 = (bf16[144,1152]{1,0:T(8,128)(2,1)}, bf16[144,1152]{1,0:T(8,128)(2,1)}, u32[]{:S(2)}, u32[]{:S(2)}) collective-permute-start(bf16[144,1152]{1,0:T(8,128)(2,1)} %get-tuple-element.204), channel_id=1, source_target_pairs={{0,24},{8,16},{16,8},{24,0},{1,25},{9,17},{17,9},{25,1},{2,26},{10... | collective-permute-start | bytes 995336 | tf_op jit(solution)/shard_map/ppermute | solution.py:73
  16.6 44.3 %collective-permute-start = (bf16[128,2304]{1,0:T(8,128)(2,1)}, bf16[128,2304]{1,0:T(8,128)(2,1)}, u32[]{:S(2)}, u32[]{:S(2)}) collective-permute-start(bf16[128,2304]{1,0:T(8,128)(2,1)} %multiply_convert_fusion.7), channel_id=1, source_target_pairs={{0,1},{1,0},{2,3},{3,2},{4,5},{5,4},{6,7},{7,6},{8,9},{9,8},{10,11... | collective-permute-start | bytes 1769480 | tf_op jit(solution)/shard_map/ppermute | solution.py:73
  64.1 63.8 %collective-permute-start.7 = (bf16[576,1152]{1,0:T(8,128)(2,1)S(1)}, bf16[576,1152]{1,0:T(8,128)(2,1)S(1)}, u32[]{:S(2)}, u32[]{:S(2)}) collective-permute-start(bf16[576,1152]{1,0:T(8,128)(2,1)S(1)} %constant_dynamic-update-slice_fusion.35), channel_id=1, source_target_pairs={{0,1},{1,0},{2,3},{3,2},{4,5},{5,4},{6,7},{7,6},{8,9},{9,8},{10,11... | collective-permute-start | bytes 3981320 | tf_op jit(solution)/shard_map/ppermute | solution.py:73
  65.7 62.3 %collective-permute-start.8 = (bf16[576,1152]{1,0:T(8,128)(2,1)S(1)}, bf16[576,1152]{1,0:T(8,128)(2,1)S(1)}, u32[]{:S(2)}, u32[]{:S(2)}) collective-permute-start(bf16[576,1152]{1,0:T(8,128)(2,1)S(1)} %constant_dynamic-update-slice_fusion.35), channel_id=1, source_target_pairs={{0,4},{4,0},{1,5},{5,1},{2,6},{6,2},{3,7},{7,3},{8,12},{12,8},{9,1... | collective-permute-start | bytes 3981320 | tf_op jit(solution)/shard_map/ppermute | solution.py:73
  67.2 41.0 %collective-permute-start.5 = (bf16[144,1152]{1,0:T(8,128)(2,1)S(1)}, bf16[144,1152]{1,0:T(8,128)(2,1)S(1)}, u32[]{:S(2)}, u32[]{:S(2)}) collective-permute-start(bf16[144,1152]{1,0:T(8,128)(2,1)S(1)} %get-tuple-element.66), channel_id=1, source_target_pairs={{0,16},{8,24},{16,0},{24,8},{1,17},{9,25},{17,1},{25,9},{2,18},{10... | collective-permute-start | bytes 995336 | tf_op jit(solution)/shard_map/ppermute | solution.py:73
  71.1 56.8 %collective-permute-start.6 = (bf16[144,1152]{1,0:T(8,128)(2,1)S(1)}, bf16[144,1152]{1,0:T(8,128)(2,1)S(1)}, u32[]{:S(2)}, u32[]{:S(2)}) collective-permute-start(bf16[144,1152]{1,0:T(8,128)(2,1)S(1)} %get-tuple-element.67), channel_id=1, source_target_pairs={{0,24},{8,16},{16,8},{24,0},{1,25},{9,17},{17,9},{25,1},{2,26},{10... | collective-permute-start | bytes 995336 | tf_op jit(solution)/shard_map/ppermute | solution.py:73
  134.2 43.9 %collective-permute-start.12 = (bf16[576,1152]{1,0:T(8,128)(2,1)S(1)}, bf16[576,1152]{1,0:T(8,128)(2,1)S(1)}, u32[]{:S(2)}, u32[]{:S(2)}) collective-permute-start(bf16[576,1152]{1,0:T(8,128)(2,1)S(1)} %constant_dynamic-update-slice_fusion.31), channel_id=1, source_target_pairs={{0,1},{1,0},{2,3},{3,2},{4,5},{5,4},{6,7},{7,6},{8,9},{9,8},{10,11... | collective-permute-start | bytes 3981320 | tf_op jit(solution)/shard_map/ppermute | solution.py:73
  134.5 45.4 %collective-permute-start.13 = (bf16[576,1152]{1,0:T(8,128)(2,1)S(1)}, bf16[576,1152]{1,0:T(8,128)(2,1)}, u32[]{:S(2)}, u32[]{:S(2)}) collective-permute-start(bf16[576,1152]{1,0:T(8,128)(2,1)S(1)} %constant_dynamic-update-slice_fusion.31), channel_id=1, source_target_pairs={{0,4},{4,0},{1,5},{5,1},{2,6},{6,2},{3,7},{7,3},{8,12},{12,8},{9,1... | collective-permute-start | bytes 3981320 | tf_op jit(solution)/shard_map/ppermute | solution.py:73
  134.8 41.7 %collective-permute-start.11 = (bf16[144,1152]{1,0:T(8,128)(2,1)S(1)}, bf16[144,1152]{1,0:T(8,128)(2,1)S(1)}, u32[]{:S(2)}, u32[]{:S(2)}) collective-permute-start(bf16[144,1152]{1,0:T(8,128)(2,1)S(1)} %copy-done.67), channel_id=1, source_target_pairs={{0,24},{8,16},{16,8},{24,0},{1,25},{9,17},{17,9},{25,1},{2,26},{10... | collective-permute-start | bytes 995336 | tf_op jit(solution)/shard_map/ppermute | solution.py:73
  164.7 53.0 %collective-permute-start.14 = (bf16[288,1152]{1,0:T(8,128)(2,1)}, bf16[288,1152]{1,0:T(8,128)(2,1)}, u32[]{:S(2)}, u32[]{:S(2)}) collective-permute-start(bf16[288,1152]{1,0:T(8,128)(2,1)} %slice.146), channel_id=1, source_target_pairs={{0,1},{1,0},{2,3},{3,2},{4,5},{5,4},{6,7},{7,6},{8,9},{9,8},{10,11... | collective-permute-start | bytes 1990664 | tf_op jit(solution)/shard_map/ppermute | solution.py:73
  176.4 41.3 %collective-permute-start.15 = (bf16[288,1152]{1,0:T(8,128)(2,1)}, bf16[288,1152]{1,0:T(8,128)(2,1)}, u32[]{:S(2)}, u32[]{:S(2)}) collective-permute-start(bf16[288,1152]{1,0:T(8,128)(2,1)} %slice.147), channel_id=1, source_target_pairs={{0,4},{4,0},{1,5},{5,1},{2,6},{6,2},{3,7},{7,3},{8,12},{12,8},{9,1... | collective-permute-start | bytes 1990664 | tf_op jit(solution)/shard_map/ppermute | solution.py:73
  198.8 140.5 %collective-permute-start.25 = (bf16[1152,1152]{1,0:T(8,128)(2,1)}, bf16[1152,1152]{1,0:T(8,128)(2,1)}, u32[]{:S(2)}, u32[]{:S(2)}) collective-permute-start(bf16[1152,1152]{1,0:T(8,128)(2,1)} %constant_dynamic-update-slice_fusion.21), channel_id=1, source_target_pairs={{0,2},{2,0},{1,3},{3,1},{4,6},{6,4},{5,7},{7,5},{8,10},{10,8},{9,1... | collective-permute-start | bytes 7962632 | tf_op jit(solution)/shard_map/ppermute | solution.py:73
  220.4 43.0 %collective-permute-start.19 = (bf16[576,1152]{1,0:T(8,128)(2,1)}, bf16[576,1152]{1,0:T(8,128)(2,1)}, u32[]{:S(2)}, u32[]{:S(2)}) collective-permute-start(bf16[576,1152]{1,0:T(8,128)(2,1)} %constant_dynamic-update-slice_fusion.27), channel_id=1, source_target_pairs={{0,1},{1,0},{2,3},{3,2},{4,5},{5,4},{6,7},{7,6},{8,9},{9,8},{10,11... | collective-permute-start | bytes 3981320 | tf_op jit(solution)/shard_map/ppermute | solution.py:73
  222.0 41.4 %collective-permute-start.20 = (bf16[576,1152]{1,0:T(8,128)(2,1)}, bf16[576,1152]{1,0:T(8,128)(2,1)}, u32[]{:S(2)}, u32[]{:S(2)}) collective-permute-start(bf16[576,1152]{1,0:T(8,128)(2,1)} %constant_dynamic-update-slice_fusion.27), channel_id=1, source_target_pairs={{0,4},{4,0},{1,5},{5,1},{2,6},{6,2},{3,7},{7,3},{8,12},{12,8},{9,1... | collective-permute-start | bytes 3981320 | tf_op jit(solution)/shard_map/ppermute | solution.py:73
  233.8 118.0 %collective-permute-start.28 = (bf16[1152,1152]{1,0:T(8,128)(2,1)}, bf16[1152,1152]{1,0:T(8,128)(2,1)S(1)}, u32[]{:S(2)}, u32[]{:S(2)}) collective-permute-start(bf16[1152,1152]{1,0:T(8,128)(2,1)} %constant_dynamic-update-slice_fusion.7), channel_id=1, source_target_pairs={{0,2},{2,0},{1,3},{3,1},{4,6},{6,4},{5,7},{7,5},{8,10},{10,8},{9,1... | collective-permute-start | bytes 7962632 | tf_op jit(solution)/shard_map/ppermute | solution.py:73
  265.4 51.8 %collective-permute-start.23 = (bf16[128,2304]{1,0:T(8,128)(2,1)S(1)}, bf16[128,2304]{1,0:T(8,128)(2,1)S(1)}, u32[]{:S(2)}, u32[]{:S(2)}) collective-permute-start(bf16[128,2304]{1,0:T(8,128)(2,1)S(1)} %multiply_convert_fusion.6), channel_id=1, source_target_pairs={{0,24},{8,16},{16,8},{24,0},{1,25},{9,17},{17,9},{25,1},{2,26},{10... | collective-permute-start | bytes 1769480 | tf_op jit(solution)/shard_map/ppermute | solution.py:73
  288.3 63.9 %collective-permute-start.27 = (bf16[1152,1152]{1,0:T(8,128)(2,1)}, bf16[1152,1152]{1,0:T(8,128)(2,1)S(1)}, u32[]{:S(2)}, u32[]{:S(2)}) collective-permute-start(bf16[1152,1152]{1,0:T(8,128)(2,1)} %constant_dynamic-update-slice_fusion.12), channel_id=1, source_target_pairs={{0,2},{2,0},{1,3},{3,1},{4,6},{6,4},{5,7},{7,5},{8,10},{10,8},{9,1... | collective-permute-start | bytes 7962632 | tf_op jit(solution)/shard_map/ppermute | solution.py:73
  381.2 53.6 %collective-permute-start.34 = (bf16[128,2304]{1,0:T(8,128)(2,1)}, bf16[128,2304]{1,0:T(8,128)(2,1)}, u32[]{:S(2)}, u32[]{:S(2)}) collective-permute-start(bf16[128,2304]{1,0:T(8,128)(2,1)} %get-tuple-element.185), channel_id=1, source_target_pairs={{0,24},{8,16},{16,8},{24,0},{1,25},{9,17},{17,9},{25,1},{2,26},{10... | collective-permute-start | bytes 1769480 | tf_op jit(solution)/shard_map/ppermute | solution.py:73
  439.4 40.4 %collective-permute-start.36 = (bf16[128,2304]{1,0:T(8,128)(2,1)}, bf16[128,2304]{1,0:T(8,128)(2,1)}, u32[]{:S(2)}, u32[]{:S(2)}) collective-permute-start(bf16[128,2304]{1,0:T(8,128)(2,1)} %get-tuple-element.212), channel_id=1, source_target_pairs={{0,16},{8,24},{16,0},{24,8},{1,17},{9,25},{17,1},{25,9},{2,18},{10... | collective-permute-start | bytes 1769480 | tf_op jit(solution)/shard_map/ppermute | solution.py:73
  440.4 52.5 %collective-permute-start.37 = (bf16[128,2304]{1,0:T(8,128)(2,1)}, bf16[128,2304]{1,0:T(8,128)(2,1)}, u32[]{:S(2)}, u32[]{:S(2)}) collective-permute-start(bf16[128,2304]{1,0:T(8,128)(2,1)} %get-tuple-element.212), channel_id=1, source_target_pairs={{0,24},{8,16},{16,8},{24,0},{1,25},{9,17},{17,9},{25,1},{2,26},{10... | collective-permute-start | bytes 1769480 | tf_op jit(solution)/shard_map/ppermute | solution.py:73
  535.8 51.0 %collective-permute-start.40 = (bf16[128,2304]{1,0:T(8,128)(2,1)S(1)}, bf16[128,2304]{1,0:T(8,128)(2,1)S(1)}, u32[]{:S(2)}, u32[]{:S(2)}) collective-permute-start(bf16[128,2304]{1,0:T(8,128)(2,1)S(1)} %get-tuple-element.182), channel_id=1, source_target_pairs={{0,24},{8,16},{16,8},{24,0},{1,25},{9,17},{17,9},{25,1},{2,26},{10... | collective-permute-start | bytes 1769480 | tf_op jit(solution)/shard_map/ppermute | solution.py:73
  686.8 82.1 %collective-permute-start.49 = (bf16[1152,2048]{1,0:T(8,128)(2,1)}, bf16[1152,2048]{1,0:T(8,128)(2,1)S(1)}, u32[]{:S(2)}, u32[]{:S(2)}) collective-permute-start(bf16[1152,2048]{1,0:T(8,128)(2,1)} %convolution_convert_fusion.6), channel_id=1, source_target_pairs={{0,2},{2,0},{1,3},{3,1},{4,6},{6,4},{5,7},{7,5},{8,10},{10,8},{9,1... | collective-permute-start | bytes 14155784 | tf_op jit(solution)/shard_map/ppermute | solution.py:73
  701.6 46.4 %collective-permute-start.55 = (bf16[576,1024]{1,0:T(8,128)(2,1)S(1)}, bf16[576,1024]{1,0:T(8,128)(2,1)S(1)}, u32[]{:S(2)}, u32[]{:S(2)}) collective-permute-start(bf16[576,1024]{1,0:T(8,128)(2,1)S(1)} %constant_dynamic-slice_fusion.22), channel_id=1, source_target_pairs={{0,4},{4,0},{1,5},{5,1},{2,6},{6,2},{3,7},{7,3},{8,12},{12,8},{9,1... | collective-permute-start | bytes 3538952 | tf_op jit(solution)/shard_map/ppermute | solution.py:73
  751.0 44.8 %collective-permute-start.56 = (bf16[144,1024]{1,0:T(8,128)(2,1)S(1)}, bf16[144,1024]{1,0:T(8,128)(2,1)S(1)}, u32[]{:S(2)}, u32[]{:S(2)}) collective-permute-start(bf16[144,1024]{1,0:T(8,128)(2,1)S(1)} %get-tuple-element.214), channel_id=1, source_target_pairs={{0,8},{8,0},{16,24},{24,16},{1,9},{9,1},{17,25},{25,17},{2,10},{10... | collective-permute-start | bytes 884744 | tf_op jit(solution)/shard_map/ppermute | solution.py:73
  792.8 54.2 %collective-permute-start.50 = (bf16[576,2048]{1,0:T(8,128)(2,1)S(1)}, bf16[576,2048]{1,0:T(8,128)(2,1)S(1)}, u32[]{:S(2)}, u32[]{:S(2)}) collective-permute-start(bf16[576,2048]{1,0:T(8,128)(2,1)S(1)} %constant_dynamic-slice_fusion.26), channel_id=1, source_target_pairs={{0,4},{4,0},{1,5},{5,1},{2,6},{6,2},{3,7},{7,3},{8,12},{12,8},{9,1... | collective-permute-start | bytes 7077896 | tf_op jit(solution)/shard_map/ppermute | solution.py:73
  800.6 51.3 %collective-permute-start.80 = (bf16[144,1152]{1,0:T(8,128)(2,1)S(1)}, bf16[144,1152]{1,0:T(8,128)(2,1)S(1)}, u32[]{:S(2)}, u32[]{:S(2)}) collective-permute-start(bf16[144,1152]{1,0:T(8,128)(2,1)S(1)} %get-tuple-element.191), channel_id=1, source_target_pairs={{0,16},{8,24},{16,0},{24,8},{1,17},{9,25},{17,1},{25,9},{2,18},{10... | collective-permute-start | bytes 995336 | tf_op jit(solution)/shard_map/ppermute | solution.py:73
  800.6 51.3 %collective-permute-start.81 = (bf16[144,1152]{1,0:T(8,128)(2,1)S(1)}, bf16[144,1152]{1,0:T(8,128)(2,1)S(1)}, u32[]{:S(2)}, u32[]{:S(2)}) collective-permute-start(bf16[144,1152]{1,0:T(8,128)(2,1)S(1)} %get-tuple-element.190), channel_id=1, source_target_pairs={{0,24},{8,16},{16,8},{24,0},{1,25},{9,17},{17,9},{25,1},{2,26},{10... | collective-permute-start | bytes 995336 | tf_op jit(solution)/shard_map/ppermute | solution.py:73
  810.2 85.7 %collective-permute-start.73 = (bf16[576,1152]{1,0:T(8,128)(2,1)S(1)}, bf16[576,1152]{1,0:T(8,128)(2,1)S(1)}, u32[]{:S(2)}, u32[]{:S(2)}) collective-permute-start(bf16[576,1152]{1,0:T(8,128)(2,1)S(1)} %get-tuple-element.170), channel_id=1, source_target_pairs={{0,1},{1,0},{2,3},{3,2},{4,5},{5,4},{6,7},{7,6},{8,9},{9,8},{10,11... | collective-permute-start | bytes 3981320 | tf_op jit(solution)/shard_map/ppermute | solution.py:73
  827.2 68.7 %collective-permute-start.75 = (bf16[576,1152]{1,0:T(8,128)(2,1)S(1)}, bf16[576,1152]{1,0:T(8,128)(2,1)S(1)}, u32[]{:S(2)}, u32[]{:S(2)}) collective-permute-start(bf16[576,1152]{1,0:T(8,128)(2,1)S(1)} %add_convert_fusion.4), channel_id=1, source_target_pairs={{0,4},{4,0},{1,5},{5,1},{2,6},{6,2},{3,7},{7,3},{8,12},{12,8},{9,1... | collective-permute-start | bytes 3981320 | tf_op jit(solution)/shard_map/ppermute | solution.py:73
  851.9 43.7 %collective-permute-start.53 = (bf16[144,2048]{1,0:T(8,128)(2,1)S(1)}, bf16[144,2048]{1,0:T(8,128)(2,1)S(1)}, u32[]{:S(2)}, u32[]{:S(2)}) collective-permute-start(bf16[144,2048]{1,0:T(8,128)(2,1)S(1)} %get-tuple-element.179), channel_id=1, source_target_pairs={{0,24},{8,16},{16,8},{24,0},{1,25},{9,17},{17,9},{25,1},{2,26},{10... | collective-permute-start | bytes 1769480 | tf_op jit(solution)/shard_map/ppermute | solution.py:73
  (195 other events, 2957.4 us)
Sparse Core Ops, SparseCore 0:
  10.9 121.1 all-gather.2
  134.4 79.1 all-gather.4

commit v4 on v1

v4 whole, which is shorter than its diff:
```python
import functools

import jax
import jax.numpy as jnp
from jax import lax
from jax.experimental import pallas as pl
from jax.experimental.pallas import tpu as pltpu
from jax.sharding import Mesh
from jax.sharding import PartitionSpec as P

HD = 256
NORM_EPS = 1e-06
SOFT_CAP = 50.0
ROPE_BASE = 10000.0
MASK_FILL = -1e30
BF = jnp.bfloat16
F32 = jnp.float32


def tree_tables(lengths_row, parents_row, row_total):
    seg_count = lengths_row.shape[0]
    seg_index = jnp.arange(seg_count, dtype=jnp.int32)
    ancestor = (seg_index[:, None] == seg_index[None, :]) | (
        parents_row[:, None] == seg_index[None, :]
    )
    for repeat in range(seg_count.bit_length()):
        ancestor = jnp.any(ancestor[:, :, None] & ancestor[None, :, :], axis=1)
    seg_ends = jnp.cumsum(lengths_row)
    seg_starts = seg_ends - lengths_row
    token_index = jnp.arange(row_total, dtype=jnp.int32)
    segment = jnp.sum((token_index[:, None] >= seg_ends[None, :]).astype(jnp.int32), axis=1)
    strict = ancestor & (seg_index[:, None] != seg_index[None, :])
    offsets = jnp.sum(jnp.where(strict, lengths_row[None, :], 0), axis=1)
    one_hot = segment[:, None] == seg_index[None, :]
    positions = (
        jnp.sum(jnp.where(one_hot, (offsets - seg_starts)[None, :], 0), axis=1) + token_index
    )
    reached = jnp.any(one_hot[:, :, None] & ancestor[None, :, :], axis=1)
    allowed = jnp.any(reached[:, None, :] & one_hot[None, :, :], axis=2) & (
        token_index[None, :] <= token_index[:, None]
    )
    return (positions, allowed)


def rope_tables(positions, width):
    half_width = width // 2
    frequency = ROPE_BASE ** (-2.0 * jnp.arange(half_width, dtype=F32) / width)
    angles = positions.astype(F32)[:, None] * frequency[None, :]
    return (jnp.cos(angles), jnp.sin(angles))


def norm_back(grad_unit, unit, inverse):
    return inverse * (grad_unit - unit * jnp.mean(grad_unit * unit, axis=-1, keepdims=True))


def gelu_parts(values):
    scale = (2.0 / jnp.pi) ** 0.5
    square = values * values
    bent = jnp.tanh(scale * (values + 0.044715 * values * square))
    half = 0.5 * (1.0 + bent)
    slope = half + 0.5 * values * (1.0 - bent * bent) * scale * (1.0 + 3 * 0.044715 * square)
    return values * half, slope


def tile_dot(left, right):
    return jnp.dot(left, right, preferred_element_type=F32)


def tile_dot_cols(left, right):
    return lax.dot_general(left, right, (((1,), (1,)), ((), ())), preferred_element_type=F32)


def spill(total, outs):
    rows = outs[0].shape[0]
    for k, out in enumerate(outs):
        out[...] = total[k * rows : (k + 1) * rows, :].astype(out.dtype)


class Weight:
    def __init__(self, *arrays):
        self.arrays, self.whole = arrays, len(arrays) == 1
        self.rows = arrays[0].shape[-2]

    def specs(self, tile):
        if not self.whole:
            return [pl.BlockSpec((self.rows, tile), lambda i, ids: (0, i))] * 2
        count = self.arrays[0].shape[-1] // tile
        return [
            pl.BlockSpec(
                (None, None, self.rows, tile), lambda i, ids, c=c: (i // count, c, 0, i % count)
            )
            for c in range(2)
        ]

    def operands(self):
        return self.arrays * 2 if self.whole else self.arrays

    def columns(self, ids):
        first, second = (0, self.rows) if self.whole else (ids[2] * self.rows, (1 - ids[2]) * self.rows)
        if not self.whole:
            first, second = (pl.multiple_of(at, 128) for at in (first, second))
        return pl.ds(first, self.rows), pl.ds(second, self.rows)


def inner(values, refs, columns):
    return sum(tile_dot(values[:, at], ref[...]) for ref, at in zip(refs, columns))


def outer_add(total, tile, refs, columns, fresh):
    for ref, at in zip(refs, columns):
        part = tile_dot_cols(tile, ref[...])
        total[:, at] = jnp.where(fresh, part, total[:, at] + part)


def forward_kernel(columns, ids, x, *refs):
    gate_w, up_w, down_w, (act, gate, up), outs, total = (
        refs[:2], refs[2:4], refs[4:6], refs[6:9], refs[9:13], refs[13]
    )
    gate_at, up_at, down_at = (find(ids) for find in columns)
    gate_tile, up_tile = inner(x, gate_w, gate_at), inner(x, up_w, up_at)
    gate[...], up[...] = gate_tile, up_tile
    act_tile = (gelu_parts(gate_tile)[0] * up_tile).astype(BF)
    act[...] = act_tile
    outer_add(total, act_tile, down_w, down_at, pl.program_id(0) == 0)

    @pl.when(pl.program_id(0) == pl.num_programs(0) - 1)
    def _():
        spill(total, outs)


def backward_kernel(columns, ids, d, *refs):
    gate_w, up_w, down_w, (gate, up), (d_gate, d_up), outs, total = (
        refs[:2], refs[2:4], refs[4:6], refs[6:8], refs[8:10], refs[10:14], refs[14]
    )
    gate_at, up_at, down_at = (find(ids) for find in columns)
    d_act = inner(d, down_w, down_at)
    bent, slope = gelu_parts(gate[...])
    gate_tile = (d_act * up[...] * slope).astype(BF)
    up_tile = (d_act * bent).astype(BF)
    d_gate[...], d_up[...] = gate_tile, up_tile
    outer_add(total, gate_tile, gate_w, gate_at, pl.program_id(0) == 0)
    outer_add(total, up_tile, up_w, up_at, False)

    @pl.when(pl.program_id(0) == pl.num_programs(0) - 1)
    def _():
        spill(total, outs)


def ffn_call(kernel, ids, values, weights, kept, made, tile):
    tokens, width = values.shape
    hidden = 2 * weights[-1].arrays[0].shape[-1] if weights[-1].whole else weights[-1].arrays[0].shape[-1]
    slot = tokens // 4
    across = pl.BlockSpec((tokens, tile), lambda i, ids: (0, i))
    whole = pl.BlockSpec((slot, width), lambda i, ids: (0, 0))
    return pl.pallas_call(
        functools.partial(kernel, [weight.columns for weight in weights]),
        grid_spec=pltpu.PrefetchScalarGridSpec(
            num_scalar_prefetch=1,
            grid=(hidden // tile,),
            in_specs=[pl.BlockSpec((tokens, width), lambda i, ids: (0, 0))]
            + [spec for weight in weights for spec in weight.specs(tile)]
            + [across] * len(kept),
            out_specs=[across] * len(made) + [whole] * 4,
            scratch_shapes=[pltpu.VMEM((tokens, width), F32)],
        ),
        out_shape=[jax.ShapeDtypeStruct((tokens, hidden), kind) for kind in made]
        + [jax.ShapeDtypeStruct((slot, width), kind) for kind in (F32, BF, BF, BF)],
        compiler_params=pltpu.CompilerParams(
            dimension_semantics=("arbitrary",), vmem_limit_bytes=58 * 2**20
        ),
        cost_estimate=pl.CostEstimate(flops=0, bytes_accessed=0, transcendentals=0),
    )(ids, values, *[array for weight in weights for array in weight.operands()], *kept)


def swap(values, axis, mask):
    size = lax.axis_size(axis)
    return lax.ppermute(values, axis, [(i, i ^ mask) for i in range(size)])


def rows_dot(left, right):
    return lax.dot_general(left, right, (((1,), (0,)), ((), ())), preferred_element_type=F32)


def cols_dot(left, right):
    return lax.dot_general(left, right, (((1,), (1,)), ((), ())), preferred_element_type=F32)


def outer_dot(left, right):
    return lax.dot_general(left, right, (((0,), (0,)), ((), ())), preferred_element_type=F32)


def close(live):
    return lax.optimization_barrier(live)


def pair_gather(values, other):
    mine = lax.axis_index("x")
    first = jnp.where(mine == 0, values, other)
    second = jnp.where(mine == 0, other, values)
    return jnp.concatenate([first, second], axis=0)


def pair_parts(partial):
    rows = partial.shape[0] // 2
    mine = lax.axis_index("x")
    sent = lax.dynamic_slice_in_dim(partial, (1 - mine) * rows, rows, 0).astype(BF)
    return sent, lax.dynamic_slice_in_dim(partial, mine * rows, rows, 0)


def pair_sum(partial):
    sent, kept = pair_parts(partial)
    return kept + swap(sent, "x", 1).astype(F32)


def rows_sum(values, axis):
    size = lax.axis_size(axis)
    if size != 2:
        return lax.psum_scatter(values, axis, scatter_dimension=0, tiled=True)
    rows, mine = values.shape[0] // 2, lax.axis_index(axis)
    sent = lax.dynamic_slice_in_dim(values, (1 - mine) * rows, rows, 0)
    return add_low(lax.dynamic_slice_in_dim(values, mine * rows, rows, 0), swap(sent, axis, 1))


def placed(rows, *pieces):
    held = jnp.zeros((rows,) + pieces[0][1].shape[1:], pieces[0][1].dtype)
    for offset, piece in pieces:
        held = lax.dynamic_update_slice_in_dim(held, piece, offset, 0)
    return held


def add_low(left, right):
    return (left.astype(F32) + right.astype(F32)).astype(BF)


def line_gather(values):
    return jnp.concatenate([values] + [swap(values, "z", k) for k in (1, 2, 3)], axis=0)


def line_parts(partial):
    rows = partial.shape[0] // 4
    parts = [partial[k * rows : (k + 1) * rows] for k in range(4)]
    return [parts[0]] + [part.astype(BF) for part in parts[1:]]


def line_place(pieces):
    here, (rows, cols) = lax.axis_index("z"), pieces[0].shape
    if rows % 16 == 0:
        return assemble(
            (len(pieces) * rows, cols), (rows, cols), [(here ^ k, 0, p) for k, p in enumerate(pieces)]
        )
    return placed(len(pieces) * rows, *[((here ^ k) * rows, p) for k, p in enumerate(pieces)])


def line_cuts(weight):
    here, cut = lax.axis_index("z"), weight.shape[1] // 4
    return [lax.dynamic_slice_in_dim(weight, (here ^ k) * cut, cut, 1) for k in range(4)]


def line_swaps(cuts):
    return [cuts[0]] + [swap(cuts[k], "z", k) for k in (1, 2, 3)]


def line_chunks(grad):
    rows, here = grad.shape[0] // 4, lax.axis_index("z")
    return [lax.dynamic_slice_in_dim(grad, (here ^ k) * rows, rows, 0) for k in range(4)]


def line_columns(pieces):
    here, (rows, cols) = lax.axis_index("z"), pieces[0].shape
    spots = [(0, here ^ k, piece) for k, piece in enumerate(pieces)]
    return assemble((rows, 4 * cols), (rows, cols), spots, F32)


def line_total(pieces):
    total = pieces[0].astype(F32)
    for piece in pieces[1:]:
        total = total + piece.astype(F32)
    return total


def y_chunks(grad):
    rows, y, z = grad.shape[0] // 8, lax.axis_index("y"), lax.axis_index("z")
    return [
        tuple(
            lax.dynamic_slice_in_dim(grad, (4 * side + (z ^ k)) * rows, rows, 0)
            for side in (y, 1 - y)
        )
        for k in range(4)
    ]


def pair_rows(mine, other, axis):
    rows, here = mine.shape[0], lax.axis_index(axis)
    return placed(2 * rows, (here * rows, mine), ((1 - here) * rows, other))


def pair_halves(values, axis):
    rows, here = values.shape[0] // 2, lax.axis_index(axis)
    return (
        lax.dynamic_slice_in_dim(values, here * rows, rows, 0),
        lax.dynamic_slice_in_dim(values, (1 - here) * rows, rows, 0),
    )


def cut_first(own):
    got = {"own": own, "x": swap(own, "x", 1)}
    if lax.axis_size("y") == 2:
        got["y"] = swap(own, "y", 1)
    return got


def cut_over_x(got):
    rows = got["own"].shape[0] // 2
    return {"over_x": swap(got["y"][:rows], "x", 1)} if "y" in got else {}


def cut_over_y(got):
    rows = got["own"].shape[0] // 2
    return {"over_y": swap(got["x"][rows:], "y", 1)} if "y" in got else {}


def cut_half(got):
    own = got["own"]
    rows, cols = own.shape
    if "y" not in got:
        both = jnp.where(
            lax.axis_index("x") == 0,
            jnp.concatenate([own, got["x"]], axis=1),
            jnp.concatenate([got["x"], own], axis=1),
        )
        return lax.all_gather(both, "y", axis=0, tiled=True)
    here, half = lax.axis_index("y"), lax.axis_index("x")
    mine, far = 2 * here, 2 * (1 - here)
    spots = [
        (mine, half, own),
        (far, half, got["y"]),
        (mine, 1 - half, got["x"]),
        (far, 1 - half, got["over_x"]),
        (far + 1, 1 - half, got["over_y"]),
    ]
    return assemble((2 * rows, 2 * cols), (rows // 2, cols), spots)


def fold_parts(both):
    cols, here = both.shape[1] // 2, lax.axis_index("x")
    mine = lax.dynamic_slice_in_dim(both, here * cols, cols, 1)
    other = lax.dynamic_slice_in_dim(both, (1 - here) * cols, cols, 1)
    (own, over_y), (over_x, across) = pair_halves(mine, "y"), pair_halves(other, "y")
    return {"own": own, "x": over_x, "y": over_y, "across": across}


def fold_first(across):
    rows = across.shape[0] // 2
    return [swap(across[:rows], "x", 1), swap(across[rows:], "y", 1)]


def fold_join(parts, got):
    rows = got[0].shape[0]
    over_y = add_low(parts["y"][:rows], got[0])
    over_x = add_low(parts["x"][rows:], got[1])
    return (
        jnp.concatenate([parts["x"][:rows], over_x]),
        jnp.concatenate([over_y, parts["y"][rows:]]),
    )


def spread_ids():
    return jnp.stack([lax.axis_index(axis) for axis in ("z", "y", "c", "x")]).astype(jnp.int32)


LIGHT = pl.CostEstimate(flops=0, bytes_accessed=0, transcendentals=0)


def kernel_params(megabytes=50):
    return pltpu.CompilerParams(
        dimension_semantics=("arbitrary",), vmem_limit_bytes=megabytes * 2**20
    )


def turned(values, cosine, sine):
    half = values.shape[1] // 2
    front, back = values[:, :half], values[:, half:]
    return jnp.concatenate([front * cosine - back * sine, back * cosine + front * sine], axis=1)


def head_probs(query, key, allowed):
    scores = tile_dot_cols(query, key)
    bent = jnp.tanh(scores * (HD**-0.5 / SOFT_CAP))
    masked = jnp.where(allowed != 0, SOFT_CAP * bent, MASK_FILL)
    weights = jnp.exp(masked - jnp.max(masked, axis=1, keepdims=True))
    return bent, weights / jnp.sum(weights, axis=1, keepdims=True)


def attention_kernel(x, weight, cosine, sine, allowed, query, key, value, attended):
    heads = query.shape[1] // HD
    proj = tile_dot(x[...], weight[...])
    key_here = turned(proj[:, heads * HD : (heads + 1) * HD], cosine[...], sine[...]).astype(BF)
    value_here = proj[:, (heads + 1) * HD :].astype(BF)
    key[...], value[...] = key_here, value_here
    for head in range(heads):
        at = slice(head * HD, (head + 1) * HD)
        query_here = turned(proj[:, at], cosine[...], sine[...]).astype(BF)
        query[:, at] = query_here
        probs = head_probs(query_here, key_here, allowed[...])[1].astype(BF)
        attended[:, at] = tile_dot(probs, value_here).astype(BF)


def attention_call(x, weight, cosine, sine, allowed, groups):
    tokens, width = x.shape
    cols = weight.shape[1] // groups
    heads = cols // HD - 2

    def here(cut):
        return pl.BlockSpec((tokens, cut), lambda g: (0, g))

    def whole(values):
        return pl.BlockSpec(values.shape, lambda g: (0, 0))

    cuts = [heads * HD, HD, HD, heads * HD]
    return pl.pallas_call(
        attention_kernel,
        grid=(groups,),
        in_specs=[
            whole(x),
            pl.BlockSpec((width, cols), lambda g: (0, g)),
            whole(cosine),
            whole(sine),
            whole(allowed),
        ],
        out_specs=[here(cut) for cut in cuts],
        out_shape=[jax.ShapeDtypeStruct((tokens, groups * cut), BF) for cut in cuts],
        compiler_params=kernel_params(),
        cost_estimate=LIGHT,
    )(x, weight, cosine, sine, allowed)


def share(ids, total, sent, kept):
    rows = sent.shape[0]
    here = ids[3]
    sent[...] = total[pl.ds(pl.multiple_of((1 - here) * rows, rows), rows), :].astype(BF)
    kept[...] = total[pl.ds(pl.multiple_of(here * rows, rows), rows), :]


def branch_kernel(ids, attended, weight, sent, kept, total):
    part = tile_dot_cols(attended[...], weight[...])
    total[...] = jnp.where(pl.program_id(0) == 0, part, total[...] + part)

    @pl.when(pl.program_id(0) == pl.num_programs(0) - 1)
    def _():
        share(ids, total, sent, kept)


def branch_call(ids, attended, weight):
    tokens, cols = attended.shape
    width = weight.shape[0]
    tile = 512
    half = pl.BlockSpec((tokens // 2, width), lambda g, ids: (0, 0))
    return pl.pallas_call(
        branch_kernel,
        grid_spec=pltpu.PrefetchScalarGridSpec(
            num_scalar_prefetch=1,
            grid=(cols // tile,),
            in_specs=[
                pl.BlockSpec((tokens, tile), lambda g, ids: (0, g)),
                pl.BlockSpec((width, tile), lambda g, ids: (0, g)),
            ],
            out_specs=[half, half],
            scratch_shapes=[pltpu.VMEM((tokens, width), F32)],
        ),
        out_shape=[jax.ShapeDtypeStruct((tokens // 2, width), kind) for kind in (BF, F32)],
        compiler_params=kernel_params(),
        cost_estimate=LIGHT,
    )(ids, attended, weight)


def attention_back_kernel(
    ids, d, out, weight, query, key, value, cosine, sine, allowed, d_qkv, sent, kept, total
):
    heads = query.shape[1] // HD
    key_here, value_here = key[...], value[...]
    d_attended = tile_dot(d[...], out[...]).astype(BF)
    d_key = d_value = 0.0
    pieces = []
    for head in range(heads):
        at = slice(head * HD, (head + 1) * HD)
        query_here, d_here = query[:, at], d_attended[:, at]
        bent, probs = head_probs(query_here, key_here, allowed[...])
        d_probs = tile_dot_cols(d_here, value_here)
        inner = jnp.sum(probs * d_probs, axis=1, keepdims=True)
        d_scores = probs * (d_probs - inner) * (HD**-0.5) * (1.0 - bent * bent)
        d_scores = d_scores.astype(BF)
        d_query = tile_dot(d_scores, key_here)
        pieces.append(turned(d_query, cosine[...], -sine[...]).astype(BF))
        d_key = d_key + outer_dot(d_scores, query_here)
        d_value = d_value + outer_dot(probs.astype(BF), d_here)
    pieces.append(turned(d_key, cosine[...], -sine[...]).astype(BF))
    pieces.append(d_value.astype(BF))
    made = jnp.concatenate(pieces, axis=1)
    d_qkv[...] = made
    part = tile_dot_cols(made, weight[...])
    total[...] = jnp.where(pl.program_id(0) == 0, part, total[...] + part)

    @pl.when(pl.program_id(0) == pl.num_programs(0) - 1)
    def _():
        share(ids, total, sent, kept)


def attention_back_call(ids, d, out, weight, query, key, value, cosine, sine, allowed, groups):
    tokens, width = d.shape
    cols = weight.shape[1] // groups
    heads = cols // HD - 2

    def here(rows, cut):
        return pl.BlockSpec((rows, cut), lambda g, ids: (0, g))

    def whole(values):
        return pl.BlockSpec(values.shape, lambda g, ids: (0, 0))

    half = pl.BlockSpec((tokens // 2, width), lambda g, ids: (0, 0))
    return pl.pallas_call(
        attention_back_kernel,
        grid_spec=pltpu.PrefetchScalarGridSpec(
            num_scalar_prefetch=1,
            grid=(groups,),
            in_specs=[
                whole(d),
                here(width, heads * HD),
                here(width, cols),
                here(tokens, heads * HD),
                here(tokens, HD),
                here(tokens, HD),
                whole(cosine),
                whole(sine),
                whole(allowed),
            ],
            out_specs=[here(tokens, cols), half, half],
            scratch_shapes=[pltpu.VMEM((tokens, width), F32)],
        ),
        out_shape=[
            jax.ShapeDtypeStruct((tokens, groups * cols), BF),
            jax.ShapeDtypeStruct((tokens // 2, width), BF),
            jax.ShapeDtypeStruct((tokens // 2, width), F32),
        ],
        compiler_params=kernel_params(),
        cost_estimate=LIGHT,
    )(ids, d, out, weight, query, key, value, cosine, sine, allowed)


def outer_kernel(which, left, right, *rest):
    got, (made, flipped) = rest[:-2], rest[-2:]

    @pl.when(pl.program_id(0) == 0)
    def _():
        flipped[...] = left[...].T

    total = tile_dot(flipped[...], right[...])
    for piece in got:
        total = total + piece[...].astype(F32)
    made[...] = total.astype(BF)


def outer_call(left, right, which, *got):
    tokens, cut, cols = left.shape[0], left.shape[1] // 2, right.shape[1]
    tile = cols // 2
    across = pl.BlockSpec((cut, tile), lambda i, which: (0, i))
    return pl.pallas_call(
        outer_kernel,
        grid_spec=pltpu.PrefetchScalarGridSpec(
            num_scalar_prefetch=1,
            grid=(cols // tile,),
            in_specs=[
                pl.BlockSpec((tokens, cut), lambda i, which: (0, which[0])),
                pl.BlockSpec((tokens, tile), lambda i, which: (0, i)),
            ]
            + [across] * len(got),
            out_specs=across,
            scratch_shapes=[pltpu.VMEM((cut, tokens), BF)],
        ),
        out_shape=jax.ShapeDtypeStruct((cut, cols), BF),
        compiler_params=kernel_params(),
        cost_estimate=LIGHT,
    )(which, left, right, *got)


def outer_halves_kernel(left, right, made, flipped):
    @pl.when(pl.program_id(0) == 0)
    def _():
        flipped[...] = left[...].T

    made[...] = tile_dot(flipped[...], right[...]).astype(BF)


def outer_halves(left, right):
    tokens, width = left.shape
    cols = right.shape[1] // 2
    tile = 384
    count = cols // tile
    return pl.pallas_call(
        outer_halves_kernel,
        grid=(2 * count,),
        in_specs=[
            pl.BlockSpec((tokens, width), lambda i: (0, 0)),
            pl.BlockSpec((tokens, tile), lambda i: (0, i)),
        ],
        out_specs=pl.BlockSpec((None, width, tile), lambda i: (i // count, 0, i % count)),
        out_shape=jax.ShapeDtypeStruct((2, width, cols), BF),
        scratch_shapes=[pltpu.VMEM((width, tokens), BF)],
        compiler_params=kernel_params(),
        cost_estimate=LIGHT,
    )(left, right)


def sum_cut(grad):
    width, cols = grad.shape[1:]
    blocks = 2 * lax.axis_size("c") * lax.axis_size("y")
    grad = grad.reshape(blocks, 2 * width // blocks, cols)
    return lax.psum_scatter(grad, ("x", "c", "y"), scatter_dimension=0, tiled=True)[0]


def gather_cut(own):
    whole = lax.all_gather(own, ("x", "c", "y"), axis=0, tiled=True)
    return whole.reshape(2, 2, -1, own.shape[1])


def outer_low(left, right, mine, theirs):
    sent = outer_call(left, right, theirs)
    return outer_call(left, right, mine, swap(sent, "c", 1))


def assemble_kernel(counts, rows, cols, *refs):
    pieces, made = refs[:-1], refs[-1]
    step, first = pl.program_id(0), 0
    for piece, count in zip(pieces, counts):

        @pl.when((step >= first) & (step < first + count))
        def _(piece=piece):
            made[...] = piece[...].astype(made.dtype)

        first += count


def assemble(shape, block, placed, kind=BF):
    counts = [array.shape[0] // block[0] for _, _, array in placed]
    steps = [(row + k, col) for (row, col, _), n in zip(placed, counts) for k in range(n)]
    rows, cols = (jnp.stack([jnp.asarray(s[i], jnp.int32) for s in steps]) for i in range(2))
    specs, first = [], 0
    for count in counts:

        def at(step, rows, cols, first=first, count=count):
            return (jnp.clip(step - first, 0, count - 1), 0)

        specs.append(pl.BlockSpec(block, at))
        first += count
    return pl.pallas_call(
        functools.partial(assemble_kernel, counts),
        grid_spec=pltpu.PrefetchScalarGridSpec(
            num_scalar_prefetch=2,
            grid=(len(steps),),
            in_specs=specs,
            out_specs=pl.BlockSpec(block, lambda step, rows, cols: (rows[step], cols[step])),
        ),
        out_shape=jax.ShapeDtypeStruct(shape, kind),
        compiler_params=kernel_params(),
        cost_estimate=LIGHT,
    )(rows, cols, *[array for _, _, array in placed])


def gain_sum(parts):
    count, width = parts.shape
    blocks = lax.axis_size("c") * lax.axis_size("y") * lax.axis_size("z")
    parts = parts.reshape(count, blocks, width // blocks).transpose(1, 0, 2)
    parts = parts + swap(parts, "x", 1)
    here, rows = lax.axis_index("c"), blocks // 2
    parts = lax.dynamic_slice_in_dim(parts, here * rows, rows, 0) + swap(
        lax.dynamic_slice_in_dim(parts, (1 - here) * rows, rows, 0), "c", 1
    )
    if lax.axis_size("y") == 2:
        here, rows = lax.axis_index("y"), blocks // 4
        parts = lax.dynamic_slice_in_dim(parts, here * rows, rows, 0) + swap(
            lax.dynamic_slice_in_dim(parts, (1 - here) * rows, rows, 0), "y", 1
        )
    else:
        parts = lax.psum_scatter(parts, "y", scatter_dimension=0, tiled=True)
    here = lax.axis_index("z")
    total = lax.dynamic_index_in_dim(parts, here, 0, keepdims=False)
    for k in (1, 2, 3):
        total = total + swap(
            lax.dynamic_index_in_dim(parts, here ^ k, 0, keepdims=False), "z", k
        )
    return total


def on_device(
    tokens,
    seg_lengths,
    parents,
    attn_gain,
    w_query,
    w_key,
    w_value,
    w_out,
    attn_post_gain,
    ffn_gain,
    w_gate,
    w_up,
    w_down,
    ffn_post_gain,
    out_grad,
):
    local_rows, width = tokens.shape
    z_size, y_size, c_size = lax.axis_size("z"), lax.axis_size("y"), lax.axis_size("c")
    shard = width // (z_size * y_size * c_size)
    group_rows = local_rows * lax.axis_size("x")
    head_cols = w_query.shape[1]
    kv_cols = w_key.shape[1]
    kv_here = kv_cols // HD
    ids = spread_ids()
    core_here, core_there = ids[2:3], 1 - ids[2:3]
    first_half, second_half = jnp.zeros(1, jnp.int32), jnp.ones(1, jnp.int32)

    def inward(values):
        lead = values.shape[:-1]
        cut = values.reshape(lead + (z_size, y_size, c_size, shard))
        count = len(lead)
        order = tuple(range(count)) + (count + 2, count + 1, count, count + 3)
        return cut.transpose(order).reshape(lead + (width,))

    def outward(values):
        lead = values.shape[:-1]
        cut = values.reshape(lead + (c_size, y_size, z_size, shard))
        count = len(lead)
        order = tuple(range(count)) + (count + 2, count + 1, count, count + 3)
        return cut.transpose(order).reshape(lead + (width,))

    pairs = y_size == 2
    row_axes = ("c", "y", "z")
    positions, allowed = tree_tables(seg_lengths[0], parents[0], group_rows)
    allowed = allowed.astype(jnp.int32)
    cosine, sine = rope_tables(positions, HD)
    attn_gain, attn_post_gain = inward(attn_gain), inward(attn_post_gain)
    ffn_gain, ffn_post_gain = inward(ffn_gain), inward(ffn_post_gain)
    state_in = inward(tokens).astype(F32)
    out_cotan = inward(out_grad).astype(F32)

    qkv_here = jnp.concatenate(
        [
            weight[:, g * (weight.shape[1] // kv_here) : (g + 1) * (weight.shape[1] // kv_here)]
            for g in range(kv_here)
            for weight in (w_query, w_key, w_value)
        ],
        axis=1,
    )
    inverse_one = lax.rsqrt(jnp.mean(state_in * state_in, axis=-1, keepdims=True) + NORM_EPS)
    unit_one = state_in * inverse_one
    normed_here = (unit_one * attn_gain).astype(BF)

    qkv_weight = lax.all_gather(qkv_here, row_axes, axis=0, tiled=True)
    out_weight = lax.all_gather(w_out.T, row_axes, axis=0, tiled=True)

    live = {"up": line_cuts(w_up), "down": line_cuts(w_down.T)}
    live["gate"] = line_swaps(line_cuts(w_gate))
    live["normed_one"] = [normed_here, swap(normed_here, "x", 1)]
    live = close(live)

    live["normed_one"] = pair_gather(*live["normed_one"])
    live["gate"] = cut_first(line_place(live["gate"]))
    live["up"] = line_swaps(live["up"])
    live = close(live)

    live["gate"] |= cut_over_x(live["gate"]) | cut_over_y(live["gate"])
    live["up"] = cut_first(line_place(live["up"]))
    live["down"] = line_swaps(live["down"])
    live["qkv"] = qkv_weight
    live = close(live)
    down_weight = gather_cut(line_place(live.pop("down")))

    live["up"] |= cut_over_x(live["up"]) | cut_over_y(live["up"])
    gate_half = cut_half(live["gate"])
    live["gate"] = [gate_half, swap(gate_half, "c", 1)]
    normed_one, qkv_weight = live["normed_one"], live["qkv"]
    query, key, value, attended = attention_call(
        normed_one, qkv_weight, cosine, sine, allowed, kv_here
    )
    live["attended"] = attended
    live = close(live)

    attended = live["attended"]
    live["branch"] = branch_call(ids, attended, out_weight)
    live = close(live)
    sent, kept = live["branch"]
    live["branch"] = [kept, swap(sent, "x", 1)]
    up_half = cut_half(live["up"])
    live["up"] = [up_half, swap(up_half, "c", 1)]
    live = close(live)
    branch = live["branch"][0] + live["branch"][1].astype(F32)
    inverse_two = lax.rsqrt(jnp.mean(branch * branch, axis=-1, keepdims=True) + NORM_EPS)
    unit_two = branch * inverse_two
    hidden = state_in + unit_two * attn_post_gain
    inverse_three = lax.rsqrt(jnp.mean(hidden * hidden, axis=-1, keepdims=True) + NORM_EPS)
    unit_three = hidden * inverse_three


    live["normed_two"] = line_gather((unit_three * ffn_gain).astype(BF))
    live = close(live)
    weights = [Weight(*live["gate"]), Weight(*live["up"]), Weight(down_weight)]
    normed_two = live["normed_two"]

    live["act"], gate_proj, up_proj, *sums = ffn_call(
        forward_kernel, ids, normed_two, weights, (), (BF, F32, F32), 384
    )
    live["sums"] = line_swaps(sums)
    live = close(live)
    ffn_out = line_total(live["sums"])
    inverse_four = lax.rsqrt(jnp.mean(ffn_out * ffn_out, axis=-1, keepdims=True) + NORM_EPS)
    unit_four = ffn_out * inverse_four
    mixed = (hidden + unit_four * ffn_post_gain).astype(BF)
    gain_four = jnp.sum(out_cotan * unit_four, axis=0)
    d_ffn = norm_back(out_cotan * ffn_post_gain, unit_four, inverse_four).astype(BF)
    live["d_ffn"] = line_gather(d_ffn)
    live = close(live)
    d_ffn, act, normed_two = live["d_ffn"], live["act"], live["normed_two"]
    grad_down = sum_cut(outer_halves(d_ffn, act))
    d_gate, d_up, *sums = ffn_call(
        backward_kernel, ids, d_ffn, weights, (gate_proj, up_proj), (BF, BF), 384
    )
    live = close({"d_gate": d_gate, "d_up": d_up, "sums": sums})

    live["sums"] = line_swaps(live["sums"])
    if pairs:
        gate = fold_parts(outer_low(normed_two, live["d_gate"], core_here, core_there))
        live["gate_got"] = fold_first(gate.pop("across"))
        live["gate"] = gate
    else:
        live["gate"] = outer_halves(normed_two, live["d_gate"])
    live["up"] = outer_halves(normed_two, live["d_up"])
    live = close({k: live[k] for k in ("sums", "up", "gate", "gate_got") if k in live})
    grad_up = sum_cut(live.pop("up"))

    d_normed_two = line_total(live["sums"])
    gain_three = jnp.sum(d_normed_two * unit_three, axis=0)
    d_hidden = out_cotan + norm_back(d_normed_two * ffn_gain, unit_three, inverse_three)
    gain_two = jnp.sum(d_hidden * unit_two, axis=0)
    d_branch = norm_back(d_hidden * attn_post_gain, unit_two, inverse_two).astype(BF)
    live["d_branch"] = [d_branch, swap(d_branch, "x", 1)]
    if pairs:
        own = live["gate"]["own"]
        over_x, over_y = fold_join(live["gate"], live.pop("gate_got"))
        live["gate"] = {"own": own, "x": over_x, "y": swap(over_y, "y", 1)}
    else:
        live["gate"] = {"own": sum_cut(live["gate"])}
    live = close({k: live[k] for k in ("d_branch", "gate")})
    d_branch = pair_gather(*live["d_branch"])

    if pairs:
        live["gate"]["x"] = swap(live["gate"]["x"], "x", 1)
    live["down"] = line_swaps(line_chunks(grad_down))
    grad_out = outer_low(d_branch, attended, core_here, core_there)
    if pairs:
        out_mine, out_far = pair_halves(grad_out, "y")
        live["out"] = [out_mine, swap(out_far, "y", 1)]
    else:
        live["out"] = [rows_sum(grad_out, "y")]
    d_qkv, sent, kept = attention_back_call(
        ids, d_branch, out_weight, qkv_weight, query, key, value, cosine, sine, allowed, kv_here
    )
    live["d_normed_one"] = [kept, sent]
    live["d_qkv"] = d_qkv
    live = close(live)

    grad_down = line_columns(live["down"])
    kept, sent = live["d_normed_one"]
    live["d_normed_one"] = [kept, swap(sent, "x", 1)]
    live["qkv"] = outer_low(normed_one, live["d_qkv"], core_here, core_there)
    live["out"] = add_low(*live["out"]) if pairs else live["out"][0]
    grad_gate = line_total(list(live["gate"].values())).astype(BF)
    live["gate"] = line_swaps(line_chunks(grad_gate))
    live = close({k: live[k] for k in ("d_normed_one", "qkv", "out", "gate")})
    grad_gate = line_columns(live["gate"])
    d_normed_one = live["d_normed_one"][0] + live["d_normed_one"][1].astype(F32)
    gain_one = jnp.sum(d_normed_one * unit_one, axis=0)
    grad_tokens = d_hidden + norm_back(d_normed_one * attn_gain, unit_one, inverse_one)

    parts = y_chunks(live["qkv"]) if pairs else line_chunks(rows_sum(live["qkv"], "y"))
    live = {"parts": parts, "out": line_swaps(line_chunks(live["out"]))}
    live["gains"] = jnp.stack([gain_one, gain_two, gain_three, gain_four], axis=0)
    if pairs:
        live["far"] = [swap(parts[k][1], "y", 1) for k in (2, 3)]
    live = close(live)
    parts, grad_out = live["parts"], line_total(live.pop("out"))

    if pairs:
        far = [add_low(parts[k][0], q) for k, q in zip((2, 3), live["far"])]
        live["near"] = [swap(parts[k][1], "y", 1) for k in (0, 1)]
    else:
        far = parts[2:]
    live["far"] = [swap(piece, "z", k) for k, piece in zip((2, 3), far)]
    gains = gain_sum(live.pop("gains"))
    live = close(live)

    if pairs:
        near = [add_low(live["parts"][k][0], q) for k, q in zip((0, 1), live["near"])]
    else:
        near = live["parts"][:2]
    grad_qkv = line_total([near[0], swap(near[1], "z", 1), *live["far"]])
    grad_up = line_columns(line_swaps(line_chunks(grad_up)))
    cols = grad_qkv.shape[1] // kv_here
    cuts = (0, cols - 2 * HD, cols - HD, cols)
    grad_query, grad_key, grad_value = (
        jnp.concatenate(
            [grad_qkv[:, g * cols + cuts[i] : g * cols + cuts[i + 1]] for g in range(kv_here)],
            axis=1,
        )
        for i in range(3)
    )
    return (
        outward(mixed),
        outward(grad_tokens),
        gains[0],
        grad_query,
        grad_key,
        grad_value,
        grad_out.T,
        gains[1],
        gains[2],
        grad_gate,
        grad_up,
        grad_down.T,
        gains[3],
    )


def solution(mesh):
    count, pair = mesh.devices.shape
    grid = Mesh(mesh.devices.reshape(4, count // 8, 2, pair), ("z", "y", "c", "x"))
    rows = ("z", "y", "c")
    return jax.shard_map(
        on_device,
        mesh=grid,
        in_specs=(
            P(rows + ("x",), None),
            P(rows, None),
            P(rows, None),
            P(),
            P(rows, "x"),
            P(rows, "x"),
            P(rows, "x"),
            P("x", rows),
            P(),
            P(),
            P(rows, "x"),
            P(rows, "x"),
            P("x", rows),
            P(),
            P(rows + ("x",), None),
        ),
        out_specs=(
            P(rows + ("x",), None),
            P(rows + ("x",), None),
            P(rows),
            P(rows, "x"),
            P(rows, "x"),
            P(rows, "x"),
            P("x", rows),
            P(rows),
            P(rows),
            P(rows, "x"),
            P(rows, "x"),
            P("x", rows),
            P(rows),
        ),
        check_vma=False,
    )
```

time: 1130 us -> 875 us (0.77)
  Pallas kernels: 0 us -> 170 us
  matrix products: 153 us -> 0 us
  waiting for transfers between devices: 595 us -> 478 us
  local copies, waits for them, and re-layouts: 176 us -> 79.8 us
  other arithmetic: 100 us -> 42.7 us
  blocking collectives: 43 us -> 0 us
  starting transfers between devices: 36.1 us -> 75.3 us
    pallas_call x0 -> x21, Pallas kernels: none -> 170 us  [the longest x2 68.7 us: ffn_call(): pl.pallas_call(functools.partial(kernel, [weight.columns for weight in we...]
    dot_general x24 -> x0, matrix products: 150 us -> none  [the longest x6 55.3 us: rows_dot(): lax.dot_general(left, right, (((1,), (0,)), ((), ())), preferred_element_...]
    all_gather x2 -> x1, waiting for transfers between devices: 73.6 us -> 0.01 us  [gather_cut(): whole = lax.all_gather(own, ('x', 'c', 'y'), axis=0, tiled=True)]
    unnamed x226 -> x228, local copies, waits for them, and re-layouts: 91.4 us -> 33.5 us
    concatenate x6 -> x8, other arithmetic: 49.8 us -> 5.94 us  [the longest x2 1.74 us: on_device(): jnp.concatenate([grad_qkv[:, g * cols + cuts[i]:g * cols + cuts[i + 1]] f...]
    psum x1 -> x0, blocking collectives: 43 us -> none  [gain_sum(): parts = lax.psum(parts, ('z', 'y', 'c', 'x'))]
    ppermute x26 -> x68, starting transfers between devices: 35.5 us -> 74.9 us  [swap(): return lax.ppermute(values, axis, [(i, i ^ mask) for i in range(size)])]
    reduce_scatter x2, waiting for transfers between devices: 27.8 us -> 0.02 us  [sum_cut(): lax.psum_scatter(grad, ('x', 'c', 'y'), scatter_dimension=0, tiled=True)[0]]
  transfers between devices with their start and end apart: 33 -> 73, of which waited for: 24 -> 35; matrix products, arithmetic and copies ran while one was open for 26% -> 10% of each run, Pallas kernels for 0% -> 15%
where the time goes in v4:
time: 875 us; the launch traced here: 861 us
  waiting for transfers between devices  478 us (55%)
  Pallas kernels  170 us (19%)
  local copies, waits for them, and re-layouts  79.8 us (9%)
  starting transfers between devices  75.3 us (9%)
  other arithmetic  42.7 us (5%)
  between operations  15.4 us (2%)
    ppermute x68, waiting for transfers between devices, swap(): return lax.ppermute(values, axis, [(i, i ^ mask) for i in range(size)])  477 us
    ppermute x68, starting transfers between devices, swap(): return lax.ppermute(values, axis, [(i, i ^ mask) for i in range(size)])  74.9 us
    pallas_call x2, Pallas kernels, ffn_call(): pl.pallas_call(functools.partial(kernel, [weight.columns for weight in we...  68.7 us
    unnamed x228, local copies, waits for them, and re-layouts  33.5 us
    pallas_call x8, Pallas kernels, assemble(): pl.pallas_call(functools.partial(assemble_kernel, counts), grid_spec=pltp...  28.2 us
    pallas_call x6, Pallas kernels, outer_call(): pl.pallas_call(outer_kernel, grid_spec=pltpu.PrefetchScalarGridSpec(num_s...  26.9 us
    pallas_call x2, Pallas kernels, outer_halves(): pl.pallas_call(outer_halves_kernel, grid=(2 * count,), in_specs=[pl.Block...  23.6 us
  transfers between devices with their start and end apart: 73, of which 35 were waited for; matrix products, arithmetic and copies ran while one was open for 10% of the time, Pallas kernels for 15%

profile of v4, /device:TPU:8, one launch (start us, length us, event | category | flops | bytes accessed | tf_op | source)
XLA Modules:
  0.0 860.9 jit_solution(16762130006010676110)
XLA Ops:
  27.8 8.2 collective-permute-done.refs_1_
  36.0 12.3 %collective-permute-done.1.refs_2_ = bf16[144,1152]{1,0:T(8,128)(2,1)S(1)} collective-permute-done((bf16[144,1152]{1,0:T(8,128)(2,1)}, bf16[144,1152]{1,0:T(8,128)(2,1)S(1)}, u32[]{:S(2)}, u32[]{:S(2)}) %collective-permute-start.1) | collective-permute-done | bytes 331808 | tf_op jit(solution)/shard_map/ppermute | solution.py:177
  48.4 18.0 %collective-permute-done.2.refs_3_ = bf16[144,1152]{1,0:T(8,128)(2,1)S(1)} collective-permute-done((bf16[144,1152]{1,0:T(8,128)(2,1)}, bf16[144,1152]{1,0:T(8,128)(2,1)S(1)}, u32[]{:S(2)}, u32[]{:S(2)}) %collective-permute-start.2) | collective-permute-done | bytes 331808 | tf_op jit(solution)/shard_map/ppermute | solution.py:177
  76.0 13.7 %collective-permute-done.6.refs_1_ = bf16[144,1152]{1,0:T(8,128)(2,1)S(1)} collective-permute-done((bf16[144,1152]{1,0:T(8,128)(2,1)}, bf16[144,1152]{1,0:T(8,128)(2,1)S(1)}, u32[]{:S(2)}, u32[]{:S(2)}) %collective-permute-start.6) | collective-permute-done | bytes 331808 | tf_op jit(solution)/shard_map/ppermute | solution.py:177
  89.7 21.0 %collective-permute-done.7.refs_2_ = bf16[144,1152]{1,0:T(8,128)(2,1)S(1)} collective-permute-done((bf16[144,1152]{1,0:T(8,128)(2,1)}, bf16[144,1152]{1,0:T(8,128)(2,1)S(1)}, u32[]{:S(2)}, u32[]{:S(2)}) %collective-permute-start.7) | collective-permute-done | bytes 331808 | tf_op jit(solution)/shard_map/ppermute | solution.py:177
  110.7 21.6 %collective-permute-done.8.refs_3_ = bf16[144,1152]{1,0:T(8,128)(2,1)S(1)} collective-permute-done((bf16[144,1152]{1,0:T(8,128)(2,1)}, bf16[144,1152]{1,0:T(8,128)(2,1)S(1)}, u32[]{:S(2)}, u32[]{:S(2)}) %collective-permute-start.8) | collective-permute-done | bytes 331808 | tf_op jit(solution)/shard_map/ppermute | solution.py:177
  141.5 8.8 %collective-permute-done.9.refs_1_ = bf16[144,1152]{1,0:T(8,128)(2,1)S(1)} collective-permute-done((bf16[144,1152]{1,0:T(8,128)(2,1)S(1)}, bf16[144,1152]{1,0:T(8,128)(2,1)S(1)}, u32[]{:S(2)}, u32[]{:S(2)}) %collective-permute-start.9) | collective-permute-done | bytes 331808 | tf_op jit(solution)/shard_map/ppermute | solution.py:177
  155.0 23.5 %collective-permute-done.11.refs_3_ = bf16[144,1152]{1,0:T(8,128)(2,1)S(1)} collective-permute-done((bf16[144,1152]{1,0:T(8,128)(2,1)S(1)}, bf16[144,1152]{1,0:T(8,128)(2,1)S(1)}, u32[]{:S(2)}, u32[]{:S(2)}) %collective-permute-start.11) | collective-permute-done | bytes 331808 | tf_op jit(solution)/shard_map/ppermute | solution.py:177
  222.5 7.9 shard_map.251.refs_2_
  232.8 18.2 %collective-permute-done.19 = bf16[128,2304]{1,0:T(8,128)(2,1)} collective-permute-done((bf16[128,2304]{1,0:T(8,128)(2,1)S(1)}, bf16[128,2304]{1,0:T(8,128)(2,1)}, u32[]{:S(2)}, u32[]{:S(2)}) %collective-permute-start.19) | collective-permute-done | bytes 589856 | tf_op jit(solution)/shard_map/ppermute | solution.py:177
  258.0 37.6 %collective-permute-done.23 = bf16[128,2304]{1,0:T(8,128)(2,1)S(1)} collective-permute-done((bf16[128,2304]{1,0:T(8,128)(2,1)S(1)}, bf16[128,2304]{1,0:T(8,128)(2,1)S(1)}, u32[]{:S(2)}, u32[]{:S(2)}) %collective-permute-start.23) | collective-permute-done | bytes 589856 | tf_op jit(solution)/shard_map/ppermute | solution.py:177
  295.6 10.7 %collective-permute-done.22 = bf16[128,2304]{1,0:T(8,128)(2,1)S(1)} collective-permute-done((bf16[128,2304]{1,0:T(8,128)(2,1)S(1)}, bf16[128,2304]{1,0:T(8,128)(2,1)S(1)}, u32[]{:S(2)}, u32[]{:S(2)}) %collective-permute-start.22) | collective-permute-done | bytes 589856 | tf_op jit(solution)/shard_map/ppermute | solution.py:177
  307.8 32.8 %shard_map.253 = (bf16[512,2304]{1,0:T(8,128)(2,1)}, f32[512,2304]{1,0:T(8,128)}, f32[512,2304]{1,0:T(8,128)}, f32[128,2304]{1,0:T(8,128)}, bf16[128,2304]{1,0:T...) custom-call(s32[4]{0:T(128)} %copy-done.39, bf16[512,2304]{1,0:T(8,128)(2,1)} %pad_maximum_fusion.x.left, ...), custom_call_target="tpu_custom_call" | custom-call | tf_op jit(solution)/shard_map/pallas_call | solution.py:155
  352.0 14.9 %collective-permute-done.24 = bf16[128,2304]{1,0:T(8,128)(2,1)} collective-permute-done((bf16[128,2304]{1,0:T(8,128)(2,1)}, bf16[128,2304]{1,0:T(8,128)(2,1)}, u32[]{:S(2)}, u32[]{:S(2)}) %collective-permute-start.24) | collective-permute-done | bytes 589856 | tf_op jit(solution)/shard_map/ppermute | solution.py:177
  366.9 16.6 %collective-permute-done.25 = bf16[128,2304]{1,0:T(8,128)(2,1)} collective-permute-done((bf16[128,2304]{1,0:T(8,128)(2,1)}, bf16[128,2304]{1,0:T(8,128)(2,1)}, u32[]{:S(2)}, u32[]{:S(2)}) %collective-permute-start.25) | collective-permute-done | bytes 589856 | tf_op jit(solution)/shard_map/ppermute | solution.py:177
  383.6 24.4 %collective-permute-done.26 = bf16[128,2304]{1,0:T(8,128)(2,1)} collective-permute-done((bf16[128,2304]{1,0:T(8,128)(2,1)}, bf16[128,2304]{1,0:T(8,128)(2,1)}, u32[]{:S(2)}, u32[]{:S(2)}) %collective-permute-start.26) | collective-permute-done | bytes 589856 | tf_op jit(solution)/shard_map/ppermute | solution.py:177
  415.8 24.8 %collective-permute-done.29 = bf16[128,2304]{1,0:T(8,128)(2,1)S(1)} collective-permute-done((bf16[128,2304]{1,0:T(8,128)(2,1)S(1)}, bf16[128,2304]{1,0:T(8,128)(2,1)S(1)}, u32[]{:S(2)}, u32[]{:S(2)}) %collective-permute-start.29) | collective-permute-done | bytes 589856 | tf_op jit(solution)/shard_map/ppermute | solution.py:177
  440.7 9.4 %collective-permute-done.28 = bf16[128,2304]{1,0:T(8,128)(2,1)S(1)} collective-permute-done((bf16[128,2304]{1,0:T(8,128)(2,1)S(1)}, bf16[128,2304]{1,0:T(8,128)(2,1)S(1)}, u32[]{:S(2)}, u32[]{:S(2)}) %collective-permute-start.28) | collective-permute-done | bytes 589856 | tf_op jit(solution)/shard_map/ppermute | solution.py:177
  450.2 11.8 %shard_map.259 = bf16[2,2304,1152]{2,1,0:T(8,128)(2,1)} custom-call(bf16[512,2304]{1,0:T(8,128)(2,1)S(1)} %pad_maximum_fusion.1.d.left, bf16[512,2304]{1,0:T(8,128)(2,1)} %get-tuple-element.275.right), custom_call_target="tpu_custom_call" | custom-call | tf_op jit(solution)/shard_map/pallas_call | solution.py:598
  462.1 35.8 %shard_map.254 = (bf16[512,2304]{1,0:T(8,128)(2,1)}, bf16[512,2304]{1,0:T(8,128)(2,1)}, f32[128,2304]{1,0:T(8,128)}, bf16[128,2304]{1,0:T(8,128)(2,1)}, bf16[128...) custom-call(s32[4]{0:T(128)} %copy-done.39, bf16[512,2304]{1,0:T(8,128)(2,1)} %copy-done.1, ...), custom_call_target="tpu_custom_call" | custom-call | tf_op jit(solution)/shard_map/pallas_call | solution.py:155
  504.6 9.1 %collective-permute-done.30.rest_0_ = bf16[1152,2304]{1,0:T(8,128)(2,1)} collective-permute-done((bf16[1152,2304]{1,0:T(8,128)(2,1)}, bf16[1152,2304]{1,0:T(8,128)(2,1)}, u32[]{:S(2)}, u32[]{:S(2)}) %collective-permute-start.30) | collective-permute-done | bytes 5308448 | tf_op jit(solution)/shard_map/ppermute | solution.py:177
  530.5 11.8 %shard_map.257 = bf16[2,2304,1152]{2,1,0:T(8,128)(2,1)} custom-call(bf16[512,2304]{1,0:T(8,128)(2,1)S(1)} %copy-done, bf16[512,2304]{1,0:T(8,128)(2,1)} %get-tuple-element.257.right), custom_call_target="tpu_custom_call" | custom-call | tf_op jit(solution)/shard_map/pallas_call | solution.py:598
  553.9 15.3 %collective-permute-done.34 = bf16[128,2304]{1,0:T(8,128)(2,1)} collective-permute-done((bf16[128,2304]{1,0:T(8,128)(2,1)}, bf16[128,2304]{1,0:T(8,128)(2,1)}, u32[]{:S(2)}, u32[]{:S(2)}) %collective-permute-start.34) | collective-permute-done | bytes 589856 | tf_op jit(solution)/shard_map/ppermute | solution.py:177
  569.2 12.8 %collective-permute-done.35 = bf16[128,2304]{1,0:T(8,128)(2,1)} collective-permute-done((bf16[128,2304]{1,0:T(8,128)(2,1)}, bf16[128,2304]{1,0:T(8,128)(2,1)}, u32[]{:S(2)}, u32[]{:S(2)}) %collective-permute-start.35) | collective-permute-done | bytes 589856 | tf_op jit(solution)/shard_map/ppermute | solution.py:177
  599.1 10.0 %collective-permute-done.36 = bf16[128,2304]{1,0:T(8,128)(2,1)S(1)} collective-permute-done((bf16[128,2304]{1,0:T(8,128)(2,1)S(1)}, bf16[128,2304]{1,0:T(8,128)(2,1)S(1)}, u32[]{:S(2)}, u32[]{:S(2)}) %collective-permute-start.36) | collective-permute-done | bytes 589856 | tf_op jit(solution)/shard_map/ppermute | solution.py:177
  633.4 11.5 %shard_map.258 = (bf16[256,2048]{1,0:T(8,128)(2,1)S(1)}, bf16[128,2304]{1,0:T(8,128)(2,1)}, f32[128,2304]{1,0:T(8,128)}) custom-call(s32[4]{0:T(128)S(1)} %copy-done.40, bf16[256,2304]{1,0:T(8,128)(2,1)} %copy-done.2, bf16[2304,1024]{1,0:T(8,128)(2,1)} %all-gather.6.cloned.1.call-done.weight.out, bf16[2304,2048]{1,0:T(8,128)(2,1)} %all-gather.4.cloned.1.call-done.weight, ...), custom_call_target="tpu_custom_call" | custom-call | tf_op jit(solution)/shard_map/pallas_call | solution.py:520
  644.9 32.2 %collective-permute-done.41 = bf16[576,1152]{1,0:T(8,128)(2,1)} collective-permute-done((bf16[576,1152]{1,0:T(8,128)(2,1)}, bf16[576,1152]{1,0:T(8,128)(2,1)}, u32[]{:S(2)}, u32[]{:S(2)}) %collective-permute-start.41) | collective-permute-done | bytes 1327136 | tf_op jit(solution)/shard_map/ppermute | solution.py:177
  711.5 8.0 collective-permute-done.47.refs_3_
  745.8 11.2 %collective-permute-done.52 = bf16[144,1024]{1,0:T(8,128)(2,1)S(1)} collective-permute-done((bf16[144,1024]{1,0:T(8,128)(2,1)S(1)}, bf16[144,1024]{1,0:T(8,128)(2,1)S(1)}, u32[]{:S(2)}, u32[]{:S(2)}) %collective-permute-start.52) | collective-permute-done | bytes 294944 | tf_op jit(solution)/shard_map/ppermute | solution.py:177
  774.6 25.1 %collective-permute-done.56 = f32[4,4,144]{2,0,1:T(4,128)S(1)} collective-permute-done((f32[4,4,144]{2,0,1:T(4,128)S(1)}, f32[4,4,144]{2,0,1:T(4,128)S(1)}, u32[]{:S(2)}, u32[]{:S(2)}) %collective-permute-start.56) | collective-permute-done | bytes 9248 | tf_op jit(solution)/shard_map/ppermute | solution.py:177
  806.1 9.1 %collective-permute-done.61 = bf16[144,2048]{1,0:T(8,128)(2,1)S(1)} collective-permute-done((bf16[144,2048]{1,0:T(8,128)(2,1)S(1)}, bf16[144,2048]{1,0:T(8,128)(2,1)S(1)}, u32[]{:S(2)}, u32[]{:S(2)}) %collective-permute-start.61) | collective-permute-done | bytes 589856 | tf_op jit(solution)/shard_map/ppermute | solution.py:177
  824.1 20.5 %collective-permute-done.65.refs_1_ = bf16[144,1152]{1,0:T(8,128)(2,1)S(1)} collective-permute-done((bf16[144,1152]{1,0:T(8,128)(2,1)S(1)}, bf16[144,1152]{1,0:T(8,128)(2,1)S(1)}, u32[]{:S(2)}, u32[]{:S(2)}) %collective-permute-start.65) | collective-permute-done | bytes 331808 | tf_op jit(solution)/shard_map/ppermute | solution.py:177
  (486 shorter events, 297.2 us)
Async XLA Ops:
  7.2 173.9 %all-gather.4.cloned.1.call-start = ((), (), s32[]{:S(2)}) async-start(), calls=%async_computation.2 | async-start | bytes 10027008 | tf_op jit(solution)/shard_map/all_gather | solution.py:757
  13.6 204.2 %all-gather.6.cloned.1.call-start = ((), (), s32[]{:S(2)}) async-start(), calls=%async_computation.3 | async-start | bytes 5013504 | tf_op jit(solution)/shard_map/all_gather | solution.py:758
  14.3 293.5 %all-gather.8.cloned.1.call-start = ((), (), s32[]{:S(2)}) async-start(), calls=%async_computation.4 | async-start | bytes 11943936 | tf_op jit(solution)/shard_map/all_gather | solution.py:621
  18.5 47.9 %collective-permute-start.2 = (bf16[144,1152]{1,0:T(8,128)(2,1)}, bf16[144,1152]{1,0:T(8,128)(2,1)S(1)}, u32[]{:S(2)}, u32[]{:S(2)}) collective-permute-start(bf16[144,1152]{1,0:T(8,128)(2,1)} %get-tuple-element.403), channel_id=1, source_target_pairs={{0,24},{8,16},{16,8},{24,0},{1,25},{9,17},{17,9},{25,1},{2,26},{10... | collective-permute-start | bytes 995336 | tf_op jit(solution)/shard_map/ppermute | solution.py:177
  24.3 42.1 %collective-permute-start.3 = (bf16[128,2304]{1,0:T(8,128)(2,1)S(1)}, bf16[128,2304]{1,0:T(8,128)(2,1)S(1)}, u32[]{:S(2)}, u32[]{:S(2)}) collective-permute-start(bf16[128,2304]{1,0:T(8,128)(2,1)S(1)} %multiply_convert_fusion.3), channel_id=1, source_target_pairs={{0,1},{1,0},{2,3},{3,2},{4,5},{5,4},{6,7},{7,6},{8,9},{9,8},{10,11... | collective-permute-start | bytes 1769480 | tf_op jit(solution)/shard_map/ppermute | solution.py:177
  68.0 64.3 %collective-permute-start.4 = (bf16[576,1152]{1,0:T(8,128)(2,1)S(1)}, bf16[576,1152]{1,0:T(8,128)(2,1)}, u32[]{:S(2)}, u32[]{:S(2)}) collective-permute-start(bf16[576,1152]{1,0:T(8,128)(2,1)S(1)} %shard_map.246.refs_0_), channel_id=1, source_target_pairs={{0,1},{1,0},{2,3},{3,2},{4,5},{5,4},{6,7},{7,6},{8,9},{9,8},{10,11... | collective-permute-start | bytes 3981320 | tf_op jit(solution)/shard_map/ppermute | solution.py:177
  69.6 62.7 %collective-permute-start.5 = (bf16[576,1152]{1,0:T(8,128)(2,1)S(1)}, bf16[576,1152]{1,0:T(8,128)(2,1)}, u32[]{:S(2)}, u32[]{:S(2)}) collective-permute-start(bf16[576,1152]{1,0:T(8,128)(2,1)S(1)} %shard_map.246.refs_0_), channel_id=1, source_target_pairs={{0,4},{4,0},{1,5},{5,1},{2,6},{6,2},{3,7},{7,3},{8,12},{12,8},{9,1... | collective-permute-start | bytes 3981320 | tf_op jit(solution)/shard_map/ppermute | solution.py:177
  71.1 39.6 %collective-permute-start.7 = (bf16[144,1152]{1,0:T(8,128)(2,1)}, bf16[144,1152]{1,0:T(8,128)(2,1)S(1)}, u32[]{:S(2)}, u32[]{:S(2)}) collective-permute-start(bf16[144,1152]{1,0:T(8,128)(2,1)} %get-tuple-element.178), channel_id=1, source_target_pairs={{0,16},{8,24},{16,0},{24,8},{1,17},{9,25},{17,1},{25,9},{2,18},{10... | collective-permute-start | bytes 995336 | tf_op jit(solution)/shard_map/ppermute | solution.py:177
  74.4 57.8 %collective-permute-start.8 = (bf16[144,1152]{1,0:T(8,128)(2,1)}, bf16[144,1152]{1,0:T(8,128)(2,1)S(1)}, u32[]{:S(2)}, u32[]{:S(2)}) collective-permute-start(bf16[144,1152]{1,0:T(8,128)(2,1)} %get-tuple-element.179), channel_id=1, source_target_pairs={{0,24},{8,16},{16,8},{24,0},{1,25},{9,17},{17,9},{25,1},{2,26},{10... | collective-permute-start | bytes 995336 | tf_op jit(solution)/shard_map/ppermute | solution.py:177
  133.1 47.0 %collective-permute-start.14 = (bf16[576,1152]{1,0:T(8,128)(2,1)S(1)}, bf16[576,1152]{1,0:T(8,128)(2,1)S(1)}, u32[]{:S(2)}, u32[]{:S(2)}) collective-permute-start(bf16[576,1152]{1,0:T(8,128)(2,1)S(1)} %shard_map.247.refs_0_), channel_id=1, source_target_pairs={{0,1},{1,0},{2,3},{3,2},{4,5},{5,4},{6,7},{7,6},{8,9},{9,8},{10,11... | collective-permute-start | bytes 3981320 | tf_op jit(solution)/shard_map/ppermute | solution.py:177
  133.3 47.8 %collective-permute-start.15 = (bf16[576,1152]{1,0:T(8,128)(2,1)S(1)}, bf16[576,1152]{1,0:T(8,128)(2,1)}, u32[]{:S(2)}, u32[]{:S(2)}) collective-permute-start(bf16[576,1152]{1,0:T(8,128)(2,1)S(1)} %shard_map.247.refs_0_), channel_id=1, source_target_pairs={{0,4},{4,0},{1,5},{5,1},{2,6},{6,2},{3,7},{7,3},{8,12},{12,8},{9,1... | collective-permute-start | bytes 3981320 | tf_op jit(solution)/shard_map/ppermute | solution.py:177
  138.9 40.3 %collective-permute-start.12 = (bf16[288,1152]{1,0:T(8,128)(2,1)S(1)}, bf16[288,1152]{1,0:T(8,128)(2,1)S(1)}, u32[]{:S(2)}, u32[]{:S(2)}) collective-permute-start(bf16[288,1152]{1,0:T(8,128)(2,1)S(1)} %slice.78), channel_id=1, source_target_pairs={{0,1},{1,0},{2,3},{3,2},{4,5},{5,4},{6,7},{7,6},{8,9},{9,8},{10,11... | collective-permute-start | bytes 1990664 | tf_op jit(solution)/shard_map/ppermute | solution.py:177
  186.3 442.0 %reduce-scatter.3.cloned.1.call-start = ((), (), s32[]{:S(2)}) async-start(), calls=%async_computation.5 | async-start | bytes 11943936 | tf_op jit(solution)/shard_map/reduce_scatter | solution.py:617
  254.1 41.5 %collective-permute-start.23 = (bf16[128,2304]{1,0:T(8,128)(2,1)S(1)}, bf16[128,2304]{1,0:T(8,128)(2,1)S(1)}, u32[]{:S(2)}, u32[]{:S(2)}) collective-permute-start(bf16[128,2304]{1,0:T(8,128)(2,1)S(1)} %multiply_convert_fusion.2), channel_id=1, source_target_pairs={{0,24},{8,16},{16,8},{24,0},{1,25},{9,17},{17,9},{25,1},{2,26},{10... | collective-permute-start | bytes 1769480 | tf_op jit(solution)/shard_map/ppermute | solution.py:177
  255.6 50.6 %collective-permute-start.22 = (bf16[128,2304]{1,0:T(8,128)(2,1)S(1)}, bf16[128,2304]{1,0:T(8,128)(2,1)S(1)}, u32[]{:S(2)}, u32[]{:S(2)}) collective-permute-start(bf16[128,2304]{1,0:T(8,128)(2,1)S(1)} %multiply_convert_fusion.2), channel_id=1, source_target_pairs={{0,16},{8,24},{16,0},{24,8},{1,17},{9,25},{17,1},{25,9},{2,18},{10... | collective-permute-start | bytes 1769480 | tf_op jit(solution)/shard_map/ppermute | solution.py:177
  257.1 49.2 %collective-permute-start.21 = (bf16[128,2304]{1,0:T(8,128)(2,1)S(1)}, bf16[128,2304]{1,0:T(8,128)(2,1)S(1)}, u32[]{:S(2)}, u32[]{:S(2)}) collective-permute-start(bf16[128,2304]{1,0:T(8,128)(2,1)S(1)} %multiply_convert_fusion.2), channel_id=1, source_target_pairs={{0,8},{8,0},{16,24},{24,16},{1,9},{9,1},{17,25},{25,17},{2,10},{10... | collective-permute-start | bytes 1769480 | tf_op jit(solution)/shard_map/ppermute | solution.py:177
  343.2 40.4 %collective-permute-start.25 = (bf16[128,2304]{1,0:T(8,128)(2,1)}, bf16[128,2304]{1,0:T(8,128)(2,1)}, u32[]{:S(2)}, u32[]{:S(2)}) collective-permute-start(bf16[128,2304]{1,0:T(8,128)(2,1)} %get-tuple-element.240), channel_id=1, source_target_pairs={{0,16},{8,24},{16,0},{24,8},{1,17},{9,25},{17,1},{25,9},{2,18},{10... | collective-permute-start | bytes 1769480 | tf_op jit(solution)/shard_map/ppermute | solution.py:177
  344.2 63.8 %collective-permute-start.26 = (bf16[128,2304]{1,0:T(8,128)(2,1)}, bf16[128,2304]{1,0:T(8,128)(2,1)}, u32[]{:S(2)}, u32[]{:S(2)}) collective-permute-start(bf16[128,2304]{1,0:T(8,128)(2,1)} %get-tuple-element.241), channel_id=1, source_target_pairs={{0,24},{8,16},{16,8},{24,0},{1,25},{9,17},{17,9},{25,1},{2,26},{10... | collective-permute-start | bytes 1769480 | tf_op jit(solution)/shard_map/ppermute | solution.py:177
  462.1 356.0 %reduce-scatter.5.cloned.1.call-start = ((), (), s32[]{:S(2)}) async-start(), calls=%async_computation.6 | async-start | bytes 11943936 | tf_op jit(solution)/shard_map/reduce_scatter | solution.py:617
  524.5 57.5 %collective-permute-start.31 = (bf16[288,1152]{1,0:T(8,128)(2,1)}, bf16[288,1152]{1,0:T(8,128)(2,1)}, u32[]{:S(2)}, u32[]{:S(2)}) collective-permute-start(bf16[288,1152]{1,0:T(8,128)(2,1)} %get-tuple-element.373), channel_id=1, source_target_pairs={{0,1},{1,0},{2,3},{3,2},{4,5},{5,4},{6,7},{7,6},{8,9},{9,8},{10,11... | collective-permute-start | bytes 1990664 | tf_op jit(solution)/shard_map/ppermute | solution.py:177
  525.0 56.9 %collective-permute-start.32 = (bf16[288,1152]{1,0:T(8,128)(2,1)}, bf16[288,1152]{1,0:T(8,128)(2,1)}, u32[]{:S(2)}, u32[]{:S(2)}) collective-permute-start(bf16[288,1152]{1,0:T(8,128)(2,1)} %get-tuple-element.372), channel_id=1, source_target_pairs={{0,4},{4,0},{1,5},{5,1},{2,6},{6,2},{3,7},{7,3},{8,12},{12,8},{9,1... | collective-permute-start | bytes 1990664 | tf_op jit(solution)/shard_map/ppermute | solution.py:177
  529.1 40.1 %collective-permute-start.34 = (bf16[128,2304]{1,0:T(8,128)(2,1)}, bf16[128,2304]{1,0:T(8,128)(2,1)}, u32[]{:S(2)}, u32[]{:S(2)}) collective-permute-start(bf16[128,2304]{1,0:T(8,128)(2,1)} %get-tuple-element.255), channel_id=1, source_target_pairs={{0,16},{8,24},{16,0},{24,8},{1,17},{9,25},{17,1},{25,9},{2,18},{10... | collective-permute-start | bytes 1769480 | tf_op jit(solution)/shard_map/ppermute | solution.py:177
  529.8 52.1 %collective-permute-start.35 = (bf16[128,2304]{1,0:T(8,128)(2,1)}, bf16[128,2304]{1,0:T(8,128)(2,1)}, u32[]{:S(2)}, u32[]{:S(2)}) collective-permute-start(bf16[128,2304]{1,0:T(8,128)(2,1)} %get-tuple-element.256), channel_id=1, source_target_pairs={{0,24},{8,16},{16,8},{24,0},{1,25},{9,17},{17,9},{25,1},{2,26},{10... | collective-permute-start | bytes 1769480 | tf_op jit(solution)/shard_map/ppermute | solution.py:177
  617.7 59.4 %collective-permute-start.41 = (bf16[576,1152]{1,0:T(8,128)(2,1)}, bf16[576,1152]{1,0:T(8,128)(2,1)}, u32[]{:S(2)}, u32[]{:S(2)}) collective-permute-start(bf16[576,1152]{1,0:T(8,128)(2,1)} %pad_maximum_fusion.2), channel_id=1, source_target_pairs={{0,1},{1,0},{2,3},{3,2},{4,5},{5,4},{6,7},{7,6},{8,9},{9,8},{10,11... | collective-permute-start | bytes 3981320 | tf_op jit(solution)/shard_map/ppermute | solution.py:177
  627.9 49.2 %collective-permute-start.43 = (bf16[576,1024]{1,0:T(8,128)(2,1)}, bf16[576,1024]{1,0:T(8,128)(2,1)}, u32[]{:S(2)}, u32[]{:S(2)}) collective-permute-start(bf16[576,1024]{1,0:T(8,128)(2,1)} %get-tuple-element.385), channel_id=1, source_target_pairs={{0,4},{4,0},{1,5},{5,1},{2,6},{6,2},{3,7},{7,3},{8,12},{12,8},{9,1... | collective-permute-start | bytes 3538952 | tf_op jit(solution)/shard_map/ppermute | solution.py:177
  629.8 47.2 %collective-permute-start.38 = (bf16[144,1152]{1,0:T(8,128)(2,1)S(1)}, bf16[144,1152]{1,0:T(8,128)(2,1)S(1)}, u32[]{:S(2)}, u32[]{:S(2)}) collective-permute-start(bf16[144,1152]{1,0:T(8,128)(2,1)S(1)} %get-tuple-element.397), channel_id=1, source_target_pairs={{0,8},{8,0},{16,24},{24,16},{1,9},{9,1},{17,25},{25,17},{2,10},{10... | collective-permute-start | bytes 995336 | tf_op jit(solution)/shard_map/ppermute | solution.py:177
  629.9 47.2 %collective-permute-start.39 = (bf16[144,1152]{1,0:T(8,128)(2,1)S(1)}, bf16[144,1152]{1,0:T(8,128)(2,1)S(1)}, u32[]{:S(2)}, u32[]{:S(2)}) collective-permute-start(bf16[144,1152]{1,0:T(8,128)(2,1)S(1)} %get-tuple-element.396), channel_id=1, source_target_pairs={{0,16},{8,24},{16,0},{24,8},{1,17},{9,25},{17,1},{25,9},{2,18},{10... | collective-permute-start | bytes 995336 | tf_op jit(solution)/shard_map/ppermute | solution.py:177
  632.0 45.1 %collective-permute-start.40 = (bf16[144,1152]{1,0:T(8,128)(2,1)S(1)}, bf16[144,1152]{1,0:T(8,128)(2,1)S(1)}, u32[]{:S(2)}, u32[]{:S(2)}) collective-permute-start(bf16[144,1152]{1,0:T(8,128)(2,1)S(1)} %get-tuple-element.395), channel_id=1, source_target_pairs={{0,24},{8,16},{16,8},{24,0},{1,25},{9,17},{17,9},{25,1},{2,26},{10... | collective-permute-start | bytes 995336 | tf_op jit(solution)/shard_map/ppermute | solution.py:177
  724.1 39.4 %collective-permute-start.49 = (bf16[144,2048]{1,0:T(8,128)(2,1)}, bf16[144,2048]{1,0:T(8,128)(2,1)}, u32[]{:S(2)}, u32[]{:S(2)}) collective-permute-start(bf16[144,2048]{1,0:T(8,128)(2,1)} %get-tuple-element.384), channel_id=1, source_target_pairs={{0,4},{4,0},{1,5},{5,1},{2,6},{6,2},{3,7},{7,3},{8,12},{12,8},{9,1... | collective-permute-start | bytes 1769480 | tf_op jit(solution)/shard_map/ppermute | solution.py:177
  770.9 44.4 %collective-permute-start.61 = (bf16[144,2048]{1,0:T(8,128)(2,1)S(1)}, bf16[144,2048]{1,0:T(8,128)(2,1)S(1)}, u32[]{:S(2)}, u32[]{:S(2)}) collective-permute-start(bf16[144,2048]{1,0:T(8,128)(2,1)S(1)} %add_convert_fusion.6), channel_id=1, source_target_pairs={{0,24},{8,16},{16,8},{24,0},{1,25},{9,17},{17,9},{25,1},{2,26},{10... | collective-permute-start | bytes 1769480 | tf_op jit(solution)/shard_map/ppermute | solution.py:177
  770.9 44.3 %collective-permute-start.62 = (bf16[144,2048]{1,0:T(8,128)(2,1)S(1)}, bf16[144,2048]{1,0:T(8,128)(2,1)S(1)}, u32[]{:S(2)}, u32[]{:S(2)}) collective-permute-start(bf16[144,2048]{1,0:T(8,128)(2,1)S(1)} %copy-done.69), channel_id=1, source_target_pairs={{0,4},{4,0},{1,5},{5,1},{2,6},{6,2},{3,7},{7,3},{8,12},{12,8},{9,1... | collective-permute-start | bytes 1769480 | tf_op jit(solution)/shard_map/ppermute | solution.py:177
  771.4 44.6 %collective-permute-start.63 = (bf16[144,2048]{1,0:T(8,128)(2,1)S(1)}, bf16[144,2048]{1,0:T(8,128)(2,1)S(1)}, u32[]{:S(2)}, u32[]{:S(2)}) collective-permute-start(bf16[144,2048]{1,0:T(8,128)(2,1)S(1)} %copy-done.68), channel_id=1, source_target_pairs={{0,4},{4,0},{1,5},{5,1},{2,6},{6,2},{3,7},{7,3},{8,12},{12,8},{9,1... | collective-permute-start | bytes 1769480 | tf_op jit(solution)/shard_map/ppermute | solution.py:177
  (149 other events, 1915.5 us)
Sparse Core Ops, SparseCore 0:
  13.7 129.8 all-gather.3
  145.9 65.0 all-gather.5
  213.4 74.5 all-gather.7
  462.2 95.6 reduce-scatter.2
  592.0 121.1 reduce-scatter.4

commit v5 on v4

--- a/solution.py
+++ b/solution.py
@@ -70,8 +70,13 @@
     return lax.dot_general(left, right, (((1,), (1,)), ((), ())), preferred_element_type=F32)
 
 
-def spill(total, outs):
-    rows = outs[0].shape[0]
+def spill(ids, total, outs):
+    rows = total.shape[0] // 4
+    if len(outs) == 1:
+        for k in range(4):
+            at = pl.multiple_of((ids[0] ^ k) * rows, rows)
+            outs[0][pl.ds(at, rows), :] = total[k * rows : (k + 1) * rows, :].astype(BF)
+        return
     for k, out in enumerate(outs):
         out[...] = total[k * rows : (k + 1) * rows, :].astype(out.dtype)
 
@@ -125,12 +130,12 @@
 
     @pl.when(pl.program_id(0) == pl.num_programs(0) - 1)
     def _():
-        spill(total, outs)
+        spill(ids, total, outs)
 
 
 def backward_kernel(columns, ids, d, *refs):
     gate_w, up_w, down_w, (gate, up), (d_gate, d_up), outs, total = (
-        refs[:2], refs[2:4], refs[4:6], refs[6:8], refs[8:10], refs[10:14], refs[14]
+        refs[:2], refs[2:4], refs[4:6], refs[6:8], refs[8:10], refs[10:-1], refs[-1]
     )
     gate_at, up_at, down_at = (find(ids) for find in columns)
     d_act = inner(d, down_w, down_at)
@@ -143,15 +148,16 @@
 
     @pl.when(pl.program_id(0) == pl.num_programs(0) - 1)
     def _():
-        spill(total, outs)
-
-
-def ffn_call(kernel, ids, values, weights, kept, made, tile):
+        spill(ids, total, outs)
+
+
+def ffn_call(kernel, ids, values, weights, kept, made, tile, natural):
     tokens, width = values.shape
     hidden = 2 * weights[-1].arrays[0].shape[-1] if weights[-1].whole else weights[-1].arrays[0].shape[-1]
     slot = tokens // 4
     across = pl.BlockSpec((tokens, tile), lambda i, ids: (0, i))
-    whole = pl.BlockSpec((slot, width), lambda i, ids: (0, 0))
+    parts = [(tokens, BF)] if natural else [(slot, F32)] + [(slot, BF)] * 3
+    whole = [pl.BlockSpec((rows, width), lambda i, ids: (0, 0)) for rows, _ in parts]
     return pl.pallas_call(
         functools.partial(kernel, [weight.columns for weight in weights]),
         grid_spec=pltpu.PrefetchScalarGridSpec(
@@ -160,11 +166,11 @@
             in_specs=[pl.BlockSpec((tokens, width), lambda i, ids: (0, 0))]
             + [spec for weight in weights for spec in weight.specs(tile)]
             + [across] * len(kept),
-            out_specs=[across] * len(made) + [whole] * 4,
+            out_specs=[across] * len(made) + whole,
             scratch_shapes=[pltpu.VMEM((tokens, width), F32)],
         ),
         out_shape=[jax.ShapeDtypeStruct((tokens, hidden), kind) for kind in made]
-        + [jax.ShapeDtypeStruct((slot, width), kind) for kind in (F32, BF, BF, BF)],
+        + [jax.ShapeDtypeStruct((rows, width), kind) for rows, kind in parts],
         compiler_params=pltpu.CompilerParams(
             dimension_semantics=("arbitrary",), vmem_limit_bytes=58 * 2**20
         ),
@@ -233,13 +239,16 @@
 
 
 def line_gather(values):
-    return jnp.concatenate([values] + [swap(values, "z", k) for k in (1, 2, 3)], axis=0)
-
-
-def line_parts(partial):
-    rows = partial.shape[0] // 4
-    parts = [partial[k * rows : (k + 1) * rows] for k in range(4)]
-    return [parts[0]] + [part.astype(BF) for part in parts[1:]]
+    near, far = swap(values, "z", 1), swap(values, "z", 2)
+    return jnp.concatenate([values, near, far, swap(far, "z", 1)], axis=0)
+
+
+def line_sum_first(parts):
+    return [*parts[:3], swap(parts[3], "z", 1)]
+
+
+def line_sum_second(parts):
+    return [parts[0], swap(parts[1], "z", 1), swap(add_low(parts[2], parts[3]), "z", 2)]
 
 
 def line_place(pieces):
@@ -582,39 +591,50 @@
     )(which, left, right, *got)
 
 
-def outer_halves_kernel(left, right, made, flipped):
-    @pl.when(pl.program_id(0) == 0)
+def outer_halves_kernel(number, which, left, *refs):
+    rights, got, (made, flipped) = refs[:number], refs[number:-2], refs[-2:]
+    step = pl.program_id(0)
+
+    @pl.when(step == 0)
     def _():
         flipped[...] = left[...].T
 
-    made[...] = tile_dot(flipped[...], right[...]).astype(BF)
-
-
-def outer_halves(left, right):
-    tokens, width = left.shape
-    cols = right.shape[1] // 2
-    tile = 384
-    count = cols // tile
+    for k, right in enumerate(rights):
+
+        @pl.when(step % number == k)
+        def _(right=right):
+            total = tile_dot(flipped[...], right[...])
+            for piece in got:
+                total = total + piece[...].astype(F32)
+            made[...] = total.astype(BF)
+
+
+def outer_halves(which, left, rights, *got):
+    tokens, cut = left.shape[0], left.shape[1] // 2
+    cols, number = rights[0].shape[1] // 2, len(rights)
+    across = pl.BlockSpec((None, cut, cols), lambda i, which: (i // number, 0, i % number))
     return pl.pallas_call(
-        outer_halves_kernel,
-        grid=(2 * count,),
-        in_specs=[
-            pl.BlockSpec((tokens, width), lambda i: (0, 0)),
-            pl.BlockSpec((tokens, tile), lambda i: (0, i)),
-        ],
-        out_specs=pl.BlockSpec((None, width, tile), lambda i: (i // count, 0, i % count)),
-        out_shape=jax.ShapeDtypeStruct((2, width, cols), BF),
-        scratch_shapes=[pltpu.VMEM((width, tokens), BF)],
+        functools.partial(outer_halves_kernel, number),
+        grid_spec=pltpu.PrefetchScalarGridSpec(
+            num_scalar_prefetch=1,
+            grid=(2 * number,),
+            in_specs=[pl.BlockSpec((tokens, cut), lambda i, which: (0, which[0]))]
+            + [pl.BlockSpec((tokens, cols), lambda i, which: (0, i // number))] * number
+            + [across] * len(got),
+            out_specs=across,
+            scratch_shapes=[pltpu.VMEM((cut, tokens), BF)],
+        ),
+        out_shape=jax.ShapeDtypeStruct((2, cut, number * cols), BF),
         compiler_params=kernel_params(),
         cost_estimate=LIGHT,
-    )(left, right)
+    )(which, left, *rights, *got)
 
 
 def sum_cut(grad):
-    width, cols = grad.shape[1:]
-    blocks = 2 * lax.axis_size("c") * lax.axis_size("y")
-    grad = grad.reshape(blocks, 2 * width // blocks, cols)
-    return lax.psum_scatter(grad, ("x", "c", "y"), scatter_dimension=0, tiled=True)[0]
+    half, cols = grad.shape[1:]
+    blocks = 2 * lax.axis_size("y")
+    grad = grad.reshape(blocks, 2 * half // blocks, cols)
+    return lax.psum_scatter(grad, ("x", "y"), scatter_dimension=0, tiled=True)[0]
 
 
 def gather_cut(own):
@@ -625,6 +645,128 @@
 def outer_low(left, right, mine, theirs):
     sent = outer_call(left, right, theirs)
     return outer_call(left, right, mine, swap(sent, "c", 1))
+
+
+def outer_quarters_kernel(ids, which, left, right, *refs):
+    (plain, flipped), refs = refs[-2:], refs[:-2]
+    got, outs = (refs[:4], refs[4:]) if len(refs) > 1 else ((), refs)
+    step, rows = pl.program_id(0), flipped.shape[0] // 2
+
+    @pl.when(step == 0)
+    def _():
+        plain[...] = left[...].T
+        for k, side in enumerate((ids[1], 1 - ids[1])):
+            at = pl.multiple_of(side * rows, rows)
+            flipped[k * rows : (k + 1) * rows, :] = plain[pl.ds(at, rows), :]
+
+    for half in range(2):
+
+        @pl.when(step == half)
+        def _(half=half):
+            for side in range(2):
+                k = half + 2 * side
+                total = tile_dot(flipped[side * rows : (side + 1) * rows, :], right[...])
+                if got:
+                    outs[k][...] = (total + got[k][...].astype(F32)).astype(BF)
+                else:
+                    outs[0][side] = total.astype(BF)
+
+
+def outer_quarters(ids, which, left, right, *got):
+    tokens, cut, cols = left.shape[0], left.shape[1] // 2, right.shape[1] // 2
+    rows = cut // 2
+    quarter = pl.BlockSpec((rows, cols), lambda i, ids, which: (0, 0))
+    taken = [
+        pl.BlockSpec((None, rows, cols), lambda i, ids, which, k=k: (k // 2, 0, k % 2))
+        for k in range(4)
+    ]
+    shape = jax.ShapeDtypeStruct((rows, cols), BF)
+    return pl.pallas_call(
+        outer_quarters_kernel,
+        grid_spec=pltpu.PrefetchScalarGridSpec(
+            num_scalar_prefetch=2,
+            grid=(2,),
+            in_specs=[
+                pl.BlockSpec((tokens, cut), lambda i, ids, which: (0, which[0])),
+                pl.BlockSpec((tokens, cols), lambda i, ids, which: (0, ids[3] ^ i)),
+            ]
+            + (taken if got else []),
+            out_specs=[quarter] * 4
+            if got
+            else pl.BlockSpec((2, rows, cols), lambda i, ids, which: (0, 0, i)),
+            scratch_shapes=[pltpu.VMEM((cut, tokens), BF)] * 2,
+        ),
+        out_shape=[shape] * 4 if got else jax.ShapeDtypeStruct((2, rows, 2 * cols), BF),
+        compiler_params=kernel_params(),
+        cost_estimate=LIGHT,
+    )(ids, which, left, right, *got * 4)
+
+
+def outer_rows_kernel(ids, which, left_a, left_b, right_a, right_b, *refs):
+    (plain, flipped), refs = refs[-2:], refs[:-2]
+    got, outs = (refs[:4], refs[4:]) if len(refs) > 1 else ((), refs)
+    step, last = pl.program_id(0), pl.num_programs(0) - 1
+    rows = flipped.shape[0] // 8
+    z, y = ids[0], ids[1]
+    order = [4 * side + (z ^ k) for side in (1 - y, y) for k in (1, 3, 0, 2)]
+    for left, when in ((left_a, 0), (left_b, last)):
+
+        @pl.when(step == when)
+        def _(left=left):
+            plain[...] = left[...].T
+            for k, block in enumerate(order):
+                at = pl.multiple_of(block * rows, rows)
+                flipped[k * rows : (k + 1) * rows, :] = plain[pl.ds(at, rows), :]
+
+    def give(right):
+        total = tile_dot(flipped[...], right[...])
+        if not got:
+            outs[0][...] = total.astype(BF)
+        for k, piece in enumerate(got):
+            part = total[2 * k * rows : (2 * k + 2) * rows, :]
+            outs[k][...] = (part + piece[...].astype(F32)).astype(BF)
+
+    @pl.when(step < last)
+    def _():
+        give(right_a)
+
+    @pl.when(step == last)
+    def _():
+        give(right_b)
+
+
+def outer_rows(ids, which, left_a, right_a, left_b, right_b, *got):
+    tokens, cut = left_a.shape[0], left_a.shape[1] // 2
+    tile = right_b.shape[1]
+    cols = right_a.shape[1] + tile
+    rows = cut // 4
+    count = cols // tile
+    half = pl.BlockSpec((tokens, cut), lambda i, ids, which: (0, which[0]))
+    across = pl.BlockSpec((rows, tile), lambda i, ids, which: (0, i))
+    taken = [pl.BlockSpec((rows, tile), lambda i, ids, which, k=k: (k, i)) for k in range(4)]
+    return pl.pallas_call(
+        outer_rows_kernel,
+        grid_spec=pltpu.PrefetchScalarGridSpec(
+            num_scalar_prefetch=2,
+            grid=(count,),
+            in_specs=[
+                half,
+                half,
+                pl.BlockSpec((tokens, tile), lambda i, ids, which: (0, jnp.minimum(i, count - 2))),
+                pl.BlockSpec((tokens, tile), lambda i, ids, which: (0, 0)),
+            ]
+            + (taken if got else []),
+            out_specs=[across] * 4
+            if got
+            else pl.BlockSpec((cut, tile), lambda i, ids, which: (0, i)),
+            scratch_shapes=[pltpu.VMEM((cut, tokens), BF)] * 2,
+        ),
+        out_shape=[jax.ShapeDtypeStruct((rows, cols), BF)] * 4
+        if got
+        else jax.ShapeDtypeStruct((cut, cols), BF),
+        compiler_params=kernel_params(),
+        cost_estimate=LIGHT,
+    )(ids, which, left_a, left_b, right_a, right_b, *got * 4)
 
 
 def assemble_kernel(counts, rows, cols, *refs):
@@ -667,27 +809,25 @@
 
 def gain_sum(parts):
     count, width = parts.shape
-    blocks = lax.axis_size("c") * lax.axis_size("y") * lax.axis_size("z")
-    parts = parts.reshape(count, blocks, width // blocks).transpose(1, 0, 2)
+    c_size, y_size, z_size = (lax.axis_size(axis) for axis in ("c", "y", "z"))
     parts = parts + swap(parts, "x", 1)
-    here, rows = lax.axis_index("c"), blocks // 2
-    parts = lax.dynamic_slice_in_dim(parts, here * rows, rows, 0) + swap(
-        lax.dynamic_slice_in_dim(parts, (1 - here) * rows, rows, 0), "c", 1
-    )
-    if lax.axis_size("y") == 2:
-        here, rows = lax.axis_index("y"), blocks // 4
-        parts = lax.dynamic_slice_in_dim(parts, here * rows, rows, 0) + swap(
-            lax.dynamic_slice_in_dim(parts, (1 - here) * rows, rows, 0), "y", 1
-        )
-    else:
-        parts = lax.psum_scatter(parts, "y", scatter_dimension=0, tiled=True)
+    parts = parts.reshape(count, c_size, y_size, z_size, -1).transpose(3, 1, 2, 0, 4)
     here = lax.axis_index("z")
     total = lax.dynamic_index_in_dim(parts, here, 0, keepdims=False)
     for k in (1, 2, 3):
-        total = total + swap(
-            lax.dynamic_index_in_dim(parts, here ^ k, 0, keepdims=False), "z", k
-        )
-    return total
+        piece = lax.dynamic_index_in_dim(parts, here ^ k, 0, keepdims=False)
+        total = total + swap(piece, "z", k)
+    here = lax.axis_index("c")
+    sent = lax.dynamic_index_in_dim(total, 1 - here, 0, keepdims=False)
+    return lax.dynamic_index_in_dim(total, here, 0, keepdims=False) + swap(sent, "c", 1)
+
+
+def sum_over_y(parts):
+    if lax.axis_size("y") != 2:
+        return lax.psum_scatter(parts, "y", scatter_dimension=0, tiled=True)[0]
+    here = lax.axis_index("y")
+    sent = lax.dynamic_index_in_dim(parts, 1 - here, 0, keepdims=False)
+    return lax.dynamic_index_in_dim(parts, here, 0, keepdims=False) + swap(sent, "y", 1)
 
 
 def on_device(
@@ -806,9 +946,9 @@
     normed_two = live["normed_two"]
 
     live["act"], gate_proj, up_proj, *sums = ffn_call(
-        forward_kernel, ids, normed_two, weights, (), (BF, F32, F32), 384
-    )
-    live["sums"] = line_swaps(sums)
+        forward_kernel, ids, normed_two, weights, (), (BF, F32, F32), 384, False
+    )
+    live["sums"] = line_sum_second(line_sum_first(sums))
     live = close(live)
     ffn_out = line_total(live["sums"])
     inverse_four = lax.rsqrt(jnp.mean(ffn_out * ffn_out, axis=-1, keepdims=True) + NORM_EPS)
@@ -819,22 +959,30 @@
     live["d_ffn"] = line_gather(d_ffn)
     live = close(live)
     d_ffn, act, normed_two = live["d_ffn"], live["act"], live["normed_two"]
-    grad_down = sum_cut(outer_halves(d_ffn, act))
+    def product(left, right, *got):
+        which = core_here if got else core_there
+        if pairs:
+            return outer_quarters(ids, which, left, right, *got)
+        made = outer_halves(which, left, (right,), *got)
+        return [made] if got else made
+
+    live = {"down": swap(product(d_ffn, act), "c", 1), "d_ffn": d_ffn, "act": act}
     d_gate, d_up, *sums = ffn_call(
-        backward_kernel, ids, d_ffn, weights, (gate_proj, up_proj), (BF, BF), 384
-    )
-    live = close({"d_gate": d_gate, "d_up": d_up, "sums": sums})
-
-    live["sums"] = line_swaps(live["sums"])
+        backward_kernel, ids, d_ffn, weights, (gate_proj, up_proj), (BF, BF), 384, False
+    )
+    live = close(live | {"d_gate": d_gate, "d_up": d_up, "sums": sums})
+
+    live["sums"] = line_sum_first(live["sums"])
+    live["down"] = product(live["d_ffn"], live["act"], live["down"])
+    d_gate, d_up = live["d_gate"], live["d_up"]
+    live |= {"up": product(normed_two, d_up), "gate": product(normed_two, d_gate)}
+    live = close({k: live[k] for k in ("sums", "down", "up", "gate", "d_gate", "d_up")})
+    live["sums"] = line_sum_second(live["sums"])
     if pairs:
-        gate = fold_parts(outer_low(normed_two, live["d_gate"], core_here, core_there))
-        live["gate_got"] = fold_first(gate.pop("across"))
-        live["gate"] = gate
-    else:
-        live["gate"] = outer_halves(normed_two, live["d_gate"])
-    live["up"] = outer_halves(normed_two, live["d_up"])
-    live = close({k: live[k] for k in ("sums", "up", "gate", "gate_got") if k in live})
-    grad_up = sum_cut(live.pop("up"))
+        *quarters, across = live["down"]
+        live["down"] = [*quarters, *fold_first(across)]
+    live["up"] = product(normed_two, live["d_up"], swap(live["up"], "c", 1))
+    live = close({k: live[k] for k in ("sums", "down", "up", "gate", "d_gate")})
 
     d_normed_two = line_total(live["sums"])
     gain_three = jnp.sum(d_normed_two * unit_three, axis=0)
@@ -842,67 +990,83 @@
     gain_two = jnp.sum(d_hidden * unit_two, axis=0)
     d_branch = norm_back(d_hidden * attn_post_gain, unit_two, inverse_two).astype(BF)
     live["d_branch"] = [d_branch, swap(d_branch, "x", 1)]
+    live["gate"] = product(normed_two, live["d_gate"], swap(live["gate"], "c", 1))
     if pairs:
-        own = live["gate"]["own"]
-        over_x, over_y = fold_join(live["gate"], live.pop("gate_got"))
-        live["gate"] = {"own": own, "x": over_x, "y": swap(over_y, "y", 1)}
+        own, over_x, over_y, *got = live["down"]
+        over_x, over_y = fold_join({"x": over_x, "y": over_y}, got)
+        live["down"] = [own, over_x, swap(over_y, "y", 1)]
     else:
-        live["gate"] = {"own": sum_cut(live["gate"])}
-    live = close({k: live[k] for k in ("d_branch", "gate")})
+        live |= {name: [sum_cut(*live[name])] for name in ("down", "up", "gate")}
+    live = close({k: live[k] for k in ("d_branch", "up", "down", "gate")})
     d_branch = pair_gather(*live["d_branch"])
 
     if pairs:
-        live["gate"]["x"] = swap(live["gate"]["x"], "x", 1)
-    live["down"] = line_swaps(line_chunks(grad_down))
-    grad_out = outer_low(d_branch, attended, core_here, core_there)
+        own, over_x, got = live["down"]
+        live["down"] = [own, got, swap(over_x, "x", 1)]
+        own, over_x, over_y, across = live["up"]
+        live["up"] = [own, over_x, over_y, swap(across, "y", 1)]
+    live = {k: live[k] for k in ("up", "down", "gate")}
+    d_qkv, d_sent, d_kept = attention_back_call(
+        ids, d_branch, out_weight, qkv_weight, query, key, value, cosine, sine, allowed, kv_here
+    )
+    live["d_normed_one"] = [d_kept, d_sent]
     if pairs:
-        out_mine, out_far = pair_halves(grad_out, "y")
-        live["out"] = [out_mine, swap(out_far, "y", 1)]
+        live["rows"] = outer_rows(ids, core_there, normed_one, d_qkv, d_branch, attended)
     else:
-        live["out"] = [rows_sum(grad_out, "y")]
-    d_qkv, sent, kept = attention_back_call(
-        ids, d_branch, out_weight, qkv_weight, query, key, value, cosine, sine, allowed, kv_here
-    )
-    live["d_normed_one"] = [kept, sent]
-    live["d_qkv"] = d_qkv
+        rows = [outer_dot(normed_one, d_qkv), outer_dot(d_branch, attended)]
+        live["rows"] = jnp.concatenate(rows, axis=1).astype(BF)
+    live = close(live | {"d_qkv": d_qkv})
+
+    if pairs:
+        products = (normed_one, live["d_qkv"], d_branch, attended)
+        live["rows"] = outer_rows(ids, core_here, *products, swap(live["rows"], "c", 1))
+        own, over_x, over_y, got = live["up"]
+        live["up"] = [own, swap(add_low(over_x, got), "x", 1), swap(over_y, "y", 1)]
+    live["down"] = line_swaps(line_chunks(line_total(live["down"]).astype(BF)))
+    live = close({k: live[k] for k in ("rows", "up", "down", "gate", "d_normed_one")})
+    grad_down = line_columns(live.pop("down"))
+
+    live["up"] = line_swaps(line_chunks(line_total(live["up"]).astype(BF)))
+    if pairs:
+        own, over_x, over_y, across = live["gate"]
+        live["gate"] = [own, over_x, over_y, swap(across, "x", 1)]
+        far_sent, near_sent, far, near = live["rows"]
+        live["rows"] = [near_sent, add_low(far, swap(far_sent, "y", 1)), near]
     live = close(live)
-
-    grad_down = line_columns(live["down"])
-    kept, sent = live["d_normed_one"]
-    live["d_normed_one"] = [kept, swap(sent, "x", 1)]
-    live["qkv"] = outer_low(normed_one, live["d_qkv"], core_here, core_there)
-    live["out"] = add_low(*live["out"]) if pairs else live["out"][0]
-    grad_gate = line_total(list(live["gate"].values())).astype(BF)
-    live["gate"] = line_swaps(line_chunks(grad_gate))
-    live = close({k: live[k] for k in ("d_normed_one", "qkv", "out", "gate")})
-    grad_gate = line_columns(live["gate"])
+    grad_up = line_columns(live.pop("up"))
+    d_kept, d_sent = live["d_normed_one"]
+    live["d_normed_one"] = [d_kept, swap(d_sent, "x", 1)]
+    if pairs:
+        near_sent, far, near = live["rows"]
+        live["rows"] = [near, swap(near_sent, "y", 1), swap(far, "z", 1)]
+        own, over_x, over_y, got = live["gate"]
+        live["gate"] = [own, swap(over_x, "x", 1), over_y, got]
+    live = close(live)
+
     d_normed_one = live["d_normed_one"][0] + live["d_normed_one"][1].astype(F32)
     gain_one = jnp.sum(d_normed_one * unit_one, axis=0)
     grad_tokens = d_hidden + norm_back(d_normed_one * attn_gain, unit_one, inverse_one)
-
-    parts = y_chunks(live["qkv"]) if pairs else line_chunks(rows_sum(live["qkv"], "y"))
-    live = {"parts": parts, "out": line_swaps(line_chunks(live["out"]))}
-    live["gains"] = jnp.stack([gain_one, gain_two, gain_three, gain_four], axis=0)
+    gains = jnp.stack([gain_one, gain_two, gain_three, gain_four], axis=0)
+    rows = live["rows"]
     if pairs:
-        live["far"] = [swap(parts[k][1], "y", 1) for k in (2, 3)]
-    live = close(live)
-    parts, grad_out = live["parts"], line_total(live.pop("out"))
-
+        far = line_total([part[shard:] for part in rows]).astype(BF)
+        own, got_x, over_y, got = live["gate"]
+        gate = [own, got_x, swap(add_low(over_y, got), "y", 1)]
+        rows = [part[:shard] for part in rows] + [swap(far, "z", 2)]
+    else:
+        gate = live["gate"]
+    live = close({"rows": rows, "gate": gate, "gains": sum_over_y(gain_sum(gains))})
+    gains = live["gains"]
+
+    grad_gate = line_total(live["gate"]).astype(BF)
+    grad_gate = line_columns(line_swaps(line_chunks(grad_gate)))
     if pairs:
-        far = [add_low(parts[k][0], q) for k, q in zip((2, 3), live["far"])]
-        live["near"] = [swap(parts[k][1], "y", 1) for k in (0, 1)]
+        grad_rows = line_total(live["rows"])
     else:
-        far = parts[2:]
-    live["far"] = [swap(piece, "z", k) for k, piece in zip((2, 3), far)]
-    gains = gain_sum(live.pop("gains"))
-    live = close(live)
-
-    if pairs:
-        near = [add_low(live["parts"][k][0], q) for k, q in zip((0, 1), live["near"])]
-    else:
-        near = live["parts"][:2]
-    grad_qkv = line_total([near[0], swap(near[1], "z", 1), *live["far"]])
-    grad_up = line_columns(line_swaps(line_chunks(grad_up)))
+        grad_rows = lax.psum_scatter(live["rows"], row_axes, scatter_dimension=0, tiled=True)
+        grad_rows = grad_rows.astype(F32)
+    out_from = grad_rows.shape[1] - attended.shape[1]
+    grad_qkv, grad_out = grad_rows[:, :out_from], grad_rows[:, out_from:]
     cols = grad_qkv.shape[1] // kv_here
     cuts = (0, cols - 2 * HD, cols - HD, cols)
     grad_query, grad_key, grad_value = (

time: 875 us -> 829 us (0.947)
  waiting for transfers between devices: 478 us -> 435 us
  local copies, waits for them, and re-layouts: 79.8 us -> 55.9 us
  Pallas kernels: 170 us -> 185 us
    ppermute x68, waiting for transfers between devices: 477 us -> 434 us  [swap(): return lax.ppermute(values, axis, [(i, i ^ mask) for i in range(size)])]
    pallas_call x8, Pallas kernels: 50.5 us -> 64.7 us  [the longest x6 49.5 us: outer_quarters(): pl.pallas_call(outer_quarters_kernel, grid_spec=pltpu.PrefetchScalarGridS...]
    dynamic_slice x6 -> x1, local copies, waits for them, and re-layouts: 10.1 us -> 0.02 us  [sum_over_y(): lax.dynamic_index_in_dim(parts, here, 0, keepdims=False)]
    unnamed x228 -> x205, local copies, waits for them, and re-layouts: 33.5 us -> 29.9 us
  transfers between devices with their start and end apart: 73 -> 71, of which waited for: 35 -> 36; matrix products, arithmetic and copies ran while one was open for 10% -> 8% of each run, Pallas kernels for 15% -> 17%
where the time goes in v5:
time: 829 us; the launch traced here: 818 us
  waiting for transfers between devices  435 us (52%)
  Pallas kernels  185 us (22%)
  starting transfers between devices  78.4 us (9%)
  local copies, waits for them, and re-layouts  55.9 us (7%)
  other arithmetic  47.7 us (6%)
  between operations  15.5 us (2%)
    ppermute x68, waiting for transfers between devices, swap(): return lax.ppermute(values, axis, [(i, i ^ mask) for i in range(size)])  434 us
    ppermute x68, starting transfers between devices, swap(): return lax.ppermute(values, axis, [(i, i ^ mask) for i in range(size)])  78.3 us
    pallas_call x2, Pallas kernels, ffn_call(): pl.pallas_call(functools.partial(kernel, [weight.columns for weight in we...  68 us
    pallas_call x6, Pallas kernels, outer_quarters(): pl.pallas_call(outer_quarters_kernel, grid_spec=pltpu.PrefetchScalarGridS...  49.5 us
    unnamed x205, local copies, waits for them, and re-layouts  29.9 us
    pallas_call x8, Pallas kernels, assemble(): pl.pallas_call(functools.partial(assemble_kernel, counts), grid_spec=pltp...  27.3 us
  transfers between devices with their start and end apart: 71, of which 36 were waited for; matrix products, arithmetic and copies ran while one was open for 8% of the time, Pallas kernels for 17%

profile of v5, /device:TPU:8, one launch (start us, length us, event | category | flops | bytes accessed | tf_op | source)
XLA Modules:
  0.0 817.5 jit_solution(13324689831429611227)
XLA Ops:
  27.7 8.4 %collective-permute-done.refs_1_ = bf16[144,1152]{1,0:T(8,128)(2,1)S(1)} collective-permute-done((bf16[144,1152]{1,0:T(8,128)(2,1)}, bf16[144,1152]{1,0:T(8,128)(2,1)S(1)}, u32[]{:S(2)}, u32[]{:S(2)}) %collective-permute-start) | collective-permute-done | bytes 331808 | tf_op jit(solution)/shard_map/ppermute | solution.py:183
  36.0 12.3 %collective-permute-done.1.refs_2_ = bf16[144,1152]{1,0:T(8,128)(2,1)S(1)} collective-permute-done((bf16[144,1152]{1,0:T(8,128)(2,1)}, bf16[144,1152]{1,0:T(8,128)(2,1)S(1)}, u32[]{:S(2)}, u32[]{:S(2)}) %collective-permute-start.1) | collective-permute-done | bytes 331808 | tf_op jit(solution)/shard_map/ppermute | solution.py:183
  48.4 18.0 %collective-permute-done.2.refs_3_ = bf16[144,1152]{1,0:T(8,128)(2,1)S(1)} collective-permute-done((bf16[144,1152]{1,0:T(8,128)(2,1)}, bf16[144,1152]{1,0:T(8,128)(2,1)S(1)}, u32[]{:S(2)}, u32[]{:S(2)}) %collective-permute-start.2) | collective-permute-done | bytes 331808 | tf_op jit(solution)/shard_map/ppermute | solution.py:183
  76.0 13.7 %collective-permute-done.6.refs_1_ = bf16[144,1152]{1,0:T(8,128)(2,1)S(1)} collective-permute-done((bf16[144,1152]{1,0:T(8,128)(2,1)}, bf16[144,1152]{1,0:T(8,128)(2,1)S(1)}, u32[]{:S(2)}, u32[]{:S(2)}) %collective-permute-start.6) | collective-permute-done | bytes 331808 | tf_op jit(solution)/shard_map/ppermute | solution.py:183
  89.7 21.0 %collective-permute-done.7.refs_2_ = bf16[144,1152]{1,0:T(8,128)(2,1)S(1)} collective-permute-done((bf16[144,1152]{1,0:T(8,128)(2,1)}, bf16[144,1152]{1,0:T(8,128)(2,1)S(1)}, u32[]{:S(2)}, u32[]{:S(2)}) %collective-permute-start.7) | collective-permute-done | bytes 331808 | tf_op jit(solution)/shard_map/ppermute | solution.py:183
  110.7 21.6 %collective-permute-done.8.refs_3_ = bf16[144,1152]{1,0:T(8,128)(2,1)S(1)} collective-permute-done((bf16[144,1152]{1,0:T(8,128)(2,1)}, bf16[144,1152]{1,0:T(8,128)(2,1)S(1)}, u32[]{:S(2)}, u32[]{:S(2)}) %collective-permute-start.8) | collective-permute-done | bytes 331808 | tf_op jit(solution)/shard_map/ppermute | solution.py:183
  155.0 23.7 %collective-permute-done.11.refs_3_ = bf16[144,1152]{1,0:T(8,128)(2,1)S(1)} collective-permute-done((bf16[144,1152]{1,0:T(8,128)(2,1)S(1)}, bf16[144,1152]{1,0:T(8,128)(2,1)S(1)}, u32[]{:S(2)}, u32[]{:S(2)}) %collective-permute-start.11) | collective-permute-done | bytes 331808 | tf_op jit(solution)/shard_map/ppermute | solution.py:183
  187.9 7.7 shard_map.249.refs_0_
  223.0 7.8 shard_map.251.refs_2_
  232.4 20.5 %collective-permute-done.19 = bf16[128,2304]{1,0:T(8,128)(2,1)} collective-permute-done((bf16[128,2304]{1,0:T(8,128)(2,1)}, bf16[128,2304]{1,0:T(8,128)(2,1)}, u32[]{:S(2)}, u32[]{:S(2)}) %collective-permute-start.19) | collective-permute-done | bytes 589856 | tf_op jit(solution)/shard_map/ppermute | solution.py:183
  260.0 24.8 %collective-permute-done.22 = bf16[128,2304]{1,0:T(8,128)(2,1)S(1)} collective-permute-done((bf16[128,2304]{1,0:T(8,128)(2,1)S(1)}, bf16[128,2304]{1,0:T(8,128)(2,1)S(1)}, u32[]{:S(2)}, u32[]{:S(2)}) %collective-permute-start.22) | collective-permute-done | bytes 589856 | tf_op jit(solution)/shard_map/ppermute | solution.py:183
  286.4 13.6 %collective-permute-done.23 = bf16[128,2304]{1,0:T(8,128)(2,1)S(1)} collective-permute-done((bf16[128,2304]{1,0:T(8,128)(2,1)S(1)}, bf16[128,2304]{1,0:T(8,128)(2,1)S(1)}, u32[]{:S(2)}, u32[]{:S(2)}) %collective-permute-start.23) | collective-permute-done | bytes 589856 | tf_op jit(solution)/shard_map/ppermute | solution.py:183
  301.6 32.4 %shard_map.253 = (bf16[512,2304]{1,0:T(8,128)(2,1)}, f32[512,2304]{1,0:T(8,128)}, f32[512,2304]{1,0:T(8,128)}, f32[128,2304]{1,0:T(8,128)}, bf16[128,2304]{1,0:T...) custom-call(s32[4]{0:T(128)} %copy-done.42, bf16[512,2304]{1,0:T(8,128)(2,1)} %pad_maximum_fusion.x.left, ...), custom_call_target="tpu_custom_call" | custom-call | tf_op jit(solution)/shard_map/pallas_call | solution.py:161
  336.2 14.4 %collective-permute-done.25 = bf16[128,2304]{1,0:T(8,128)(2,1)S(1)} collective-permute-done((bf16[128,2304]{1,0:T(8,128)(2,1)}, bf16[128,2304]{1,0:T(8,128)(2,1)S(1)}, u32[]{:S(2)}, u32[]{:S(2)}) %collective-permute-start.25) | collective-permute-done | bytes 589856 | tf_op jit(solution)/shard_map/ppermute | solution.py:183
  369.8 8.4 %collective-permute-done.26 = bf16[128,2304]{1,0:T(8,128)(2,1)} collective-permute-done((bf16[128,2304]{1,0:T(8,128)(2,1)}, bf16[128,2304]{1,0:T(8,128)(2,1)}, u32[]{:S(2)}, u32[]{:S(2)}) %collective-permute-start.26) | collective-permute-done | bytes 589856 | tf_op jit(solution)/shard_map/ppermute | solution.py:183
  385.7 18.7 %collective-permute-done.28 = bf16[128,2304]{1,0:T(8,128)(2,1)S(1)} collective-permute-done((bf16[128,2304]{1,0:T(8,128)(2,1)S(1)}, bf16[128,2304]{1,0:T(8,128)(2,1)S(1)}, u32[]{:S(2)}, u32[]{:S(2)}) %collective-permute-start.28) | collective-permute-done | bytes 589856 | tf_op jit(solution)/shard_map/ppermute | solution.py:183
  405.6 13.8 %collective-permute-done.29 = bf16[128,2304]{1,0:T(8,128)(2,1)S(1)} collective-permute-done((bf16[128,2304]{1,0:T(8,128)(2,1)S(1)}, bf16[128,2304]{1,0:T(8,128)(2,1)S(1)}, u32[]{:S(2)}, u32[]{:S(2)}) %collective-permute-start.29) | collective-permute-done | bytes 589856 | tf_op jit(solution)/shard_map/ppermute | solution.py:183
  427.2 35.6 %shard_map.254 = (bf16[512,2304]{1,0:T(8,128)(2,1)}, bf16[512,2304]{1,0:T(8,128)(2,1)}, f32[128,2304]{1,0:T(8,128)}, bf16[128,2304]{1,0:T(8,128)(2,1)}, bf16[128...) custom-call(s32[4]{0:T(128)} %copy-done.42, bf16[512,2304]{1,0:T(8,128)(2,1)} %copy-done.1, ...), custom_call_target="tpu_custom_call" | custom-call | tf_op jit(solution)/shard_map/pallas_call | solution.py:161
  478.0 8.7 %shard_map.256 = (bf16[576,1152]{1,0:T(8,128)(2,1)S(1)}, bf16[576,1152]{1,0:T(8,128)(2,1)S(1)}, bf16[576,1152]{1,0:T(8,128)(2,1)S(1)}, bf16[576,1152]{1,0:T(8,128)(2,1)}) custom-call(s32[4]{0:T(128)S(1)} %copy-done.44, s32[1]{0:T(128)} %bitcast.26.which, bf16[512,2304]{1,0:T(8,128)(2,1)} %copy-done.1, bf16[512,2304]{1,0:T(8,128)(2,1)} %get-tuple-element.331.right, ...), custom_call_target="tpu_custom_call" | custom-call | tf_op jit(solution)/shard_map/pallas_call | solution.py:684
  496.9 9.3 %shard_map.259 = (bf16[576,1152]{1,0:T(8,128)(2,1)S(1)}, bf16[576,1152]{1,0:T(8,128)(2,1)S(1)}, bf16[576,1152]{1,0:T(8,128)(2,1)}, bf16[576,1152]{1,0:T(8,128)(2,1)}) custom-call(s32[4]{0:T(128)S(1)} %copy-done.44, s32[1]{0:T(128)} %bitcast.26.which, bf16[512,2304]{1,0:T(8,128)(2,1)} %pad_maximum_fusion.x.left, bf16[512,2304]{1,0:T(8,128)(2,1)} %get-tuple-element.352.right, ...), custom_call_target="tpu_custom_call" | custom-call | tf_op jit(solution)/shard_map/pallas_call | solution.py:684
  506.2 11.8 %collective-permute-done.34 = bf16[128,2304]{1,0:T(8,128)(2,1)S(1)} collective-permute-done((bf16[128,2304]{1,0:T(8,128)(2,1)}, bf16[128,2304]{1,0:T(8,128)(2,1)S(1)}, u32[]{:S(2)}, u32[]{:S(2)}) %collective-permute-start.34) | collective-permute-done | bytes 589856 | tf_op jit(solution)/shard_map/ppermute | solution.py:183
  532.5 9.1 %shard_map.260 = (bf16[576,1152]{1,0:T(8,128)(2,1)S(1)}, bf16[576,1152]{1,0:T(8,128)(2,1)}, bf16[576,1152]{1,0:T(8,128)(2,1)S(1)}, bf16[576,1152]{1,0:T(8,128)(2,1)}) custom-call(s32[4]{0:T(128)S(1)} %copy-done.44, s32[1]{0:T(128)} %bitcast.26.which, bf16[512,2304]{1,0:T(8,128)(2,1)} %pad_maximum_fusion.x.left, bf16[512,2304]{1,0:T(8,128)(2,1)} %get-tuple-element.366.right, ...), custom_call_target="tpu_custom_call" | custom-call | tf_op jit(solution)/shard_map/pallas_call | solution.py:684
  546.0 9.5 %collective-permute-done.38 = bf16[576,1152]{1,0:T(8,128)(2,1)} collective-permute-done((bf16[576,1152]{1,0:T(8,128)(2,1)}, bf16[576,1152]{1,0:T(8,128)(2,1)}, u32[]{:S(2)}, u32[]{:S(2)}) %collective-permute-start.38) | collective-permute-done | bytes 1327136 | tf_op jit(solution)/shard_map/ppermute | solution.py:183
  559.2 13.2 %shard_map.261 = (bf16[256,2048]{1,0:T(8,128)(2,1)S(1)}, bf16[128,2304]{1,0:T(8,128)(2,1)S(1)}, f32[128,2304]{1,0:T(8,128)}) custom-call(s32[4]{0:T(128)S(1)} %copy-done.44, bf16[256,2304]{1,0:T(8,128)(2,1)} %pad_maximum_fusion.5.d.left_b, bf16[2304,1024]{1,0:T(8,128)(2,1)} %all-gather.6.cloned.1.call-done.weight.out, ...), custom_call_target="tpu_custom_call" | custom-call | tf_op jit(solution)/shard_map/pallas_call | solution.py:529
  598.7 9.2 %shard_map.263 = (bf16[288,3072]{1,0:T(8,128)(2,1)}, bf16[288,3072]{1,0:T(8,128)(2,1)}, bf16[288,3072]{1,0:T(8,128)(2,1)}, bf16[288,3072]{1,0:T(8,128)(2,1)}) custom-call(s32[4]{0:T(128)S(1)} %copy-done.44, s32[1]{0:T(128)} %bitcast.26.which, bf16[256,2304]{1,0:T(8,128)(2,1)S(1)} %pad_maximum_fusion.4.x.left_a, bf16[256,2304]{1,0:T(8,128)(2,1)S(1)} %copy-done.2, ...), custom_call_target="tpu_custom_call" | custom-call | tf_op jit(solution)/shard_map/pallas_call | solution.py:747
  607.9 11.7 %collective-permute-done.43.refs_2_ = bf16[144,1152]{1,0:T(8,128)(2,1)S(1)} collective-permute-done((bf16[144,1152]{1,0:T(8,128)(2,1)S(1)}, bf16[144,1152]{1,0:T(8,128)(2,1)S(1)}, u32[]{:S(2)}, u32[]{:S(2)}) %collective-permute-start.43) | collective-permute-done | bytes 331808 | tf_op jit(solution)/shard_map/ppermute | solution.py:183
  635.6 31.1 %collective-permute-done.49 = bf16[288,3072]{1,0:T(8,128)(2,1)S(1)} collective-permute-done((bf16[288,3072]{1,0:T(8,128)(2,1)}, bf16[288,3072]{1,0:T(8,128)(2,1)S(1)}, u32[]{:S(2)}, u32[]{:S(2)}) %collective-permute-start.49) | collective-permute-done | bytes 1769504 | tf_op jit(solution)/shard_map/ppermute | solution.py:183
  682.9 29.2 %collective-permute-done.53 = bf16[128,2304]{1,0:T(8,128)(2,1)} collective-permute-done((bf16[128,2304]{1,0:T(8,128)(2,1)S(1)}, bf16[128,2304]{1,0:T(8,128)(2,1)}, u32[]{:S(2)}, u32[]{:S(2)}) %collective-permute-start.53) | collective-permute-done | bytes 589856 | tf_op jit(solution)/shard_map/ppermute | solution.py:183
  738.7 10.2 %collective-permute-done.62 = f32[4,144]{1,0:T(4,128)S(1)} collective-permute-done((f32[4,144]{1,0:T(4,128)S(1)}, f32[4,144]{1,0:T(4,128)S(1)}, u32[]{:S(2)}, u32[]{:S(2)}) %collective-permute-start.62) | collective-permute-done | bytes 2336 | tf_op jit(solution)/shard_map/ppermute | solution.py:183
  748.8 20.0 %collective-permute-done.64 = bf16[144,3072]{1,0:T(8,128)(2,1)} collective-permute-done((bf16[144,3072]{1,0:T(8,128)(2,1)}, bf16[144,3072]{1,0:T(8,128)(2,1)}, u32[]{:S(2)}, u32[]{:S(2)}) %collective-permute-start.64) | collective-permute-done | bytes 884768 | tf_op jit(solution)/shard_map/ppermute | solution.py:183
  781.4 9.1 %collective-permute-done.65.refs_1_ = bf16[144,1152]{1,0:T(8,128)(2,1)S(1)} collective-permute-done((bf16[144,1152]{1,0:T(8,128)(2,1)S(1)}, bf16[144,1152]{1,0:T(8,128)(2,1)S(1)}, u32[]{:S(2)}, u32[]{:S(2)}) %collective-permute-start.65) | collective-permute-done | bytes 331808 | tf_op jit(solution)/shard_map/ppermute | solution.py:183
  790.4 10.0 %collective-permute-done.66.refs_2_ = bf16[144,1152]{1,0:T(8,128)(2,1)S(1)} collective-permute-done((bf16[144,1152]{1,0:T(8,128)(2,1)S(1)}, bf16[144,1152]{1,0:T(8,128)(2,1)S(1)}, u32[]{:S(2)}, u32[]{:S(2)}) %collective-permute-start.66) | collective-permute-done | bytes 331808 | tf_op jit(solution)/shard_map/ppermute | solution.py:183
  (459 shorter events, 293.5 us)
Async XLA Ops:
  7.2 174.2 %all-gather.4.cloned.1.call-start = ((), (), s32[]{:S(2)}) async-start(), calls=%async_computation | async-start | bytes 10027008 | tf_op jit(solution)/shard_map/all_gather | solution.py:897
  13.6 204.3 %all-gather.6.cloned.1.call-start = ((), (), s32[]{:S(2)}) async-start(), calls=%async_computation.1 | async-start | bytes 5013504 | tf_op jit(solution)/shard_map/all_gather | solution.py:898
  14.3 287.3 %all-gather.8.cloned.1.call-start = ((), (), s32[]{:S(2)}) async-start(), calls=%async_computation.2 | async-start | bytes 11943936 | tf_op jit(solution)/shard_map/all_gather | solution.py:641
  15.4 33.0 %collective-permute-start.1 = (bf16[144,1152]{1,0:T(8,128)(2,1)}, bf16[144,1152]{1,0:T(8,128)(2,1)S(1)}, u32[]{:S(2)}, u32[]{:S(2)}) collective-permute-start(bf16[144,1152]{1,0:T(8,128)(2,1)} %get-tuple-element.540), channel_id=1, source_target_pairs={{0,16},{8,24},{16,0},{24,8},{1,17},{9,25},{17,1},{25,9},{2,18},{10... | collective-permute-start | bytes 995336 | tf_op jit(solution)/shard_map/ppermute | solution.py:183
  18.5 47.9 %collective-permute-start.2 = (bf16[144,1152]{1,0:T(8,128)(2,1)}, bf16[144,1152]{1,0:T(8,128)(2,1)S(1)}, u32[]{:S(2)}, u32[]{:S(2)}) collective-permute-start(bf16[144,1152]{1,0:T(8,128)(2,1)} %get-tuple-element.537), channel_id=1, source_target_pairs={{0,24},{8,16},{16,8},{24,0},{1,25},{9,17},{17,9},{25,1},{2,26},{10... | collective-permute-start | bytes 995336 | tf_op jit(solution)/shard_map/ppermute | solution.py:183
  24.0 42.4 %collective-permute-start.3 = (bf16[128,2304]{1,0:T(8,128)(2,1)S(1)}, bf16[128,2304]{1,0:T(8,128)(2,1)S(1)}, u32[]{:S(2)}, u32[]{:S(2)}) collective-permute-start(bf16[128,2304]{1,0:T(8,128)(2,1)S(1)} %multiply_convert_fusion.3), channel_id=1, source_target_pairs={{0,1},{1,0},{2,3},{3,2},{4,5},{5,4},{6,7},{7,6},{8,9},{9,8},{10,11... | collective-permute-start | bytes 1769480 | tf_op jit(solution)/shard_map/ppermute | solution.py:183
  68.0 64.3 %collective-permute-start.4 = (bf16[576,1152]{1,0:T(8,128)(2,1)S(1)}, bf16[576,1152]{1,0:T(8,128)(2,1)}, u32[]{:S(2)}, u32[]{:S(2)}) collective-permute-start(bf16[576,1152]{1,0:T(8,128)(2,1)S(1)} %shard_map.246.refs_0_), channel_id=1, source_target_pairs={{0,1},{1,0},{2,3},{3,2},{4,5},{5,4},{6,7},{7,6},{8,9},{9,8},{10,11... | collective-permute-start | bytes 3981320 | tf_op jit(solution)/shard_map/ppermute | solution.py:183
  69.6 62.7 %collective-permute-start.5 = (bf16[576,1152]{1,0:T(8,128)(2,1)S(1)}, bf16[576,1152]{1,0:T(8,128)(2,1)}, u32[]{:S(2)}, u32[]{:S(2)}) collective-permute-start(bf16[576,1152]{1,0:T(8,128)(2,1)S(1)} %shard_map.246.refs_0_), channel_id=1, source_target_pairs={{0,4},{4,0},{1,5},{5,1},{2,6},{6,2},{3,7},{7,3},{8,12},{12,8},{9,1... | collective-permute-start | bytes 3981320 | tf_op jit(solution)/shard_map/ppermute | solution.py:183
  71.1 39.6 %collective-permute-start.7 = (bf16[144,1152]{1,0:T(8,128)(2,1)}, bf16[144,1152]{1,0:T(8,128)(2,1)S(1)}, u32[]{:S(2)}, u32[]{:S(2)}) collective-permute-start(bf16[144,1152]{1,0:T(8,128)(2,1)} %get-tuple-element.249), channel_id=1, source_target_pairs={{0,16},{8,24},{16,0},{24,8},{1,17},{9,25},{17,1},{25,9},{2,18},{10... | collective-permute-start | bytes 995336 | tf_op jit(solution)/shard_map/ppermute | solution.py:183
  74.4 57.8 %collective-permute-start.8 = (bf16[144,1152]{1,0:T(8,128)(2,1)}, bf16[144,1152]{1,0:T(8,128)(2,1)S(1)}, u32[]{:S(2)}, u32[]{:S(2)}) collective-permute-start(bf16[144,1152]{1,0:T(8,128)(2,1)} %get-tuple-element.250), channel_id=1, source_target_pairs={{0,24},{8,16},{16,8},{24,0},{1,25},{9,17},{17,9},{25,1},{2,26},{10... | collective-permute-start | bytes 995336 | tf_op jit(solution)/shard_map/ppermute | solution.py:183
  133.0 47.3 %collective-permute-start.14 = (bf16[576,1152]{1,0:T(8,128)(2,1)S(1)}, bf16[576,1152]{1,0:T(8,128)(2,1)S(1)}, u32[]{:S(2)}, u32[]{:S(2)}) collective-permute-start(bf16[576,1152]{1,0:T(8,128)(2,1)S(1)} %shard_map.247.refs_0_), channel_id=1, source_target_pairs={{0,1},{1,0},{2,3},{3,2},{4,5},{5,4},{6,7},{7,6},{8,9},{9,8},{10,11... | collective-permute-start | bytes 3981320 | tf_op jit(solution)/shard_map/ppermute | solution.py:183
  133.3 48.1 %collective-permute-start.15 = (bf16[576,1152]{1,0:T(8,128)(2,1)S(1)}, bf16[576,1152]{1,0:T(8,128)(2,1)}, u32[]{:S(2)}, u32[]{:S(2)}) collective-permute-start(bf16[576,1152]{1,0:T(8,128)(2,1)S(1)} %shard_map.247.refs_0_), channel_id=1, source_target_pairs={{0,4},{4,0},{1,5},{5,1},{2,6},{6,2},{3,7},{7,3},{8,12},{12,8},{9,1... | collective-permute-start | bytes 3981320 | tf_op jit(solution)/shard_map/ppermute | solution.py:183
  139.9 39.5 %collective-permute-start.12 = (bf16[288,1152]{1,0:T(8,128)(2,1)S(1)}, bf16[288,1152]{1,0:T(8,128)(2,1)S(1)}, u32[]{:S(2)}, u32[]{:S(2)}) collective-permute-start(bf16[288,1152]{1,0:T(8,128)(2,1)S(1)} %slice.106), channel_id=1, source_target_pairs={{0,1},{1,0},{2,3},{3,2},{4,5},{5,4},{6,7},{7,6},{8,9},{9,8},{10,11... | collective-permute-start | bytes 1990664 | tf_op jit(solution)/shard_map/ppermute | solution.py:183
  334.8 35.0 %collective-permute-start.24 = (bf16[128,2304]{1,0:T(8,128)(2,1)}, bf16[128,2304]{1,0:T(8,128)(2,1)}, u32[]{:S(2)}, u32[]{:S(2)}) collective-permute-start(bf16[128,2304]{1,0:T(8,128)(2,1)} %get-tuple-element.310), channel_id=1, source_target_pairs={{0,8},{8,0},{16,24},{24,16},{1,9},{9,1},{17,25},{25,17},{2,10},{10... | collective-permute-start | bytes 1769480 | tf_op jit(solution)/shard_map/ppermute | solution.py:183
  427.2 35.6 %collective-permute-start.30 = (bf16[2,576,2304]{2,1,0:T(8,128)(2,1)}, bf16[2,576,2304]{2,1,0:T(8,128)(2,1)}, u32[]{:S(2)}, u32[]{:S(2)}) collective-permute-start(bf16[2,576,2304]{2,1,0:T(8,128)(2,1)} %shard_map.255), channel_id=1, source_target_pairs={{0,2},{2,0},{1,3},{3,1},{4,6},{6,4},{5,7},{7,5},{8,10},{10,8},{9,1... | collective-permute-start | bytes 15925256 | tf_op jit(solution)/shard_map/ppermute | solution.py:183
  488.7 33.5 %collective-permute-start.32 = (bf16[288,1152]{1,0:T(8,128)(2,1)S(1)}, bf16[288,1152]{1,0:T(8,128)(2,1)S(1)}, u32[]{:S(2)}, u32[]{:S(2)}) collective-permute-start(bf16[288,1152]{1,0:T(8,128)(2,1)S(1)} %get-tuple-element.532), channel_id=1, source_target_pairs={{0,1},{1,0},{2,3},{3,2},{4,5},{5,4},{6,7},{7,6},{8,9},{9,8},{10,11... | collective-permute-start | bytes 1990664 | tf_op jit(solution)/shard_map/ppermute | solution.py:183
  489.3 32.8 %collective-permute-start.33 = (bf16[288,1152]{1,0:T(8,128)(2,1)S(1)}, bf16[288,1152]{1,0:T(8,128)(2,1)S(1)}, u32[]{:S(2)}, u32[]{:S(2)}) collective-permute-start(bf16[288,1152]{1,0:T(8,128)(2,1)S(1)} %get-tuple-element.531), channel_id=1, source_target_pairs={{0,4},{4,0},{1,5},{5,1},{2,6},{6,2},{3,7},{7,3},{8,12},{12,8},{9,1... | collective-permute-start | bytes 1990664 | tf_op jit(solution)/shard_map/ppermute | solution.py:183
  524.2 31.3 %collective-permute-start.38 = (bf16[576,1152]{1,0:T(8,128)(2,1)}, bf16[576,1152]{1,0:T(8,128)(2,1)}, u32[]{:S(2)}, u32[]{:S(2)}) collective-permute-start(bf16[576,1152]{1,0:T(8,128)(2,1)} %pad_maximum_fusion.3), channel_id=1, source_target_pairs={{0,4},{4,0},{1,5},{5,1},{2,6},{6,2},{3,7},{7,3},{8,12},{12,8},{9,1... | collective-permute-start | bytes 3981320 | tf_op jit(solution)/shard_map/ppermute | solution.py:183
  556.9 30.2 %collective-permute-start.41 = (bf16[576,1152]{1,0:T(8,128)(2,1)}, bf16[576,1152]{1,0:T(8,128)(2,1)}, u32[]{:S(2)}, u32[]{:S(2)}) collective-permute-start(bf16[576,1152]{1,0:T(8,128)(2,1)} %get-tuple-element.394), channel_id=1, source_target_pairs={{0,4},{4,0},{1,5},{5,1},{2,6},{6,2},{3,7},{7,3},{8,12},{12,8},{9,1... | collective-permute-start | bytes 3981320 | tf_op jit(solution)/shard_map/ppermute | solution.py:183
  589.8 36.9 %collective-permute-start.46 = (bf16[576,1152]{1,0:T(8,128)(2,1)}, bf16[576,1152]{1,0:T(8,128)(2,1)}, u32[]{:S(2)}, u32[]{:S(2)}) collective-permute-start(bf16[576,1152]{1,0:T(8,128)(2,1)} %add_convert_fusion.4), channel_id=1, source_target_pairs={{0,1},{1,0},{2,3},{3,2},{4,5},{5,4},{6,7},{7,6},{8,9},{9,8},{10,11... | collective-permute-start | bytes 3981320 | tf_op jit(solution)/shard_map/ppermute | solution.py:183
  590.5 36.2 %collective-permute-start.47 = (bf16[576,1152]{1,0:T(8,128)(2,1)}, bf16[576,1152]{1,0:T(8,128)(2,1)}, u32[]{:S(2)}, u32[]{:S(2)}) collective-permute-start(bf16[576,1152]{1,0:T(8,128)(2,1)} %get-tuple-element.413), channel_id=1, source_target_pairs={{0,4},{4,0},{1,5},{5,1},{2,6},{6,2},{3,7},{7,3},{8,12},{12,8},{9,1... | collective-permute-start | bytes 3981320 | tf_op jit(solution)/shard_map/ppermute | solution.py:183
  626.7 39.9 %collective-permute-start.49 = (bf16[288,3072]{1,0:T(8,128)(2,1)}, bf16[288,3072]{1,0:T(8,128)(2,1)S(1)}, u32[]{:S(2)}, u32[]{:S(2)}) collective-permute-start(bf16[288,3072]{1,0:T(8,128)(2,1)} %get-tuple-element.422), channel_id=1, source_target_pairs={{0,4},{4,0},{1,5},{5,1},{2,6},{6,2},{3,7},{7,3},{8,12},{12,8},{9,1... | collective-permute-start | bytes 5308424 | tf_op jit(solution)/shard_map/ppermute | solution.py:183
  628.3 40.3 %collective-permute-start.48 = (bf16[576,1152]{1,0:T(8,128)(2,1)S(1)}, bf16[576,1152]{1,0:T(8,128)(2,1)S(1)}, u32[]{:S(2)}, u32[]{:S(2)}) collective-permute-start(bf16[576,1152]{1,0:T(8,128)(2,1)S(1)} %copy-done.95), channel_id=1, source_target_pairs={{0,1},{1,0},{2,3},{3,2},{4,5},{5,4},{6,7},{7,6},{8,9},{9,8},{10,11... | collective-permute-start | bytes 3981320 | tf_op jit(solution)/shard_map/ppermute | solution.py:183
  632.0 36.6 %collective-permute-start.50 = (bf16[144,1152]{1,0:T(8,128)(2,1)S(1)}, bf16[144,1152]{1,0:T(8,128)(2,1)S(1)}, u32[]{:S(2)}, u32[]{:S(2)}) collective-permute-start(bf16[144,1152]{1,0:T(8,128)(2,1)S(1)} %get-tuple-element.525), channel_id=1, source_target_pairs={{0,8},{8,0},{16,24},{24,16},{1,9},{9,1},{17,25},{25,17},{2,10},{10... | collective-permute-start | bytes 995336 | tf_op jit(solution)/shard_map/ppermute | solution.py:183
  632.1 36.5 %collective-permute-start.51 = (bf16[144,1152]{1,0:T(8,128)(2,1)S(1)}, bf16[144,1152]{1,0:T(8,128)(2,1)S(1)}, u32[]{:S(2)}, u32[]{:S(2)}) collective-permute-start(bf16[144,1152]{1,0:T(8,128)(2,1)S(1)} %get-tuple-element.524), channel_id=1, source_target_pairs={{0,16},{8,24},{16,0},{24,8},{1,17},{9,25},{17,1},{25,9},{2,18},{10... | collective-permute-start | bytes 995336 | tf_op jit(solution)/shard_map/ppermute | solution.py:183
  635.1 33.5 %collective-permute-start.52 = (bf16[144,1152]{1,0:T(8,128)(2,1)S(1)}, bf16[144,1152]{1,0:T(8,128)(2,1)S(1)}, u32[]{:S(2)}, u32[]{:S(2)}) collective-permute-start(bf16[144,1152]{1,0:T(8,128)(2,1)S(1)} %get-tuple-element.523), channel_id=1, source_target_pairs={{0,24},{8,16},{16,8},{24,0},{1,25},{9,17},{17,9},{25,1},{2,26},{10... | collective-permute-start | bytes 995336 | tf_op jit(solution)/shard_map/ppermute | solution.py:183
  668.6 43.5 %collective-permute-start.55 = (bf16[288,3072]{1,0:T(8,128)(2,1)}, bf16[288,3072]{1,0:T(8,128)(2,1)}, u32[]{:S(2)}, u32[]{:S(2)}) collective-permute-start(bf16[288,3072]{1,0:T(8,128)(2,1)} %get-tuple-element.434), channel_id=1, source_target_pairs={{0,4},{4,0},{1,5},{5,1},{2,6},{6,2},{3,7},{7,3},{8,12},{12,8},{9,1... | collective-permute-start | bytes 5308424 | tf_op jit(solution)/shard_map/ppermute | solution.py:183
  670.1 41.9 %collective-permute-start.56 = (bf16[288,3072]{1,0:T(8,128)(2,1)}, bf16[288,3072]{1,0:T(8,128)(2,1)}, u32[]{:S(2)}, u32[]{:S(2)}) collective-permute-start(bf16[288,3072]{1,0:T(8,128)(2,1)} %add_convert_fusion), channel_id=1, source_target_pairs={{0,8},{8,0},{16,24},{24,16},{1,9},{9,1},{17,25},{25,17},{2,10},{10... | collective-permute-start | bytes 5308424 | tf_op jit(solution)/shard_map/ppermute | solution.py:183
  670.1 41.9 %collective-permute-start.54 = (bf16[576,1152]{1,0:T(8,128)(2,1)}, bf16[576,1152]{1,0:T(8,128)(2,1)}, u32[]{:S(2)}, u32[]{:S(2)}) collective-permute-start(bf16[576,1152]{1,0:T(8,128)(2,1)} %get-tuple-element.430), channel_id=1, source_target_pairs={{0,1},{1,0},{2,3},{3,2},{4,5},{5,4},{6,7},{7,6},{8,9},{9,8},{10,11... | collective-permute-start | bytes 3981320 | tf_op jit(solution)/shard_map/ppermute | solution.py:183
  671.5 40.6 %collective-permute-start.53 = (bf16[128,2304]{1,0:T(8,128)(2,1)S(1)}, bf16[128,2304]{1,0:T(8,128)(2,1)}, u32[]{:S(2)}, u32[]{:S(2)}) collective-permute-start(bf16[128,2304]{1,0:T(8,128)(2,1)S(1)} %copy-done.46), channel_id=1, source_target_pairs={{0,1},{1,0},{2,3},{3,2},{4,5},{5,4},{6,7},{7,6},{8,9},{9,8},{10,11... | collective-permute-start | bytes 1769480 | tf_op jit(solution)/shard_map/ppermute | solution.py:183
  722.4 46.4 %collective-permute-start.63 = (bf16[576,1152]{1,0:T(8,128)(2,1)}, bf16[576,1152]{1,0:T(8,128)(2,1)}, u32[]{:S(2)}, u32[]{:S(2)}) collective-permute-start(bf16[576,1152]{1,0:T(8,128)(2,1)} %add_convert_fusion.2), channel_id=1, source_target_pairs={{0,4},{4,0},{1,5},{5,1},{2,6},{6,2},{3,7},{7,3},{8,12},{12,8},{9,1... | collective-permute-start | bytes 3981320 | tf_op jit(solution)/shard_map/ppermute | solution.py:183
  729.1 39.7 %collective-permute-start.64 = (bf16[144,3072]{1,0:T(8,128)(2,1)}, bf16[144,3072]{1,0:T(8,128)(2,1)}, u32[]{:S(2)}, u32[]{:S(2)}) collective-permute-start(bf16[144,3072]{1,0:T(8,128)(2,1)} %add_convert_fusion.6), channel_id=1, source_target_pairs={{0,16},{8,24},{16,0},{24,8},{1,17},{9,25},{17,1},{25,9},{2,18},{10... | collective-permute-start | bytes 2654216 | tf_op jit(solution)/shard_map/ppermute | solution.py:183
  (135 other events, 1767.4 us)
Sparse Core Ops, SparseCore 0:
  13.7 128.6 all-gather.3
  144.7 69.3 all-gather.5
  216.6 74.2 all-gather.7

commit v6 on v5

--- a/solution.py
+++ b/solution.py
@@ -71,12 +71,7 @@
 
 
 def spill(ids, total, outs):
-    rows = total.shape[0] // 4
-    if len(outs) == 1:
-        for k in range(4):
-            at = pl.multiple_of((ids[0] ^ k) * rows, rows)
-            outs[0][pl.ds(at, rows), :] = total[k * rows : (k + 1) * rows, :].astype(BF)
-        return
+    rows = outs[0].shape[0]
     for k, out in enumerate(outs):
         out[...] = total[k * rows : (k + 1) * rows, :].astype(out.dtype)
 
@@ -90,21 +85,13 @@
         if not self.whole:
             return [pl.BlockSpec((self.rows, tile), lambda i, ids: (0, i))] * 2
         count = self.arrays[0].shape[-1] // tile
-        return [
-            pl.BlockSpec(
-                (None, None, self.rows, tile), lambda i, ids, c=c: (i // count, c, 0, i % count)
-            )
-            for c in range(2)
-        ]
-
-    def operands(self):
-        return self.arrays * 2 if self.whole else self.arrays
+        return [pl.BlockSpec((None, self.rows, tile), lambda i, ids: (i // count, 0, i % count))]
 
     def columns(self, ids):
-        first, second = (0, self.rows) if self.whole else (ids[2] * self.rows, (1 - ids[2]) * self.rows)
-        if not self.whole:
-            first, second = (pl.multiple_of(at, 128) for at in (first, second))
-        return pl.ds(first, self.rows), pl.ds(second, self.rows)
+        if self.whole:
+            return (pl.ds(0, self.rows),)
+        starts = (pl.multiple_of(core * self.rows, 128) for core in (ids[2], 1 - ids[2]))
+        return tuple(pl.ds(start, self.rows) for start in starts)
 
 
 def inner(values, refs, columns):
@@ -117,16 +104,17 @@
         total[:, at] = jnp.where(fresh, part, total[:, at] + part)
 
 
-def forward_kernel(columns, ids, x, *refs):
-    gate_w, up_w, down_w, (act, gate, up), outs, total = (
-        refs[:2], refs[2:4], refs[4:6], refs[6:9], refs[9:13], refs[13]
-    )
-    gate_at, up_at, down_at = (find(ids) for find in columns)
+def up_kernel(columns, ids, x, *refs):
+    gate_w, up_w, (act, gate, up) = refs[:2], refs[2:4], refs[4:]
+    gate_at, up_at = (find(ids) for find in columns)
     gate_tile, up_tile = inner(x, gate_w, gate_at), inner(x, up_w, up_at)
     gate[...], up[...] = gate_tile, up_tile
-    act_tile = (gelu_parts(gate_tile)[0] * up_tile).astype(BF)
-    act[...] = act_tile
-    outer_add(total, act_tile, down_w, down_at, pl.program_id(0) == 0)
+    act[...] = (gelu_parts(gate_tile)[0] * up_tile).astype(BF)
+
+
+def down_kernel(columns, ids, act, *refs):
+    down_w, outs, total = refs[:1], refs[1:-1], refs[-1]
+    outer_add(total, act[...], down_w, columns[0](ids), pl.program_id(0) == 0)
 
     @pl.when(pl.program_id(0) == pl.num_programs(0) - 1)
     def _():
@@ -135,7 +123,7 @@
 
 def backward_kernel(columns, ids, d, *refs):
     gate_w, up_w, down_w, (gate, up), (d_gate, d_up), outs, total = (
-        refs[:2], refs[2:4], refs[4:6], refs[6:8], refs[8:10], refs[10:-1], refs[-1]
+        refs[:2], refs[2:4], refs[4:5], refs[5:7], refs[7:9], refs[9:-1], refs[-1]
     )
     gate_at, up_at, down_at = (find(ids) for find in columns)
     d_act = inner(d, down_w, down_at)
@@ -151,31 +139,38 @@
         spill(ids, total, outs)
 
 
-def ffn_call(kernel, ids, values, weights, kept, made, tile, natural):
-    tokens, width = values.shape
-    hidden = 2 * weights[-1].arrays[0].shape[-1] if weights[-1].whole else weights[-1].arrays[0].shape[-1]
-    slot = tokens // 4
+def ffn_call(kernel, ids, values, weights, kept, made, tile, width):
+    tokens = (values or kept)[0].shape[0]
+    cols = weights[-1].arrays[0].shape[-1]
+    hidden = 2 * cols if weights[-1].whole else cols
     across = pl.BlockSpec((tokens, tile), lambda i, ids: (0, i))
-    parts = [(tokens, BF)] if natural else [(slot, F32)] + [(slot, BF)] * 3
-    whole = [pl.BlockSpec((rows, width), lambda i, ids: (0, 0)) for rows, _ in parts]
+    parts = [F32, BF, BF, BF] if width else []
     return pl.pallas_call(
         functools.partial(kernel, [weight.columns for weight in weights]),
         grid_spec=pltpu.PrefetchScalarGridSpec(
             num_scalar_prefetch=1,
             grid=(hidden // tile,),
-            in_specs=[pl.BlockSpec((tokens, width), lambda i, ids: (0, 0))]
+            in_specs=[pl.BlockSpec(array.shape, lambda i, ids: (0, 0)) for array in values]
+            + ([] if values else [across] * len(kept))
             + [spec for weight in weights for spec in weight.specs(tile)]
-            + [across] * len(kept),
-            out_specs=[across] * len(made) + whole,
-            scratch_shapes=[pltpu.VMEM((tokens, width), F32)],
+            + ([across] * len(kept) if values else []),
+            out_specs=[across] * len(made)
+            + [pl.BlockSpec((tokens // 4, width), lambda i, ids: (0, 0)) for _ in parts],
+            scratch_shapes=[pltpu.VMEM((tokens, width), F32)] if width else [],
         ),
         out_shape=[jax.ShapeDtypeStruct((tokens, hidden), kind) for kind in made]
-        + [jax.ShapeDtypeStruct((rows, width), kind) for rows, kind in parts],
+        + [jax.ShapeDtypeStruct((tokens // 4, width), kind) for kind in parts],
         compiler_params=pltpu.CompilerParams(
             dimension_semantics=("arbitrary",), vmem_limit_bytes=58 * 2**20
         ),
         cost_estimate=pl.CostEstimate(flops=0, bytes_accessed=0, transcendentals=0),
-    )(ids, values, *[array for weight in weights for array in weight.operands()], *kept)
+    )(
+        ids,
+        *values,
+        *([] if values else kept),
+        *[array for weight in weights for array in weight.arrays],
+        *(kept if values else []),
+    )
 
 
 def swap(values, axis, mask):
@@ -358,8 +353,7 @@
     return {"own": own, "x": over_x, "y": over_y, "across": across}
 
 
-def fold_first(across):
-    rows = across.shape[0] // 2
+def fold_first(across, rows):
     return [swap(across[:rows], "x", 1), swap(across[rows:], "y", 1)]
 
 
@@ -639,7 +633,7 @@
 
 def gather_cut(own):
     whole = lax.all_gather(own, ("x", "c", "y"), axis=0, tiled=True)
-    return whole.reshape(2, 2, -1, own.shape[1])
+    return whole.reshape(2, -1, own.shape[1])
 
 
 def outer_low(left, right, mine, theirs):
@@ -661,7 +655,7 @@
 
     for half in range(2):
 
-        @pl.when(step == half)
+        @pl.when(step % 2 == half)
         def _(half=half):
             for side in range(2):
                 k = half + 2 * side
@@ -672,12 +666,12 @@
                     outs[0][side] = total.astype(BF)
 
 
-def outer_quarters(ids, which, left, right, *got):
+def outer_quarters(ids, which, left, right, *got, place=0):
     tokens, cut, cols = left.shape[0], left.shape[1] // 2, right.shape[1] // 2
     rows = cut // 2
     quarter = pl.BlockSpec((rows, cols), lambda i, ids, which: (0, 0))
     taken = [
-        pl.BlockSpec((None, rows, cols), lambda i, ids, which, k=k: (k // 2, 0, k % 2))
+        pl.BlockSpec((None, rows, cols), lambda i, ids, which, k=k: (2 * place + k // 2, 0, k % 2))
         for k in range(4)
     ]
     shape = jax.ShapeDtypeStruct((rows, cols), BF)
@@ -700,6 +694,49 @@
         compiler_params=kernel_params(),
         cost_estimate=LIGHT,
     )(ids, which, left, right, *got * 4)
+
+
+def outer_pair_kernel(ids, which, left, right_a, right_b, made, plain, flipped):
+    step, rows = pl.program_id(0), flipped.shape[0] // 2
+
+    @pl.when(step == 0)
+    def _():
+        plain[...] = left[...].T
+        for k, side in enumerate((ids[1], 1 - ids[1])):
+            at = pl.multiple_of(side * rows, rows)
+            flipped[k * rows : (k + 1) * rows, :] = plain[pl.ds(at, rows), :]
+
+    for k, right in enumerate((right_a, right_b)):
+
+        @pl.when(step // 2 == k)
+        def _(right=right):
+            for side in range(2):
+                at = slice(side * rows, (side + 1) * rows)
+                made[side] = tile_dot(flipped[at, :], right[...]).astype(BF)
+
+
+def outer_pair(ids, which, left, right_a, right_b):
+    tokens, cut, cols = left.shape[0], left.shape[1] // 2, right_a.shape[1] // 2
+    rows = cut // 2
+    return pl.pallas_call(
+        outer_pair_kernel,
+        grid_spec=pltpu.PrefetchScalarGridSpec(
+            num_scalar_prefetch=2,
+            grid=(4,),
+            in_specs=[
+                pl.BlockSpec((tokens, cut), lambda i, ids, which: (0, which[0])),
+                pl.BlockSpec((tokens, cols), lambda i, ids, which: (0, ids[3] ^ jnp.minimum(i, 1))),
+                pl.BlockSpec(
+                    (tokens, cols), lambda i, ids, which: (0, ids[3] ^ jnp.maximum(i - 2, 0))
+                ),
+            ],
+            out_specs=pl.BlockSpec((2, rows, cols), lambda i, ids, which: (i // 2, 0, i % 2)),
+            scratch_shapes=[pltpu.VMEM((cut, tokens), BF)] * 2,
+        ),
+        out_shape=jax.ShapeDtypeStruct((4, rows, 2 * cols), BF),
+        compiler_params=kernel_params(),
+        cost_estimate=LIGHT,
+    )(ids, which, left, right_a, right_b)
 
 
 def outer_rows_kernel(ids, which, left_a, left_b, right_a, right_b, *refs):
@@ -808,26 +845,28 @@
 
 
 def gain_sum(parts):
-    count, width = parts.shape
+    count = parts.shape[0]
     c_size, y_size, z_size = (lax.axis_size(axis) for axis in ("c", "y", "z"))
     parts = parts + swap(parts, "x", 1)
-    parts = parts.reshape(count, c_size, y_size, z_size, -1).transpose(3, 1, 2, 0, 4)
+    parts = parts.reshape(count, c_size, y_size, z_size, -1).transpose(1, 2, 3, 0, 4)
+    here = lax.axis_index("c")
+    sent = lax.dynamic_index_in_dim(parts, 1 - here, 0, keepdims=False)
+    return lax.dynamic_index_in_dim(parts, here, 0, keepdims=False) + swap(sent, "c", 1)
+
+
+def gain_sum_last(parts):
+    if lax.axis_size("y") == 2:
+        here = lax.axis_index("y")
+        sent = lax.dynamic_index_in_dim(parts, 1 - here, 0, keepdims=False)
+        parts = lax.dynamic_index_in_dim(parts, here, 0, keepdims=False) + swap(sent, "y", 1)
+    else:
+        parts = lax.psum_scatter(parts, "y", scatter_dimension=0, tiled=True)[0]
     here = lax.axis_index("z")
     total = lax.dynamic_index_in_dim(parts, here, 0, keepdims=False)
     for k in (1, 2, 3):
         piece = lax.dynamic_index_in_dim(parts, here ^ k, 0, keepdims=False)
         total = total + swap(piece, "z", k)
-    here = lax.axis_index("c")
-    sent = lax.dynamic_index_in_dim(total, 1 - here, 0, keepdims=False)
-    return lax.dynamic_index_in_dim(total, here, 0, keepdims=False) + swap(sent, "c", 1)
-
-
-def sum_over_y(parts):
-    if lax.axis_size("y") != 2:
-        return lax.psum_scatter(parts, "y", scatter_dimension=0, tiled=True)[0]
-    here = lax.axis_index("y")
-    sent = lax.dynamic_index_in_dim(parts, 1 - here, 0, keepdims=False)
-    return lax.dynamic_index_in_dim(parts, here, 0, keepdims=False) + swap(sent, "y", 1)
+    return total
 
 
 def on_device(
@@ -912,7 +951,7 @@
     live["down"] = line_swaps(live["down"])
     live["qkv"] = qkv_weight
     live = close(live)
-    down_weight = gather_cut(line_place(live.pop("down")))
+    live["down"] = line_place(live["down"])
 
     live["up"] |= cut_over_x(live["up"]) | cut_over_y(live["up"])
     gate_half = cut_half(live["gate"])
@@ -929,9 +968,9 @@
     live = close(live)
     sent, kept = live["branch"]
     live["branch"] = [kept, swap(sent, "x", 1)]
-    up_half = cut_half(live["up"])
-    live["up"] = [up_half, swap(up_half, "c", 1)]
+    live["up"] = cut_half(live["up"])
     live = close(live)
+    down_weight = gather_cut(live.pop("down"))
     branch = live["branch"][0] + live["branch"][1].astype(F32)
     inverse_two = lax.rsqrt(jnp.mean(branch * branch, axis=-1, keepdims=True) + NORM_EPS)
     unit_two = branch * inverse_two
@@ -941,14 +980,16 @@
 
 
     live["normed_two"] = line_gather((unit_three * ffn_gain).astype(BF))
+    live["up"] = [live["up"], swap(live["up"], "c", 1)]
     live = close(live)
-    weights = [Weight(*live["gate"]), Weight(*live["up"]), Weight(down_weight)]
-    normed_two = live["normed_two"]
-
-    live["act"], gate_proj, up_proj, *sums = ffn_call(
-        forward_kernel, ids, normed_two, weights, (), (BF, F32, F32), 384, False
-    )
-    live["sums"] = line_sum_second(line_sum_first(sums))
+    gate_weight, up_weight = Weight(*live["gate"]), Weight(*live["up"])
+    down_weight, normed_two = Weight(down_weight), live["normed_two"]
+
+    act, gate_proj, up_proj = ffn_call(
+        up_kernel, ids, [normed_two], [gate_weight, up_weight], [], (BF, F32, F32), 256, 0
+    )
+    sums = ffn_call(down_kernel, ids, [], [down_weight], [act], (), 1152, width)
+    live = {"act": act, "sums": line_sum_second(line_sum_first(sums))}
     live = close(live)
     ffn_out = line_total(live["sums"])
     inverse_four = lax.rsqrt(jnp.mean(ffn_out * ffn_out, axis=-1, keepdims=True) + NORM_EPS)
@@ -958,31 +999,51 @@
     d_ffn = norm_back(out_cotan * ffn_post_gain, unit_four, inverse_four).astype(BF)
     live["d_ffn"] = line_gather(d_ffn)
     live = close(live)
-    d_ffn, act, normed_two = live["d_ffn"], live["act"], live["normed_two"]
-    def product(left, right, *got):
+    d_ffn, act = live["d_ffn"], live["act"]
+    def product(left, right, *got, place=0):
         which = core_here if got else core_there
         if pairs:
-            return outer_quarters(ids, which, left, right, *got)
+            return outer_quarters(ids, which, left, right, *got, place=place)
         made = outer_halves(which, left, (right,), *got)
         return [made] if got else made
 
-    live = {"down": swap(product(d_ffn, act), "c", 1), "d_ffn": d_ffn, "act": act}
+    def first_sums(quarters, rows):
+        if not pairs:
+            return quarters
+        *quarters, across = quarters
+        return [*quarters, *fold_first(across, rows)]
+
+    def second_sums(quarters):
+        if not pairs:
+            return [sum_cut(*quarters)]
+        own, over_x, over_y, *got = quarters
+        over_x, over_y = fold_join({"x": over_x, "y": over_y}, got)
+        return [own, swap(over_x, "x", 1), swap(over_y, "y", 1)]
+
+    def over_line(terms):
+        return line_swaps(line_chunks(line_total(terms).astype(BF)))
+
+    live = {"down": product(d_ffn, act, swap(product(d_ffn, act), "c", 1))}
+    weights = [gate_weight, up_weight, down_weight]
     d_gate, d_up, *sums = ffn_call(
-        backward_kernel, ids, d_ffn, weights, (gate_proj, up_proj), (BF, BF), 384, False
+        backward_kernel, ids, [d_ffn], weights, [gate_proj, up_proj], (BF, BF), 384, width
     )
     live = close(live | {"d_gate": d_gate, "d_up": d_up, "sums": sums})
 
+    d_gate, d_up = live["d_gate"], live["d_up"]
     live["sums"] = line_sum_first(live["sums"])
-    live["down"] = product(live["d_ffn"], live["act"], live["down"])
-    d_gate, d_up = live["d_gate"], live["d_up"]
-    live |= {"up": product(normed_two, d_up), "gate": product(normed_two, d_gate)}
-    live = close({k: live[k] for k in ("sums", "down", "up", "gate", "d_gate", "d_up")})
+    live["down"] = first_sums(live["down"], 2 * shard)
+    if pairs:
+        live["sent"] = [outer_pair(ids, core_there, normed_two, d_up, d_gate)]
+    else:
+        live["sent"] = [product(normed_two, d_up), product(normed_two, d_gate)]
+    live = close(live)
     live["sums"] = line_sum_second(live["sums"])
-    if pairs:
-        *quarters, across = live["down"]
-        live["down"] = [*quarters, *fold_first(across)]
-    live["up"] = product(normed_two, live["d_up"], swap(live["up"], "c", 1))
-    live = close({k: live[k] for k in ("sums", "down", "up", "gate", "d_gate")})
+    live["down"] = second_sums(live["down"])
+    got = [swap(part, "c", 1) for part in live["sent"]]
+    live["up"] = product(normed_two, live["d_up"], got[0], place=0)
+    live["gate"] = product(normed_two, live["d_gate"], got[-1], place=1)
+    live = close({k: live[k] for k in ("sums", "down", "up", "gate")})
 
     d_normed_two = line_total(live["sums"])
     gain_three = jnp.sum(d_normed_two * unit_three, axis=0)
@@ -990,80 +1051,57 @@
     gain_two = jnp.sum(d_hidden * unit_two, axis=0)
     d_branch = norm_back(d_hidden * attn_post_gain, unit_two, inverse_two).astype(BF)
     live["d_branch"] = [d_branch, swap(d_branch, "x", 1)]
-    live["gate"] = product(normed_two, live["d_gate"], swap(live["gate"], "c", 1))
-    if pairs:
-        own, over_x, over_y, *got = live["down"]
-        over_x, over_y = fold_join({"x": over_x, "y": over_y}, got)
-        live["down"] = [own, over_x, swap(over_y, "y", 1)]
-    else:
-        live |= {name: [sum_cut(*live[name])] for name in ("down", "up", "gate")}
-    live = close({k: live[k] for k in ("d_branch", "up", "down", "gate")})
+    live["up"] = first_sums(live["up"], 2 * shard)
+    live["gate"] = first_sums(live["gate"], shard)
+    live = close({k: live[k] for k in ("d_branch", "down", "up", "gate")})
     d_branch = pair_gather(*live["d_branch"])
 
-    if pairs:
-        own, over_x, got = live["down"]
-        live["down"] = [own, got, swap(over_x, "x", 1)]
-        own, over_x, over_y, across = live["up"]
-        live["up"] = [own, over_x, over_y, swap(across, "y", 1)]
-    live = {k: live[k] for k in ("up", "down", "gate")}
+    live = {k: live[k] for k in ("down", "up", "gate")}
+    live["down"], live["up"] = over_line(live["down"]), second_sums(live["up"])
     d_qkv, d_sent, d_kept = attention_back_call(
         ids, d_branch, out_weight, qkv_weight, query, key, value, cosine, sine, allowed, kv_here
     )
-    live["d_normed_one"] = [d_kept, d_sent]
     if pairs:
         live["rows"] = outer_rows(ids, core_there, normed_one, d_qkv, d_branch, attended)
     else:
         rows = [outer_dot(normed_one, d_qkv), outer_dot(d_branch, attended)]
         live["rows"] = jnp.concatenate(rows, axis=1).astype(BF)
-    live = close(live | {"d_qkv": d_qkv})
-
+    live = close(live | {"d_qkv": d_qkv, "d_normed_one": [d_kept, d_sent]})
+    grad_down = line_columns(live["down"])
+
+    live["up"], live["gate"] = over_line(live["up"]), second_sums(live["gate"])
     if pairs:
         products = (normed_one, live["d_qkv"], d_branch, attended)
         live["rows"] = outer_rows(ids, core_here, *products, swap(live["rows"], "c", 1))
-        own, over_x, over_y, got = live["up"]
-        live["up"] = [own, swap(add_low(over_x, got), "x", 1), swap(over_y, "y", 1)]
-    live["down"] = line_swaps(line_chunks(line_total(live["down"]).astype(BF)))
-    live = close({k: live[k] for k in ("rows", "up", "down", "gate", "d_normed_one")})
-    grad_down = line_columns(live.pop("down"))
-
-    live["up"] = line_swaps(line_chunks(line_total(live["up"]).astype(BF)))
+    live = close({k: live[k] for k in ("up", "gate", "rows", "d_normed_one")})
+    grad_up = line_columns(live["up"])
+
+    d_kept, d_sent = live["d_normed_one"]
+    live = {"gate": over_line(live["gate"]), "rows": live["rows"]}
+    live["d_normed_one"] = [d_kept, swap(d_sent, "x", 1)]
     if pairs:
-        own, over_x, over_y, across = live["gate"]
-        live["gate"] = [own, over_x, over_y, swap(across, "x", 1)]
         far_sent, near_sent, far, near = live["rows"]
         live["rows"] = [near_sent, add_low(far, swap(far_sent, "y", 1)), near]
     live = close(live)
-    grad_up = line_columns(live.pop("up"))
-    d_kept, d_sent = live["d_normed_one"]
-    live["d_normed_one"] = [d_kept, swap(d_sent, "x", 1)]
-    if pairs:
-        near_sent, far, near = live["rows"]
-        live["rows"] = [near, swap(near_sent, "y", 1), swap(far, "z", 1)]
-        own, over_x, over_y, got = live["gate"]
-        live["gate"] = [own, swap(over_x, "x", 1), over_y, got]
-    live = close(live)
-
+    grad_gate = line_columns(live["gate"])
     d_normed_one = live["d_normed_one"][0] + live["d_normed_one"][1].astype(F32)
     gain_one = jnp.sum(d_normed_one * unit_one, axis=0)
     grad_tokens = d_hidden + norm_back(d_normed_one * attn_gain, unit_one, inverse_one)
     gains = jnp.stack([gain_one, gain_two, gain_three, gain_four], axis=0)
+
+    live = {"rows": live["rows"], "gains": gain_sum(gains)}
+    if pairs:
+        near_sent, far, near = live["rows"]
+        live["rows"] = [near, swap(near_sent, "y", 1), swap(far, "z", 1)]
+    live = close(live)
+
+    gains = gain_sum_last(live["gains"])
     rows = live["rows"]
     if pairs:
         far = line_total([part[shard:] for part in rows]).astype(BF)
-        own, got_x, over_y, got = live["gate"]
-        gate = [own, got_x, swap(add_low(over_y, got), "y", 1)]
-        rows = [part[:shard] for part in rows] + [swap(far, "z", 2)]
+        grad_rows = line_total([part[:shard] for part in rows] + [swap(far, "z", 2)])
     else:
-        gate = live["gate"]
-    live = close({"rows": rows, "gate": gate, "gains": sum_over_y(gain_sum(gains))})
-    gains = live["gains"]
-
-    grad_gate = line_total(live["gate"]).astype(BF)
-    grad_gate = line_columns(line_swaps(line_chunks(grad_gate)))
-    if pairs:
-        grad_rows = line_total(live["rows"])
-    else:
-        grad_rows = lax.psum_scatter(live["rows"], row_axes, scatter_dimension=0, tiled=True)
+        grad_rows = lax.psum_scatter(rows, row_axes, scatter_dimension=0, tiled=True)
         grad_rows = grad_rows.astype(F32)
     out_from = grad_rows.shape[1] - attended.shape[1]
     grad_qkv, grad_out = grad_rows[:, :out_from], grad_rows[:, out_from:]

time: 829 us -> 783 us (0.945)
  waiting for transfers between devices: 435 us -> 390 us
  local copies, waits for them, and re-layouts: 55.9 us -> 66.9 us
    ppermute x68 -> x69, waiting for transfers between devices: 434 us -> 383 us  [swap(): return lax.ppermute(values, axis, [(i, i ^ mask) for i in range(size)])]
    pallas_call x6 -> x4, Pallas kernels: 49.5 us -> 34.3 us  [outer_quarters(): pl.pallas_call(outer_quarters_kernel, grid_spec=pltpu.PrefetchScalarGridS...]
    pallas_call x0 -> x1, Pallas kernels: none -> 11.7 us  [outer_pair(): pl.pallas_call(outer_pair_kernel, grid_spec=pltpu.PrefetchScalarGridSpec(...]
    ppermute x68 -> x69, starting transfers between devices: 78.3 us -> 72.6 us  [swap(): return lax.ppermute(values, axis, [(i, i ^ mask) for i in range(size)])]
    unnamed x205 -> x222, local copies, waits for them, and re-layouts: 29.9 us -> 34.6 us
    pallas_call x2 -> x3, Pallas kernels: 68 us -> 67.6 us  [ffn_call(): pl.pallas_call(functools.partial(kernel, [weight.columns for weight in we...]
  transfers between devices with their start and end apart: 71 -> 72, of which waited for: 36 -> 34; matrix products, arithmetic and copies ran while one was open for 8% -> 9% of each run, Pallas kernels for 17% -> 19%
where the time goes in v6:
time: 783 us; the launch traced here: 776 us
  waiting for transfers between devices  390 us (50%)
  Pallas kernels  180 us (23%)
  starting transfers between devices  72.7 us (9%)
  local copies, waits for them, and re-layouts  66.9 us (9%)
  other arithmetic  51.7 us (7%)
  between operations  15.5 us (2%)
    ppermute x69, waiting for transfers between devices, swap(): return lax.ppermute(values, axis, [(i, i ^ mask) for i in range(size)])  383 us
    ppermute x69, starting transfers between devices, swap(): return lax.ppermute(values, axis, [(i, i ^ mask) for i in range(size)])  72.6 us
    pallas_call x3, Pallas kernels, ffn_call(): pl.pallas_call(functools.partial(kernel, [weight.columns for weight in we...  67.6 us
    unnamed x222, local copies, waits for them, and re-layouts  34.6 us
    pallas_call x4, Pallas kernels, outer_quarters(): pl.pallas_call(outer_quarters_kernel, grid_spec=pltpu.PrefetchScalarGridS...  34.3 us
    pallas_call x8, Pallas kernels, assemble(): pl.pallas_call(functools.partial(assemble_kernel, counts), grid_spec=pltp...  26.9 us
  transfers between devices with their start and end apart: 72, of which 34 were waited for; matrix products, arithmetic and copies ran while one was open for 9% of the time, Pallas kernels for 19%

profile of v6, /device:TPU:8, one launch (start us, length us, event | category | flops | bytes accessed | tf_op | source)
XLA Modules:
  0.0 776.1 jit_solution(16980602882613675288)
XLA Ops:
  26.3 8.0 %collective-permute-done.refs_1_ = bf16[144,1152]{1,0:T(8,128)(2,1)S(1)} collective-permute-done((bf16[144,1152]{1,0:T(8,128)(2,1)}, bf16[144,1152]{1,0:T(8,128)(2,1)S(1)}, u32[]{:S(2)}, u32[]{:S(2)}) %collective-permute-start) | collective-permute-done | bytes 331808 | tf_op jit(solution)/shard_map/ppermute | solution.py:178
  34.3 13.9 %collective-permute-done.1.refs_2_ = bf16[144,1152]{1,0:T(8,128)(2,1)S(1)} collective-permute-done((bf16[144,1152]{1,0:T(8,128)(2,1)}, bf16[144,1152]{1,0:T(8,128)(2,1)S(1)}, u32[]{:S(2)}, u32[]{:S(2)}) %collective-permute-start.1) | collective-permute-done | bytes 331808 | tf_op jit(solution)/shard_map/ppermute | solution.py:178
  48.3 17.0 %collective-permute-done.2.refs_3_ = bf16[144,1152]{1,0:T(8,128)(2,1)S(1)} collective-permute-done((bf16[144,1152]{1,0:T(8,128)(2,1)}, bf16[144,1152]{1,0:T(8,128)(2,1)S(1)}, u32[]{:S(2)}, u32[]{:S(2)}) %collective-permute-start.2) | collective-permute-done | bytes 331808 | tf_op jit(solution)/shard_map/ppermute | solution.py:178
  75.3 14.2 %collective-permute-done.6.refs_1_ = bf16[144,1152]{1,0:T(8,128)(2,1)S(1)} collective-permute-done((bf16[144,1152]{1,0:T(8,128)(2,1)}, bf16[144,1152]{1,0:T(8,128)(2,1)S(1)}, u32[]{:S(2)}, u32[]{:S(2)}) %collective-permute-start.6) | collective-permute-done | bytes 331808 | tf_op jit(solution)/shard_map/ppermute | solution.py:178
  89.5 20.5 %collective-permute-done.7.refs_2_ = bf16[144,1152]{1,0:T(8,128)(2,1)S(1)} collective-permute-done((bf16[144,1152]{1,0:T(8,128)(2,1)}, bf16[144,1152]{1,0:T(8,128)(2,1)S(1)}, u32[]{:S(2)}, u32[]{:S(2)}) %collective-permute-start.7) | collective-permute-done | bytes 331808 | tf_op jit(solution)/shard_map/ppermute | solution.py:178
  110.1 21.5 %collective-permute-done.8.refs_3_ = bf16[144,1152]{1,0:T(8,128)(2,1)S(1)} collective-permute-done((bf16[144,1152]{1,0:T(8,128)(2,1)}, bf16[144,1152]{1,0:T(8,128)(2,1)S(1)}, u32[]{:S(2)}, u32[]{:S(2)}) %collective-permute-start.8) | collective-permute-done | bytes 331808 | tf_op jit(solution)/shard_map/ppermute | solution.py:178
  142.3 7.4 collective-permute-done.9.refs_1_
  153.2 22.2 %collective-permute-done.11.refs_3_ = bf16[144,1152]{1,0:T(8,128)(2,1)} collective-permute-done((bf16[144,1152]{1,0:T(8,128)(2,1)}, bf16[144,1152]{1,0:T(8,128)(2,1)}, u32[]{:S(2)}, u32[]{:S(2)}) %collective-permute-start.11) | collective-permute-done | bytes 331808 | tf_op jit(solution)/shard_map/ppermute | solution.py:178
  176.8 8.0 %shard_map.250.refs_0_ = bf16[1152,2304]{1,0:T(8,128)(2,1)} custom-call(s32[8]{0:T(128)S(1)} %stack.51.rows, s32[8]{0:T(128)S(1)} %stack.54.cols, bf16[576,1152]{1,0:T(8,128)(2,1)S(1)} %copy-done.7, bf16[576,1152]{1,0:T(8,128)(2,1)} %collective-permute-done.5.refs_1_, bf16[576,1152]{1,0:T(8,128)(2,1)} %collective-permute-done.4.refs_2_, ...), custom_call_target="tpu_custom_call" | custom-call | tf_op jit(solution)/shard_map/pallas_call | solution.py:833
  223.7 7.7 shard_map.252.refs_2_
  244.9 23.8 %collective-permute-done.21 = bf16[128,2304]{1,0:T(8,128)(2,1)S(1)} collective-permute-done((bf16[128,2304]{1,0:T(8,128)(2,1)S(1)}, bf16[128,2304]{1,0:T(8,128)(2,1)S(1)}, u32[]{:S(2)}, u32[]{:S(2)}) %collective-permute-start.21) | collective-permute-done | bytes 589856 | tf_op jit(solution)/shard_map/ppermute | solution.py:178
  271.5 13.4 %collective-permute-done.22 = bf16[128,2304]{1,0:T(8,128)(2,1)S(1)} collective-permute-done((bf16[128,2304]{1,0:T(8,128)(2,1)S(1)}, bf16[128,2304]{1,0:T(8,128)(2,1)S(1)}, u32[]{:S(2)}, u32[]{:S(2)}) %collective-permute-start.22) | collective-permute-done | bytes 589856 | tf_op jit(solution)/shard_map/ppermute | solution.py:178
  286.5 20.9 %shard_map.253 = (bf16[512,2304]{1,0:T(8,128)(2,1)}, f32[512,2304]{1,0:T(8,128)}, f32[512,2304]{1,0:T(8,128)}) custom-call(s32[4]{0:T(128)} %pad_add_fusion.1.ids, bf16[512,2304]{1,0:T(8,128)(2,1)} %pad_maximum_fusion.x.left, bf16[1152,2304]{1,0:T(8,128)(2,1)} %shard_map.250.refs_0_, bf16[1152,2304]{1,0:T(8,128)(2,1)} %collective-permute-done.16.refs_1_, ...), custom_call_target="tpu_custom_call" | custom-call | tf_op jit(solution)/shard_map/pallas_call | solution.py:148
  307.4 12.1 %shard_map.254 = (f32[128,2304]{1,0:T(8,128)}, bf16[128,2304]{1,0:T(8,128)(2,1)}, bf16[128,2304]{1,0:T(8,128)(2,1)}, bf16[128,2304]{1,0:T(8,128)(2,1)}) custom-call(s32[4]{0:T(128)} %pad_add_fusion.1.ids, bf16[512,2304]{1,0:T(8,128)(2,1)} %get-tuple-element.307.act.right, bf16[2,2304,1152]{2,1,0:T(8,128)(2,1)} %bitcast.93), custom_call_target="tpu_custom_call" | custom-call | tf_op jit(solution)/shard_map/pallas_call | solution.py:148
  321.6 14.4 %collective-permute-done.25 = bf16[128,2304]{1,0:T(8,128)(2,1)S(1)} collective-permute-done((bf16[128,2304]{1,0:T(8,128)(2,1)}, bf16[128,2304]{1,0:T(8,128)(2,1)S(1)}, u32[]{:S(2)}, u32[]{:S(2)}) %collective-permute-start.25) | collective-permute-done | bytes 589856 | tf_op jit(solution)/shard_map/ppermute | solution.py:178
  347.6 7.9 %collective-permute-done.24 = bf16[128,2304]{1,0:T(8,128)(2,1)} collective-permute-done((bf16[128,2304]{1,0:T(8,128)(2,1)}, bf16[128,2304]{1,0:T(8,128)(2,1)}, u32[]{:S(2)}, u32[]{:S(2)}) %collective-permute-start.24) | collective-permute-done | bytes 589856 | tf_op jit(solution)/shard_map/ppermute | solution.py:178
  370.5 18.7 %collective-permute-done.28 = bf16[128,2304]{1,0:T(8,128)(2,1)S(1)} collective-permute-done((bf16[128,2304]{1,0:T(8,128)(2,1)S(1)}, bf16[128,2304]{1,0:T(8,128)(2,1)S(1)}, u32[]{:S(2)}, u32[]{:S(2)}) %collective-permute-start.28) | collective-permute-done | bytes 589856 | tf_op jit(solution)/shard_map/ppermute | solution.py:178
  392.4 11.9 %collective-permute-done.29 = bf16[128,2304]{1,0:T(8,128)(2,1)S(1)} collective-permute-done((bf16[128,2304]{1,0:T(8,128)(2,1)S(1)}, bf16[128,2304]{1,0:T(8,128)(2,1)S(1)}, u32[]{:S(2)}, u32[]{:S(2)}) %collective-permute-start.29) | collective-permute-done | bytes 589856 | tf_op jit(solution)/shard_map/ppermute | solution.py:178
  404.6 7.5 shard_map.256
  412.1 34.6 %shard_map.255 = (bf16[512,2304]{1,0:T(8,128)(2,1)}, bf16[512,2304]{1,0:T(8,128)(2,1)}, f32[128,2304]{1,0:T(8,128)}, bf16[128,2304]{1,0:T(8,128)(2,1)}, bf16[128...) custom-call(s32[4]{0:T(128)} %pad_add_fusion.1.ids, bf16[512,2304]{1,0:T(8,128)(2,1)} %copy-done.1, ...), custom_call_target="tpu_custom_call" | custom-call | tf_op jit(solution)/shard_map/pallas_call | solution.py:148
  446.7 9.1 %shard_map.257 = (bf16[576,1152]{1,0:T(8,128)(2,1)S(1)}, bf16[576,1152]{1,0:T(8,128)(2,1)S(1)}, bf16[576,1152]{1,0:T(8,128)(2,1)S(1)}, bf16[576,1152]{1,0:T(8,128)(2,1)}) custom-call(s32[4]{0:T(128)S(1)} %copy-done.50, s32[1]{0:T(128)} %bitcast.26.which, bf16[512,2304]{1,0:T(8,128)(2,1)} %copy-done.1, bf16[512,2304]{1,0:T(8,128)(2,1)} %get-tuple-element.307.act.right, ...), custom_call_target="tpu_custom_call" | custom-call | tf_op jit(solution)/shard_map/pallas_call | solution.py:678
  461.0 11.7 %shard_map.258 = bf16[4,576,2304]{2,1,0:T(8,128)(2,1)} custom-call(s32[4]{0:T(128)S(1)} %copy-done.50, s32[1]{0:T(128)S(6)} %sub.44.which, bf16[512,2304]{1,0:T(8,128)(2,1)S(1)} %copy-done, bf16[512,2304]{1,0:T(8,128)(2,1)} %get-tuple-element.341.right_a.right, bf16[512,2304]{1,0:T(8,128)(2,1)} %get-tuple-element.331.right_b.right), custom_call_target="tpu_custom_call" | custom-call | tf_op jit(solution)/shard_map/pallas_call | solution.py:721
  484.8 9.1 %collective-permute-done.36.refs_0_.refs_1_.refs_2_.refs_3_ = bf16[4,576,2304]{2,1,0:T(8,128)(2,1)} collective-permute-done((bf16[4,576,2304]{2,1,0:T(8,128)(2,1)}, bf16[4,576,2304]{2,1,0:T(8,128)(2,1)}, u32[]{:S(2)}, u32[]{:S(2)}) %collective-permute-start.36) | collective-permute-done | bytes 10616864 | tf_op jit(solution)/shard_map/ppermute | solution.py:178
  493.9 8.7 %shard_map.259 = (bf16[576,1152]{1,0:T(8,128)(2,1)S(1)}, bf16[576,1152]{1,0:T(8,128)(2,1)S(1)}, bf16[576,1152]{1,0:T(8,128)(2,1)S(1)}, bf16[576,1152]{1,0:T(8,128)(2,1)}) custom-call(s32[4]{0:T(128)S(1)} %copy-done.50, s32[1]{0:T(128)} %bitcast.26.which, bf16[512,2304]{1,0:T(8,128)(2,1)} %pad_maximum_fusion.x.left, ...), custom_call_target="tpu_custom_call" | custom-call | tf_op jit(solution)/shard_map/pallas_call | solution.py:678
  505.8 8.9 %shard_map.260 = (bf16[576,1152]{1,0:T(8,128)(2,1)S(1)}, bf16[576,1152]{1,0:T(8,128)(2,1)S(1)}, bf16[576,1152]{1,0:T(8,128)(2,1)S(1)}, bf16[576,1152]{1,0:T(8,128)(2,1)}) custom-call(s32[4]{0:T(128)S(1)} %copy-done.50, s32[1]{0:T(128)} %bitcast.26.which, bf16[512,2304]{1,0:T(8,128)(2,1)} %pad_maximum_fusion.x.left, ...), custom_call_target="tpu_custom_call" | custom-call | tf_op jit(solution)/shard_map/pallas_call | solution.py:678
  529.9 30.4 %collective-permute-done.40 = bf16[144,1152]{1,0:T(8,128)(2,1)} collective-permute-done((bf16[144,1152]{1,0:T(8,128)(2,1)}, bf16[144,1152]{1,0:T(8,128)(2,1)}, u32[]{:S(2)}, u32[]{:S(2)}) %collective-permute-start.40) | collective-permute-done | bytes 331808 | tf_op jit(solution)/shard_map/ppermute | solution.py:178
  576.4 13.2 %shard_map.261 = (bf16[256,2048]{1,0:T(8,128)(2,1)S(1)}, bf16[128,2304]{1,0:T(8,128)(2,1)S(1)}, f32[128,2304]{1,0:T(8,128)}) custom-call(s32[4]{0:T(128)S(1)} %copy-done.51, bf16[256,2304]{1,0:T(8,128)(2,1)} %pad_maximum_fusion.9.d.left_b, bf16[2304,1024]{1,0:T(8,128)(2,1)} %all-gather.6.cloned.1.call-done.weight.out, ...), custom_call_target="tpu_custom_call" | custom-call | tf_op jit(solution)/shard_map/pallas_call | solution.py:523
  617.5 9.0 %shard_map.263 = (bf16[288,3072]{1,0:T(8,128)(2,1)}, bf16[288,3072]{1,0:T(8,128)(2,1)}, bf16[288,3072]{1,0:T(8,128)(2,1)}, bf16[288,3072]{1,0:T(8,128)(2,1)}) custom-call(s32[4]{0:T(128)S(1)} %copy-done.51, s32[1]{0:T(128)} %bitcast.26.which, bf16[256,2304]{1,0:T(8,128)(2,1)S(1)} %pad_maximum_fusion.8.x.left_a, bf16[256,2304]{1,0:T(8,128)(2,1)S(1)} %copy-done.2, ...), custom_call_target="tpu_custom_call" | custom-call | tf_op jit(solution)/shard_map/pallas_call | solution.py:784
  626.5 7.3 collective-permute-done.53.refs_2_
  648.5 32.4 %collective-permute-done.59 = bf16[288,3072]{1,0:T(8,128)(2,1)S(1)} collective-permute-done((bf16[288,3072]{1,0:T(8,128)(2,1)}, bf16[288,3072]{1,0:T(8,128)(2,1)S(1)}, u32[]{:S(2)}, u32[]{:S(2)}) %collective-permute-start.59) | collective-permute-done | bytes 1769504 | tf_op jit(solution)/shard_map/ppermute | solution.py:178
  695.7 26.1 %collective-permute-done.62 = bf16[288,3072]{1,0:T(8,128)(2,1)} collective-permute-done((bf16[288,3072]{1,0:T(8,128)(2,1)}, bf16[288,3072]{1,0:T(8,128)(2,1)}, u32[]{:S(2)}, u32[]{:S(2)}) %collective-permute-start.62) | collective-permute-done | bytes 1769504 | tf_op jit(solution)/shard_map/ppermute | solution.py:178
  739.8 24.6 %collective-permute-done.67 = f32[4,144]{1,0:T(4,128)S(1)} collective-permute-done((f32[4,144]{1,0:T(4,128)S(1)}, f32[4,144]{1,0:T(4,128)S(1)}, u32[]{:S(2)}, u32[]{:S(2)}) %collective-permute-start.67) | collective-permute-done | bytes 2336 | tf_op jit(solution)/shard_map/ppermute | solution.py:178
  (488 shorter events, 264.0 us)
Async XLA Ops:
  7.2 168.3 %all-gather.4.cloned.1.call-start = ((), (), s32[]{:S(2)}) async-start(), calls=%async_computation | async-start | bytes 10027008 | tf_op jit(solution)/shard_map/all_gather | solution.py:936
  13.6 203.6 %all-gather.6.cloned.1.call-start = ((), (), s32[]{:S(2)}) async-start(), calls=%async_computation.1 | async-start | bytes 5013504 | tf_op jit(solution)/shard_map/all_gather | solution.py:937
  17.7 47.6 %collective-permute-start.2 = (bf16[144,1152]{1,0:T(8,128)(2,1)}, bf16[144,1152]{1,0:T(8,128)(2,1)S(1)}, u32[]{:S(2)}, u32[]{:S(2)}) collective-permute-start(bf16[144,1152]{1,0:T(8,128)(2,1)} %get-tuple-element.505), channel_id=1, source_target_pairs={{0,24},{8,16},{16,8},{24,0},{1,25},{9,17},{17,9},{25,1},{2,26},{10... | collective-permute-start | bytes 995336 | tf_op jit(solution)/shard_map/ppermute | solution.py:178
  18.2 289.2 %all-gather.8.cloned.1.call-start = ((), (), s32[]{:S(2)}) async-start(), calls=%async_computation.2 | async-start | bytes 11943936 | tf_op jit(solution)/shard_map/all_gather | solution.py:635
  22.8 42.5 %collective-permute-start.3 = (bf16[128,2304]{1,0:T(8,128)(2,1)S(1)}, bf16[128,2304]{1,0:T(8,128)(2,1)S(1)}, u32[]{:S(2)}, u32[]{:S(2)}) collective-permute-start(bf16[128,2304]{1,0:T(8,128)(2,1)S(1)} %multiply_convert_fusion.3), channel_id=1, source_target_pairs={{0,1},{1,0},{2,3},{3,2},{4,5},{5,4},{6,7},{7,6},{8,9},{9,8},{10,11... | collective-permute-start | bytes 1769480 | tf_op jit(solution)/shard_map/ppermute | solution.py:178
  67.1 64.5 %collective-permute-start.4 = (bf16[576,1152]{1,0:T(8,128)(2,1)S(1)}, bf16[576,1152]{1,0:T(8,128)(2,1)}, u32[]{:S(2)}, u32[]{:S(2)}) collective-permute-start(bf16[576,1152]{1,0:T(8,128)(2,1)S(1)} %shard_map.246.refs_0_), channel_id=1, source_target_pairs={{0,1},{1,0},{2,3},{3,2},{4,5},{5,4},{6,7},{7,6},{8,9},{9,8},{10,11... | collective-permute-start | bytes 3981320 | tf_op jit(solution)/shard_map/ppermute | solution.py:178
  68.6 63.0 %collective-permute-start.5 = (bf16[576,1152]{1,0:T(8,128)(2,1)S(1)}, bf16[576,1152]{1,0:T(8,128)(2,1)}, u32[]{:S(2)}, u32[]{:S(2)}) collective-permute-start(bf16[576,1152]{1,0:T(8,128)(2,1)S(1)} %shard_map.246.refs_0_), channel_id=1, source_target_pairs={{0,4},{4,0},{1,5},{5,1},{2,6},{6,2},{3,7},{7,3},{8,12},{12,8},{9,1... | collective-permute-start | bytes 3981320 | tf_op jit(solution)/shard_map/ppermute | solution.py:178
  70.2 39.9 %collective-permute-start.7 = (bf16[144,1152]{1,0:T(8,128)(2,1)}, bf16[144,1152]{1,0:T(8,128)(2,1)S(1)}, u32[]{:S(2)}, u32[]{:S(2)}) collective-permute-start(bf16[144,1152]{1,0:T(8,128)(2,1)} %get-tuple-element.232), channel_id=1, source_target_pairs={{0,16},{8,24},{16,0},{24,8},{1,17},{9,25},{17,1},{25,9},{2,18},{10... | collective-permute-start | bytes 995336 | tf_op jit(solution)/shard_map/ppermute | solution.py:178
  73.9 57.8 %collective-permute-start.8 = (bf16[144,1152]{1,0:T(8,128)(2,1)}, bf16[144,1152]{1,0:T(8,128)(2,1)S(1)}, u32[]{:S(2)}, u32[]{:S(2)}) collective-permute-start(bf16[144,1152]{1,0:T(8,128)(2,1)} %get-tuple-element.233), channel_id=1, source_target_pairs={{0,24},{8,16},{16,8},{24,0},{1,25},{9,17},{17,9},{25,1},{2,26},{10... | collective-permute-start | bytes 995336 | tf_op jit(solution)/shard_map/ppermute | solution.py:178
  132.4 43.1 %collective-permute-start.14 = (bf16[576,1152]{1,0:T(8,128)(2,1)S(1)}, bf16[576,1152]{1,0:T(8,128)(2,1)}, u32[]{:S(2)}, u32[]{:S(2)}) collective-permute-start(bf16[576,1152]{1,0:T(8,128)(2,1)S(1)} %shard_map.247.refs_0_), channel_id=1, source_target_pairs={{0,1},{1,0},{2,3},{3,2},{4,5},{5,4},{6,7},{7,6},{8,9},{9,8},{10,11... | collective-permute-start | bytes 3981320 | tf_op jit(solution)/shard_map/ppermute | solution.py:178
  132.8 42.7 %collective-permute-start.15 = (bf16[576,1152]{1,0:T(8,128)(2,1)S(1)}, bf16[576,1152]{1,0:T(8,128)(2,1)}, u32[]{:S(2)}, u32[]{:S(2)}) collective-permute-start(bf16[576,1152]{1,0:T(8,128)(2,1)S(1)} %shard_map.247.refs_0_), channel_id=1, source_target_pairs={{0,4},{4,0},{1,5},{5,1},{2,6},{6,2},{3,7},{7,3},{8,12},{12,8},{9,1... | collective-permute-start | bytes 3981320 | tf_op jit(solution)/shard_map/ppermute | solution.py:178
  138.6 36.8 %collective-permute-start.12 = (bf16[288,1152]{1,0:T(8,128)(2,1)}, bf16[288,1152]{1,0:T(8,128)(2,1)S(1)}, u32[]{:S(2)}, u32[]{:S(2)}) collective-permute-start(bf16[288,1152]{1,0:T(8,128)(2,1)} %slice.142), channel_id=1, source_target_pairs={{0,1},{1,0},{2,3},{3,2},{4,5},{5,4},{6,7},{7,6},{8,9},{9,8},{10,11... | collective-permute-start | bytes 1990664 | tf_op jit(solution)/shard_map/ppermute | solution.py:178
  237.8 48.7 %collective-permute-start.23 = (bf16[1152,2304]{1,0:T(8,128)(2,1)}, bf16[1152,2304]{1,0:T(8,128)(2,1)}, u32[]{:S(2)}, u32[]{:S(2)}) collective-permute-start(bf16[1152,2304]{1,0:T(8,128)(2,1)} %shard_map.252.refs_2_), channel_id=1, source_target_pairs={{0,2},{2,0},{1,3},{3,1},{4,6},{6,4},{5,7},{7,5},{8,10},{10,8},{9,1... | collective-permute-start | bytes 15925256 | tf_op jit(solution)/shard_map/ppermute | solution.py:178
  478.7 37.2 %collective-permute-start.34 = (bf16[576,1152]{1,0:T(8,128)(2,1)}, bf16[576,1152]{1,0:T(8,128)(2,1)}, u32[]{:S(2)}, u32[]{:S(2)}) collective-permute-start(bf16[576,1152]{1,0:T(8,128)(2,1)} %pad_maximum_fusion.2), channel_id=1, source_target_pairs={{0,1},{1,0},{2,3},{3,2},{4,5},{5,4},{6,7},{7,6},{8,9},{9,8},{10,11... | collective-permute-start | bytes 3981320 | tf_op jit(solution)/shard_map/ppermute | solution.py:178
  479.6 36.3 %collective-permute-start.35 = (bf16[576,1152]{1,0:T(8,128)(2,1)S(1)}, bf16[576,1152]{1,0:T(8,128)(2,1)}, u32[]{:S(2)}, u32[]{:S(2)}) collective-permute-start(bf16[576,1152]{1,0:T(8,128)(2,1)S(1)} %pad_maximum_fusion.3), channel_id=1, source_target_pairs={{0,4},{4,0},{1,5},{5,1},{2,6},{6,2},{3,7},{7,3},{8,12},{12,8},{9,1... | collective-permute-start | bytes 3981320 | tf_op jit(solution)/shard_map/ppermute | solution.py:178
  480.1 35.7 %collective-permute-start.37 = (bf16[128,2304]{1,0:T(8,128)(2,1)}, bf16[128,2304]{1,0:T(8,128)(2,1)S(1)}, u32[]{:S(2)}, u32[]{:S(2)}) collective-permute-start(bf16[128,2304]{1,0:T(8,128)(2,1)} %get-tuple-element.338), channel_id=1, source_target_pairs={{0,8},{8,0},{16,24},{24,16},{1,9},{9,1},{17,25},{25,17},{2,10},{10... | collective-permute-start | bytes 1769480 | tf_op jit(solution)/shard_map/ppermute | solution.py:178
  521.0 39.3 %collective-permute-start.41 = (bf16[432,1152]{1,0:T(8,128)(2,1)}, bf16[432,1152]{1,0:T(8,128)(2,1)}, u32[]{:S(2)}, u32[]{:S(2)}) collective-permute-start(bf16[432,1152]{1,0:T(8,128)(2,1)} %slice.159), channel_id=1, source_target_pairs={{0,4},{4,0},{1,5},{5,1},{2,6},{6,2},{3,7},{7,3},{8,12},{12,8},{9,1... | collective-permute-start | bytes 2985992 | tf_op jit(solution)/shard_map/ppermute | solution.py:178
  523.3 37.0 %collective-permute-start.42 = (bf16[288,1152]{1,0:T(8,128)(2,1)}, bf16[288,1152]{1,0:T(8,128)(2,1)}, u32[]{:S(2)}, u32[]{:S(2)}) collective-permute-start(bf16[288,1152]{1,0:T(8,128)(2,1)} %get-tuple-element.498), channel_id=1, source_target_pairs={{0,1},{1,0},{2,3},{3,2},{4,5},{5,4},{6,7},{7,6},{8,9},{9,8},{10,11... | collective-permute-start | bytes 1990664 | tf_op jit(solution)/shard_map/ppermute | solution.py:178
  523.9 36.4 %collective-permute-start.43 = (bf16[288,1152]{1,0:T(8,128)(2,1)}, bf16[288,1152]{1,0:T(8,128)(2,1)}, u32[]{:S(2)}, u32[]{:S(2)}) collective-permute-start(bf16[288,1152]{1,0:T(8,128)(2,1)} %get-tuple-element.497), channel_id=1, source_target_pairs={{0,4},{4,0},{1,5},{5,1},{2,6},{6,2},{3,7},{7,3},{8,12},{12,8},{9,1... | collective-permute-start | bytes 1990664 | tf_op jit(solution)/shard_map/ppermute | solution.py:178
  562.9 38.8 %collective-permute-start.47 = (bf16[576,1152]{1,0:T(8,128)(2,1)S(1)}, bf16[576,1152]{1,0:T(8,128)(2,1)S(1)}, u32[]{:S(2)}, u32[]{:S(2)}) collective-permute-start(bf16[576,1152]{1,0:T(8,128)(2,1)S(1)} %pad_maximum_fusion.4), channel_id=1, source_target_pairs={{0,1},{1,0},{2,3},{3,2},{4,5},{5,4},{6,7},{7,6},{8,9},{9,8},{10,11... | collective-permute-start | bytes 3981320 | tf_op jit(solution)/shard_map/ppermute | solution.py:178
  565.6 36.2 %collective-permute-start.48 = (bf16[576,1152]{1,0:T(8,128)(2,1)S(1)}, bf16[576,1152]{1,0:T(8,128)(2,1)S(1)}, u32[]{:S(2)}, u32[]{:S(2)}) collective-permute-start(bf16[576,1152]{1,0:T(8,128)(2,1)S(1)} %pad_maximum_fusion.5), channel_id=1, source_target_pairs={{0,4},{4,0},{1,5},{5,1},{2,6},{6,2},{3,7},{7,3},{8,12},{12,8},{9,1... | collective-permute-start | bytes 3981320 | tf_op jit(solution)/shard_map/ppermute | solution.py:178
  603.9 37.1 %collective-permute-start.49 = (bf16[576,1152]{1,0:T(8,128)(2,1)S(1)}, bf16[576,1152]{1,0:T(8,128)(2,1)}, u32[]{:S(2)}, u32[]{:S(2)}) collective-permute-start(bf16[576,1152]{1,0:T(8,128)(2,1)S(1)} %pad_maximum_fusion.6), channel_id=1, source_target_pairs={{0,1},{1,0},{2,3},{3,2},{4,5},{5,4},{6,7},{7,6},{8,9},{9,8},{10,11... | collective-permute-start | bytes 3981320 | tf_op jit(solution)/shard_map/ppermute | solution.py:178
  641.0 39.8 %collective-permute-start.59 = (bf16[288,3072]{1,0:T(8,128)(2,1)}, bf16[288,3072]{1,0:T(8,128)(2,1)S(1)}, u32[]{:S(2)}, u32[]{:S(2)}) collective-permute-start(bf16[288,3072]{1,0:T(8,128)(2,1)} %get-tuple-element.404), channel_id=1, source_target_pairs={{0,4},{4,0},{1,5},{5,1},{2,6},{6,2},{3,7},{7,3},{8,12},{12,8},{9,1... | collective-permute-start | bytes 5308424 | tf_op jit(solution)/shard_map/ppermute | solution.py:178
  641.8 41.0 %collective-permute-start.55 = (bf16[128,2304]{1,0:T(8,128)(2,1)S(1)}, bf16[128,2304]{1,0:T(8,128)(2,1)S(1)}, u32[]{:S(2)}, u32[]{:S(2)}) collective-permute-start(bf16[128,2304]{1,0:T(8,128)(2,1)S(1)} %get-tuple-element.398), channel_id=1, source_target_pairs={{0,1},{1,0},{2,3},{3,2},{4,5},{5,4},{6,7},{7,6},{8,9},{9,8},{10,11... | collective-permute-start | bytes 1769480 | tf_op jit(solution)/shard_map/ppermute | solution.py:178
  644.9 37.9 %collective-permute-start.56 = (bf16[144,1152]{1,0:T(8,128)(2,1)S(1)}, bf16[144,1152]{1,0:T(8,128)(2,1)S(1)}, u32[]{:S(2)}, u32[]{:S(2)}) collective-permute-start(bf16[144,1152]{1,0:T(8,128)(2,1)S(1)} %get-tuple-element.487), channel_id=1, source_target_pairs={{0,8},{8,0},{16,24},{24,16},{1,9},{9,1},{17,25},{25,17},{2,10},{10... | collective-permute-start | bytes 995336 | tf_op jit(solution)/shard_map/ppermute | solution.py:178
  644.9 37.8 %collective-permute-start.57 = (bf16[144,1152]{1,0:T(8,128)(2,1)S(1)}, bf16[144,1152]{1,0:T(8,128)(2,1)S(1)}, u32[]{:S(2)}, u32[]{:S(2)}) collective-permute-start(bf16[144,1152]{1,0:T(8,128)(2,1)S(1)} %get-tuple-element.486), channel_id=1, source_target_pairs={{0,16},{8,24},{16,0},{24,8},{1,17},{9,25},{17,1},{25,9},{2,18},{10... | collective-permute-start | bytes 995336 | tf_op jit(solution)/shard_map/ppermute | solution.py:178
  647.5 35.3 %collective-permute-start.58 = (bf16[144,1152]{1,0:T(8,128)(2,1)S(1)}, bf16[144,1152]{1,0:T(8,128)(2,1)S(1)}, u32[]{:S(2)}, u32[]{:S(2)}) collective-permute-start(bf16[144,1152]{1,0:T(8,128)(2,1)S(1)} %get-tuple-element.485), channel_id=1, source_target_pairs={{0,24},{8,16},{16,8},{24,0},{1,25},{9,17},{17,9},{25,1},{2,26},{10... | collective-permute-start | bytes 995336 | tf_op jit(solution)/shard_map/ppermute | solution.py:178
  682.8 39.0 %collective-permute-start.62 = (bf16[288,3072]{1,0:T(8,128)(2,1)}, bf16[288,3072]{1,0:T(8,128)(2,1)}, u32[]{:S(2)}, u32[]{:S(2)}) collective-permute-start(bf16[288,3072]{1,0:T(8,128)(2,1)} %get-tuple-element.409), channel_id=1, source_target_pairs={{0,4},{4,0},{1,5},{5,1},{2,6},{6,2},{3,7},{7,3},{8,12},{12,8},{9,1... | collective-permute-start | bytes 5308424 | tf_op jit(solution)/shard_map/ppermute | solution.py:178
  683.5 38.7 %collective-permute-start.63 = (bf16[288,3072]{1,0:T(8,128)(2,1)}, bf16[288,3072]{1,0:T(8,128)(2,1)}, u32[]{:S(2)}, u32[]{:S(2)}) collective-permute-start(bf16[288,3072]{1,0:T(8,128)(2,1)} %add_convert_fusion), channel_id=1, source_target_pairs={{0,8},{8,0},{16,24},{24,16},{1,9},{9,1},{17,25},{25,17},{2,10},{10... | collective-permute-start | bytes 5308424 | tf_op jit(solution)/shard_map/ppermute | solution.py:178
  726.7 38.3 %collective-permute-start.68 = (bf16[144,3072]{1,0:T(8,128)(2,1)}, bf16[144,3072]{1,0:T(8,128)(2,1)}, u32[]{:S(2)}, u32[]{:S(2)}) collective-permute-start(bf16[144,3072]{1,0:T(8,128)(2,1)} %add_convert_fusion.5), channel_id=1, source_target_pairs={{0,16},{8,24},{16,0},{24,8},{1,17},{9,25},{17,1},{25,9},{2,18},{10... | collective-permute-start | bytes 2654216 | tf_op jit(solution)/shard_map/ppermute | solution.py:178
  727.3 37.0 %collective-permute-start.67 = (f32[4,144]{1,0:T(4,128)S(1)}, f32[4,144]{1,0:T(4,128)S(1)}, u32[]{:S(2)}, u32[]{:S(2)}) collective-permute-start(f32[4,144]{1,0:T(4,128)S(1)} %bitcast.109), channel_id=1, source_target_pairs={{0,24},{8,16},{16,8},{24,0},{1,25},{9,17},{17,9},{25,1},{2,26},{10... | collective-permute-start | bytes 6920 | tf_op jit(solution)/shard_map/ppermute | solution.py:178
  728.6 35.8 %collective-permute-start.66 = (f32[4,144]{1,0:T(4,128)S(1)}, f32[4,144]{1,0:T(4,128)S(1)}, u32[]{:S(2)}, u32[]{:S(2)}) collective-permute-start(f32[4,144]{1,0:T(4,128)S(1)} %bitcast.110), channel_id=1, source_target_pairs={{0,16},{8,24},{16,0},{24,8},{1,17},{9,25},{17,1},{25,9},{2,18},{10... | collective-permute-start | bytes 6920 | tf_op jit(solution)/shard_map/ppermute | solution.py:178
  (145 other events, 2003.9 us)
Sparse Core Ops, SparseCore 0:
  13.7 132.9 all-gather.3
  149.0 68.1 all-gather.5
  237.9 62.3 all-gather.7

commit v7 on v6

--- a/solution.py
+++ b/solution.py
@@ -394,11 +394,21 @@
     return bent, weights / jnp.sum(weights, axis=1, keepdims=True)
 
 
-def attention_kernel(x, weight, cosine, sine, allowed, query, key, value, attended):
+def share(ids, total, sent, kept):
+    rows = sent.shape[0]
+    here = ids[3]
+    sent[...] = total[pl.ds(pl.multiple_of((1 - here) * rows, rows), rows), :].astype(BF)
+    kept[...] = total[pl.ds(pl.multiple_of(here * rows, rows), rows), :]
+
+
+def attention_kernel(
+    ids, x, weight, cosine, sine, allowed, query, key, value, attended, sent, kept, total
+):
     heads = query.shape[1] // HD
-    proj = tile_dot(x[...], weight[...])
-    key_here = turned(proj[:, heads * HD : (heads + 1) * HD], cosine[...], sine[...]).astype(BF)
-    value_here = proj[:, (heads + 1) * HD :].astype(BF)
+    keys = heads * HD
+    proj = tile_dot(x[...], weight[:, : keys + 2 * HD])
+    key_here = turned(proj[:, keys : keys + HD], cosine[...], sine[...]).astype(BF)
+    value_here = proj[:, keys + HD :].astype(BF)
     key[...], value[...] = key_here, value_here
     for head in range(heads):
         at = slice(head * HD, (head + 1) * HD)
@@ -406,46 +416,7 @@
         query[:, at] = query_here
         probs = head_probs(query_here, key_here, allowed[...])[1].astype(BF)
         attended[:, at] = tile_dot(probs, value_here).astype(BF)
-
-
-def attention_call(x, weight, cosine, sine, allowed, groups):
-    tokens, width = x.shape
-    cols = weight.shape[1] // groups
-    heads = cols // HD - 2
-
-    def here(cut):
-        return pl.BlockSpec((tokens, cut), lambda g: (0, g))
-
-    def whole(values):
-        return pl.BlockSpec(values.shape, lambda g: (0, 0))
-
-    cuts = [heads * HD, HD, HD, heads * HD]
-    return pl.pallas_call(
-        attention_kernel,
-        grid=(groups,),
-        in_specs=[
-            whole(x),
-            pl.BlockSpec((width, cols), lambda g: (0, g)),
-            whole(cosine),
-            whole(sine),
-            whole(allowed),
-        ],
-        out_specs=[here(cut) for cut in cuts],
-        out_shape=[jax.ShapeDtypeStruct((tokens, groups * cut), BF) for cut in cuts],
-        compiler_params=kernel_params(),
-        cost_estimate=LIGHT,
-    )(x, weight, cosine, sine, allowed)
-
-
-def share(ids, total, sent, kept):
-    rows = sent.shape[0]
-    here = ids[3]
-    sent[...] = total[pl.ds(pl.multiple_of((1 - here) * rows, rows), rows), :].astype(BF)
-    kept[...] = total[pl.ds(pl.multiple_of(here * rows, rows), rows), :]
-
-
-def branch_kernel(ids, attended, weight, sent, kept, total):
-    part = tile_dot_cols(attended[...], weight[...])
+    part = tile_dot_cols(attended[...], weight[:, keys + 2 * HD :])
     total[...] = jnp.where(pl.program_id(0) == 0, part, total[...] + part)
 
     @pl.when(pl.program_id(0) == pl.num_programs(0) - 1)
@@ -453,35 +424,49 @@
         share(ids, total, sent, kept)
 
 
-def branch_call(ids, attended, weight):
-    tokens, cols = attended.shape
-    width = weight.shape[0]
-    tile = 512
-    half = pl.BlockSpec((tokens // 2, width), lambda g, ids: (0, 0))
+def attention_specs(tokens, width, cols, heads):
+    def here(rows, cut):
+        return pl.BlockSpec((rows, cut), lambda g, ids: (0, g))
+
+    def whole(rows, cut):
+        return pl.BlockSpec((rows, cut), lambda g, ids: (0, 0))
+
+    first = [whole(tokens, width), here(width, cols)]
+    tables = [whole(tokens, HD // 2), whole(tokens, HD // 2), whole(tokens, tokens)]
+    held = [here(tokens, cut) for cut in (heads * HD, HD, HD)]
+    halves = [whole(tokens // 2, width)] * 2
+    return first, tables, held, halves, here
+
+
+def attention_call(ids, x, weight, cosine, sine, allowed, groups):
+    tokens, width = x.shape
+    cols = weight.shape[1] // groups
+    heads = (cols // HD - 2) // 2
+    first, tables, held, halves, here = attention_specs(tokens, width, cols, heads)
+    shapes = [groups * cut for cut in (heads * HD, HD, HD, heads * HD)]
     return pl.pallas_call(
-        branch_kernel,
+        attention_kernel,
         grid_spec=pltpu.PrefetchScalarGridSpec(
             num_scalar_prefetch=1,
-            grid=(cols // tile,),
-            in_specs=[
-                pl.BlockSpec((tokens, tile), lambda g, ids: (0, g)),
-                pl.BlockSpec((width, tile), lambda g, ids: (0, g)),
-            ],
-            out_specs=[half, half],
+            grid=(groups,),
+            in_specs=first + tables,
+            out_specs=held + [here(tokens, heads * HD)] + halves,
             scratch_shapes=[pltpu.VMEM((tokens, width), F32)],
         ),
-        out_shape=[jax.ShapeDtypeStruct((tokens // 2, width), kind) for kind in (BF, F32)],
+        out_shape=[jax.ShapeDtypeStruct((tokens, cut), BF) for cut in shapes]
+        + [jax.ShapeDtypeStruct((tokens // 2, width), kind) for kind in (BF, F32)],
         compiler_params=kernel_params(),
         cost_estimate=LIGHT,
-    )(ids, attended, weight)
+    )(ids, x, weight, cosine, sine, allowed)
 
 
 def attention_back_kernel(
-    ids, d, out, weight, query, key, value, cosine, sine, allowed, d_qkv, sent, kept, total
+    ids, d, weight, cosine, sine, allowed, query, key, value, d_qkv, sent, kept, total
 ):
     heads = query.shape[1] // HD
+    cut = (heads + 2) * HD
     key_here, value_here = key[...], value[...]
-    d_attended = tile_dot(d[...], out[...]).astype(BF)
+    d_attended = tile_dot(d[...], weight[:, cut:]).astype(BF)
     d_key = d_value = 0.0
     pieces = []
     for head in range(heads):
@@ -500,7 +485,7 @@
     pieces.append(d_value.astype(BF))
     made = jnp.concatenate(pieces, axis=1)
     d_qkv[...] = made
-    part = tile_dot_cols(made, weight[...])
+    part = tile_dot_cols(made, weight[:, :cut])
     total[...] = jnp.where(pl.program_id(0) == 0, part, total[...] + part)
 
     @pl.when(pl.program_id(0) == pl.num_programs(0) - 1)
@@ -508,45 +493,29 @@
         share(ids, total, sent, kept)
 
 
-def attention_back_call(ids, d, out, weight, query, key, value, cosine, sine, allowed, groups):
+def attention_back_call(ids, d, weight, cosine, sine, allowed, query, key, value, groups):
     tokens, width = d.shape
     cols = weight.shape[1] // groups
-    heads = cols // HD - 2
-
-    def here(rows, cut):
-        return pl.BlockSpec((rows, cut), lambda g, ids: (0, g))
-
-    def whole(values):
-        return pl.BlockSpec(values.shape, lambda g, ids: (0, 0))
-
-    half = pl.BlockSpec((tokens // 2, width), lambda g, ids: (0, 0))
+    heads = (cols // HD - 2) // 2
+    first, tables, held, halves, here = attention_specs(tokens, width, cols, heads)
+    cut = (heads + 2) * HD
     return pl.pallas_call(
         attention_back_kernel,
         grid_spec=pltpu.PrefetchScalarGridSpec(
             num_scalar_prefetch=1,
             grid=(groups,),
-            in_specs=[
-                whole(d),
-                here(width, heads * HD),
-                here(width, cols),
-                here(tokens, heads * HD),
-                here(tokens, HD),
-                here(tokens, HD),
-                whole(cosine),
-                whole(sine),
-                whole(allowed),
-            ],
-            out_specs=[here(tokens, cols), half, half],
+            in_specs=first + tables + held,
+            out_specs=[here(tokens, cut)] + halves,
             scratch_shapes=[pltpu.VMEM((tokens, width), F32)],
         ),
         out_shape=[
-            jax.ShapeDtypeStruct((tokens, groups * cols), BF),
+            jax.ShapeDtypeStruct((tokens, groups * cut), BF),
             jax.ShapeDtypeStruct((tokens // 2, width), BF),
             jax.ShapeDtypeStruct((tokens // 2, width), F32),
         ],
         compiler_params=kernel_params(),
         cost_estimate=LIGHT,
-    )(ids, d, out, weight, query, key, value, cosine, sine, allowed)
+    )(ids, d, weight, cosine, sine, allowed, query, key, value)
 
 
 def outer_kernel(which, left, right, *rest):
@@ -921,11 +890,11 @@
     state_in = inward(tokens).astype(F32)
     out_cotan = inward(out_grad).astype(F32)
 
-    qkv_here = jnp.concatenate(
+    qkvo_here = jnp.concatenate(
         [
             weight[:, g * (weight.shape[1] // kv_here) : (g + 1) * (weight.shape[1] // kv_here)]
             for g in range(kv_here)
-            for weight in (w_query, w_key, w_value)
+            for weight in (w_query, w_key, w_value, w_out.T)
         ],
         axis=1,
     )
@@ -933,8 +902,7 @@
     unit_one = state_in * inverse_one
     normed_here = (unit_one * attn_gain).astype(BF)
 
-    qkv_weight = lax.all_gather(qkv_here, row_axes, axis=0, tiled=True)
-    out_weight = lax.all_gather(w_out.T, row_axes, axis=0, tiled=True)
+    qkvo_weight = lax.all_gather(qkvo_here, row_axes, axis=0, tiled=True)
 
     live = {"up": line_cuts(w_up), "down": line_cuts(w_down.T)}
     live["gate"] = line_swaps(line_cuts(w_gate))
@@ -949,26 +917,19 @@
     live["gate"] |= cut_over_x(live["gate"]) | cut_over_y(live["gate"])
     live["up"] = cut_first(line_place(live["up"]))
     live["down"] = line_swaps(live["down"])
-    live["qkv"] = qkv_weight
     live = close(live)
     live["down"] = line_place(live["down"])
 
     live["up"] |= cut_over_x(live["up"]) | cut_over_y(live["up"])
-    gate_half = cut_half(live["gate"])
-    live["gate"] = [gate_half, swap(gate_half, "c", 1)]
-    normed_one, qkv_weight = live["normed_one"], live["qkv"]
-    query, key, value, attended = attention_call(
-        normed_one, qkv_weight, cosine, sine, allowed, kv_here
-    )
-    live["attended"] = attended
+    normed_one = live["normed_one"]
+    query, key, value, attended, *live["branch"] = attention_call(
+        ids, normed_one, qkvo_weight, cosine, sine, allowed, kv_here
+    )
     live = close(live)
 
-    attended = live["attended"]
-    live["branch"] = branch_call(ids, attended, out_weight)
-    live = close(live)
     sent, kept = live["branch"]
     live["branch"] = [kept, swap(sent, "x", 1)]
-    live["up"] = cut_half(live["up"])
+    live["gate"], live["up"] = cut_half(live["gate"]), cut_half(live["up"])
     live = close(live)
     down_weight = gather_cut(live.pop("down"))
     branch = live["branch"][0] + live["branch"][1].astype(F32)
@@ -980,7 +941,7 @@
 
 
     live["normed_two"] = line_gather((unit_three * ffn_gain).astype(BF))
-    live["up"] = [live["up"], swap(live["up"], "c", 1)]
+    live |= {name: [live[name], swap(live[name], "c", 1)] for name in ("gate", "up")}
     live = close(live)
     gate_weight, up_weight = Weight(*live["gate"]), Weight(*live["up"])
     down_weight, normed_two = Weight(down_weight), live["normed_two"]
@@ -1059,7 +1020,7 @@
     live = {k: live[k] for k in ("down", "up", "gate")}
     live["down"], live["up"] = over_line(live["down"]), second_sums(live["up"])
     d_qkv, d_sent, d_kept = attention_back_call(
-        ids, d_branch, out_weight, qkv_weight, query, key, value, cosine, sine, allowed, kv_here
+        ids, d_branch, qkvo_weight, cosine, sine, allowed, query, key, value, kv_here
     )
     if pairs:
         live["rows"] = outer_rows(ids, core_there, normed_one, d_qkv, d_branch, attended)

time: 783 us -> 779 us (level)
    unnamed x222 -> x234, local copies, waits for them, and re-layouts: 34.6 us -> 32.5 us
  transfers between devices with their start and end apart: 72 -> 71, of which waited for: 34 -> 30; matrix products, arithmetic and copies ran while one was open for 9% -> 9% of each run, Pallas kernels for 19% -> 20%
where the time goes in v7:
time: 779 us; the launch traced here: 772 us
  waiting for transfers between devices  385 us (49%)
  Pallas kernels  181 us (23%)
  starting transfers between devices  75 us (10%)
  local copies, waits for them, and re-layouts  63.6 us (8%)
  other arithmetic  51.1 us (7%)
  between operations  15.8 us (2%)
    ppermute x69, waiting for transfers between devices, swap(): return lax.ppermute(values, axis, [(i, i ^ mask) for i in range(size)])  385 us
    ppermute x69, starting transfers between devices, swap(): return lax.ppermute(values, axis, [(i, i ^ mask) for i in range(size)])  74.9 us
    pallas_call x3, Pallas kernels, ffn_call(): pl.pallas_call(functools.partial(kernel, [weight.columns for weight in we...  67.6 us
    pallas_call x4, Pallas kernels, outer_quarters(): pl.pallas_call(outer_quarters_kernel, grid_spec=pltpu.PrefetchScalarGridS...  34.4 us
    unnamed x234, local copies, waits for them, and re-layouts  32.5 us
    pallas_call x8, Pallas kernels, assemble(): pl.pallas_call(functools.partial(assemble_kernel, counts), grid_spec=pltp...  29 us
  transfers between devices with their start and end apart: 71, of which 30 were waited for; matrix products, arithmetic and copies ran while one was open for 9% of the time, Pallas kernels for 20%

profile of v7, /device:TPU:8, one launch (start us, length us, event | category | flops | bytes accessed | tf_op | source)
XLA Modules:
  0.0 771.9 jit_solution(10826572783549629502)
XLA Ops:
  34.1 9.7 %collective-permute-done.1.refs_2_ = bf16[144,1152]{1,0:T(8,128)(2,1)S(1)} collective-permute-done((bf16[144,1152]{1,0:T(8,128)(2,1)}, bf16[144,1152]{1,0:T(8,128)(2,1)S(1)}, u32[]{:S(2)}, u32[]{:S(2)}) %collective-permute-start.1) | collective-permute-done | bytes 331808 | tf_op jit(solution)/shard_map/ppermute | solution.py:178
  43.7 25.0 %collective-permute-done.2.refs_3_ = bf16[144,1152]{1,0:T(8,128)(2,1)S(1)} collective-permute-done((bf16[144,1152]{1,0:T(8,128)(2,1)S(1)}, bf16[144,1152]{1,0:T(8,128)(2,1)S(1)}, u32[]{:S(2)}, u32[]{:S(2)}) %collective-permute-start.2) | collective-permute-done | bytes 331808 | tf_op jit(solution)/shard_map/ppermute | solution.py:178
  80.4 9.1 %collective-permute-done.6.refs_1_ = bf16[144,1152]{1,0:T(8,128)(2,1)S(1)} collective-permute-done((bf16[144,1152]{1,0:T(8,128)(2,1)S(1)}, bf16[144,1152]{1,0:T(8,128)(2,1)S(1)}, u32[]{:S(2)}, u32[]{:S(2)}) %collective-permute-start.6) | collective-permute-done | bytes 331808 | tf_op jit(solution)/shard_map/ppermute | solution.py:178
  89.5 23.0 %collective-permute-done.7.refs_2_ = bf16[144,1152]{1,0:T(8,128)(2,1)S(1)} collective-permute-done((bf16[144,1152]{1,0:T(8,128)(2,1)S(1)}, bf16[144,1152]{1,0:T(8,128)(2,1)S(1)}, u32[]{:S(2)}, u32[]{:S(2)}) %collective-permute-start.7) | collective-permute-done | bytes 331808 | tf_op jit(solution)/shard_map/ppermute | solution.py:178
  112.5 21.6 %collective-permute-done.8.refs_3_ = bf16[144,1152]{1,0:T(8,128)(2,1)S(1)} collective-permute-done((bf16[144,1152]{1,0:T(8,128)(2,1)S(1)}, bf16[144,1152]{1,0:T(8,128)(2,1)S(1)}, u32[]{:S(2)}, u32[]{:S(2)}) %collective-permute-start.8) | collective-permute-done | bytes 331808 | tf_op jit(solution)/shard_map/ppermute | solution.py:178
  148.2 17.1 %collective-permute-done.9.refs_1_ = bf16[144,1152]{1,0:T(8,128)(2,1)S(1)} collective-permute-done((bf16[144,1152]{1,0:T(8,128)(2,1)}, bf16[144,1152]{1,0:T(8,128)(2,1)S(1)}, u32[]{:S(2)}, u32[]{:S(2)}) %collective-permute-start.9) | collective-permute-done | bytes 331808 | tf_op jit(solution)/shard_map/ppermute | solution.py:178
  166.4 9.1 %collective-permute-done.10.refs_2_ = bf16[144,1152]{1,0:T(8,128)(2,1)S(1)} collective-permute-done((bf16[144,1152]{1,0:T(8,128)(2,1)}, bf16[144,1152]{1,0:T(8,128)(2,1)S(1)}, u32[]{:S(2)}, u32[]{:S(2)}) %collective-permute-start.10) | collective-permute-done | bytes 331808 | tf_op jit(solution)/shard_map/ppermute | solution.py:178
  176.9 12.6 %collective-permute-done.11.refs_3_ = bf16[144,1152]{1,0:T(8,128)(2,1)S(1)} collective-permute-done((bf16[144,1152]{1,0:T(8,128)(2,1)S(1)}, bf16[144,1152]{1,0:T(8,128)(2,1)S(1)}, u32[]{:S(2)}, u32[]{:S(2)}) %collective-permute-start.11) | collective-permute-done | bytes 331808 | tf_op jit(solution)/shard_map/ppermute | solution.py:178
  200.4 10.2 %shard_map.248 = (bf16[256,1024]{1,0:T(8,128)(2,1)S(1)}, bf16[256,512]{1,0:T(8,128)(2,1)S(1)}, bf16[256,512]{1,0:T(8,128)(2,1)S(1)}, bf16[256,1024]{1,0:T(8,128)...) custom-call(s32[4]{0:T(128)S(1)} %copy-done.40, bf16[256,2304]{1,0:T(8,128)(2,1)} %pad_maximum_fusion.8.x.left_a, ...), custom_call_target="tpu_custom_call" | custom-call | tf_op jit(solution)/shard_map/pallas_call | solution.py:447
  218.2 7.6 shard_map.250.refs_0_
  225.8 8.3 %shard_map.251.refs_2_ = bf16[1152,2304]{1,0:T(8,128)(2,1)} custom-call(s32[8]{0:T(128)S(1)} %copy-done.52, s32[8]{0:T(128)S(1)} %copy-done.50, bf16[576,1152]{1,0:T(8,128)(2,1)} %shard_map.247.refs_0_, bf16[576,1152]{1,0:T(8,128)(2,1)} %collective-permute-done.15.refs_1_, bf16[576,1152]{1,0:T(8,128)(2,1)} %collective-permute-done.14.refs_2_, ...), custom_call_target="tpu_custom_call" | custom-call | tf_op jit(solution)/shard_map/pallas_call | solution.py:802
  242.3 22.7 %collective-permute-done.21 = bf16[128,2304]{1,0:T(8,128)(2,1)S(1)} collective-permute-done((bf16[128,2304]{1,0:T(8,128)(2,1)S(1)}, bf16[128,2304]{1,0:T(8,128)(2,1)S(1)}, u32[]{:S(2)}, u32[]{:S(2)}) %collective-permute-start.21) | collective-permute-done | bytes 589856 | tf_op jit(solution)/shard_map/ppermute | solution.py:178
  268.5 12.9 %collective-permute-done.22 = bf16[128,2304]{1,0:T(8,128)(2,1)S(1)} collective-permute-done((bf16[128,2304]{1,0:T(8,128)(2,1)S(1)}, bf16[128,2304]{1,0:T(8,128)(2,1)S(1)}, u32[]{:S(2)}, u32[]{:S(2)}) %collective-permute-start.22) | collective-permute-done | bytes 589856 | tf_op jit(solution)/shard_map/ppermute | solution.py:178
  283.0 21.0 %shard_map.252 = (bf16[512,2304]{1,0:T(8,128)(2,1)}, f32[512,2304]{1,0:T(8,128)}, f32[512,2304]{1,0:T(8,128)}) custom-call(s32[4]{0:T(128)} %pad_add_fusion.ids, bf16[512,2304]{1,0:T(8,128)(2,1)} %pad_maximum_fusion.x.left, bf16[1152,2304]{1,0:T(8,128)(2,1)} %shard_map.250.refs_0_, bf16[1152,2304]{1,0:T(8,128)(2,1)} %collective-permute-done.19.refs_1_, ...), custom_call_target="tpu_custom_call" | custom-call | tf_op jit(solution)/shard_map/pallas_call | solution.py:148
  304.0 12.1 %shard_map.253 = (f32[128,2304]{1,0:T(8,128)}, bf16[128,2304]{1,0:T(8,128)(2,1)}, bf16[128,2304]{1,0:T(8,128)(2,1)}, bf16[128,2304]{1,0:T(8,128)(2,1)}) custom-call(s32[4]{0:T(128)} %pad_add_fusion.ids, bf16[512,2304]{1,0:T(8,128)(2,1)} %get-tuple-element.290.act.right, bf16[2,2304,1152]{2,1,0:T(8,128)(2,1)} %bitcast.93), custom_call_target="tpu_custom_call" | custom-call | tf_op jit(solution)/shard_map/pallas_call | solution.py:148
  318.2 14.5 %collective-permute-done.25 = bf16[128,2304]{1,0:T(8,128)(2,1)S(1)} collective-permute-done((bf16[128,2304]{1,0:T(8,128)(2,1)}, bf16[128,2304]{1,0:T(8,128)(2,1)S(1)}, u32[]{:S(2)}, u32[]{:S(2)}) %collective-permute-start.25) | collective-permute-done | bytes 589856 | tf_op jit(solution)/shard_map/ppermute | solution.py:178
  339.7 11.7 %collective-permute-done.24 = bf16[128,2304]{1,0:T(8,128)(2,1)} collective-permute-done((bf16[128,2304]{1,0:T(8,128)(2,1)}, bf16[128,2304]{1,0:T(8,128)(2,1)}, u32[]{:S(2)}, u32[]{:S(2)}) %collective-permute-start.24) | collective-permute-done | bytes 589856 | tf_op jit(solution)/shard_map/ppermute | solution.py:178
  365.1 18.8 %collective-permute-done.28 = bf16[128,2304]{1,0:T(8,128)(2,1)S(1)} collective-permute-done((bf16[128,2304]{1,0:T(8,128)(2,1)S(1)}, bf16[128,2304]{1,0:T(8,128)(2,1)S(1)}, u32[]{:S(2)}, u32[]{:S(2)}) %collective-permute-start.28) | collective-permute-done | bytes 589856 | tf_op jit(solution)/shard_map/ppermute | solution.py:178
  387.1 12.2 %collective-permute-done.29 = bf16[128,2304]{1,0:T(8,128)(2,1)S(1)} collective-permute-done((bf16[128,2304]{1,0:T(8,128)(2,1)S(1)}, bf16[128,2304]{1,0:T(8,128)(2,1)S(1)}, u32[]{:S(2)}, u32[]{:S(2)}) %collective-permute-start.29) | collective-permute-done | bytes 589856 | tf_op jit(solution)/shard_map/ppermute | solution.py:178
  407.1 34.6 %shard_map.254 = (bf16[512,2304]{1,0:T(8,128)(2,1)}, bf16[512,2304]{1,0:T(8,128)(2,1)}, f32[128,2304]{1,0:T(8,128)}, bf16[128,2304]{1,0:T(8,128)(2,1)}, bf16[128...) custom-call(s32[4]{0:T(128)} %pad_add_fusion.ids, bf16[512,2304]{1,0:T(8,128)(2,1)} %copy-done.1, ...), custom_call_target="tpu_custom_call" | custom-call | tf_op jit(solution)/shard_map/pallas_call | solution.py:148
  441.7 9.2 %shard_map.256 = (bf16[576,1152]{1,0:T(8,128)(2,1)S(1)}, bf16[576,1152]{1,0:T(8,128)(2,1)S(1)}, bf16[576,1152]{1,0:T(8,128)(2,1)S(1)}, bf16[576,1152]{1,0:T(8,128)(2,1)}) custom-call(s32[4]{0:T(128)S(1)} %copy-done.42, s32[1]{0:T(128)} %bitcast.5.which, bf16[512,2304]{1,0:T(8,128)(2,1)} %copy-done.1, bf16[512,2304]{1,0:T(8,128)(2,1)} %get-tuple-element.290.act.right, ...), custom_call_target="tpu_custom_call" | custom-call | tf_op jit(solution)/shard_map/pallas_call | solution.py:647
  456.8 11.8 %shard_map.257 = bf16[4,576,2304]{2,1,0:T(8,128)(2,1)} custom-call(s32[4]{0:T(128)S(1)} %copy-done.42, s32[1]{0:T(128)S(6)} %sub.44.which, bf16[512,2304]{1,0:T(8,128)(2,1)S(1)} %copy-done, bf16[512,2304]{1,0:T(8,128)(2,1)} %get-tuple-element.324.right_a.right, bf16[512,2304]{1,0:T(8,128)(2,1)} %get-tuple-element.314.right_b.right), custom_call_target="tpu_custom_call" | custom-call | tf_op jit(solution)/shard_map/pallas_call | solution.py:690
  476.8 11.9 %collective-permute-done.36.refs_0_.refs_1_.refs_2_.refs_3_ = bf16[4,576,2304]{2,1,0:T(8,128)(2,1)} collective-permute-done((bf16[4,576,2304]{2,1,0:T(8,128)(2,1)}, bf16[4,576,2304]{2,1,0:T(8,128)(2,1)}, u32[]{:S(2)}, u32[]{:S(2)}) %collective-permute-start.36) | collective-permute-done | bytes 10616864 | tf_op jit(solution)/shard_map/ppermute | solution.py:178
  488.7 8.7 %shard_map.258 = (bf16[576,1152]{1,0:T(8,128)(2,1)S(1)}, bf16[576,1152]{1,0:T(8,128)(2,1)S(1)}, bf16[576,1152]{1,0:T(8,128)(2,1)S(1)}, bf16[576,1152]{1,0:T(8,128)(2,1)}) custom-call(s32[4]{0:T(128)S(1)} %copy-done.42, s32[1]{0:T(128)} %bitcast.5.which, bf16[512,2304]{1,0:T(8,128)(2,1)} %pad_maximum_fusion.x.left, ...), custom_call_target="tpu_custom_call" | custom-call | tf_op jit(solution)/shard_map/pallas_call | solution.py:647
  499.6 9.0 %shard_map.259 = (bf16[576,1152]{1,0:T(8,128)(2,1)S(1)}, bf16[576,1152]{1,0:T(8,128)(2,1)S(1)}, bf16[576,1152]{1,0:T(8,128)(2,1)S(1)}, bf16[576,1152]{1,0:T(8,128)(2,1)}) custom-call(s32[4]{0:T(128)S(1)} %copy-done.42, s32[1]{0:T(128)} %bitcast.5.which, bf16[512,2304]{1,0:T(8,128)(2,1)} %pad_maximum_fusion.x.left, ...), custom_call_target="tpu_custom_call" | custom-call | tf_op jit(solution)/shard_map/pallas_call | solution.py:647
  523.6 31.3 %collective-permute-done.40 = bf16[144,1152]{1,0:T(8,128)(2,1)} collective-permute-done((bf16[144,1152]{1,0:T(8,128)(2,1)S(1)}, bf16[144,1152]{1,0:T(8,128)(2,1)}, u32[]{:S(2)}, u32[]{:S(2)}) %collective-permute-start.40) | collective-permute-done | bytes 331808 | tf_op jit(solution)/shard_map/ppermute | solution.py:178
  571.7 13.1 %shard_map.260 = (bf16[256,2048]{1,0:T(8,128)(2,1)S(1)}, bf16[128,2304]{1,0:T(8,128)(2,1)S(1)}, f32[128,2304]{1,0:T(8,128)}) custom-call(s32[4]{0:T(128)S(1)} %copy-done.43, bf16[256,2304]{1,0:T(8,128)(2,1)} %pad_maximum_fusion.9.d.left_b, bf16[2304,3072]{1,0:T(8,128)(2,1)} %all-gather.3.cloned.1.call-done.weight, f32[256,128]{1,0:T(8,128)S(1)} %get-tuple-element.512.cosine, ...), custom_call_target="tpu_custom_call" | custom-call | tf_op jit(solution)/shard_map/pallas_call | solution.py:502
  612.1 9.0 %shard_map.262 = (bf16[288,3072]{1,0:T(8,128)(2,1)}, bf16[288,3072]{1,0:T(8,128)(2,1)}, bf16[288,3072]{1,0:T(8,128)(2,1)}, bf16[288,3072]{1,0:T(8,128)(2,1)}) custom-call(s32[4]{0:T(128)S(1)} %copy-done.43, s32[1]{0:T(128)} %bitcast.5.which, bf16[256,2304]{1,0:T(8,128)(2,1)S(1)} %copy-done.2, bf16[256,2304]{1,0:T(8,128)(2,1)S(1)} %copy-done.3, ...), custom_call_target="tpu_custom_call" | custom-call | tf_op jit(solution)/shard_map/pallas_call | solution.py:753
  628.1 8.3 %collective-permute-done.54.refs_3_ = bf16[144,1152]{1,0:T(8,128)(2,1)S(1)} collective-permute-done((bf16[144,1152]{1,0:T(8,128)(2,1)S(1)}, bf16[144,1152]{1,0:T(8,128)(2,1)S(1)}, u32[]{:S(2)}, u32[]{:S(2)}) %collective-permute-start.54) | collective-permute-done | bytes 331808 | tf_op jit(solution)/shard_map/ppermute | solution.py:178
  644.3 32.0 %collective-permute-done.59 = bf16[288,3072]{1,0:T(8,128)(2,1)S(1)} collective-permute-done((bf16[288,3072]{1,0:T(8,128)(2,1)}, bf16[288,3072]{1,0:T(8,128)(2,1)S(1)}, u32[]{:S(2)}, u32[]{:S(2)}) %collective-permute-start.59) | collective-permute-done | bytes 1769504 | tf_op jit(solution)/shard_map/ppermute | solution.py:178
  693.2 24.2 %collective-permute-done.62 = bf16[288,3072]{1,0:T(8,128)(2,1)} collective-permute-done((bf16[288,3072]{1,0:T(8,128)(2,1)}, bf16[288,3072]{1,0:T(8,128)(2,1)}, u32[]{:S(2)}, u32[]{:S(2)}) %collective-permute-start.62) | collective-permute-done | bytes 1769504 | tf_op jit(solution)/shard_map/ppermute | solution.py:178
  734.2 25.7 %collective-permute-done.67 = f32[4,144]{1,0:T(4,128)S(1)} collective-permute-done((f32[4,144]{1,0:T(4,128)S(1)}, f32[4,144]{1,0:T(4,128)S(1)}, u32[]{:S(2)}, u32[]{:S(2)}) %collective-permute-start.67) | collective-permute-done | bytes 2336 | tf_op jit(solution)/shard_map/ppermute | solution.py:178
  (496 shorter events, 248.3 us)
Async XLA Ops:
  7.2 192.6 %all-gather.3.cloned.1.call-start = ((), (), s32[]{:S(2)}) async-start(), calls=%async_computation | async-start | bytes 15040512 | tf_op jit(solution)/shard_map/all_gather | solution.py:905
  13.8 290.2 %all-gather.5.cloned.1.call-start = ((), (), s32[]{:S(2)}) async-start(), calls=%async_computation.1 | async-start | bytes 11943936 | tf_op jit(solution)/shard_map/all_gather | solution.py:604
  17.9 50.9 %collective-permute-start.2 = (bf16[144,1152]{1,0:T(8,128)(2,1)S(1)}, bf16[144,1152]{1,0:T(8,128)(2,1)S(1)}, u32[]{:S(2)}, u32[]{:S(2)}) collective-permute-start(bf16[144,1152]{1,0:T(8,128)(2,1)S(1)} %get-tuple-element.489), channel_id=1, source_target_pairs={{0,24},{8,16},{16,8},{24,0},{1,25},{9,17},{17,9},{25,1},{2,26},{10... | collective-permute-start | bytes 995336 | tf_op jit(solution)/shard_map/ppermute | solution.py:178
  24.5 45.0 %collective-permute-start.3 = (bf16[128,2304]{1,0:T(8,128)(2,1)}, bf16[128,2304]{1,0:T(8,128)(2,1)}, u32[]{:S(2)}, u32[]{:S(2)}) collective-permute-start(bf16[128,2304]{1,0:T(8,128)(2,1)} %multiply_convert_fusion.3), channel_id=1, source_target_pairs={{0,1},{1,0},{2,3},{3,2},{4,5},{5,4},{6,7},{7,6},{8,9},{9,8},{10,11... | collective-permute-start | bytes 1769480 | tf_op jit(solution)/shard_map/ppermute | solution.py:178
  71.4 62.7 %collective-permute-start.4 = (bf16[576,1152]{1,0:T(8,128)(2,1)S(1)}, bf16[576,1152]{1,0:T(8,128)(2,1)S(1)}, u32[]{:S(2)}, u32[]{:S(2)}) collective-permute-start(bf16[576,1152]{1,0:T(8,128)(2,1)S(1)} %shard_map.246.refs_0_), channel_id=1, source_target_pairs={{0,1},{1,0},{2,3},{3,2},{4,5},{5,4},{6,7},{7,6},{8,9},{9,8},{10,11... | collective-permute-start | bytes 3981320 | tf_op jit(solution)/shard_map/ppermute | solution.py:178
  72.0 63.2 %collective-permute-start.5 = (bf16[576,1152]{1,0:T(8,128)(2,1)S(1)}, bf16[576,1152]{1,0:T(8,128)(2,1)}, u32[]{:S(2)}, u32[]{:S(2)}) collective-permute-start(bf16[576,1152]{1,0:T(8,128)(2,1)S(1)} %shard_map.246.refs_0_), channel_id=1, source_target_pairs={{0,4},{4,0},{1,5},{5,1},{2,6},{6,2},{3,7},{7,3},{8,12},{12,8},{9,1... | collective-permute-start | bytes 3981320 | tf_op jit(solution)/shard_map/ppermute | solution.py:178
  73.8 38.6 %collective-permute-start.7 = (bf16[144,1152]{1,0:T(8,128)(2,1)S(1)}, bf16[144,1152]{1,0:T(8,128)(2,1)S(1)}, u32[]{:S(2)}, u32[]{:S(2)}) collective-permute-start(bf16[144,1152]{1,0:T(8,128)(2,1)S(1)} %get-tuple-element.224), channel_id=1, source_target_pairs={{0,16},{8,24},{16,0},{24,8},{1,17},{9,25},{17,1},{25,9},{2,18},{10... | collective-permute-start | bytes 995336 | tf_op jit(solution)/shard_map/ppermute | solution.py:178
  77.9 56.1 %collective-permute-start.8 = (bf16[144,1152]{1,0:T(8,128)(2,1)S(1)}, bf16[144,1152]{1,0:T(8,128)(2,1)S(1)}, u32[]{:S(2)}, u32[]{:S(2)}) collective-permute-start(bf16[144,1152]{1,0:T(8,128)(2,1)S(1)} %get-tuple-element.225), channel_id=1, source_target_pairs={{0,24},{8,16},{16,8},{24,0},{1,25},{9,17},{17,9},{25,1},{2,26},{10... | collective-permute-start | bytes 995336 | tf_op jit(solution)/shard_map/ppermute | solution.py:178
  137.4 52.2 %collective-permute-start.14 = (bf16[576,1152]{1,0:T(8,128)(2,1)}, bf16[576,1152]{1,0:T(8,128)(2,1)}, u32[]{:S(2)}, u32[]{:S(2)}) collective-permute-start(bf16[576,1152]{1,0:T(8,128)(2,1)} %shard_map.247.refs_0_), channel_id=1, source_target_pairs={{0,1},{1,0},{2,3},{3,2},{4,5},{5,4},{6,7},{7,6},{8,9},{9,8},{10,11... | collective-permute-start | bytes 3981320 | tf_op jit(solution)/shard_map/ppermute | solution.py:178
  139.2 50.3 %collective-permute-start.15 = (bf16[576,1152]{1,0:T(8,128)(2,1)}, bf16[576,1152]{1,0:T(8,128)(2,1)}, u32[]{:S(2)}, u32[]{:S(2)}) collective-permute-start(bf16[576,1152]{1,0:T(8,128)(2,1)} %shard_map.247.refs_0_), channel_id=1, source_target_pairs={{0,4},{4,0},{1,5},{5,1},{2,6},{6,2},{3,7},{7,3},{8,12},{12,8},{9,1... | collective-permute-start | bytes 3981320 | tf_op jit(solution)/shard_map/ppermute | solution.py:178
  146.2 43.3 %collective-permute-start.12 = (bf16[288,1152]{1,0:T(8,128)(2,1)S(1)}, bf16[288,1152]{1,0:T(8,128)(2,1)S(1)}, u32[]{:S(2)}, u32[]{:S(2)}) collective-permute-start(bf16[288,1152]{1,0:T(8,128)(2,1)S(1)} %slice.148), channel_id=1, source_target_pairs={{0,1},{1,0},{2,3},{3,2},{4,5},{5,4},{6,7},{7,6},{8,9},{9,8},{10,11... | collective-permute-start | bytes 1990664 | tf_op jit(solution)/shard_map/ppermute | solution.py:178
  234.1 48.9 %collective-permute-start.19 = (bf16[1152,2304]{1,0:T(8,128)(2,1)}, bf16[1152,2304]{1,0:T(8,128)(2,1)}, u32[]{:S(2)}, u32[]{:S(2)}) collective-permute-start(bf16[1152,2304]{1,0:T(8,128)(2,1)} %shard_map.250.refs_0_), channel_id=1, source_target_pairs={{0,2},{2,0},{1,3},{3,1},{4,6},{6,4},{5,7},{7,5},{8,10},{10,8},{9,1... | collective-permute-start | bytes 15925256 | tf_op jit(solution)/shard_map/ppermute | solution.py:178
  234.2 48.8 %collective-permute-start.23 = (bf16[1152,2304]{1,0:T(8,128)(2,1)}, bf16[1152,2304]{1,0:T(8,128)(2,1)}, u32[]{:S(2)}, u32[]{:S(2)}) collective-permute-start(bf16[1152,2304]{1,0:T(8,128)(2,1)} %shard_map.251.refs_2_), channel_id=1, source_target_pairs={{0,2},{2,0},{1,3},{3,1},{4,6},{6,4},{5,7},{7,5},{8,10},{10,8},{9,1... | collective-permute-start | bytes 15925256 | tf_op jit(solution)/shard_map/ppermute | solution.py:178
  472.3 37.3 %collective-permute-start.34 = (bf16[576,1152]{1,0:T(8,128)(2,1)S(1)}, bf16[576,1152]{1,0:T(8,128)(2,1)}, u32[]{:S(2)}, u32[]{:S(2)}) collective-permute-start(bf16[576,1152]{1,0:T(8,128)(2,1)S(1)} %pad_maximum_fusion.2), channel_id=1, source_target_pairs={{0,1},{1,0},{2,3},{3,2},{4,5},{5,4},{6,7},{7,6},{8,9},{9,8},{10,11... | collective-permute-start | bytes 3981320 | tf_op jit(solution)/shard_map/ppermute | solution.py:178
  473.1 36.5 %collective-permute-start.35 = (bf16[576,1152]{1,0:T(8,128)(2,1)S(1)}, bf16[576,1152]{1,0:T(8,128)(2,1)}, u32[]{:S(2)}, u32[]{:S(2)}) collective-permute-start(bf16[576,1152]{1,0:T(8,128)(2,1)S(1)} %pad_maximum_fusion.3), channel_id=1, source_target_pairs={{0,4},{4,0},{1,5},{5,1},{2,6},{6,2},{3,7},{7,3},{8,12},{12,8},{9,1... | collective-permute-start | bytes 3981320 | tf_op jit(solution)/shard_map/ppermute | solution.py:178
  473.6 36.0 %collective-permute-start.37 = (bf16[128,2304]{1,0:T(8,128)(2,1)}, bf16[128,2304]{1,0:T(8,128)(2,1)S(1)}, u32[]{:S(2)}, u32[]{:S(2)}) collective-permute-start(bf16[128,2304]{1,0:T(8,128)(2,1)} %get-tuple-element.321), channel_id=1, source_target_pairs={{0,8},{8,0},{16,24},{24,16},{1,9},{9,1},{17,25},{25,17},{2,10},{10... | collective-permute-start | bytes 1769480 | tf_op jit(solution)/shard_map/ppermute | solution.py:178
  515.5 40.1 %collective-permute-start.41 = (bf16[432,1152]{1,0:T(8,128)(2,1)}, bf16[432,1152]{1,0:T(8,128)(2,1)}, u32[]{:S(2)}, u32[]{:S(2)}) collective-permute-start(bf16[432,1152]{1,0:T(8,128)(2,1)} %slice.167), channel_id=1, source_target_pairs={{0,4},{4,0},{1,5},{5,1},{2,6},{6,2},{3,7},{7,3},{8,12},{12,8},{9,1... | collective-permute-start | bytes 2985992 | tf_op jit(solution)/shard_map/ppermute | solution.py:178
  517.8 37.0 %collective-permute-start.42 = (bf16[288,1152]{1,0:T(8,128)(2,1)}, bf16[288,1152]{1,0:T(8,128)(2,1)}, u32[]{:S(2)}, u32[]{:S(2)}) collective-permute-start(bf16[288,1152]{1,0:T(8,128)(2,1)} %get-tuple-element.482), channel_id=1, source_target_pairs={{0,1},{1,0},{2,3},{3,2},{4,5},{5,4},{6,7},{7,6},{8,9},{9,8},{10,11... | collective-permute-start | bytes 1990664 | tf_op jit(solution)/shard_map/ppermute | solution.py:178
  518.2 36.7 %collective-permute-start.43 = (bf16[288,1152]{1,0:T(8,128)(2,1)}, bf16[288,1152]{1,0:T(8,128)(2,1)}, u32[]{:S(2)}, u32[]{:S(2)}) collective-permute-start(bf16[288,1152]{1,0:T(8,128)(2,1)} %get-tuple-element.481), channel_id=1, source_target_pairs={{0,4},{4,0},{1,5},{5,1},{2,6},{6,2},{3,7},{7,3},{8,12},{12,8},{9,1... | collective-permute-start | bytes 1990664 | tf_op jit(solution)/shard_map/ppermute | solution.py:178
  558.4 38.6 %collective-permute-start.47 = (bf16[576,1152]{1,0:T(8,128)(2,1)S(1)}, bf16[576,1152]{1,0:T(8,128)(2,1)S(1)}, u32[]{:S(2)}, u32[]{:S(2)}) collective-permute-start(bf16[576,1152]{1,0:T(8,128)(2,1)S(1)} %pad_maximum_fusion.4), channel_id=1, source_target_pairs={{0,1},{1,0},{2,3},{3,2},{4,5},{5,4},{6,7},{7,6},{8,9},{9,8},{10,11... | collective-permute-start | bytes 3981320 | tf_op jit(solution)/shard_map/ppermute | solution.py:178
  561.1 36.0 %collective-permute-start.48 = (bf16[576,1152]{1,0:T(8,128)(2,1)S(1)}, bf16[576,1152]{1,0:T(8,128)(2,1)}, u32[]{:S(2)}, u32[]{:S(2)}) collective-permute-start(bf16[576,1152]{1,0:T(8,128)(2,1)S(1)} %pad_maximum_fusion.5), channel_id=1, source_target_pairs={{0,4},{4,0},{1,5},{5,1},{2,6},{6,2},{3,7},{7,3},{8,12},{12,8},{9,1... | collective-permute-start | bytes 3981320 | tf_op jit(solution)/shard_map/ppermute | solution.py:178
  598.7 37.6 %collective-permute-start.49 = (bf16[576,1152]{1,0:T(8,128)(2,1)S(1)}, bf16[576,1152]{1,0:T(8,128)(2,1)}, u32[]{:S(2)}, u32[]{:S(2)}) collective-permute-start(bf16[576,1152]{1,0:T(8,128)(2,1)S(1)} %pad_maximum_fusion.6), channel_id=1, source_target_pairs={{0,1},{1,0},{2,3},{3,2},{4,5},{5,4},{6,7},{7,6},{8,9},{9,8},{10,11... | collective-permute-start | bytes 3981320 | tf_op jit(solution)/shard_map/ppermute | solution.py:178
  600.7 35.7 %collective-permute-start.50 = (bf16[576,1152]{1,0:T(8,128)(2,1)S(1)}, bf16[576,1152]{1,0:T(8,128)(2,1)S(1)}, u32[]{:S(2)}, u32[]{:S(2)}) collective-permute-start(bf16[576,1152]{1,0:T(8,128)(2,1)S(1)} %pad_maximum_fusion.7), channel_id=1, source_target_pairs={{0,4},{4,0},{1,5},{5,1},{2,6},{6,2},{3,7},{7,3},{8,12},{12,8},{9,1... | collective-permute-start | bytes 3981320 | tf_op jit(solution)/shard_map/ppermute | solution.py:178
  636.4 39.9 %collective-permute-start.59 = (bf16[288,3072]{1,0:T(8,128)(2,1)}, bf16[288,3072]{1,0:T(8,128)(2,1)S(1)}, u32[]{:S(2)}, u32[]{:S(2)}) collective-permute-start(bf16[288,3072]{1,0:T(8,128)(2,1)} %get-tuple-element.388), channel_id=1, source_target_pairs={{0,4},{4,0},{1,5},{5,1},{2,6},{6,2},{3,7},{7,3},{8,12},{12,8},{9,1... | collective-permute-start | bytes 5308424 | tf_op jit(solution)/shard_map/ppermute | solution.py:178
  637.1 41.1 %collective-permute-start.55 = (bf16[128,2304]{1,0:T(8,128)(2,1)S(1)}, bf16[128,2304]{1,0:T(8,128)(2,1)S(1)}, u32[]{:S(2)}, u32[]{:S(2)}) collective-permute-start(bf16[128,2304]{1,0:T(8,128)(2,1)S(1)} %get-tuple-element.382), channel_id=1, source_target_pairs={{0,1},{1,0},{2,3},{3,2},{4,5},{5,4},{6,7},{7,6},{8,9},{9,8},{10,11... | collective-permute-start | bytes 1769480 | tf_op jit(solution)/shard_map/ppermute | solution.py:178
  640.6 37.6 %collective-permute-start.56 = (bf16[144,1152]{1,0:T(8,128)(2,1)S(1)}, bf16[144,1152]{1,0:T(8,128)(2,1)S(1)}, u32[]{:S(2)}, u32[]{:S(2)}) collective-permute-start(bf16[144,1152]{1,0:T(8,128)(2,1)S(1)} %get-tuple-element.471), channel_id=1, source_target_pairs={{0,8},{8,0},{16,24},{24,16},{1,9},{9,1},{17,25},{25,17},{2,10},{10... | collective-permute-start | bytes 995336 | tf_op jit(solution)/shard_map/ppermute | solution.py:178
  640.7 37.5 %collective-permute-start.57 = (bf16[144,1152]{1,0:T(8,128)(2,1)S(1)}, bf16[144,1152]{1,0:T(8,128)(2,1)S(1)}, u32[]{:S(2)}, u32[]{:S(2)}) collective-permute-start(bf16[144,1152]{1,0:T(8,128)(2,1)S(1)} %get-tuple-element.470), channel_id=1, source_target_pairs={{0,16},{8,24},{16,0},{24,8},{1,17},{9,25},{17,1},{25,9},{2,18},{10... | collective-permute-start | bytes 995336 | tf_op jit(solution)/shard_map/ppermute | solution.py:178
  678.2 39.1 %collective-permute-start.62 = (bf16[288,3072]{1,0:T(8,128)(2,1)}, bf16[288,3072]{1,0:T(8,128)(2,1)}, u32[]{:S(2)}, u32[]{:S(2)}) collective-permute-start(bf16[288,3072]{1,0:T(8,128)(2,1)} %get-tuple-element.393), channel_id=1, source_target_pairs={{0,4},{4,0},{1,5},{5,1},{2,6},{6,2},{3,7},{7,3},{8,12},{12,8},{9,1... | collective-permute-start | bytes 5308424 | tf_op jit(solution)/shard_map/ppermute | solution.py:178
  678.6 38.8 %collective-permute-start.63 = (bf16[288,3072]{1,0:T(8,128)(2,1)}, bf16[288,3072]{1,0:T(8,128)(2,1)}, u32[]{:S(2)}, u32[]{:S(2)}) collective-permute-start(bf16[288,3072]{1,0:T(8,128)(2,1)} %add_convert_fusion), channel_id=1, source_target_pairs={{0,8},{8,0},{16,24},{24,16},{1,9},{9,1},{17,25},{25,17},{2,10},{10... | collective-permute-start | bytes 5308424 | tf_op jit(solution)/shard_map/ppermute | solution.py:178
  722.2 38.3 %collective-permute-start.68 = (bf16[144,3072]{1,0:T(8,128)(2,1)}, bf16[144,3072]{1,0:T(8,128)(2,1)}, u32[]{:S(2)}, u32[]{:S(2)}) collective-permute-start(bf16[144,3072]{1,0:T(8,128)(2,1)} %add_convert_fusion.5), channel_id=1, source_target_pairs={{0,16},{8,24},{16,0},{24,8},{1,17},{9,25},{17,1},{25,9},{2,18},{10... | collective-permute-start | bytes 2654216 | tf_op jit(solution)/shard_map/ppermute | solution.py:178
  722.9 37.0 %collective-permute-start.67 = (f32[4,144]{1,0:T(4,128)S(1)}, f32[4,144]{1,0:T(4,128)S(1)}, u32[]{:S(2)}, u32[]{:S(2)}) collective-permute-start(f32[4,144]{1,0:T(4,128)S(1)} %bitcast.110), channel_id=1, source_target_pairs={{0,24},{8,16},{16,8},{24,0},{1,25},{9,17},{17,9},{25,1},{2,26},{10... | collective-permute-start | bytes 6920 | tf_op jit(solution)/shard_map/ppermute | solution.py:178
  724.1 35.9 %collective-permute-start.66 = (f32[4,144]{1,0:T(4,128)S(1)}, f32[4,144]{1,0:T(4,128)S(1)}, u32[]{:S(2)}, u32[]{:S(2)}) collective-permute-start(f32[4,144]{1,0:T(4,128)S(1)} %bitcast.111), channel_id=1, source_target_pairs={{0,16},{8,24},{16,0},{24,8},{1,17},{9,25},{17,1},{25,9},{2,18},{10... | collective-permute-start | bytes 6920 | tf_op jit(solution)/shard_map/ppermute | solution.py:178
  (149 other events, 2066.5 us)
Sparse Core Ops, SparseCore 0:
  13.9 172.8 all-gather.2
  234.2 63.0 all-gather.4

commit v8 on v7

--- a/solution.py
+++ b/solution.py
@@ -125,14 +125,16 @@
     gate_w, up_w, down_w, (gate, up), (d_gate, d_up), outs, total = (
         refs[:2], refs[2:4], refs[4:5], refs[5:7], refs[7:9], refs[9:-1], refs[-1]
     )
-    gate_at, up_at, down_at = (find(ids) for find in columns)
+    gate_at, _, down_at = (find(ids) for find in columns)
     d_act = inner(d, down_w, down_at)
     bent, slope = gelu_parts(gate[...])
     gate_tile = (d_act * up[...] * slope).astype(BF)
     up_tile = (d_act * bent).astype(BF)
     d_gate[...], d_up[...] = gate_tile, up_tile
-    outer_add(total, gate_tile, gate_w, gate_at, pl.program_id(0) == 0)
-    outer_add(total, up_tile, up_w, up_at, False)
+    fresh = pl.program_id(0) == 0
+    for at, gate_ref, up_ref in zip(gate_at, gate_w, up_w):
+        part = tile_dot_cols(gate_tile, gate_ref[...]) + tile_dot_cols(up_tile, up_ref[...])
+        total[:, at] = jnp.where(fresh, part, total[:, at] + part)
 
     @pl.when(pl.program_id(0) == pl.num_programs(0) - 1)
     def _():

time: 779 us -> 779 us (level)
  no operation moved by 1% of the time
where the time goes in v8:
time: 779 us; the launch traced here: 772 us
  waiting for transfers between devices  385 us (49%)
  Pallas kernels  182 us (23%)
  starting transfers between devices  75 us (10%)
  local copies, waits for them, and re-layouts  63.5 us (8%)
  other arithmetic  51.1 us (7%)
  between operations  15.8 us (2%)
    ppermute x69, waiting for transfers between devices, swap(): return lax.ppermute(values, axis, [(i, i ^ mask) for i in range(size)])  385 us
    ppermute x69, starting transfers between devices, swap(): return lax.ppermute(values, axis, [(i, i ^ mask) for i in range(size)])  75 us
    pallas_call x3, Pallas kernels, ffn_call(): pl.pallas_call(functools.partial(kernel, [weight.columns for weight in we...  67.9 us
    pallas_call x4, Pallas kernels, outer_quarters(): pl.pallas_call(outer_quarters_kernel, grid_spec=pltpu.PrefetchScalarGridS...  34.3 us
    unnamed x234, local copies, waits for them, and re-layouts  32.4 us
    pallas_call x8, Pallas kernels, assemble(): pl.pallas_call(functools.partial(assemble_kernel, counts), grid_spec=pltp...  29.1 us
  transfers between devices with their start and end apart: 71, of which 30 were waited for; matrix products, arithmetic and copies ran while one was open for 9% of the time, Pallas kernels for 20%

profile of v8, /device:TPU:8, one launch (start us, length us, event | category | flops | bytes accessed | tf_op | source)
XLA Modules:
  0.0 772.2 jit_solution(17319477617989487382)
XLA Ops:
  34.1 9.7 %collective-permute-done.1.refs_2_ = bf16[144,1152]{1,0:T(8,128)(2,1)S(1)} collective-permute-done((bf16[144,1152]{1,0:T(8,128)(2,1)}, bf16[144,1152]{1,0:T(8,128)(2,1)S(1)}, u32[]{:S(2)}, u32[]{:S(2)}) %collective-permute-start.1) | collective-permute-done | bytes 331808 | tf_op jit(solution)/shard_map/ppermute | solution.py:180
  43.7 25.0 %collective-permute-done.2.refs_3_ = bf16[144,1152]{1,0:T(8,128)(2,1)S(1)} collective-permute-done((bf16[144,1152]{1,0:T(8,128)(2,1)S(1)}, bf16[144,1152]{1,0:T(8,128)(2,1)S(1)}, u32[]{:S(2)}, u32[]{:S(2)}) %collective-permute-start.2) | collective-permute-done | bytes 331808 | tf_op jit(solution)/shard_map/ppermute | solution.py:180
  80.6 9.1 %collective-permute-done.6.refs_1_ = bf16[144,1152]{1,0:T(8,128)(2,1)S(1)} collective-permute-done((bf16[144,1152]{1,0:T(8,128)(2,1)S(1)}, bf16[144,1152]{1,0:T(8,128)(2,1)S(1)}, u32[]{:S(2)}, u32[]{:S(2)}) %collective-permute-start.6) | collective-permute-done | bytes 331808 | tf_op jit(solution)/shard_map/ppermute | solution.py:180
  89.7 22.8 %collective-permute-done.7.refs_2_ = bf16[144,1152]{1,0:T(8,128)(2,1)S(1)} collective-permute-done((bf16[144,1152]{1,0:T(8,128)(2,1)S(1)}, bf16[144,1152]{1,0:T(8,128)(2,1)S(1)}, u32[]{:S(2)}, u32[]{:S(2)}) %collective-permute-start.7) | collective-permute-done | bytes 331808 | tf_op jit(solution)/shard_map/ppermute | solution.py:180
  112.5 21.7 %collective-permute-done.8.refs_3_ = bf16[144,1152]{1,0:T(8,128)(2,1)S(1)} collective-permute-done((bf16[144,1152]{1,0:T(8,128)(2,1)S(1)}, bf16[144,1152]{1,0:T(8,128)(2,1)S(1)}, u32[]{:S(2)}, u32[]{:S(2)}) %collective-permute-start.8) | collective-permute-done | bytes 331808 | tf_op jit(solution)/shard_map/ppermute | solution.py:180
  148.3 17.2 %collective-permute-done.9.refs_1_ = bf16[144,1152]{1,0:T(8,128)(2,1)S(1)} collective-permute-done((bf16[144,1152]{1,0:T(8,128)(2,1)}, bf16[144,1152]{1,0:T(8,128)(2,1)S(1)}, u32[]{:S(2)}, u32[]{:S(2)}) %collective-permute-start.9) | collective-permute-done | bytes 331808 | tf_op jit(solution)/shard_map/ppermute | solution.py:180
  166.5 9.1 %collective-permute-done.10.refs_2_ = bf16[144,1152]{1,0:T(8,128)(2,1)S(1)} collective-permute-done((bf16[144,1152]{1,0:T(8,128)(2,1)}, bf16[144,1152]{1,0:T(8,128)(2,1)S(1)}, u32[]{:S(2)}, u32[]{:S(2)}) %collective-permute-start.10) | collective-permute-done | bytes 331808 | tf_op jit(solution)/shard_map/ppermute | solution.py:180
  177.0 12.5 %collective-permute-done.11.refs_3_ = bf16[144,1152]{1,0:T(8,128)(2,1)S(1)} collective-permute-done((bf16[144,1152]{1,0:T(8,128)(2,1)S(1)}, bf16[144,1152]{1,0:T(8,128)(2,1)S(1)}, u32[]{:S(2)}, u32[]{:S(2)}) %collective-permute-start.11) | collective-permute-done | bytes 331808 | tf_op jit(solution)/shard_map/ppermute | solution.py:180
  200.4 10.2 %shard_map.248 = (bf16[256,1024]{1,0:T(8,128)(2,1)S(1)}, bf16[256,512]{1,0:T(8,128)(2,1)S(1)}, bf16[256,512]{1,0:T(8,128)(2,1)S(1)}, bf16[256,1024]{1,0:T(8,128)...) custom-call(s32[4]{0:T(128)S(1)} %copy-done.40, bf16[256,2304]{1,0:T(8,128)(2,1)} %pad_maximum_fusion.8.x.left_a, ...), custom_call_target="tpu_custom_call" | custom-call | tf_op jit(solution)/shard_map/pallas_call | solution.py:449
  218.2 7.6 shard_map.250.refs_0_
  225.8 8.3 %shard_map.251.refs_2_ = bf16[1152,2304]{1,0:T(8,128)(2,1)} custom-call(s32[8]{0:T(128)S(1)} %copy-done.52, s32[8]{0:T(128)S(1)} %copy-done.50, bf16[576,1152]{1,0:T(8,128)(2,1)} %shard_map.247.refs_0_, bf16[576,1152]{1,0:T(8,128)(2,1)} %collective-permute-done.15.refs_1_, bf16[576,1152]{1,0:T(8,128)(2,1)} %collective-permute-done.14.refs_2_, ...), custom_call_target="tpu_custom_call" | custom-call | tf_op jit(solution)/shard_map/pallas_call | solution.py:804
  242.3 22.7 %collective-permute-done.21 = bf16[128,2304]{1,0:T(8,128)(2,1)S(1)} collective-permute-done((bf16[128,2304]{1,0:T(8,128)(2,1)S(1)}, bf16[128,2304]{1,0:T(8,128)(2,1)S(1)}, u32[]{:S(2)}, u32[]{:S(2)}) %collective-permute-start.21) | collective-permute-done | bytes 589856 | tf_op jit(solution)/shard_map/ppermute | solution.py:180
  268.5 12.9 %collective-permute-done.22 = bf16[128,2304]{1,0:T(8,128)(2,1)S(1)} collective-permute-done((bf16[128,2304]{1,0:T(8,128)(2,1)S(1)}, bf16[128,2304]{1,0:T(8,128)(2,1)S(1)}, u32[]{:S(2)}, u32[]{:S(2)}) %collective-permute-start.22) | collective-permute-done | bytes 589856 | tf_op jit(solution)/shard_map/ppermute | solution.py:180
  283.0 21.0 %shard_map.252 = (bf16[512,2304]{1,0:T(8,128)(2,1)}, f32[512,2304]{1,0:T(8,128)}, f32[512,2304]{1,0:T(8,128)}) custom-call(s32[4]{0:T(128)} %pad_add_fusion.ids, bf16[512,2304]{1,0:T(8,128)(2,1)} %pad_maximum_fusion.x.left, bf16[1152,2304]{1,0:T(8,128)(2,1)} %shard_map.250.refs_0_, bf16[1152,2304]{1,0:T(8,128)(2,1)} %collective-permute-done.19.refs_1_, ...), custom_call_target="tpu_custom_call" | custom-call | tf_op jit(solution)/shard_map/pallas_call | solution.py:150
  304.0 12.4 %shard_map.253 = (f32[128,2304]{1,0:T(8,128)}, bf16[128,2304]{1,0:T(8,128)(2,1)}, bf16[128,2304]{1,0:T(8,128)(2,1)}, bf16[128,2304]{1,0:T(8,128)(2,1)}) custom-call(s32[4]{0:T(128)} %pad_add_fusion.ids, bf16[512,2304]{1,0:T(8,128)(2,1)} %get-tuple-element.290.act.right, bf16[2,2304,1152]{2,1,0:T(8,128)(2,1)} %bitcast.93), custom_call_target="tpu_custom_call" | custom-call | tf_op jit(solution)/shard_map/pallas_call | solution.py:150
  318.5 14.4 %collective-permute-done.25 = bf16[128,2304]{1,0:T(8,128)(2,1)S(1)} collective-permute-done((bf16[128,2304]{1,0:T(8,128)(2,1)}, bf16[128,2304]{1,0:T(8,128)(2,1)S(1)}, u32[]{:S(2)}, u32[]{:S(2)}) %collective-permute-start.25) | collective-permute-done | bytes 589856 | tf_op jit(solution)/shard_map/ppermute | solution.py:180
  340.0 11.7 %collective-permute-done.24 = bf16[128,2304]{1,0:T(8,128)(2,1)} collective-permute-done((bf16[128,2304]{1,0:T(8,128)(2,1)}, bf16[128,2304]{1,0:T(8,128)(2,1)}, u32[]{:S(2)}, u32[]{:S(2)}) %collective-permute-start.24) | collective-permute-done | bytes 589856 | tf_op jit(solution)/shard_map/ppermute | solution.py:180
  365.4 18.9 %collective-permute-done.28 = bf16[128,2304]{1,0:T(8,128)(2,1)S(1)} collective-permute-done((bf16[128,2304]{1,0:T(8,128)(2,1)S(1)}, bf16[128,2304]{1,0:T(8,128)(2,1)S(1)}, u32[]{:S(2)}, u32[]{:S(2)}) %collective-permute-start.28) | collective-permute-done | bytes 589856 | tf_op jit(solution)/shard_map/ppermute | solution.py:180
  387.5 12.2 %collective-permute-done.29 = bf16[128,2304]{1,0:T(8,128)(2,1)S(1)} collective-permute-done((bf16[128,2304]{1,0:T(8,128)(2,1)S(1)}, bf16[128,2304]{1,0:T(8,128)(2,1)S(1)}, u32[]{:S(2)}, u32[]{:S(2)}) %collective-permute-start.29) | collective-permute-done | bytes 589856 | tf_op jit(solution)/shard_map/ppermute | solution.py:180
  407.4 34.6 %shard_map.254 = (bf16[512,2304]{1,0:T(8,128)(2,1)}, bf16[512,2304]{1,0:T(8,128)(2,1)}, f32[128,2304]{1,0:T(8,128)}, bf16[128,2304]{1,0:T(8,128)(2,1)}, bf16[128...) custom-call(s32[4]{0:T(128)} %pad_add_fusion.ids, bf16[512,2304]{1,0:T(8,128)(2,1)} %copy-done.1, ...), custom_call_target="tpu_custom_call" | custom-call | tf_op jit(solution)/shard_map/pallas_call | solution.py:150
  441.9 8.9 %shard_map.256 = (bf16[576,1152]{1,0:T(8,128)(2,1)S(1)}, bf16[576,1152]{1,0:T(8,128)(2,1)S(1)}, bf16[576,1152]{1,0:T(8,128)(2,1)S(1)}, bf16[576,1152]{1,0:T(8,128)(2,1)}) custom-call(s32[4]{0:T(128)S(1)} %copy-done.42, s32[1]{0:T(128)} %bitcast.5.which, bf16[512,2304]{1,0:T(8,128)(2,1)} %copy-done.1, bf16[512,2304]{1,0:T(8,128)(2,1)} %get-tuple-element.290.act.right, ...), custom_call_target="tpu_custom_call" | custom-call | tf_op jit(solution)/shard_map/pallas_call | solution.py:649
  456.9 11.8 %shard_map.257 = bf16[4,576,2304]{2,1,0:T(8,128)(2,1)} custom-call(s32[4]{0:T(128)S(1)} %copy-done.42, s32[1]{0:T(128)S(6)} %sub.44.which, bf16[512,2304]{1,0:T(8,128)(2,1)S(1)} %copy-done, bf16[512,2304]{1,0:T(8,128)(2,1)} %get-tuple-element.324.right_a.right, bf16[512,2304]{1,0:T(8,128)(2,1)} %get-tuple-element.314.right_b.right), custom_call_target="tpu_custom_call" | custom-call | tf_op jit(solution)/shard_map/pallas_call | solution.py:692
  476.9 11.9 %collective-permute-done.36.refs_0_.refs_1_.refs_2_.refs_3_ = bf16[4,576,2304]{2,1,0:T(8,128)(2,1)} collective-permute-done((bf16[4,576,2304]{2,1,0:T(8,128)(2,1)}, bf16[4,576,2304]{2,1,0:T(8,128)(2,1)}, u32[]{:S(2)}, u32[]{:S(2)}) %collective-permute-start.36) | collective-permute-done | bytes 10616864 | tf_op jit(solution)/shard_map/ppermute | solution.py:180
  488.7 8.7 %shard_map.258 = (bf16[576,1152]{1,0:T(8,128)(2,1)S(1)}, bf16[576,1152]{1,0:T(8,128)(2,1)S(1)}, bf16[576,1152]{1,0:T(8,128)(2,1)S(1)}, bf16[576,1152]{1,0:T(8,128)(2,1)}) custom-call(s32[4]{0:T(128)S(1)} %copy-done.42, s32[1]{0:T(128)} %bitcast.5.which, bf16[512,2304]{1,0:T(8,128)(2,1)} %pad_maximum_fusion.x.left, ...), custom_call_target="tpu_custom_call" | custom-call | tf_op jit(solution)/shard_map/pallas_call | solution.py:649
  499.6 9.1 %shard_map.259 = (bf16[576,1152]{1,0:T(8,128)(2,1)S(1)}, bf16[576,1152]{1,0:T(8,128)(2,1)S(1)}, bf16[576,1152]{1,0:T(8,128)(2,1)S(1)}, bf16[576,1152]{1,0:T(8,128)(2,1)}) custom-call(s32[4]{0:T(128)S(1)} %copy-done.42, s32[1]{0:T(128)} %bitcast.5.which, bf16[512,2304]{1,0:T(8,128)(2,1)} %pad_maximum_fusion.x.left, ...), custom_call_target="tpu_custom_call" | custom-call | tf_op jit(solution)/shard_map/pallas_call | solution.py:649
  523.8 31.3 %collective-permute-done.40 = bf16[144,1152]{1,0:T(8,128)(2,1)} collective-permute-done((bf16[144,1152]{1,0:T(8,128)(2,1)S(1)}, bf16[144,1152]{1,0:T(8,128)(2,1)}, u32[]{:S(2)}, u32[]{:S(2)}) %collective-permute-start.40) | collective-permute-done | bytes 331808 | tf_op jit(solution)/shard_map/ppermute | solution.py:180
  571.9 13.1 %shard_map.260 = (bf16[256,2048]{1,0:T(8,128)(2,1)S(1)}, bf16[128,2304]{1,0:T(8,128)(2,1)S(1)}, f32[128,2304]{1,0:T(8,128)}) custom-call(s32[4]{0:T(128)S(1)} %copy-done.43, bf16[256,2304]{1,0:T(8,128)(2,1)} %pad_maximum_fusion.9.d.left_b, bf16[2304,3072]{1,0:T(8,128)(2,1)} %all-gather.3.cloned.1.call-done.weight, f32[256,128]{1,0:T(8,128)S(1)} %get-tuple-element.512.cosine, ...), custom_call_target="tpu_custom_call" | custom-call | tf_op jit(solution)/shard_map/pallas_call | solution.py:504
  612.3 9.3 %shard_map.262 = (bf16[288,3072]{1,0:T(8,128)(2,1)}, bf16[288,3072]{1,0:T(8,128)(2,1)}, bf16[288,3072]{1,0:T(8,128)(2,1)}, bf16[288,3072]{1,0:T(8,128)(2,1)}) custom-call(s32[4]{0:T(128)S(1)} %copy-done.43, s32[1]{0:T(128)} %bitcast.5.which, bf16[256,2304]{1,0:T(8,128)(2,1)S(1)} %copy-done.2, bf16[256,2304]{1,0:T(8,128)(2,1)S(1)} %copy-done.3, ...), custom_call_target="tpu_custom_call" | custom-call | tf_op jit(solution)/shard_map/pallas_call | solution.py:755
  628.3 8.3 %collective-permute-done.54.refs_3_ = bf16[144,1152]{1,0:T(8,128)(2,1)S(1)} collective-permute-done((bf16[144,1152]{1,0:T(8,128)(2,1)S(1)}, bf16[144,1152]{1,0:T(8,128)(2,1)S(1)}, u32[]{:S(2)}, u32[]{:S(2)}) %collective-permute-start.54) | collective-permute-done | bytes 331808 | tf_op jit(solution)/shard_map/ppermute | solution.py:180
  644.4 32.0 %collective-permute-done.59 = bf16[288,3072]{1,0:T(8,128)(2,1)S(1)} collective-permute-done((bf16[288,3072]{1,0:T(8,128)(2,1)}, bf16[288,3072]{1,0:T(8,128)(2,1)S(1)}, u32[]{:S(2)}, u32[]{:S(2)}) %collective-permute-start.59) | collective-permute-done | bytes 1769504 | tf_op jit(solution)/shard_map/ppermute | solution.py:180
  693.3 24.2 %collective-permute-done.62 = bf16[288,3072]{1,0:T(8,128)(2,1)} collective-permute-done((bf16[288,3072]{1,0:T(8,128)(2,1)}, bf16[288,3072]{1,0:T(8,128)(2,1)}, u32[]{:S(2)}, u32[]{:S(2)}) %collective-permute-start.62) | collective-permute-done | bytes 1769504 | tf_op jit(solution)/shard_map/ppermute | solution.py:180
  734.4 25.7 %collective-permute-done.67 = f32[4,144]{1,0:T(4,128)S(1)} collective-permute-done((f32[4,144]{1,0:T(4,128)S(1)}, f32[4,144]{1,0:T(4,128)S(1)}, u32[]{:S(2)}, u32[]{:S(2)}) %collective-permute-start.67) | collective-permute-done | bytes 2336 | tf_op jit(solution)/shard_map/ppermute | solution.py:180
  (496 shorter events, 248.1 us)
Async XLA Ops:
  7.2 192.6 %all-gather.3.cloned.1.call-start = ((), (), s32[]{:S(2)}) async-start(), calls=%async_computation | async-start | bytes 15040512 | tf_op jit(solution)/shard_map/all_gather | solution.py:907
  13.8 290.2 %all-gather.5.cloned.1.call-start = ((), (), s32[]{:S(2)}) async-start(), calls=%async_computation.1 | async-start | bytes 11943936 | tf_op jit(solution)/shard_map/all_gather | solution.py:606
  17.9 50.9 %collective-permute-start.2 = (bf16[144,1152]{1,0:T(8,128)(2,1)S(1)}, bf16[144,1152]{1,0:T(8,128)(2,1)S(1)}, u32[]{:S(2)}, u32[]{:S(2)}) collective-permute-start(bf16[144,1152]{1,0:T(8,128)(2,1)S(1)} %get-tuple-element.489), channel_id=1, source_target_pairs={{0,24},{8,16},{16,8},{24,0},{1,25},{9,17},{17,9},{25,1},{2,26},{10... | collective-permute-start | bytes 995336 | tf_op jit(solution)/shard_map/ppermute | solution.py:180
  24.5 45.0 %collective-permute-start.3 = (bf16[128,2304]{1,0:T(8,128)(2,1)}, bf16[128,2304]{1,0:T(8,128)(2,1)}, u32[]{:S(2)}, u32[]{:S(2)}) collective-permute-start(bf16[128,2304]{1,0:T(8,128)(2,1)} %multiply_convert_fusion.3), channel_id=1, source_target_pairs={{0,1},{1,0},{2,3},{3,2},{4,5},{5,4},{6,7},{7,6},{8,9},{9,8},{10,11... | collective-permute-start | bytes 1769480 | tf_op jit(solution)/shard_map/ppermute | solution.py:180
  71.6 62.6 %collective-permute-start.4 = (bf16[576,1152]{1,0:T(8,128)(2,1)S(1)}, bf16[576,1152]{1,0:T(8,128)(2,1)S(1)}, u32[]{:S(2)}, u32[]{:S(2)}) collective-permute-start(bf16[576,1152]{1,0:T(8,128)(2,1)S(1)} %shard_map.246.refs_0_), channel_id=1, source_target_pairs={{0,1},{1,0},{2,3},{3,2},{4,5},{5,4},{6,7},{7,6},{8,9},{9,8},{10,11... | collective-permute-start | bytes 3981320 | tf_op jit(solution)/shard_map/ppermute | solution.py:180
  72.2 63.1 %collective-permute-start.5 = (bf16[576,1152]{1,0:T(8,128)(2,1)S(1)}, bf16[576,1152]{1,0:T(8,128)(2,1)}, u32[]{:S(2)}, u32[]{:S(2)}) collective-permute-start(bf16[576,1152]{1,0:T(8,128)(2,1)S(1)} %shard_map.246.refs_0_), channel_id=1, source_target_pairs={{0,4},{4,0},{1,5},{5,1},{2,6},{6,2},{3,7},{7,3},{8,12},{12,8},{9,1... | collective-permute-start | bytes 3981320 | tf_op jit(solution)/shard_map/ppermute | solution.py:180
  73.8 38.6 %collective-permute-start.7 = (bf16[144,1152]{1,0:T(8,128)(2,1)S(1)}, bf16[144,1152]{1,0:T(8,128)(2,1)S(1)}, u32[]{:S(2)}, u32[]{:S(2)}) collective-permute-start(bf16[144,1152]{1,0:T(8,128)(2,1)S(1)} %get-tuple-element.224), channel_id=1, source_target_pairs={{0,16},{8,24},{16,0},{24,8},{1,17},{9,25},{17,1},{25,9},{2,18},{10... | collective-permute-start | bytes 995336 | tf_op jit(solution)/shard_map/ppermute | solution.py:180
  78.1 56.0 %collective-permute-start.8 = (bf16[144,1152]{1,0:T(8,128)(2,1)S(1)}, bf16[144,1152]{1,0:T(8,128)(2,1)S(1)}, u32[]{:S(2)}, u32[]{:S(2)}) collective-permute-start(bf16[144,1152]{1,0:T(8,128)(2,1)S(1)} %get-tuple-element.225), channel_id=1, source_target_pairs={{0,24},{8,16},{16,8},{24,0},{1,25},{9,17},{17,9},{25,1},{2,26},{10... | collective-permute-start | bytes 995336 | tf_op jit(solution)/shard_map/ppermute | solution.py:180
  137.5 52.1 %collective-permute-start.14 = (bf16[576,1152]{1,0:T(8,128)(2,1)}, bf16[576,1152]{1,0:T(8,128)(2,1)}, u32[]{:S(2)}, u32[]{:S(2)}) collective-permute-start(bf16[576,1152]{1,0:T(8,128)(2,1)} %shard_map.247.refs_0_), channel_id=1, source_target_pairs={{0,1},{1,0},{2,3},{3,2},{4,5},{5,4},{6,7},{7,6},{8,9},{9,8},{10,11... | collective-permute-start | bytes 3981320 | tf_op jit(solution)/shard_map/ppermute | solution.py:180
  139.2 50.3 %collective-permute-start.15 = (bf16[576,1152]{1,0:T(8,128)(2,1)}, bf16[576,1152]{1,0:T(8,128)(2,1)}, u32[]{:S(2)}, u32[]{:S(2)}) collective-permute-start(bf16[576,1152]{1,0:T(8,128)(2,1)} %shard_map.247.refs_0_), channel_id=1, source_target_pairs={{0,4},{4,0},{1,5},{5,1},{2,6},{6,2},{3,7},{7,3},{8,12},{12,8},{9,1... | collective-permute-start | bytes 3981320 | tf_op jit(solution)/shard_map/ppermute | solution.py:180
  146.3 43.3 %collective-permute-start.12 = (bf16[288,1152]{1,0:T(8,128)(2,1)S(1)}, bf16[288,1152]{1,0:T(8,128)(2,1)S(1)}, u32[]{:S(2)}, u32[]{:S(2)}) collective-permute-start(bf16[288,1152]{1,0:T(8,128)(2,1)S(1)} %slice.148), channel_id=1, source_target_pairs={{0,1},{1,0},{2,3},{3,2},{4,5},{5,4},{6,7},{7,6},{8,9},{9,8},{10,11... | collective-permute-start | bytes 1990664 | tf_op jit(solution)/shard_map/ppermute | solution.py:180
  234.1 48.9 %collective-permute-start.19 = (bf16[1152,2304]{1,0:T(8,128)(2,1)}, bf16[1152,2304]{1,0:T(8,128)(2,1)}, u32[]{:S(2)}, u32[]{:S(2)}) collective-permute-start(bf16[1152,2304]{1,0:T(8,128)(2,1)} %shard_map.250.refs_0_), channel_id=1, source_target_pairs={{0,2},{2,0},{1,3},{3,1},{4,6},{6,4},{5,7},{7,5},{8,10},{10,8},{9,1... | collective-permute-start | bytes 15925256 | tf_op jit(solution)/shard_map/ppermute | solution.py:180
  234.2 48.8 %collective-permute-start.23 = (bf16[1152,2304]{1,0:T(8,128)(2,1)}, bf16[1152,2304]{1,0:T(8,128)(2,1)}, u32[]{:S(2)}, u32[]{:S(2)}) collective-permute-start(bf16[1152,2304]{1,0:T(8,128)(2,1)} %shard_map.251.refs_2_), channel_id=1, source_target_pairs={{0,2},{2,0},{1,3},{3,1},{4,6},{6,4},{5,7},{7,5},{8,10},{10,8},{9,1... | collective-permute-start | bytes 15925256 | tf_op jit(solution)/shard_map/ppermute | solution.py:180
  472.4 37.5 %collective-permute-start.34 = (bf16[576,1152]{1,0:T(8,128)(2,1)S(1)}, bf16[576,1152]{1,0:T(8,128)(2,1)}, u32[]{:S(2)}, u32[]{:S(2)}) collective-permute-start(bf16[576,1152]{1,0:T(8,128)(2,1)S(1)} %pad_maximum_fusion.2), channel_id=1, source_target_pairs={{0,1},{1,0},{2,3},{3,2},{4,5},{5,4},{6,7},{7,6},{8,9},{9,8},{10,11... | collective-permute-start | bytes 3981320 | tf_op jit(solution)/shard_map/ppermute | solution.py:180
  473.2 36.7 %collective-permute-start.35 = (bf16[576,1152]{1,0:T(8,128)(2,1)S(1)}, bf16[576,1152]{1,0:T(8,128)(2,1)}, u32[]{:S(2)}, u32[]{:S(2)}) collective-permute-start(bf16[576,1152]{1,0:T(8,128)(2,1)S(1)} %pad_maximum_fusion.3), channel_id=1, source_target_pairs={{0,4},{4,0},{1,5},{5,1},{2,6},{6,2},{3,7},{7,3},{8,12},{12,8},{9,1... | collective-permute-start | bytes 3981320 | tf_op jit(solution)/shard_map/ppermute | solution.py:180
  473.6 36.2 %collective-permute-start.37 = (bf16[128,2304]{1,0:T(8,128)(2,1)}, bf16[128,2304]{1,0:T(8,128)(2,1)S(1)}, u32[]{:S(2)}, u32[]{:S(2)}) collective-permute-start(bf16[128,2304]{1,0:T(8,128)(2,1)} %get-tuple-element.321), channel_id=1, source_target_pairs={{0,8},{8,0},{16,24},{24,16},{1,9},{9,1},{17,25},{25,17},{2,10},{10... | collective-permute-start | bytes 1769480 | tf_op jit(solution)/shard_map/ppermute | solution.py:180
  515.7 40.1 %collective-permute-start.41 = (bf16[432,1152]{1,0:T(8,128)(2,1)}, bf16[432,1152]{1,0:T(8,128)(2,1)}, u32[]{:S(2)}, u32[]{:S(2)}) collective-permute-start(bf16[432,1152]{1,0:T(8,128)(2,1)} %slice.167), channel_id=1, source_target_pairs={{0,4},{4,0},{1,5},{5,1},{2,6},{6,2},{3,7},{7,3},{8,12},{12,8},{9,1... | collective-permute-start | bytes 2985992 | tf_op jit(solution)/shard_map/ppermute | solution.py:180
  518.0 37.0 %collective-permute-start.42 = (bf16[288,1152]{1,0:T(8,128)(2,1)}, bf16[288,1152]{1,0:T(8,128)(2,1)}, u32[]{:S(2)}, u32[]{:S(2)}) collective-permute-start(bf16[288,1152]{1,0:T(8,128)(2,1)} %get-tuple-element.482), channel_id=1, source_target_pairs={{0,1},{1,0},{2,3},{3,2},{4,5},{5,4},{6,7},{7,6},{8,9},{9,8},{10,11... | collective-permute-start | bytes 1990664 | tf_op jit(solution)/shard_map/ppermute | solution.py:180
  518.4 36.7 %collective-permute-start.43 = (bf16[288,1152]{1,0:T(8,128)(2,1)}, bf16[288,1152]{1,0:T(8,128)(2,1)}, u32[]{:S(2)}, u32[]{:S(2)}) collective-permute-start(bf16[288,1152]{1,0:T(8,128)(2,1)} %get-tuple-element.481), channel_id=1, source_target_pairs={{0,4},{4,0},{1,5},{5,1},{2,6},{6,2},{3,7},{7,3},{8,12},{12,8},{9,1... | collective-permute-start | bytes 1990664 | tf_op jit(solution)/shard_map/ppermute | solution.py:180
  558.6 38.6 %collective-permute-start.47 = (bf16[576,1152]{1,0:T(8,128)(2,1)S(1)}, bf16[576,1152]{1,0:T(8,128)(2,1)S(1)}, u32[]{:S(2)}, u32[]{:S(2)}) collective-permute-start(bf16[576,1152]{1,0:T(8,128)(2,1)S(1)} %pad_maximum_fusion.4), channel_id=1, source_target_pairs={{0,1},{1,0},{2,3},{3,2},{4,5},{5,4},{6,7},{7,6},{8,9},{9,8},{10,11... | collective-permute-start | bytes 3981320 | tf_op jit(solution)/shard_map/ppermute | solution.py:180
  561.2 36.0 %collective-permute-start.48 = (bf16[576,1152]{1,0:T(8,128)(2,1)S(1)}, bf16[576,1152]{1,0:T(8,128)(2,1)}, u32[]{:S(2)}, u32[]{:S(2)}) collective-permute-start(bf16[576,1152]{1,0:T(8,128)(2,1)S(1)} %pad_maximum_fusion.5), channel_id=1, source_target_pairs={{0,4},{4,0},{1,5},{5,1},{2,6},{6,2},{3,7},{7,3},{8,12},{12,8},{9,1... | collective-permute-start | bytes 3981320 | tf_op jit(solution)/shard_map/ppermute | solution.py:180
  598.9 37.6 %collective-permute-start.49 = (bf16[576,1152]{1,0:T(8,128)(2,1)S(1)}, bf16[576,1152]{1,0:T(8,128)(2,1)}, u32[]{:S(2)}, u32[]{:S(2)}) collective-permute-start(bf16[576,1152]{1,0:T(8,128)(2,1)S(1)} %pad_maximum_fusion.6), channel_id=1, source_target_pairs={{0,1},{1,0},{2,3},{3,2},{4,5},{5,4},{6,7},{7,6},{8,9},{9,8},{10,11... | collective-permute-start | bytes 3981320 | tf_op jit(solution)/shard_map/ppermute | solution.py:180
  600.9 35.7 %collective-permute-start.50 = (bf16[576,1152]{1,0:T(8,128)(2,1)S(1)}, bf16[576,1152]{1,0:T(8,128)(2,1)S(1)}, u32[]{:S(2)}, u32[]{:S(2)}) collective-permute-start(bf16[576,1152]{1,0:T(8,128)(2,1)S(1)} %pad_maximum_fusion.7), channel_id=1, source_target_pairs={{0,4},{4,0},{1,5},{5,1},{2,6},{6,2},{3,7},{7,3},{8,12},{12,8},{9,1... | collective-permute-start | bytes 3981320 | tf_op jit(solution)/shard_map/ppermute | solution.py:180
  636.6 39.9 %collective-permute-start.59 = (bf16[288,3072]{1,0:T(8,128)(2,1)}, bf16[288,3072]{1,0:T(8,128)(2,1)S(1)}, u32[]{:S(2)}, u32[]{:S(2)}) collective-permute-start(bf16[288,3072]{1,0:T(8,128)(2,1)} %get-tuple-element.388), channel_id=1, source_target_pairs={{0,4},{4,0},{1,5},{5,1},{2,6},{6,2},{3,7},{7,3},{8,12},{12,8},{9,1... | collective-permute-start | bytes 5308424 | tf_op jit(solution)/shard_map/ppermute | solution.py:180
  637.3 41.1 %collective-permute-start.55 = (bf16[128,2304]{1,0:T(8,128)(2,1)S(1)}, bf16[128,2304]{1,0:T(8,128)(2,1)S(1)}, u32[]{:S(2)}, u32[]{:S(2)}) collective-permute-start(bf16[128,2304]{1,0:T(8,128)(2,1)S(1)} %get-tuple-element.382), channel_id=1, source_target_pairs={{0,1},{1,0},{2,3},{3,2},{4,5},{5,4},{6,7},{7,6},{8,9},{9,8},{10,11... | collective-permute-start | bytes 1769480 | tf_op jit(solution)/shard_map/ppermute | solution.py:180
  640.8 37.6 %collective-permute-start.56 = (bf16[144,1152]{1,0:T(8,128)(2,1)S(1)}, bf16[144,1152]{1,0:T(8,128)(2,1)S(1)}, u32[]{:S(2)}, u32[]{:S(2)}) collective-permute-start(bf16[144,1152]{1,0:T(8,128)(2,1)S(1)} %get-tuple-element.471), channel_id=1, source_target_pairs={{0,8},{8,0},{16,24},{24,16},{1,9},{9,1},{17,25},{25,17},{2,10},{10... | collective-permute-start | bytes 995336 | tf_op jit(solution)/shard_map/ppermute | solution.py:180
  640.9 37.5 %collective-permute-start.57 = (bf16[144,1152]{1,0:T(8,128)(2,1)S(1)}, bf16[144,1152]{1,0:T(8,128)(2,1)S(1)}, u32[]{:S(2)}, u32[]{:S(2)}) collective-permute-start(bf16[144,1152]{1,0:T(8,128)(2,1)S(1)} %get-tuple-element.470), channel_id=1, source_target_pairs={{0,16},{8,24},{16,0},{24,8},{1,17},{9,25},{17,1},{25,9},{2,18},{10... | collective-permute-start | bytes 995336 | tf_op jit(solution)/shard_map/ppermute | solution.py:180
  678.4 39.1 %collective-permute-start.62 = (bf16[288,3072]{1,0:T(8,128)(2,1)}, bf16[288,3072]{1,0:T(8,128)(2,1)}, u32[]{:S(2)}, u32[]{:S(2)}) collective-permute-start(bf16[288,3072]{1,0:T(8,128)(2,1)} %get-tuple-element.393), channel_id=1, source_target_pairs={{0,4},{4,0},{1,5},{5,1},{2,6},{6,2},{3,7},{7,3},{8,12},{12,8},{9,1... | collective-permute-start | bytes 5308424 | tf_op jit(solution)/shard_map/ppermute | solution.py:180
  678.8 38.8 %collective-permute-start.63 = (bf16[288,3072]{1,0:T(8,128)(2,1)}, bf16[288,3072]{1,0:T(8,128)(2,1)}, u32[]{:S(2)}, u32[]{:S(2)}) collective-permute-start(bf16[288,3072]{1,0:T(8,128)(2,1)} %add_convert_fusion), channel_id=1, source_target_pairs={{0,8},{8,0},{16,24},{24,16},{1,9},{9,1},{17,25},{25,17},{2,10},{10... | collective-permute-start | bytes 5308424 | tf_op jit(solution)/shard_map/ppermute | solution.py:180
  722.4 38.3 %collective-permute-start.68 = (bf16[144,3072]{1,0:T(8,128)(2,1)}, bf16[144,3072]{1,0:T(8,128)(2,1)}, u32[]{:S(2)}, u32[]{:S(2)}) collective-permute-start(bf16[144,3072]{1,0:T(8,128)(2,1)} %add_convert_fusion.5), channel_id=1, source_target_pairs={{0,16},{8,24},{16,0},{24,8},{1,17},{9,25},{17,1},{25,9},{2,18},{10... | collective-permute-start | bytes 2654216 | tf_op jit(solution)/shard_map/ppermute | solution.py:180
  723.1 37.0 %collective-permute-start.67 = (f32[4,144]{1,0:T(4,128)S(1)}, f32[4,144]{1,0:T(4,128)S(1)}, u32[]{:S(2)}, u32[]{:S(2)}) collective-permute-start(f32[4,144]{1,0:T(4,128)S(1)} %bitcast.110), channel_id=1, source_target_pairs={{0,24},{8,16},{16,8},{24,0},{1,25},{9,17},{17,9},{25,1},{2,26},{10... | collective-permute-start | bytes 6920 | tf_op jit(solution)/shard_map/ppermute | solution.py:180
  724.3 35.9 %collective-permute-start.66 = (f32[4,144]{1,0:T(4,128)S(1)}, f32[4,144]{1,0:T(4,128)S(1)}, u32[]{:S(2)}, u32[]{:S(2)}) collective-permute-start(f32[4,144]{1,0:T(4,128)S(1)} %bitcast.111), channel_id=1, source_target_pairs={{0,16},{8,24},{16,0},{24,8},{1,17},{9,25},{17,1},{25,9},{2,18},{10... | collective-permute-start | bytes 6920 | tf_op jit(solution)/shard_map/ppermute | solution.py:180
  (149 other events, 2067.0 us)
Sparse Core Ops, SparseCore 0:
  13.9 172.7 all-gather.2
  234.2 63.0 all-gather.4
